TPU v7x, 32 devices: a whole 2x2x4 slice. The times are simulated.
32 devices in a mesh: mp: 2 (over y), row: 8 (over z, x), col: 2 (over core).
Axes of the slice: x: 2, y: 2, z: 4, core: 2. Of those that a mesh axis runs over, the one named last changes fastest.
Arguments:
- ancestor_cov: float32 [2048, 4, 2, 128], P(('mp', 'row'), None, 'col'), parts along dimension 0, as said below
- panel_factor: float32 [1536, 2, 512], P(('mp', 'row'), None, 'col'), parts along dimension 0, may hold values from -0.1875 to 0.1875
- diag_inverse: float32 [1024, 2, 512], P('mp', None, 'row'), parts along dimension 0, as said below
- structure: int32 [4, 6], P('mp'), parts along dimension 0, may hold values from 0 to 7, as said below
- live_counts: int32 [4], P('mp'), parts along dimension 0, may hold values from 1 to 6, as said below
Outputs:
- panel_cov: float32 [2048, 2, 512], P(('mp', 'row'), None, 'col'), parts along dimension 0
- diag_cov: float32 [1024, 2, 512], P(('mp', 'row'), None, 'col'), parts along dimension 0
There are 2 independent parts, one for each index of `mp`. A program takes and returns all parts, laid end to end along the dimension named above; each array names one. Nothing has to cross between parts.
Inputs may be any that keep to these rules, and one draw needn't show every extreme that they name: ancestor_cov is symmetric as the matrix C. Each diag_inverse[:, m, :] is lower triangular. `structure`: for each member the first live_counts entries are distinct ancestor tile rows in increasing order; the later entries are padding and are not used. `live_counts`: in every draw one of the two supernodes uses all 6 slots.
All inputs are finite; a program needn't handle non-finite values.
Results may differ from a plain program's by a relative error of at most 0.0001.
Values sent between devices are 32-bit elements; how exact they have to be, the bound alone decides.
No kernel may reach another device: no remote copies, remote signals or barrier semaphores. Data moves between devices by JAX's collectives and lax.ppermute only.
A program may use at most 128 MiB of HBM per device.

v0:
```python
import jax
import jax.numpy as jnp
from jax import lax
from jax.sharding import PartitionSpec as P


def local(ancestor_cov, panel_factor, diag_inverse, structure, live_counts):
    tile_rows = ancestor_cov.shape[0]
    local_blocks = ancestor_cov.shape[1]
    col_count = lax.axis_size("col")
    col_id = lax.axis_index("col")
    row_id = lax.axis_index("row")
    flat_cov = ancestor_cov.reshape(tile_rows, local_blocks * tile_rows)
    half_width = panel_factor.shape[2]
    slot_total = structure.shape[1]
    whole_inverse = lax.all_gather(diag_inverse, "row", axis=2, tiled=True)
    inverse_part = lax.dynamic_slice_in_dim(whole_inverse, col_id * half_width, half_width, 0)
    factor_term = jnp.einsum(
        "rsk,ksn->rsn", panel_factor, inverse_part, precision=lax.Precision.HIGHEST
    )
    slot_index = jnp.arange(slot_total, dtype=jnp.int32)
    slot_alive = slot_index[None, :] < live_counts[:, None]
    own_slot = slot_alive & (structure == row_id)
    in_struct = jnp.any(own_slot, axis=1)
    own_pos = jnp.sum(jnp.where(own_slot, slot_index[None, :], 0), axis=1)
    tile_offsets = jnp.arange(tile_rows, dtype=jnp.int32)
    factor_rows = lax.psum(factor_term, "col")
    arrived = lax.all_gather(factor_rows, "row", axis=0, tiled=True)
    row_count = arrived.shape[0]
    global_row = jnp.arange(row_count, dtype=jnp.int32)
    slot_of = global_row // tile_rows
    offset = global_row % tile_rows
    chooser = (slot_of[:, None] == slot_index[None, :]).astype(jnp.int32)
    product_list = []
    owned_list = []
    for member in range(2):
        anc_block = jnp.sum(chooser * structure[member][None, :], axis=1)
        is_live = slot_of < live_counts[member]
        is_match = is_live & (anc_block % col_count == col_id)
        column_index = anc_block // col_count * tile_rows + offset
        sig_cols = jnp.take(flat_cov, column_index, axis=1)
        weighted = jnp.where(is_match[:, None], arrived[:, member, :], 0.0)
        product_list.append(
            jnp.dot(
                sig_cols,
                weighted,
                precision=lax.Precision.HIGHEST,
                preferred_element_type=jnp.float32,
            )
        )
        source = own_pos[member] * tile_rows + tile_offsets
        in_range = in_struct[member] & (source >= 0) & (source < row_count)
        fetched = jnp.take(arrived[:, member, :], jnp.clip(source, 0, row_count - 1), axis=0)
        owned_list.append(jnp.where(in_range[:, None], fetched, 0.0))
    partial_sum = jnp.stack(product_list, axis=1)
    owned = jnp.stack(owned_list, axis=1)
    summed_all = lax.psum(partial_sum, "col")
    product_half = lax.dynamic_slice_in_dim(summed_all, col_id * half_width, half_width, 2)
    panel_cov = -product_half * in_struct.astype(jnp.float32)[None, :, None]
    spread_term = lax.psum_scatter(
        jnp.einsum("tsi,tsn->isn", owned, product_half, precision=lax.Precision.HIGHEST),
        "row",
        scatter_dimension=0,
        tiled=True,
    )
    inverse_half = lax.dynamic_slice_in_dim(whole_inverse, col_id * half_width, half_width, 2)
    base_term = jnp.einsum(
        "ksi,ksn->isn", diag_inverse, inverse_half, precision=lax.Precision.HIGHEST
    )
    diag_cov = base_term + spread_term
    return (panel_cov, diag_cov)


def solution(mesh):
    placed = (
        P(("mp", "row"), None, "col", None),
        P(("mp", "row"), None, "col"),
        P("mp", None, "row"),
        P("mp", None),
        P("mp"),
    )
    return jax.shard_map(
        local,
        mesh=mesh,
        in_specs=placed,
        out_specs=(P(("mp", "row"), None, "col"), P(("mp", "row"), None, "col")),
        check_vma=False,
    )
```

profile of v0, /device:TPU:1, one launch (start us, length us, event | category | flops | bytes accessed | tf_op | source)
XLA Modules:
  0.0 246.8 jit_solution(8577177868238596412)
XLA Ops:
  7.2 1.9 copy.24
  9.2 51.8 %all-gather.3.cloned.1.call-done = f32[512,2,512]{0,1,2:T(2,128)} async-done(((f32[512,2,64]{0,1,2:T(2,128)}), f32[512,2,512]{0,1,2:T(2,128)}) %all-gather.3.cloned.1.call-update) | async-done | bytes 2097168 | tf_op jit(solution)/shard_map/all_gather | solution.py:16
  61.0 1.6 constant_dynamic-slice_fusion.1
  62.6 1.9 convolution_bitcast_fusion.1
  64.6 18.6 %all-reduce.3.cloned.1.call-done = f32[96,2,512]{2,0,1:T(8,128)} async-done(((f32[96,2,512]{2,0,1:T(8,128)}), f32[96,2,512]{2,0,1:T(8,128)}) %all-reduce.3.cloned.1.call-update) | async-done | bytes 393232 | tf_op jit(solution)/shard_map/psum | solution.py:27
  83.5 0.6 fusion.58
  86.2 1.3 compare_and_fusion
  87.5 2.3 gather_fusion.1
  89.8 1.6 gather_fusion
  92.1 1.3 compare_and_fusion.4
  93.5 52.7 %all-gather.5.cloned.1.call-done = f32[768,2,512]{2,0,1:T(8,128)} async-done(((f32[96,2,512]{2,0,1:T(8,128)}), f32[768,2,512]{2,0,1:T(8,128)}) %all-gather.5.cloned.1.call-update) | async-done | bytes 3145744 | tf_op jit(solution)/shard_map/all_gather | solution.py:28
  146.1 2.7 %fusion.4 = f32[128,1,512]{2,0,1:T(8,128)S(1)} fusion(pred[768]{0:T(1024)(128)(4,1)S(1)} %get-tuple-element.36, f32[768,128]{1,0:T(8,128)S(1)} %gather_fusion, pred[768]{0:T(1024)(128)(4,1)S(1)} %get-tuple-element.37, f32[768,2,512]{2,0,1:T(8,128)} %all-gather.5.cloned.1.call-done), kind=kOutput, calls=%fused_computation.12 | convolution fusion | flops 604471296 | bytes 2229760 | tf_op jit(solution)/shard_map/dot_general | solution.py:44
  148.8 3.0 %fusion.7 = f32[128,1,512]{2,0,1:T(8,128)S(1)} fusion(pred[768]{0:T(1024)(128)(4,1)S(1)} %get-tuple-element.21, f32[768,128]{1,0:T(8,128)} %gather_fusion.1, pred[768]{0:T(1024)(128)(4,1)S(1)} %get-tuple-element.16, f32[768,2,512]{2,0,1:T(8,128)} %all-gather.5.cloned.1.call-done), kind=kOutput, calls=%fused_computation.13 | convolution fusion | flops 604471296 | bytes 2229760 | tf_op jit(solution)/shard_map/dot_general | solution.py:44
  151.8 0.8 pad_maximum_fusion
  152.7 1.9 slice_bitcast_fusion.1
  154.7 2.4 gather_fusion.2
  157.1 0.8 gather_fusion.3
  158.1 13.3 %all-reduce.5.cloned.1.call-done = f32[128,2,512]{2,0,1:T(8,128)} async-done(((f32[128,2,512]{2,0,1:T(8,128)}), f32[128,2,512]{2,0,1:T(8,128)}) %all-reduce.5.cloned.1.call-update) | async-done | bytes 524304 | tf_op jit(solution)/shard_map/psum | solution.py:57
  171.4 3.0 %convolution_bitcast_fusion = f32[512,2,256]{2,0,1:T(8,128)} fusion(f32[128,1,512]{2,0,1:T(8,128)S(1)} %fusion.24, f32[128,1,512]{2,0,1:T(8,128)S(1)} %fusion.25, f32[128,2,512]{2,0,1:T(8,128)} %all-reduce.5.cloned.1.call-done, s32[]{:T(128)S(6)} %select_n.92), kind=kOutput, calls=%fused_computation.10 | convolution fusion | flops 402784256 | bytes 1835012 | tf_op jit(solution)/shard_map/tsi,tsn->isn/dot_general | solution.py:61
  174.8 0.6 copy-done.4
  175.5 0.9 copy.30
  176.4 60.9 %reduce-scatter.2.cloned.1.call-done = f32[64,2,256]{2,0,1:T(8,128)} async-done(((f32[512,2,256]{2,0,1:T(8,128)}), f32[64,2,256]{2,0,1:T(8,128)}) %reduce-scatter.2.cloned.1.call-update) | async-done | bytes 131088 | tf_op jit(solution)/shard_map/reduce_scatter | solution.py:60
  237.3 2.2 fusion.10
  239.5 0.8 copy.31
  (44 shorter events, 2.7 us)
Async XLA Ops:
  7.2 55.4 %copy-start = (f32[96,2,256]{2,1,0:T(2,128)S(1)}, f32[96,2,256]{2,1,0:T(2,128)}, u32[]{:S(2)}) copy-start(f32[96,2,256]{2,1,0:T(2,128)} %param.10) | copy-start | bytes 589828
  7.2 53.8 %all-gather.3.cloned.1.call-start = ((), (), s32[]{:S(2)}) async-start(), calls=%async_computation.1 | async-start | bytes 2359296 | tf_op jit(solution)/shard_map/all_gather | solution.py:16
  9.1 74.0 %all-reduce.3.cloned.1.call-start = ((), (), s32[]{:S(2)}) async-start(), calls=%async_computation.2 | async-start | bytes 786432 | tf_op jit(solution)/shard_map/psum | solution.py:27
  62.6 20.7 %copy-start.6 = (s32[2]{0:T(128)S(1)}, s32[2]{0:T(128)}, u32[]{:S(2)}) copy-start(s32[2]{0:T(128)} %param.13) | copy-start | bytes 28
  62.6 20.7 %copy-start.7 = (s32[2,6]{1,0:T(2,128)S(1)}, s32[2,6]{1,0:T(2,128)}, u32[]{:S(2)}) copy-start(s32[2,6]{1,0:T(2,128)} %param.12) | copy-start | bytes 148
  62.6 22.7 %copy-start.5 = (f32[128,4,1,128]{3,2,1,0:T(1,128)S(1)}, f32[128,4,1,128]{3,2,1,0:T(1,128)}, u32[]{:S(2)}) copy-start(f32[128,4,1,128]{3,2,1,0:T(1,128)} %param.9) | copy-start | bytes 786436
  64.6 81.6 %all-gather.5.cloned.1.call-start = ((), (), s32[]{:S(2)}) async-start(), calls=%async_computation.3 | async-start | bytes 3538944 | tf_op jit(solution)/shard_map/all_gather | solution.py:28
  83.2 88.2 %all-reduce.5.cloned.1.call-start = ((), (), s32[]{:S(2)}) async-start(), calls=%async_computation.4 | async-start | bytes 1048576 | tf_op jit(solution)/shard_map/psum | solution.py:57
  148.8 3.9 %copy-start.1 = (f32[768,2,512]{2,0,1:T(8,128)S(1)}, f32[768,2,512]{2,0,1:T(8,128)}, u32[]{:S(2)}) copy-start(f32[768,2,512]{2,0,1:T(8,128)} %all-gather.5.cloned.1.call-done) | copy-start | bytes 9437188
  152.7 84.6 %reduce-scatter.2.cloned.1.call-start = ((), (), s32[]{:S(2)}) async-start(), calls=%async_computation.5 | async-start | bytes 1179648 | tf_op jit(solution)/shard_map/reduce_scatter | solution.py:60
  154.7 2.4 copy-start.2
  158.1 16.3 %copy-start.3 = (f32[512,2,512]{0,1,2:T(2,128)S(1)}, f32[512,2,512]{0,1,2:T(2,128)}, u32[]{:S(2)}) copy-start(f32[512,2,512]{0,1,2:T(2,128)} %all-gather.3.cloned.1.call-done) | copy-start | bytes 6291460
  174.4 1.0 copy-start.4
Sparse Core Ops, SparseCore 0:
  10.7 50.2 all-gather.2
  64.7 18.4 all-reduce.2
  85.6 60.4 all-gather.4
  152.8 18.5 all-reduce.4
  174.7 62.6 reduce-scatter.1
where the time goes:
time: 249 us; the launch traced here: 247 us
  waiting for transfers between devices  197 us (79%)
  local copies, waits for them, and re-layouts  17 us (7%)
  between operations  15.3 us (6%)
  matrix products  12.7 us (5%)
  other arithmetic  4.18 us (2%)
    reduce_scatter x1, waiting for transfers between devices, local(): lax.psum_scatter(jnp.einsum('tsi,tsn->isn', owned, product_half, precisio...  60.9 us
    all_gather x1, waiting for transfers between devices, local(): arrived = lax.all_gather(factor_rows, 'row', axis=0, tiled=True)  52.7 us
    all_gather x1, waiting for transfers between devices, local(): whole_inverse = lax.all_gather(diag_inverse, 'row', axis=2, tiled=True)  51.8 us
    psum x1, waiting for transfers between devices, local(): factor_rows = lax.psum(factor_term, 'col')  18.6 us
    psum x1, waiting for transfers between devices, local(): summed_all = lax.psum(partial_sum, 'col')  13.3 us
    dot_general x2, matrix products, local(): jnp.dot(sig_cols, weighted, precision=lax.Precision.HIGHEST, preferred_el...  5.67 us
  transfers between devices with their start and end apart: 5, of which 5 were waited for; matrix products, arithmetic and copies ran while one was open for 6% of the time, Pallas kernels for 0%

commit v1 on v0

--- a/solution.py
+++ b/solution.py
@@ -1,10 +1,139 @@
+import functools
+
 import jax
 import jax.numpy as jnp
 from jax import lax
+from jax.experimental import pallas as pl
+from jax.experimental.pallas import tpu as pltpu
 from jax.sharding import PartitionSpec as P
 
-
-def local(ancestor_cov, panel_factor, diag_inverse, structure, live_counts):
+F32 = jnp.float32
+BF16 = jnp.bfloat16
+NT = (((1,), (1,)), ((), ()))
+NN = (((1,), (0,)), ((), ()))
+TN = (((0,), (0,)), ((), ()))
+VMEM_LIMIT = 48 * 1024 * 1024
+
+
+def halves(value):
+    high = value.astype(BF16)
+    low = (value - high.astype(F32)).astype(BF16)
+    return high, low
+
+
+def dot3(left, right, dims):
+    left_high, left_low = left
+    right_high, right_low = right
+
+    def one(a, b):
+        return lax.dot_general(a, b, dims, preferred_element_type=F32)
+
+    return one(left_high, right_low) + one(left_low, right_high) + one(left_high, right_high)
+
+
+def main_kernel(rows, tile, slots, *refs):
+    structure, live, place = refs[:3]
+    c_own, c_sib, c_near, c_near_sib = refs[3:7]
+    factor_blocks = refs[7:7 + rows]
+    inverse_blocks = refs[7 + rows:7 + 2 * rows]
+    panel_keep, panel_send = refs[7 + 2 * rows:9 + 2 * rows]
+    diag_out = refs[9 + 2 * rows:9 + 3 * rows]
+    pick_high, pick_low, f_high, f_low, d_high, d_low, own_f, diag_part = refs[9 + 3 * rows:]
+    row = place[0]
+    col = place[1]
+    share = factor_blocks[0].shape[0]
+    width = inverse_blocks[0].shape[0]
+    half = panel_keep.shape[1]
+    for step in range(rows):
+        source = row ^ step
+        high, low = halves(factor_blocks[step][...])
+        at = pl.ds(pl.multiple_of(source * share, share), share)
+        f_high[at, :] = high
+        f_low[at, :] = low
+        high, low = halves(inverse_blocks[step][...])
+        at = pl.ds(pl.multiple_of(source * width, width), width)
+        d_high[at, :] = high
+        d_low[at, :] = low
+    local_blocks = c_own.shape[0] // tile
+    for slot in range(slots):
+        anc = structure[col, slot]
+        alive = slot < live[col]
+        block = anc // 2
+        mine = anc % 2 == col
+        for part, (here, there) in enumerate(((c_own, c_sib), (c_near, c_near_sib))):
+            at = pl.ds(block, tile, stride=local_blocks)
+            value = jnp.where(mine, here[at, :], there[at, :])
+            value = jnp.where(alive, value, 0.0)
+            high, low = halves(value)
+            pick_high[part * tile:(part + 1) * tile, slot * tile:(slot + 1) * tile] = high
+            pick_low[part * tile:(part + 1) * tile, slot * tile:(slot + 1) * tile] = low
+    inverse = (d_high[...], d_low[...])
+    own_f[...] = jnp.zeros_like(own_f)
+    in_struct = False
+    for slot in range(slots):
+        alive = slot < live[col]
+        for part in range(2):
+            hit = alive & (structure[col, slot] == row ^ part)
+            if part == 0:
+                in_struct = in_struct | hit
+
+            @pl.when(hit)
+            def _(slot=slot, part=part):
+                own_f[0, part * tile:(part + 1) * tile, :] = f_high[slot * tile:(slot + 1) * tile, :]
+                own_f[1, part * tile:(part + 1) * tile, :] = f_low[slot * tile:(slot + 1) * tile, :]
+
+    grown = dot3((pick_high[...], pick_low[...]), (f_high[...], f_low[...]), NN)
+    product = dot3(halves(grown), inverse, NT)
+    scaled = dot3((own_f[0], own_f[1]), inverse, NT)
+    panel = jnp.where(in_struct, -product[:tile], 0.0)
+
+    @pl.when(col == 0)
+    def _():
+        panel_keep[...] = panel[:, :half]
+        panel_send[...] = panel[:, half:]
+
+    @pl.when(col == 1)
+    def _():
+        panel_keep[...] = panel[:, half:]
+        panel_send[...] = panel[:, :half]
+
+    diag_part[...] = dot3(halves(scaled), halves(product), TN)
+    at = pl.ds(pl.multiple_of(row * width, width), width)
+    base = dot3((d_high[at, :], d_low[at, :]), inverse, NT)
+    diag_part[at, :] = diag_part[at, :] + base
+    for step in range(rows // 2):
+        at = pl.ds(pl.multiple_of((row ^ (2 * step)) * width, width), width)
+        block = diag_part[at, :]
+        for other in range(2):
+            @pl.when(col == other)
+            def _():
+                diag_out[2 * step][...] = block[:, other * half:(other + 1) * half]
+                diag_out[2 * step + 1][...] = block[:, (1 - other) * half:(2 - other) * half]
+
+
+def last_kernel(count, *refs):
+    place, keep, got = refs[:3]
+    pieces = refs[3:3 + count]
+    panel_out, diag_out = refs[3 + count:]
+    col = place[1]
+    lanes = 128
+    same = pieces[0][...]
+    cross = pieces[1][...]
+    for step in range(1, count // 2):
+        same = same + pieces[2 * step][...]
+        cross = cross + pieces[2 * step + 1][...]
+    values = ((panel_out, keep[...], got[...]), (diag_out, same, cross))
+    for out, mine, other in values:
+        first = jnp.where(col == 0, mine, other)
+        second = jnp.where(col == 0, other, mine)
+        lane_blocks = mine.shape[1] // lanes
+        for block in range(lane_blocks):
+            at = slice(block * lanes, (block + 1) * lanes)
+            out[pl.ds(2 * block, mine.shape[0], stride=2 * lane_blocks), :] = first[:, at]
+            out[pl.ds(2 * block + 1, mine.shape[0], stride=2 * lane_blocks), :] = second[:, at]
+
+
+def many_rows(ancestor_cov, panel_factor, diag_inverse, structure, live_counts):
     tile_rows = ancestor_cov.shape[0]
     local_blocks = ancestor_cov.shape[1]
     col_count = lax.axis_size("col")
@@ -71,6 +200,85 @@
     return (panel_cov, diag_cov)
 
 
+def local(ancestor_cov, panel_factor, diag_inverse, structure, live_counts):
+    rows = lax.axis_size("row")
+    if rows != 8:
+        return many_rows(ancestor_cov, panel_factor, diag_inverse, structure, live_counts)
+    tile = ancestor_cov.shape[0]
+    local_blocks = ancestor_cov.shape[1]
+    share, _, half = panel_factor.shape
+    whole, _, width = diag_inverse.shape
+    slots = structure.shape[1]
+    col = lax.axis_index("col")
+    row = lax.axis_index("row")
+
+    def move(value, step, flip):
+        pairs = [
+            (r * 2 + c, (r ^ step) * 2 + (c ^ flip)) for r in range(rows) for c in range(2)
+        ]
+        return lax.ppermute(value, ("row", "col"), pairs)
+
+    c_own = ancestor_cov.reshape(tile * local_blocks, 128)
+    c_near = move(c_own, 1, 0)
+    c_sib = move(c_own, 0, 1)
+    inverse_own = lax.dynamic_index_in_dim(diag_inverse.transpose(1, 2, 0), col, 0, keepdims=False)
+    f_keep = lax.dynamic_index_in_dim(panel_factor, col, 1, keepdims=False)
+    f_send = lax.dynamic_index_in_dim(panel_factor, 1 - col, 1, keepdims=False)
+    f_got = move(f_send, 0, 1)
+    inverse = [inverse_own] + [move(inverse_own, 2 * k, 0) for k in range(1, rows // 2)]
+    factor_own = jnp.concatenate(
+        [jnp.where(col == 0, f_keep, f_got), jnp.where(col == 0, f_got, f_keep)], axis=1
+    )
+    factor = [factor_own] + [move(factor_own, 2 * k, 0) for k in range(1, rows // 2)]
+    c_near_sib = move(c_near, 0, 1)
+    inverse_near = [move(value, 1, 0) for value in inverse]
+    factor_near = [move(value, 1, 0) for value in factor]
+    inverse_blocks = [v for pair in zip(inverse, inverse_near) for v in pair]
+    factor_blocks = [v for pair in zip(factor, factor_near) for v in pair]
+    place = jnp.stack([row, col]).astype(jnp.int32)
+    smem = pl.BlockSpec(memory_space=pltpu.SMEM)
+    vmem = pl.BlockSpec(memory_space=pltpu.VMEM)
+    outs = pl.pallas_call(
+        functools.partial(main_kernel, rows, tile, slots),
+        out_shape=[jax.ShapeDtypeStruct((tile, half), F32)] * 2
+        + [jax.ShapeDtypeStruct((width, half), F32)] * rows,
+        in_specs=[smem] * 3 + [vmem] * (4 + 2 * rows),
+        out_specs=[vmem] * (2 + rows),
+        scratch_shapes=[
+            pltpu.VMEM((2 * tile, slots * tile), BF16),
+            pltpu.VMEM((2 * tile, slots * tile), BF16),
+            pltpu.VMEM((slots * tile, whole), BF16),
+            pltpu.VMEM((slots * tile, whole), BF16),
+            pltpu.VMEM((whole, whole), BF16),
+            pltpu.VMEM((whole, whole), BF16),
+            pltpu.VMEM((2, 2 * tile, whole), BF16),
+            pltpu.VMEM((whole, whole), F32),
+        ],
+        compiler_params=pltpu.CompilerParams(vmem_limit_bytes=VMEM_LIMIT),
+        name="products",
+    )(structure, live_counts, place, c_own, c_sib, c_near, c_near_sib, *factor_blocks, *inverse_blocks)
+    panel_keep, panel_send = outs[:2]
+    diag_pieces = outs[2:]
+    pieces = [diag_pieces[0]] + [move(diag_pieces[j], 2 * (j // 2), j % 2) for j in range(1, rows)]
+    panel_got = move(panel_send, 0, 1)
+    panel, diag = pl.pallas_call(
+        functools.partial(last_kernel, rows),
+        out_shape=[
+            jax.ShapeDtypeStruct((tile * 2 * half // 128, 128), F32),
+            jax.ShapeDtypeStruct((width * 2 * half // 128, 128), F32),
+        ],
+        in_specs=[smem] + [vmem] * (2 + rows),
+        out_specs=[vmem] * 2,
+        compiler_params=pltpu.CompilerParams(vmem_limit_bytes=VMEM_LIMIT),
+        name="sums",
+    )(place, panel_keep, panel_got, *pieces)
+
+    def unfold(value, count):
+        return value.reshape(count, half // 128, 2, 128).transpose(0, 2, 1, 3).reshape(count, 2, half)
+
+    return unfold(panel, tile), unfold(diag, width)
+
+
 def solution(mesh):
     placed = (
         P(("mp", "row"), None, "col", None),

time: 249 us -> 75.6 us (0.30)
  waiting for transfers between devices: 197 us -> 29 us
  starting transfers between devices: 0.2 us -> 33.5 us
  between operations: 15.3 us -> 0.74 us
  matrix products: 12.7 us -> 0 us
  local copies, waits for them, and re-layouts: 17 us -> 5.8 us
  Pallas kernels: 0 us -> 5.56 us
  other arithmetic: 4.18 us -> 0.1 us
    all_gather x2 -> x0, waiting for transfers between devices: 104 us -> none  [the longest x1 52.7 us: local(): arrived = lax.all_gather(factor_rows, 'row', axis=0, tiled=True)]
    reduce_scatter x1 -> x0, waiting for transfers between devices: 60.9 us -> none  [local(): lax.psum_scatter(jnp.einsum('tsi,tsn->isn', owned, product_half, precisio...]
    ppermute x0 -> x26, starting transfers between devices: none -> 33.5 us  [move(): return lax.ppermute(value, ('row', 'col'), pairs)]
    psum x2 -> x0, waiting for transfers between devices: 31.9 us -> none  [the longest x1 18.6 us: local(): factor_rows = lax.psum(factor_term, 'col')]
    ppermute x0 -> x26, waiting for transfers between devices: none -> 29 us  [move(): return lax.ppermute(value, ('row', 'col'), pairs)]
    dot_general x5 -> x0, matrix products: 12.7 us -> none  [the longest x2 5.67 us: local(): jnp.dot(sig_cols, weighted, precision=lax.Precision.HIGHEST, preferred_el...]
    gather x4 -> x0, local copies, waits for them, and re-layouts: 7.01 us -> none  [the longest x2 3.85 us: local(): sig_cols = jnp.take(flat_cov, column_index, axis=1)]
    pallas_call x0 -> x2, Pallas kernels: none -> 5.56 us  [the longest x1 4.21 us: local(): pl.pallas_call(functools.partial(main_kernel, rows, tile, slots), out_sha...]
  transfers between devices with their start and end apart: 5 -> 26, of which waited for: 5 -> 7; matrix products, arithmetic and copies ran while one was open for 6% -> 0% of each run, Pallas kernels for 0% -> 0%
where the time goes in v1:
time: 75.6 us; the launch traced here: 74.7 us
  starting transfers between devices  33.5 us (44%)
  waiting for transfers between devices  29 us (38%)
  local copies, waits for them, and re-layouts  5.8 us (8%)
  Pallas kernels  5.56 us (7%)
    ppermute x26, starting transfers between devices, move(): return lax.ppermute(value, ('row', 'col'), pairs)  33.5 us
    ppermute x26, waiting for transfers between devices, move(): return lax.ppermute(value, ('row', 'col'), pairs)  29 us
    unnamed x23, local copies, waits for them, and re-layouts  5.62 us
    pallas_call x1, Pallas kernels, local(): pl.pallas_call(functools.partial(main_kernel, rows, tile, slots), out_sha...  4.21 us
  transfers between devices with their start and end apart: 26, of which 7 were waited for; matrix products, arithmetic and copies ran while one was open for 0% of the time, Pallas kernels for 0%

profile of v1, /device:TPU:1, one launch (start us, length us, event | category | flops | bytes accessed | tf_op | source)
XLA Modules:
  0.0 74.7 jit_solution(9985718805179151166)
XLA Ops:
  1.6 4.2 %collective-permute-start.16 = (f32[64,512]{1,0:T(8,128)S(1)}, f32[64,512]{1,0:T(8,128)S(1)}, u32[]{:S(2)}, u32[]{:S(2)}) collective-permute-start(f32[64,512]{1,0:T(8,128)S(1)} %dynamic-slice_bitcast_fusion.refs_15_), channel_id=1, source_target_pairs={{0,12},{1,13},{2,14},{3,15},{4,8},{5,9},{6,10},{7,11},{8,4},{9,5},... | collective-permute-start | bytes 393224 | tf_op jit(solution)/shard_map/ppermute | solution.py:219
  6.4 1.3 %collective-permute-start.3 = (f32[96,256]{1,0:T(8,128)S(1)}, f32[96,256]{1,0:T(8,128)S(1)}, u32[]{:S(2)}, u32[]{:S(2)}) collective-permute-start(f32[96,256]{1,0:T(8,128)S(1)} %bitcast.29), channel_id=1, source_target_pairs={{0,1},{1,0},{2,3},{3,2},{4,5},{5,4},{6,7},{7,6},{8,9},{9,8},{10,11... | collective-permute-start | bytes 294920 | tf_op jit(solution)/shard_map/ppermute | solution.py:219
  7.7 1.4 %collective-permute-start.11 = (f32[64,512]{1,0:T(8,128)S(1)}, f32[64,512]{1,0:T(8,128)S(1)}, u32[]{:S(2)}, u32[]{:S(2)}) collective-permute-start(f32[64,512]{1,0:T(8,128)S(1)} %dynamic-slice_bitcast_fusion.refs_15_), channel_id=1, source_target_pairs={{0,2},{1,3},{2,0},{3,1},{4,6},{5,7},{6,4},{7,5},{8,10},{9,11},{10,... | collective-permute-start | bytes 393224 | tf_op jit(solution)/shard_map/ppermute | solution.py:219
  10.5 6.0 %collective-permute-done.14.refs_19_ = f32[64,512]{1,0:T(8,128)S(1)} collective-permute-done((f32[64,512]{1,0:T(8,128)S(1)}, f32[64,512]{1,0:T(8,128)S(1)}, u32[]{:S(2)}, u32[]{:S(2)}) %collective-permute-start.14) | collective-permute-done | bytes 131104 | tf_op jit(solution)/shard_map/ppermute | solution.py:219
  16.5 1.2 %collective-permute-start.15 = (f32[64,512]{1,0:T(8,128)S(1)}, f32[64,512]{1,0:T(8,128)S(1)}, u32[]{:S(2)}, u32[]{:S(2)}) collective-permute-start(f32[64,512]{1,0:T(8,128)S(1)} %collective-permute-done.14.refs_19_), channel_id=1, source_target_pairs={{0,2},{1,3},{2,0},{3,1},{4,6},{5,7},{6,4},{7,5},{8,10},{9,11},{10,... | collective-permute-start | bytes 393224 | tf_op jit(solution)/shard_map/ppermute | solution.py:219
  18.0 2.0 %collective-permute-start = (f32[512,128]{1,0:T(8,128)S(1)}, f32[512,128]{1,0:T(8,128)S(1)}, u32[]{:S(2)}, u32[]{:S(2)}) collective-permute-start(f32[512,128]{1,0:T(8,128)S(1)} %bitcast.27), channel_id=1, source_target_pairs={{0,1},{1,0},{2,3},{3,2},{4,5},{5,4},{6,7},{7,6},{8,9},{9,8},{10,11... | collective-permute-start | bytes 786440 | tf_op jit(solution)/shard_map/ppermute | solution.py:219
  20.0 1.2 %collective-permute-done.17.refs_22_ = f32[64,512]{1,0:T(8,128)S(1)} collective-permute-done((f32[64,512]{1,0:T(8,128)S(1)}, f32[64,512]{1,0:T(8,128)S(1)}, u32[]{:S(2)}, u32[]{:S(2)}) %collective-permute-start.17) | collective-permute-done | bytes 131104 | tf_op jit(solution)/shard_map/ppermute | solution.py:219
  21.8 3.5 %collective-permute-start.9 = (f32[96,512]{1,0:T(8,128)S(1)}, f32[96,512]{1,0:T(8,128)S(1)}, u32[]{:S(2)}, u32[]{:S(2)}) collective-permute-start(f32[96,512]{1,0:T(8,128)S(1)} %pad_maximum_fusion.refs_7_), channel_id=1, source_target_pairs={{0,12},{1,13},{2,14},{3,15},{4,8},{5,9},{6,10},{7,11},{8,4},{9,5},... | collective-permute-start | bytes 589832 | tf_op jit(solution)/shard_map/ppermute | solution.py:219
  27.5 1.6 %collective-permute-start.5 = (f32[96,512]{1,0:T(8,128)S(1)}, f32[96,512]{1,0:T(8,128)S(1)}, u32[]{:S(2)}, u32[]{:S(2)}) collective-permute-start(f32[96,512]{1,0:T(8,128)S(1)} %pad_maximum_fusion.refs_7_), channel_id=1, source_target_pairs={{0,4},{1,5},{2,6},{3,7},{4,0},{5,1},{6,2},{7,3},{8,12},{9,13},{10,... | collective-permute-start | bytes 589832 | tf_op jit(solution)/shard_map/ppermute | solution.py:219
  29.1 1.9 %collective-permute-start.2 = (f32[512,128]{1,0:T(8,128)S(1)}, f32[512,128]{1,0:T(8,128)S(1)}, u32[]{:S(2)}, u32[]{:S(2)}) collective-permute-start(f32[512,128]{1,0:T(8,128)S(1)} %collective-permute-done.1.refs_5_), channel_id=1, source_target_pairs={{0,1},{1,0},{2,3},{3,2},{4,5},{5,4},{6,7},{7,6},{8,9},{9,8},{10,11... | collective-permute-start | bytes 786440 | tf_op jit(solution)/shard_map/ppermute | solution.py:219
  30.9 1.2 %collective-permute-start.4 = (f32[96,512]{1,0:T(8,128)S(1)}, f32[96,512]{1,0:T(8,128)S(1)}, u32[]{:S(2)}, u32[]{:S(2)}) collective-permute-start(f32[96,512]{1,0:T(8,128)S(1)} %pad_maximum_fusion.refs_7_), channel_id=1, source_target_pairs={{0,2},{1,3},{2,0},{3,1},{4,6},{5,7},{6,4},{7,5},{8,10},{9,11},{10,... | collective-permute-start | bytes 589832 | tf_op jit(solution)/shard_map/ppermute | solution.py:219
  32.4 8.5 %collective-permute-done.7.refs_11_ = f32[96,512]{1,0:T(8,128)S(1)} collective-permute-done((f32[96,512]{1,0:T(8,128)S(1)}, f32[96,512]{1,0:T(8,128)S(1)}, u32[]{:S(2)}, u32[]{:S(2)}) %collective-permute-start.7) | collective-permute-done | bytes 196640 | tf_op jit(solution)/shard_map/ppermute | solution.py:219
  40.9 1.2 %collective-permute-start.8 = (f32[96,512]{1,0:T(8,128)S(1)}, f32[96,512]{1,0:T(8,128)S(1)}, u32[]{:S(2)}, u32[]{:S(2)}) collective-permute-start(f32[96,512]{1,0:T(8,128)S(1)} %collective-permute-done.7.refs_11_), channel_id=1, source_target_pairs={{0,2},{1,3},{2,0},{3,1},{4,6},{5,7},{6,4},{7,5},{8,10},{9,11},{10,... | collective-permute-start | bytes 589832 | tf_op jit(solution)/shard_map/ppermute | solution.py:219
  42.4 3.0 %collective-permute-done.8.refs_12_ = f32[96,512]{1,0:T(8,128)S(1)} collective-permute-done((f32[96,512]{1,0:T(8,128)S(1)}, f32[96,512]{1,0:T(8,128)S(1)}, u32[]{:S(2)}, u32[]{:S(2)}) %collective-permute-start.8) | collective-permute-done | bytes 196640 | tf_op jit(solution)/shard_map/ppermute | solution.py:219
  45.4 4.3 %collective-permute-done.6.refs_10_ = f32[96,512]{1,0:T(8,128)S(1)} collective-permute-done((f32[96,512]{1,0:T(8,128)S(1)}, f32[96,512]{1,0:T(8,128)S(1)}, u32[]{:S(2)}, u32[]{:S(2)}) %collective-permute-start.6) | collective-permute-done | bytes 196640 | tf_op jit(solution)/shard_map/ppermute | solution.py:219
  52.5 4.2 %products.1 = (f32[128,256]{1,0:T(8,128)S(1)}, f32[128,256]{1,0:T(8,128)S(1)}, f32[64,256]{1,0:T(8,128)S(1)}, f32[64,256]{1,0:T(8,128)S(1)}, f32[64,256]{1,0:T(8...) custom-call(s32[2,6]{1,0:T(2,128)S(1)} %copy-done.8, ...), custom_call_target="tpu_custom_call" | custom-call | tf_op jit(solution)/shard_map/products/pallas_call | solution.py:241
  56.7 2.7 %collective-permute-start.19 = (f32[64,256]{1,0:T(8,128)S(1)}, f32[64,256]{1,0:T(8,128)S(1)}, u32[]{:S(2)}, u32[]{:S(2)}) collective-permute-start(f32[64,256]{1,0:T(8,128)S(1)} %get-tuple-element.17), channel_id=1, source_target_pairs={{0,1},{1,0},{2,3},{3,2},{4,5},{5,4},{6,7},{7,6},{8,9},{9,8},{10,11... | collective-permute-start | bytes 196616 | tf_op jit(solution)/shard_map/ppermute | solution.py:219
  59.4 1.1 %collective-permute-start.20 = (f32[64,256]{1,0:T(8,128)S(1)}, f32[64,256]{1,0:T(8,128)S(1)}, u32[]{:S(2)}, u32[]{:S(2)}) collective-permute-start(f32[64,256]{1,0:T(8,128)S(1)} %get-tuple-element.18), channel_id=1, source_target_pairs={{0,4},{1,5},{2,6},{3,7},{4,0},{5,1},{6,2},{7,3},{8,12},{9,13},{10,... | collective-permute-start | bytes 196616 | tf_op jit(solution)/shard_map/ppermute | solution.py:219
  61.3 1.4 %collective-permute-start.22 = (f32[64,256]{1,0:T(8,128)S(1)}, f32[64,256]{1,0:T(8,128)S(1)}, u32[]{:S(2)}, u32[]{:S(2)}) collective-permute-start(f32[64,256]{1,0:T(8,128)S(1)} %get-tuple-element.20), channel_id=1, source_target_pairs={{0,8},{1,9},{2,10},{3,11},{4,12},{5,13},{6,14},{7,15},{8,0},{9,1},... | collective-permute-start | bytes 196616 | tf_op jit(solution)/shard_map/ppermute | solution.py:219
  62.6 1.5 %collective-permute-start.23 = (f32[64,256]{1,0:T(8,128)S(1)}, f32[64,256]{1,0:T(8,128)S(1)}, u32[]{:S(2)}, u32[]{:S(2)}) collective-permute-start(f32[64,256]{1,0:T(8,128)S(1)} %get-tuple-element.21), channel_id=1, source_target_pairs={{0,9},{1,8},{2,11},{3,10},{4,13},{5,12},{6,15},{7,14},{8,1},{9,0},... | collective-permute-start | bytes 196616 | tf_op jit(solution)/shard_map/ppermute | solution.py:219
  64.1 1.7 %collective-permute-start.24 = (f32[64,256]{1,0:T(8,128)S(1)}, f32[64,256]{1,0:T(8,128)S(1)}, u32[]{:S(2)}, u32[]{:S(2)}) collective-permute-start(f32[64,256]{1,0:T(8,128)S(1)} %get-tuple-element.22), channel_id=1, source_target_pairs={{0,12},{1,13},{2,14},{3,15},{4,8},{5,9},{6,10},{7,11},{8,4},{9,5},... | collective-permute-start | bytes 196616 | tf_op jit(solution)/shard_map/ppermute | solution.py:219
  65.9 1.6 %collective-permute-start.25 = (f32[64,256]{1,0:T(8,128)S(1)}, f32[64,256]{1,0:T(8,128)S(1)}, u32[]{:S(2)}, u32[]{:S(2)}) collective-permute-start(f32[64,256]{1,0:T(8,128)S(1)} %get-tuple-element.23), channel_id=1, source_target_pairs={{0,13},{1,12},{2,15},{3,14},{4,9},{5,8},{6,11},{7,10},{8,5},{9,4},... | collective-permute-start | bytes 196616 | tf_op jit(solution)/shard_map/ppermute | solution.py:219
  67.5 5.8 %collective-permute-done.23.refs_8_ = f32[64,256]{1,0:T(8,128)S(1)} collective-permute-done((f32[64,256]{1,0:T(8,128)S(1)}, f32[64,256]{1,0:T(8,128)S(1)}, u32[]{:S(2)}, u32[]{:S(2)}) %collective-permute-start.23) | collective-permute-done | bytes 65568 | tf_op jit(solution)/shard_map/ppermute | solution.py:219
  73.4 1.4 %sums.1 = (f32[512,128]{1,0:T(8,128)}, f32[256,128]{1,0:T(8,128)}) custom-call(s32[2]{0:T(128)S(1)} %pad_add_fusion.refs_2_.refs_0_, f32[128,256]{1,0:T(8,128)S(1)} %get-tuple-element.14.refs_1_, f32[128,256]{1,0:T(8,128)S(1)} %collective-permute-done.18.refs_2_, f32[64,256]{1,0:T(8,128)S(1)} %get-tuple-element.16.refs_3_, ...), custom_call_target="tpu_custom_call" | custom-call | tf_op jit(solution)/shard_map/sums/pallas_call | solution.py:264
  (58 shorter events, 10.2 us)
Async XLA Ops:
  1.6 8.4 %collective-permute-start.16 = (f32[64,512]{1,0:T(8,128)S(1)}, f32[64,512]{1,0:T(8,128)S(1)}, u32[]{:S(2)}, u32[]{:S(2)}) collective-permute-start(f32[64,512]{1,0:T(8,128)S(1)} %dynamic-slice_bitcast_fusion.refs_15_), channel_id=1, source_target_pairs={{0,12},{1,13},{2,14},{3,15},{4,8},{5,9},{6,10},{7,11},{8,4},{9,5},... | collective-permute-start | bytes 393224 | tf_op jit(solution)/shard_map/ppermute | solution.py:219
  5.8 10.7 %collective-permute-start.14 = (f32[64,512]{1,0:T(8,128)S(1)}, f32[64,512]{1,0:T(8,128)S(1)}, u32[]{:S(2)}, u32[]{:S(2)}) collective-permute-start(f32[64,512]{1,0:T(8,128)S(1)} %dynamic-slice_bitcast_fusion.refs_15_), channel_id=1, source_target_pairs={{0,8},{1,9},{2,10},{3,11},{4,12},{5,13},{6,14},{7,15},{8,0},{9,1},... | collective-permute-start | bytes 393224 | tf_op jit(solution)/shard_map/ppermute | solution.py:219
  5.8 11.9 %collective-permute-start.12 = (f32[64,512]{1,0:T(8,128)S(1)}, f32[64,512]{1,0:T(8,128)S(1)}, u32[]{:S(2)}, u32[]{:S(2)}) collective-permute-start(f32[64,512]{1,0:T(8,128)S(1)} %dynamic-slice_bitcast_fusion.refs_15_), channel_id=1, source_target_pairs={{0,4},{1,5},{2,6},{3,7},{4,0},{5,1},{6,2},{7,3},{8,12},{9,13},{10,... | collective-permute-start | bytes 393224 | tf_op jit(solution)/shard_map/ppermute | solution.py:219
  7.7 10.3 %collective-permute-start.11 = (f32[64,512]{1,0:T(8,128)S(1)}, f32[64,512]{1,0:T(8,128)S(1)}, u32[]{:S(2)}, u32[]{:S(2)}) collective-permute-start(f32[64,512]{1,0:T(8,128)S(1)} %dynamic-slice_bitcast_fusion.refs_15_), channel_id=1, source_target_pairs={{0,2},{1,3},{2,0},{3,1},{4,6},{5,7},{6,4},{7,5},{8,10},{9,11},{10,... | collective-permute-start | bytes 393224 | tf_op jit(solution)/shard_map/ppermute | solution.py:219
  9.1 20.0 %collective-permute-start.1 = (f32[512,128]{1,0:T(8,128)S(1)}, f32[512,128]{1,0:T(8,128)S(1)}, u32[]{:S(2)}, u32[]{:S(2)}) collective-permute-start(f32[512,128]{1,0:T(8,128)S(1)} %bitcast.26), channel_id=1, source_target_pairs={{0,2},{1,3},{2,0},{3,1},{4,6},{5,7},{6,4},{7,5},{8,10},{9,11},{10,... | collective-permute-start | bytes 786440 | tf_op jit(solution)/shard_map/ppermute | solution.py:219
  10.0 11.2 %collective-permute-start.17 = (f32[64,512]{1,0:T(8,128)S(1)}, f32[64,512]{1,0:T(8,128)S(1)}, u32[]{:S(2)}, u32[]{:S(2)}) collective-permute-start(f32[64,512]{1,0:T(8,128)S(1)} %collective-permute-done.16.refs_21_), channel_id=1, source_target_pairs={{0,2},{1,3},{2,0},{3,1},{4,6},{5,7},{6,4},{7,5},{8,10},{9,11},{10,... | collective-permute-start | bytes 393224 | tf_op jit(solution)/shard_map/ppermute | solution.py:219
  16.5 8.8 %collective-permute-start.15 = (f32[64,512]{1,0:T(8,128)S(1)}, f32[64,512]{1,0:T(8,128)S(1)}, u32[]{:S(2)}, u32[]{:S(2)}) collective-permute-start(f32[64,512]{1,0:T(8,128)S(1)} %collective-permute-done.14.refs_19_), channel_id=1, source_target_pairs={{0,2},{1,3},{2,0},{3,1},{4,6},{5,7},{6,4},{7,5},{8,10},{9,11},{10,... | collective-permute-start | bytes 393224 | tf_op jit(solution)/shard_map/ppermute | solution.py:219
  17.7 9.1 %collective-permute-start.13 = (f32[64,512]{1,0:T(8,128)S(1)}, f32[64,512]{1,0:T(8,128)S(1)}, u32[]{:S(2)}, u32[]{:S(2)}) collective-permute-start(f32[64,512]{1,0:T(8,128)S(1)} %collective-permute-done.12.refs_17_), channel_id=1, source_target_pairs={{0,2},{1,3},{2,0},{3,1},{4,6},{5,7},{6,4},{7,5},{8,10},{9,11},{10,... | collective-permute-start | bytes 393224 | tf_op jit(solution)/shard_map/ppermute | solution.py:219
  18.0 12.9 %collective-permute-start = (f32[512,128]{1,0:T(8,128)S(1)}, f32[512,128]{1,0:T(8,128)S(1)}, u32[]{:S(2)}, u32[]{:S(2)}) collective-permute-start(f32[512,128]{1,0:T(8,128)S(1)} %bitcast.27), channel_id=1, source_target_pairs={{0,1},{1,0},{2,3},{3,2},{4,5},{5,4},{6,7},{7,6},{8,9},{9,8},{10,11... | collective-permute-start | bytes 786440 | tf_op jit(solution)/shard_map/ppermute | solution.py:219
  21.8 10.3 %collective-permute-start.9 = (f32[96,512]{1,0:T(8,128)S(1)}, f32[96,512]{1,0:T(8,128)S(1)}, u32[]{:S(2)}, u32[]{:S(2)}) collective-permute-start(f32[96,512]{1,0:T(8,128)S(1)} %pad_maximum_fusion.refs_7_), channel_id=1, source_target_pairs={{0,12},{1,13},{2,14},{3,15},{4,8},{5,9},{6,10},{7,11},{8,4},{9,5},... | collective-permute-start | bytes 589832 | tf_op jit(solution)/shard_map/ppermute | solution.py:219
  26.0 14.9 %collective-permute-start.7 = (f32[96,512]{1,0:T(8,128)S(1)}, f32[96,512]{1,0:T(8,128)S(1)}, u32[]{:S(2)}, u32[]{:S(2)}) collective-permute-start(f32[96,512]{1,0:T(8,128)S(1)} %pad_maximum_fusion.refs_7_), channel_id=1, source_target_pairs={{0,8},{1,9},{2,10},{3,11},{4,12},{5,13},{6,14},{7,15},{8,0},{9,1},... | collective-permute-start | bytes 589832 | tf_op jit(solution)/shard_map/ppermute | solution.py:219
  27.5 14.6 %collective-permute-start.5 = (f32[96,512]{1,0:T(8,128)S(1)}, f32[96,512]{1,0:T(8,128)S(1)}, u32[]{:S(2)}, u32[]{:S(2)}) collective-permute-start(f32[96,512]{1,0:T(8,128)S(1)} %pad_maximum_fusion.refs_7_), channel_id=1, source_target_pairs={{0,4},{1,5},{2,6},{3,7},{4,0},{5,1},{6,2},{7,3},{8,12},{9,13},{10,... | collective-permute-start | bytes 589832 | tf_op jit(solution)/shard_map/ppermute | solution.py:219
  29.1 20.7 %collective-permute-start.2 = (f32[512,128]{1,0:T(8,128)S(1)}, f32[512,128]{1,0:T(8,128)S(1)}, u32[]{:S(2)}, u32[]{:S(2)}) collective-permute-start(f32[512,128]{1,0:T(8,128)S(1)} %collective-permute-done.1.refs_5_), channel_id=1, source_target_pairs={{0,1},{1,0},{2,3},{3,2},{4,5},{5,4},{6,7},{7,6},{8,9},{9,8},{10,11... | collective-permute-start | bytes 786440 | tf_op jit(solution)/shard_map/ppermute | solution.py:219
  30.9 11.5 %collective-permute-start.4 = (f32[96,512]{1,0:T(8,128)S(1)}, f32[96,512]{1,0:T(8,128)S(1)}, u32[]{:S(2)}, u32[]{:S(2)}) collective-permute-start(f32[96,512]{1,0:T(8,128)S(1)} %pad_maximum_fusion.refs_7_), channel_id=1, source_target_pairs={{0,2},{1,3},{2,0},{3,1},{4,6},{5,7},{6,4},{7,5},{8,10},{9,11},{10,... | collective-permute-start | bytes 589832 | tf_op jit(solution)/shard_map/ppermute | solution.py:219
  32.1 10.3 %collective-permute-start.10 = (f32[96,512]{1,0:T(8,128)S(1)}, f32[96,512]{1,0:T(8,128)S(1)}, u32[]{:S(2)}, u32[]{:S(2)}) collective-permute-start(f32[96,512]{1,0:T(8,128)S(1)} %collective-permute-done.9.refs_13_), channel_id=1, source_target_pairs={{0,2},{1,3},{2,0},{3,1},{4,6},{5,7},{6,4},{7,5},{8,10},{9,11},{10,... | collective-permute-start | bytes 589832 | tf_op jit(solution)/shard_map/ppermute | solution.py:219
  42.1 7.7 %collective-permute-start.6 = (f32[96,512]{1,0:T(8,128)S(1)}, f32[96,512]{1,0:T(8,128)S(1)}, u32[]{:S(2)}, u32[]{:S(2)}) collective-permute-start(f32[96,512]{1,0:T(8,128)S(1)} %collective-permute-done.5.refs_9_), channel_id=1, source_target_pairs={{0,2},{1,3},{2,0},{3,1},{4,6},{5,7},{6,4},{7,5},{8,10},{9,11},{10,... | collective-permute-start | bytes 589832 | tf_op jit(solution)/shard_map/ppermute | solution.py:219
  56.7 5.9 %collective-permute-start.19 = (f32[64,256]{1,0:T(8,128)S(1)}, f32[64,256]{1,0:T(8,128)S(1)}, u32[]{:S(2)}, u32[]{:S(2)}) collective-permute-start(f32[64,256]{1,0:T(8,128)S(1)} %get-tuple-element.17), channel_id=1, source_target_pairs={{0,1},{1,0},{2,3},{3,2},{4,5},{5,4},{6,7},{7,6},{8,9},{9,8},{10,11... | collective-permute-start | bytes 196616 | tf_op jit(solution)/shard_map/ppermute | solution.py:219
  59.4 4.8 %collective-permute-start.20 = (f32[64,256]{1,0:T(8,128)S(1)}, f32[64,256]{1,0:T(8,128)S(1)}, u32[]{:S(2)}, u32[]{:S(2)}) collective-permute-start(f32[64,256]{1,0:T(8,128)S(1)} %get-tuple-element.18), channel_id=1, source_target_pairs={{0,4},{1,5},{2,6},{3,7},{4,0},{5,1},{6,2},{7,3},{8,12},{9,13},{10,... | collective-permute-start | bytes 196616 | tf_op jit(solution)/shard_map/ppermute | solution.py:219
  60.4 5.5 %collective-permute-start.21 = (f32[64,256]{1,0:T(8,128)S(1)}, f32[64,256]{1,0:T(8,128)S(1)}, u32[]{:S(2)}, u32[]{:S(2)}) collective-permute-start(f32[64,256]{1,0:T(8,128)S(1)} %get-tuple-element.19), channel_id=1, source_target_pairs={{0,5},{1,4},{2,7},{3,6},{4,1},{5,0},{6,3},{7,2},{8,13},{9,12},{10,... | collective-permute-start | bytes 196616 | tf_op jit(solution)/shard_map/ppermute | solution.py:219
  61.1 12.3 %collective-permute-start.18 = (f32[128,256]{1,0:T(8,128)S(1)}, f32[128,256]{1,0:T(8,128)S(1)}, u32[]{:S(2)}, u32[]{:S(2)}) collective-permute-start(f32[128,256]{1,0:T(8,128)S(1)} %get-tuple-element.15), channel_id=1, source_target_pairs={{0,1},{1,0},{2,3},{3,2},{4,5},{5,4},{6,7},{7,6},{8,9},{9,8},{10,11... | collective-permute-start | bytes 393224 | tf_op jit(solution)/shard_map/ppermute | solution.py:219
  61.3 6.3 %collective-permute-start.22 = (f32[64,256]{1,0:T(8,128)S(1)}, f32[64,256]{1,0:T(8,128)S(1)}, u32[]{:S(2)}, u32[]{:S(2)}) collective-permute-start(f32[64,256]{1,0:T(8,128)S(1)} %get-tuple-element.20), channel_id=1, source_target_pairs={{0,8},{1,9},{2,10},{3,11},{4,12},{5,13},{6,14},{7,15},{8,0},{9,1},... | collective-permute-start | bytes 196616 | tf_op jit(solution)/shard_map/ppermute | solution.py:219
  62.6 10.7 %collective-permute-start.23 = (f32[64,256]{1,0:T(8,128)S(1)}, f32[64,256]{1,0:T(8,128)S(1)}, u32[]{:S(2)}, u32[]{:S(2)}) collective-permute-start(f32[64,256]{1,0:T(8,128)S(1)} %get-tuple-element.21), channel_id=1, source_target_pairs={{0,9},{1,8},{2,11},{3,10},{4,13},{5,12},{6,15},{7,14},{8,1},{9,0},... | collective-permute-start | bytes 196616 | tf_op jit(solution)/shard_map/ppermute | solution.py:219
  64.1 9.2 %collective-permute-start.24 = (f32[64,256]{1,0:T(8,128)S(1)}, f32[64,256]{1,0:T(8,128)S(1)}, u32[]{:S(2)}, u32[]{:S(2)}) collective-permute-start(f32[64,256]{1,0:T(8,128)S(1)} %get-tuple-element.22), channel_id=1, source_target_pairs={{0,12},{1,13},{2,14},{3,15},{4,8},{5,9},{6,10},{7,11},{8,4},{9,5},... | collective-permute-start | bytes 196616 | tf_op jit(solution)/shard_map/ppermute | solution.py:219
  65.9 7.5 %collective-permute-start.25 = (f32[64,256]{1,0:T(8,128)S(1)}, f32[64,256]{1,0:T(8,128)S(1)}, u32[]{:S(2)}, u32[]{:S(2)}) collective-permute-start(f32[64,256]{1,0:T(8,128)S(1)} %get-tuple-element.23), channel_id=1, source_target_pairs={{0,13},{1,12},{2,15},{3,14},{4,9},{5,8},{6,11},{7,10},{8,5},{9,4},... | collective-permute-start | bytes 196616 | tf_op jit(solution)/shard_map/ppermute | solution.py:219
  (13 other events, 36.0 us)

commit v2 on v1

--- a/solution.py
+++ b/solution.py
@@ -12,7 +12,7 @@
 NT = (((1,), (1,)), ((), ()))
 NN = (((1,), (0,)), ((), ()))
 TN = (((0,), (0,)), ((), ()))
-VMEM_LIMIT = 48 * 1024 * 1024
+VMEM_LIMIT = 20 * 1024 * 1024
 
 
 def halves(value):
@@ -35,23 +35,22 @@
     structure, live, place = refs[:3]
     c_own, c_sib, c_near, c_near_sib = refs[3:7]
     factor_blocks = refs[7:7 + rows]
-    inverse_blocks = refs[7 + rows:7 + 2 * rows]
-    panel_keep, panel_send = refs[7 + 2 * rows:9 + 2 * rows]
-    diag_out = refs[9 + 2 * rows:9 + 3 * rows]
-    pick_high, pick_low, f_high, f_low, d_high, d_low, own_f, diag_part = refs[9 + 3 * rows:]
+    inverse_blocks = refs[7 + rows:7 + rows + rows // 2]
+    panel_keep, panel_send, diag_out = refs[7 + rows + rows // 2:10 + rows + rows // 2]
+    pick_high, pick_low, f_high, f_low, d_high, d_low, own_f, diag_part = refs[10 + rows + rows // 2:]
     row = place[0]
     col = place[1]
     share = factor_blocks[0].shape[0]
-    width = inverse_blocks[0].shape[0]
+    width = inverse_blocks[0].shape[0] // 2
     half = panel_keep.shape[1]
     for step in range(rows):
-        source = row ^ step
         high, low = halves(factor_blocks[step][...])
-        at = pl.ds(pl.multiple_of(source * share, share), share)
+        at = pl.ds(pl.multiple_of((row ^ step) * share, share), share)
         f_high[at, :] = high
         f_low[at, :] = low
+    for step in range(rows // 2):
         high, low = halves(inverse_blocks[step][...])
-        at = pl.ds(pl.multiple_of(source * width, width), width)
+        at = pl.ds(pl.multiple_of((row // 2 ^ step) * 2 * width, 2 * width), 2 * width)
         d_high[at, :] = high
         d_low[at, :] = low
     local_blocks = c_own.shape[0] // tile
@@ -102,35 +101,27 @@
     base = dot3((d_high[at, :], d_low[at, :]), inverse, NT)
     diag_part[at, :] = diag_part[at, :] + base
     for step in range(rows // 2):
-        at = pl.ds(pl.multiple_of((row ^ (2 * step)) * width, width), width)
-        block = diag_part[at, :]
+        at = pl.ds(pl.multiple_of((2 * step + row % 2) * width, width), width)
         for other in range(2):
-            @pl.when(col == other)
-            def _():
-                diag_out[2 * step][...] = block[:, other * half:(other + 1) * half]
-                diag_out[2 * step + 1][...] = block[:, (1 - other) * half:(2 - other) * half]
-
-
-def last_kernel(count, *refs):
-    place, keep, got = refs[:3]
-    pieces = refs[3:3 + count]
-    panel_out, diag_out = refs[3 + count:]
+            diag_out[2 * step + other] = diag_part[at, other * half:(other + 1) * half]
+
+
+def last_kernel(place, keep, got, pieces, panel_out, diag_out):
     col = place[1]
     lanes = 128
-    same = pieces[0][...]
-    cross = pieces[1][...]
-    for step in range(1, count // 2):
-        same = same + pieces[2 * step][...]
-        cross = cross + pieces[2 * step + 1][...]
-    values = ((panel_out, keep[...], got[...]), (diag_out, same, cross))
-    for out, mine, other in values:
-        first = jnp.where(col == 0, mine, other)
-        second = jnp.where(col == 0, other, mine)
-        lane_blocks = mine.shape[1] // lanes
-        for block in range(lane_blocks):
-            at = slice(block * lanes, (block + 1) * lanes)
-            out[pl.ds(2 * block, mine.shape[0], stride=2 * lane_blocks), :] = first[:, at]
-            out[pl.ds(2 * block + 1, mine.shape[0], stride=2 * lane_blocks), :] = second[:, at]
+    count = pieces.shape[0]
+    members = [pieces[m] for m in range(2)]
+    for step in range(2, count):
+        members[step % 2] = members[step % 2] + pieces[step]
+    keep_value = keep[...]
+    got_value = got[...]
+    panels = (jnp.where(col == 0, keep_value, got_value), jnp.where(col == 0, got_value, keep_value))
+    for out, values in ((panel_out, panels), (diag_out, members)):
+        blocks = values[0].shape[1] // lanes
+        for block in range(blocks):
+            for member in range(2):
+                at = pl.ds(2 * block + member, values[0].shape[0], stride=2 * blocks)
+                out[at, :] = values[member][:, block * lanes:(block + 1) * lanes]
 
 
 def many_rows(ancestor_cov, panel_factor, diag_inverse, structure, live_counts):
@@ -218,32 +209,40 @@
         ]
         return lax.ppermute(value, ("row", "col"), pairs)
 
+    def ordered(mine, other, index):
+        return jnp.concatenate(
+            [jnp.where(index == 0, mine, other), jnp.where(index == 0, other, mine)], axis=0
+        )
+
     c_own = ancestor_cov.reshape(tile * local_blocks, 128)
     c_near = move(c_own, 1, 0)
-    c_sib = move(c_own, 0, 1)
-    inverse_own = lax.dynamic_index_in_dim(diag_inverse.transpose(1, 2, 0), col, 0, keepdims=False)
     f_keep = lax.dynamic_index_in_dim(panel_factor, col, 1, keepdims=False)
     f_send = lax.dynamic_index_in_dim(panel_factor, 1 - col, 1, keepdims=False)
     f_got = move(f_send, 0, 1)
-    inverse = [inverse_own] + [move(inverse_own, 2 * k, 0) for k in range(1, rows // 2)]
+    inverse_own = lax.dynamic_index_in_dim(diag_inverse.transpose(1, 2, 0), col, 0, keepdims=False)
+    inverse_pair = ordered(inverse_own, move(inverse_own, 1, 0), row % 2)
     factor_own = jnp.concatenate(
         [jnp.where(col == 0, f_keep, f_got), jnp.where(col == 0, f_got, f_keep)], axis=1
     )
-    factor = [factor_own] + [move(factor_own, 2 * k, 0) for k in range(1, rows // 2)]
+
+    def spread(value):
+        far = move(value, 4, 0)
+        return [value, move(value, 2, 0), far, move(far, 2, 0)]
+
+    factor = spread(factor_own)
+    inverse_blocks = spread(inverse_pair)
+    factor_blocks = [v for block in factor for v in (block, move(block, 1, 0))]
+    c_sib = move(c_own, 0, 1)
     c_near_sib = move(c_near, 0, 1)
-    inverse_near = [move(value, 1, 0) for value in inverse]
-    factor_near = [move(value, 1, 0) for value in factor]
-    inverse_blocks = [v for pair in zip(inverse, inverse_near) for v in pair]
-    factor_blocks = [v for pair in zip(factor, factor_near) for v in pair]
     place = jnp.stack([row, col]).astype(jnp.int32)
     smem = pl.BlockSpec(memory_space=pltpu.SMEM)
     vmem = pl.BlockSpec(memory_space=pltpu.VMEM)
     outs = pl.pallas_call(
         functools.partial(main_kernel, rows, tile, slots),
         out_shape=[jax.ShapeDtypeStruct((tile, half), F32)] * 2
-        + [jax.ShapeDtypeStruct((width, half), F32)] * rows,
-        in_specs=[smem] * 3 + [vmem] * (4 + 2 * rows),
-        out_specs=[vmem] * (2 + rows),
+        + [jax.ShapeDtypeStruct((rows, width, half), F32)],
+        in_specs=[smem] * 3 + [vmem] * (4 + rows + rows // 2),
+        out_specs=[vmem] * 3,
         scratch_shapes=[
             pltpu.VMEM((2 * tile, slots * tile), BF16),
             pltpu.VMEM((2 * tile, slots * tile), BF16),
@@ -257,21 +256,25 @@
         compiler_params=pltpu.CompilerParams(vmem_limit_bytes=VMEM_LIMIT),
         name="products",
     )(structure, live_counts, place, c_own, c_sib, c_near, c_near_sib, *factor_blocks, *inverse_blocks)
-    panel_keep, panel_send = outs[:2]
-    diag_pieces = outs[2:]
-    pieces = [diag_pieces[0]] + [move(diag_pieces[j], 2 * (j // 2), j % 2) for j in range(1, rows)]
+    panel_keep, panel_send, diag_pieces = outs
     panel_got = move(panel_send, 0, 1)
+    groups = [
+        [(2 * z + x) * 2 + c for z in range(rows // 2) for c in range(2)] for x in range(2)
+    ]
+    pieces = lax.all_to_all(
+        diag_pieces, ("row", "col"), 0, 0, axis_index_groups=groups, tiled=True
+    )
     panel, diag = pl.pallas_call(
-        functools.partial(last_kernel, rows),
+        last_kernel,
         out_shape=[
             jax.ShapeDtypeStruct((tile * 2 * half // 128, 128), F32),
             jax.ShapeDtypeStruct((width * 2 * half // 128, 128), F32),
         ],
-        in_specs=[smem] + [vmem] * (2 + rows),
+        in_specs=[smem] + [vmem] * 3,
         out_specs=[vmem] * 2,
         compiler_params=pltpu.CompilerParams(vmem_limit_bytes=VMEM_LIMIT),
         name="sums",
-    )(place, panel_keep, panel_got, *pieces)
+    )(place, panel_keep, panel_got, pieces)
 
     def unfold(value, count):
         return value.reshape(count, half // 128, 2, 128).transpose(0, 2, 1, 3).reshape(count, 2, half)

time: 75.6 us -> 72.9 us (0.964)
  waiting for transfers between devices: 29 us -> 36.6 us
  starting transfers between devices: 33.5 us -> 26.7 us
  local copies, waits for them, and re-layouts: 5.8 us -> 1.31 us
  Pallas kernels: 5.56 us -> 6.39 us
    all_to_all x0 -> x1, waiting for transfers between devices: none -> 13.1 us  [local(): lax.all_to_all(diag_pieces, ('row', 'col'), 0, 0, axis_index_groups=group...]
    ppermute x26 -> x16, starting transfers between devices: 33.5 us -> 20.7 us  [move(): return lax.ppermute(value, ('row', 'col'), pairs)]
    all_to_all x0 -> x1, starting transfers between devices: none -> 6.07 us  [local(): lax.all_to_all(diag_pieces, ('row', 'col'), 0, 0, axis_index_groups=group...]
    unnamed x23 -> x9, local copies, waits for them, and re-layouts: 5.62 us -> 0.03 us
    ppermute x26 -> x16, waiting for transfers between devices: 29 us -> 23.4 us  [move(): return lax.ppermute(value, ('row', 'col'), pairs)]
    dynamic_slice x1, local copies, waits for them, and re-layouts: 0.17 us -> 1.27 us  [local(): f_keep = lax.dynamic_index_in_dim(panel_factor, col, 1, keepdims=False)]
    pallas_call x1, Pallas kernels: 4.21 us -> 5.05 us  [local(): pl.pallas_call(functools.partial(main_kernel, rows, tile, slots), out_sha...]
  transfers between devices with their start and end apart: 26 -> 17, of which waited for: 7 -> 11; matrix products, arithmetic and copies ran while one was open for 0% -> 2% of each run, Pallas kernels for 0% -> 0%
where the time goes in v2:
time: 72.9 us; the launch traced here: 71.9 us
  waiting for transfers between devices  36.6 us (50%)
  starting transfers between devices  26.7 us (37%)
  Pallas kernels  6.39 us (9%)
  local copies, waits for them, and re-layouts  1.31 us (2%)
  between operations  0.75 us (1%)
    ppermute x16, waiting for transfers between devices, move(): return lax.ppermute(value, ('row', 'col'), pairs)  23.4 us
    ppermute x16, starting transfers between devices, move(): return lax.ppermute(value, ('row', 'col'), pairs)  20.7 us
    all_to_all x1, waiting for transfers between devices, local(): lax.all_to_all(diag_pieces, ('row', 'col'), 0, 0, axis_index_groups=group...  13.1 us
    all_to_all x1, starting transfers between devices, local(): lax.all_to_all(diag_pieces, ('row', 'col'), 0, 0, axis_index_groups=group...  6.07 us
    pallas_call x1, Pallas kernels, local(): pl.pallas_call(functools.partial(main_kernel, rows, tile, slots), out_sha...  5.05 us
  transfers between devices with their start and end apart: 17, of which 11 were waited for; matrix products, arithmetic and copies ran while one was open for 2% of the time, Pallas kernels for 0%

profile of v2, /device:TPU:1, one launch (start us, length us, event | category | flops | bytes accessed | tf_op | source)
XLA Modules:
  0.0 71.9 jit_solution(8433087293377055783)
XLA Ops:
  0.6 2.1 %collective-permute-start.1 = (f32[512,128]{1,0:T(8,128)}, f32[512,128]{1,0:T(8,128)S(1)}, u32[]{:S(2)}, u32[]{:S(2)}) collective-permute-start(f32[512,128]{1,0:T(8,128)} %bitcast.28), channel_id=1, source_target_pairs={{0,2},{1,3},{2,0},{3,1},{4,6},{5,7},{6,4},{7,5},{8,10},{9,11},{10,... | collective-permute-start | bytes 786440 | tf_op jit(solution)/shard_map/ppermute | solution.py:210
  2.7 1.0 %collective-permute-start = (f32[512,128]{1,0:T(8,128)}, f32[512,128]{1,0:T(8,128)S(1)}, u32[]{:S(2)}, u32[]{:S(2)}) collective-permute-start(f32[512,128]{1,0:T(8,128)} %bitcast.29), channel_id=1, source_target_pairs={{0,1},{1,0},{2,3},{3,2},{4,5},{5,4},{6,7},{7,6},{8,9},{9,8},{10,11... | collective-permute-start | bytes 786440 | tf_op jit(solution)/shard_map/ppermute | solution.py:210
  3.7 1.3 %constant_dynamic-slice_fusion.1 = (f32[96,1,256]{2,1,0:T(1,128)S(1)}, f32[96,1,256]{2,1,0:T(1,128)S(1)}) fusion(f32[96,2,256]{2,1,0:T(2,128)} %param.6, s32[]{:T(128)S(6)} %select_n.41, s32[]{:T(128)S(6)} %select_n.42), kind=kLoop, calls=%fused_computation.10 | loop fusion | bytes 393224 | tf_op jit(solution)/shard_map/jit(dynamic_index_in_dim)/dynamic_slice | solution.py:219
  5.2 1.2 %collective-permute-done.3 = f32[96,256]{1,0:T(8,128)S(1)} collective-permute-done((f32[96,256]{1,0:T(8,128)S(1)}, f32[96,256]{1,0:T(8,128)S(1)}, u32[]{:S(2)}, u32[]{:S(2)}) %collective-permute-start.3) | collective-permute-done | bytes 98336 | tf_op jit(solution)/shard_map/ppermute | solution.py:210
  6.4 2.4 %collective-permute-start.7 = (f32[96,512]{1,0:T(8,128)S(1)}, f32[96,512]{1,0:T(8,128)S(1)}, u32[]{:S(2)}, u32[]{:S(2)}) collective-permute-start(f32[96,512]{1,0:T(8,128)S(1)} %pad_maximum_fusion.1.refs_7_), channel_id=1, source_target_pairs={{0,8},{1,9},{2,10},{3,11},{4,12},{5,13},{6,14},{7,15},{8,0},{9,1},... | collective-permute-start | bytes 589832 | tf_op jit(solution)/shard_map/ppermute | solution.py:210
  8.8 3.0 %collective-permute-done.11 = f32[64,512]{1,0:T(8,128)S(1)} collective-permute-done((f32[64,512]{1,0:T(8,128)S(1)}, f32[64,512]{1,0:T(8,128)S(1)}, u32[]{:S(2)}, u32[]{:S(2)}) %collective-permute-start.11) | collective-permute-done | bytes 131104 | tf_op jit(solution)/shard_map/ppermute | solution.py:210
  11.9 2.3 %collective-permute-start.13 = (f32[128,512]{1,0:T(8,128)S(1)}, f32[128,512]{1,0:T(8,128)S(1)}, u32[]{:S(2)}, u32[]{:S(2)}) collective-permute-start(f32[128,512]{1,0:T(8,128)S(1)} %pad_maximum_fusion.refs_15_), channel_id=1, source_target_pairs={{0,8},{1,9},{2,10},{3,11},{4,12},{5,13},{6,14},{7,15},{8,0},{9,1},... | collective-permute-start | bytes 786440 | tf_op jit(solution)/shard_map/ppermute | solution.py:210
  14.2 1.3 %collective-permute-start.5 = (f32[96,512]{1,0:T(8,128)S(1)}, f32[96,512]{1,0:T(8,128)S(1)}, u32[]{:S(2)}, u32[]{:S(2)}) collective-permute-start(f32[96,512]{1,0:T(8,128)S(1)} %pad_maximum_fusion.1.refs_7_), channel_id=1, source_target_pairs={{0,4},{1,5},{2,6},{3,7},{4,0},{5,1},{6,2},{7,3},{8,12},{9,13},{10,... | collective-permute-start | bytes 589832 | tf_op jit(solution)/shard_map/ppermute | solution.py:210
  15.6 1.2 %collective-permute-start.4 = (f32[96,512]{1,0:T(8,128)S(1)}, f32[96,512]{1,0:T(8,128)S(1)}, u32[]{:S(2)}, u32[]{:S(2)}) collective-permute-start(f32[96,512]{1,0:T(8,128)S(1)} %pad_maximum_fusion.1.refs_7_), channel_id=1, source_target_pairs={{0,2},{1,3},{2,0},{3,1},{4,6},{5,7},{6,4},{7,5},{8,10},{9,11},{10,... | collective-permute-start | bytes 589832 | tf_op jit(solution)/shard_map/ppermute | solution.py:210
  16.8 6.0 %collective-permute-done.7.refs_11_ = f32[96,512]{1,0:T(8,128)S(1)} collective-permute-done((f32[96,512]{1,0:T(8,128)S(1)}, f32[96,512]{1,0:T(8,128)S(1)}, u32[]{:S(2)}, u32[]{:S(2)}) %collective-permute-start.7) | collective-permute-done | bytes 196640 | tf_op jit(solution)/shard_map/ppermute | solution.py:210
  22.9 1.5 %collective-permute-start.9 = (f32[96,512]{1,0:T(8,128)S(1)}, f32[96,512]{1,0:T(8,128)S(1)}, u32[]{:S(2)}, u32[]{:S(2)}) collective-permute-start(f32[96,512]{1,0:T(8,128)S(1)} %collective-permute-done.7.refs_11_), channel_id=1, source_target_pairs={{0,4},{1,5},{2,6},{3,7},{4,0},{5,1},{6,2},{7,3},{8,12},{9,13},{10,... | collective-permute-start | bytes 589832 | tf_op jit(solution)/shard_map/ppermute | solution.py:210
  24.4 6.9 %collective-permute-start.2 = (f32[512,128]{1,0:T(8,128)S(1)}, f32[512,128]{1,0:T(8,128)S(1)}, u32[]{:S(2)}, u32[]{:S(2)}) collective-permute-start(f32[512,128]{1,0:T(8,128)S(1)} %collective-permute-done.1.refs_5_), channel_id=1, source_target_pairs={{0,1},{1,0},{2,3},{3,2},{4,5},{5,4},{6,7},{7,6},{8,9},{9,8},{10,11... | collective-permute-start | bytes 786440 | tf_op jit(solution)/shard_map/ppermute | solution.py:210
  31.4 0.3 collective-permute-start.8
  31.9 1.0 %collective-permute-start.6 = (f32[96,512]{1,0:T(8,128)S(1)}, f32[96,512]{1,0:T(8,128)S(1)}, u32[]{:S(2)}, u32[]{:S(2)}) collective-permute-start(f32[96,512]{1,0:T(8,128)S(1)} %collective-permute-done.5.refs_9_), channel_id=1, source_target_pairs={{0,2},{1,3},{2,0},{3,1},{4,6},{5,7},{6,4},{7,5},{8,10},{9,11},{10,... | collective-permute-start | bytes 589832 | tf_op jit(solution)/shard_map/ppermute | solution.py:210
  32.9 3.2 %collective-permute-done.9.refs_13_ = f32[96,512]{1,0:T(8,128)S(1)} collective-permute-done((f32[96,512]{1,0:T(8,128)S(1)}, f32[96,512]{1,0:T(8,128)S(1)}, u32[]{:S(2)}, u32[]{:S(2)}) %collective-permute-start.9) | collective-permute-done | bytes 196640 | tf_op jit(solution)/shard_map/ppermute | solution.py:210
  36.5 1.5 %collective-permute-done.8.refs_12_ = f32[96,512]{1,0:T(8,128)S(1)} collective-permute-done((f32[96,512]{1,0:T(8,128)S(1)}, f32[96,512]{1,0:T(8,128)S(1)}, u32[]{:S(2)}, u32[]{:S(2)}) %collective-permute-start.8) | collective-permute-done | bytes 196640 | tf_op jit(solution)/shard_map/ppermute | solution.py:210
  38.0 2.8 %collective-permute-done.6.refs_10_ = f32[96,512]{1,0:T(8,128)S(1)} collective-permute-done((f32[96,512]{1,0:T(8,128)S(1)}, f32[96,512]{1,0:T(8,128)S(1)}, u32[]{:S(2)}, u32[]{:S(2)}) %collective-permute-start.6) | collective-permute-done | bytes 196640 | tf_op jit(solution)/shard_map/ppermute | solution.py:210
  40.7 1.0 %collective-permute-done.14.refs_18_ = f32[128,512]{1,0:T(8,128)S(1)} collective-permute-done((f32[128,512]{1,0:T(8,128)S(1)}, f32[128,512]{1,0:T(8,128)S(1)}, u32[]{:S(2)}, u32[]{:S(2)}) %collective-permute-start.14) | collective-permute-done | bytes 262176 | tf_op jit(solution)/shard_map/ppermute | solution.py:210
  41.7 3.2 %collective-permute-done.10.refs_14_ = f32[96,512]{1,0:T(8,128)S(1)} collective-permute-done((f32[96,512]{1,0:T(8,128)S(1)}, f32[96,512]{1,0:T(8,128)S(1)}, u32[]{:S(2)}, u32[]{:S(2)}) %collective-permute-start.10) | collective-permute-done | bytes 196640 | tf_op jit(solution)/shard_map/ppermute | solution.py:210
  44.9 5.1 %products.1 = (f32[128,256]{1,0:T(8,128)S(1)}, f32[128,256]{1,0:T(8,128)S(1)}, f32[8,64,256]{2,1,0:T(8,128)}) custom-call(s32[2,6]{1,0:T(2,128)S(1)} %copy-done.1, s32[2]{0:T(128)S(1)} %copy-done.2, s32[2]{0:T(128)S(1)} %pad_add_fusion.refs_2_.place, f32[512,128]{1,0:T(8,128)S(1)} %bitcast.30, f32[512,128]{1,0:T(8,128)S(1)} %collective-permute-done.refs_4_, ...), custom_call_target="tpu_custom_call" | custom-call | tf_op jit(solution)/shard_map/products/pallas_call | solution.py:240
  50.0 6.1 %all-to-all-start = ((f32[8,64,256]{2,1,0:T(8,128)}), f32[8,64,256]{2,1,0:T(8,128)S(1)}, u32[]{:S(2)}, u32[]{:S(2)}) async-start(f32[8,64,256]{2,1,0:T(8,128)} %get-tuple-element.9), calls=%async_computation | async-start | bytes 1048576 | tf_op jit(solution)/shard_map/all_to_all | solution.py:264
  56.1 1.3 %collective-permute-done.15.got = f32[128,256]{1,0:T(8,128)S(1)} collective-permute-done((f32[128,256]{1,0:T(8,128)S(1)}, f32[128,256]{1,0:T(8,128)S(1)}, u32[]{:S(2)}, u32[]{:S(2)}) %collective-permute-start.15) | collective-permute-done | bytes 131104 | tf_op jit(solution)/shard_map/ppermute | solution.py:210
  57.4 13.1 %all-to-all-done.pieces = f32[8,64,256]{2,1,0:T(8,128)S(1)} async-done(((f32[8,64,256]{2,1,0:T(8,128)}), f32[8,64,256]{2,1,0:T(8,128)S(1)}, u32[]{:S(2)}, u32[]{:S(2)}) %all-to-all-start) | async-done | bytes 524320 | tf_op jit(solution)/shard_map/all_to_all | solution.py:264
  70.6 1.3 %sums.1 = (f32[512,128]{1,0:T(8,128)}, f32[256,128]{1,0:T(8,128)}) custom-call(s32[2]{0:T(128)S(1)} %pad_add_fusion.refs_2_.place, f32[128,256]{1,0:T(8,128)S(1)} %get-tuple-element.7.keep, f32[128,256]{1,0:T(8,128)S(1)} %collective-permute-done.15.got, f32[8,64,256]{2,1,0:T(8,128)S(1)} %all-to-all-done.pieces), custom_call_target="tpu_custom_call" | custom-call | tf_op jit(solution)/shard_map/sums/pallas_call | solution.py:267
  (28 shorter events, 1.0 us)
Async XLA Ops:
  0.6 14.8 %collective-permute-start.1 = (f32[512,128]{1,0:T(8,128)}, f32[512,128]{1,0:T(8,128)S(1)}, u32[]{:S(2)}, u32[]{:S(2)}) collective-permute-start(f32[512,128]{1,0:T(8,128)} %bitcast.28), channel_id=1, source_target_pairs={{0,2},{1,3},{2,0},{3,1},{4,6},{5,7},{6,4},{7,5},{8,10},{9,11},{10,... | collective-permute-start | bytes 786440 | tf_op jit(solution)/shard_map/ppermute | solution.py:210
  2.7 12.9 %collective-permute-start = (f32[512,128]{1,0:T(8,128)}, f32[512,128]{1,0:T(8,128)S(1)}, u32[]{:S(2)}, u32[]{:S(2)}) collective-permute-start(f32[512,128]{1,0:T(8,128)} %bitcast.29), channel_id=1, source_target_pairs={{0,1},{1,0},{2,3},{3,2},{4,5},{5,4},{6,7},{7,6},{8,9},{9,8},{10,11... | collective-permute-start | bytes 786440 | tf_op jit(solution)/shard_map/ppermute | solution.py:210
  3.7 1.4 %copy-start.3 = (f32[512,2,64]{0,2,1:T(8,128)S(1)}, f32[512,2,64]{0,2,1:T(8,128)}, u32[]{:S(2)}) copy-start(f32[512,2,64]{0,2,1:T(8,128)} %param.7) | copy-start | bytes 786436
  5.0 1.4 %collective-permute-start.3 = (f32[96,256]{1,0:T(8,128)S(1)}, f32[96,256]{1,0:T(8,128)S(1)}, u32[]{:S(2)}, u32[]{:S(2)}) collective-permute-start(f32[96,256]{1,0:T(8,128)S(1)} %bitcast.31), channel_id=1, source_target_pairs={{0,1},{1,0},{2,3},{3,2},{4,5},{5,4},{6,7},{7,6},{8,9},{9,8},{10,11... | collective-permute-start | bytes 294920 | tf_op jit(solution)/shard_map/ppermute | solution.py:210
  5.1 6.7 %collective-permute-start.11 = (f32[64,512]{1,0:T(8,128)S(1)}, f32[64,512]{1,0:T(8,128)S(1)}, u32[]{:S(2)}, u32[]{:S(2)}) collective-permute-start(f32[64,512]{1,0:T(8,128)S(1)} %dynamic-slice_bitcast_fusion), channel_id=1, source_target_pairs={{0,2},{1,3},{2,0},{3,1},{4,6},{5,7},{6,4},{7,5},{8,10},{9,11},{10,... | collective-permute-start | bytes 393224 | tf_op jit(solution)/shard_map/ppermute | solution.py:210
  6.4 16.5 %collective-permute-start.7 = (f32[96,512]{1,0:T(8,128)S(1)}, f32[96,512]{1,0:T(8,128)S(1)}, u32[]{:S(2)}, u32[]{:S(2)}) collective-permute-start(f32[96,512]{1,0:T(8,128)S(1)} %pad_maximum_fusion.1.refs_7_), channel_id=1, source_target_pairs={{0,8},{1,9},{2,10},{3,11},{4,12},{5,13},{6,14},{7,15},{8,0},{9,1},... | collective-permute-start | bytes 589832 | tf_op jit(solution)/shard_map/ppermute | solution.py:210
  11.8 33.1 %copy-start = (f32[128,4,1,128]{3,2,1,0:T(1,128)S(1)}, f32[128,4,1,128]{3,2,1,0:T(1,128)}, u32[]{:S(2)}) copy-start(f32[128,4,1,128]{3,2,1,0:T(1,128)} %param.5) | copy-start | bytes 786436
  11.9 19.5 %collective-permute-start.13 = (f32[128,512]{1,0:T(8,128)S(1)}, f32[128,512]{1,0:T(8,128)S(1)}, u32[]{:S(2)}, u32[]{:S(2)}) collective-permute-start(f32[128,512]{1,0:T(8,128)S(1)} %pad_maximum_fusion.refs_15_), channel_id=1, source_target_pairs={{0,8},{1,9},{2,10},{3,11},{4,12},{5,13},{6,14},{7,15},{8,0},{9,1},... | collective-permute-start | bytes 786440 | tf_op jit(solution)/shard_map/ppermute | solution.py:210
  14.2 10.3 %collective-permute-start.5 = (f32[96,512]{1,0:T(8,128)S(1)}, f32[96,512]{1,0:T(8,128)S(1)}, u32[]{:S(2)}, u32[]{:S(2)}) collective-permute-start(f32[96,512]{1,0:T(8,128)S(1)} %pad_maximum_fusion.1.refs_7_), channel_id=1, source_target_pairs={{0,4},{1,5},{2,6},{3,7},{4,0},{5,1},{6,2},{7,3},{8,12},{9,13},{10,... | collective-permute-start | bytes 589832 | tf_op jit(solution)/shard_map/ppermute | solution.py:210
  15.5 16.4 %collective-permute-start.12 = (f32[128,512]{1,0:T(8,128)S(1)}, f32[128,512]{1,0:T(8,128)S(1)}, u32[]{:S(2)}, u32[]{:S(2)}) collective-permute-start(f32[128,512]{1,0:T(8,128)S(1)} %pad_maximum_fusion.refs_15_), channel_id=1, source_target_pairs={{0,4},{1,5},{2,6},{3,7},{4,0},{5,1},{6,2},{7,3},{8,12},{9,13},{10,... | collective-permute-start | bytes 786440 | tf_op jit(solution)/shard_map/ppermute | solution.py:210
  15.6 15.7 %collective-permute-start.4 = (f32[96,512]{1,0:T(8,128)S(1)}, f32[96,512]{1,0:T(8,128)S(1)}, u32[]{:S(2)}, u32[]{:S(2)}) collective-permute-start(f32[96,512]{1,0:T(8,128)S(1)} %pad_maximum_fusion.1.refs_7_), channel_id=1, source_target_pairs={{0,2},{1,3},{2,0},{3,1},{4,6},{5,7},{6,4},{7,5},{8,10},{9,11},{10,... | collective-permute-start | bytes 589832 | tf_op jit(solution)/shard_map/ppermute | solution.py:210
  22.9 13.2 %collective-permute-start.9 = (f32[96,512]{1,0:T(8,128)S(1)}, f32[96,512]{1,0:T(8,128)S(1)}, u32[]{:S(2)}, u32[]{:S(2)}) collective-permute-start(f32[96,512]{1,0:T(8,128)S(1)} %collective-permute-done.7.refs_11_), channel_id=1, source_target_pairs={{0,4},{1,5},{2,6},{3,7},{4,0},{5,1},{6,2},{7,3},{8,12},{9,13},{10,... | collective-permute-start | bytes 589832 | tf_op jit(solution)/shard_map/ppermute | solution.py:210
  24.4 16.3 %collective-permute-start.2 = (f32[512,128]{1,0:T(8,128)S(1)}, f32[512,128]{1,0:T(8,128)S(1)}, u32[]{:S(2)}, u32[]{:S(2)}) collective-permute-start(f32[512,128]{1,0:T(8,128)S(1)} %collective-permute-done.1.refs_5_), channel_id=1, source_target_pairs={{0,1},{1,0},{2,3},{3,2},{4,5},{5,4},{6,7},{7,6},{8,9},{9,8},{10,11... | collective-permute-start | bytes 786440 | tf_op jit(solution)/shard_map/ppermute | solution.py:210
  31.4 10.3 %collective-permute-start.14 = (f32[128,512]{1,0:T(8,128)S(1)}, f32[128,512]{1,0:T(8,128)S(1)}, u32[]{:S(2)}, u32[]{:S(2)}) collective-permute-start(f32[128,512]{1,0:T(8,128)S(1)} %collective-permute-done.13.refs_17_), channel_id=1, source_target_pairs={{0,4},{1,5},{2,6},{3,7},{4,0},{5,1},{6,2},{7,3},{8,12},{9,13},{10,... | collective-permute-start | bytes 786440 | tf_op jit(solution)/shard_map/ppermute | solution.py:210
  31.4 6.6 %collective-permute-start.8 = (f32[96,512]{1,0:T(8,128)S(1)}, f32[96,512]{1,0:T(8,128)S(1)}, u32[]{:S(2)}, u32[]{:S(2)}) collective-permute-start(f32[96,512]{1,0:T(8,128)S(1)} %collective-permute-done.7.refs_11_), channel_id=1, source_target_pairs={{0,2},{1,3},{2,0},{3,1},{4,6},{5,7},{6,4},{7,5},{8,10},{9,11},{10,... | collective-permute-start | bytes 589832 | tf_op jit(solution)/shard_map/ppermute | solution.py:210
  31.9 8.8 %collective-permute-start.6 = (f32[96,512]{1,0:T(8,128)S(1)}, f32[96,512]{1,0:T(8,128)S(1)}, u32[]{:S(2)}, u32[]{:S(2)}) collective-permute-start(f32[96,512]{1,0:T(8,128)S(1)} %collective-permute-done.5.refs_9_), channel_id=1, source_target_pairs={{0,2},{1,3},{2,0},{3,1},{4,6},{5,7},{6,4},{7,5},{8,10},{9,11},{10,... | collective-permute-start | bytes 589832 | tf_op jit(solution)/shard_map/ppermute | solution.py:210
  36.1 8.8 %collective-permute-start.10 = (f32[96,512]{1,0:T(8,128)S(1)}, f32[96,512]{1,0:T(8,128)S(1)}, u32[]{:S(2)}, u32[]{:S(2)}) collective-permute-start(f32[96,512]{1,0:T(8,128)S(1)} %collective-permute-done.9.refs_13_), channel_id=1, source_target_pairs={{0,2},{1,3},{2,0},{3,1},{4,6},{5,7},{6,4},{7,5},{8,10},{9,11},{10,... | collective-permute-start | bytes 589832 | tf_op jit(solution)/shard_map/ppermute | solution.py:210
  36.4 8.6 %copy-start.1 = (s32[2,6]{1,0:T(2,128)S(1)}, s32[2,6]{1,0:T(2,128)}, u32[]{:S(2)}) copy-start(s32[2,6]{1,0:T(2,128)} %refs_0_.1) | copy-start | bytes 148
  36.4 8.6 %copy-start.2 = (s32[2]{0:T(128)S(1)}, s32[2]{0:T(128)}, u32[]{:S(2)}) copy-start(s32[2]{0:T(128)} %refs_1_.1) | copy-start | bytes 28
  50.0 20.6 %all-to-all-start = ((f32[8,64,256]{2,1,0:T(8,128)}), f32[8,64,256]{2,1,0:T(8,128)S(1)}, u32[]{:S(2)}, u32[]{:S(2)}) async-start(f32[8,64,256]{2,1,0:T(8,128)} %get-tuple-element.9), calls=%async_computation | async-start | bytes 1048576 | tf_op jit(solution)/shard_map/all_to_all | solution.py:264
  56.1 1.3 %collective-permute-start.15 = (f32[128,256]{1,0:T(8,128)S(1)}, f32[128,256]{1,0:T(8,128)S(1)}, u32[]{:S(2)}, u32[]{:S(2)}) collective-permute-start(f32[128,256]{1,0:T(8,128)S(1)} %get-tuple-element.8), channel_id=1, source_target_pairs={{0,1},{1,0},{2,3},{3,2},{4,5},{5,4},{6,7},{7,6},{8,9},{9,8},{10,11... | collective-permute-start | bytes 393224 | tf_op jit(solution)/shard_map/ppermute | solution.py:210

commit v3 on v0

--- a/solution.py
+++ b/solution.py
@@ -1,10 +1,168 @@
+import functools
+
 import jax
 import jax.numpy as jnp
 from jax import lax
+from jax.experimental import pallas as pl
+from jax.experimental.pallas import tpu as pltpu
 from jax.sharding import PartitionSpec as P
 
-
-def local(ancestor_cov, panel_factor, diag_inverse, structure, live_counts):
+F32 = jnp.float32
+BF16 = jnp.bfloat16
+NT = (((1,), (1,)), ((), ()))
+NN = (((1,), (0,)), ((), ()))
+TN = (((0,), (0,)), ((), ()))
+VMEM_LIMIT = 20 * 1024 * 1024
+
+
+def halves(value):
+    high = value.astype(BF16)
+    low = (value - high.astype(F32)).astype(BF16)
+    return high, low
+
+
+def dot3(left, right, dims):
+    left_high, left_low = left
+    right_high, right_low = right
+
+    def one(a, b):
+        return lax.dot_general(a, b, dims, preferred_element_type=F32)
+
+    return one(left_high, right_low) + one(left_low, right_high) + one(left_high, right_high)
+
+
+def pack_kernel(place, factor, inverse, own, send):
+    x = place[1]
+    c = place[2]
+    half = own.shape[1]
+    share = factor.shape[0] * 128 // (2 * half)
+    blocks = half // 128
+    for out, member in ((own, x), (send, 1 - x)):
+        for block in range(blocks):
+            at = pl.ds(2 * block + member, share, stride=2 * blocks)
+            out[:share, block * 128:(block + 1) * 128] = factor[at, :]
+        out[share:, :] = inverse[member, :, pl.ds(pl.multiple_of(c * half, half), half)]
+
+
+def product_kernel(share, tile, slots, *refs):
+    structure, live, place, c_keep, c_got = refs[:5]
+    mine = refs[5:12]
+    theirs = refs[12:15]
+    panel_out = refs[15:19]
+    w_out = refs[19:23]
+    f_high, f_low, d_high, d_low, pick_high, pick_low, product = refs[23:]
+    z, x, c = place[0], place[1], place[2]
+    member = x
+    half = mine[0].shape[1]
+    width = mine[0].shape[0] - share
+    near = 1 - x
+    mine_at = []
+    for index, step in ((0, 0), (2, 2), (4, 1)):
+        mine_at += [(index, 0, 2 * (z ^ step) + x), (index + 1, 0, 2 * (z ^ step) + near)]
+    mine_at += [(6, 0, 2 * (z ^ 3) + x), (6, share + width, 2 * (z ^ 3) + near)]
+    block = share + width
+    theirs_at = [(0, 0, 2 * z + x), (0, block, 2 * z + near)]
+    for index, step in ((0, 2), (2, 1)):
+        theirs_at += [(1, index * block, 2 * (z ^ step) + x), (1, (index + 1) * block, 2 * (z ^ step) + near)]
+    theirs_at += [(2, 0, 2 * (z ^ 3) + x), (2, block, 2 * (z ^ 3) + near)]
+    for lanes, pieces, table in ((0, mine, mine_at), (half, theirs, theirs_at)):
+        for index, first, source in table:
+            high, low = halves(pieces[index][first:first + share, :])
+            at = pl.ds(pl.multiple_of(source * share, share), share)
+            f_high[at, lanes:lanes + half] = high
+            f_low[at, lanes:lanes + half] = low
+            high, low = halves(pieces[index][first + share:first + block, :])
+            at = pl.ds(pl.multiple_of(source * width, width), width)
+            d_high[at, lanes:lanes + half] = high
+            d_low[at, lanes:lanes + half] = low
+    part = tile // 2
+    blocks = c_keep.shape[1] // part
+    in_struct = [False, False]
+    for slot in range(slots):
+        anc = structure[member, slot]
+        alive = slot < live[member]
+        own_column = anc % 2 == c
+        rows = pl.ds(anc // 2, part, stride=blocks)
+        for which in range(2):
+            value = jnp.where(own_column, c_keep[which, rows, :], c_got[which, rows, :])
+            high, low = halves(jnp.where(alive, value, 0.0))
+            at = pl.ds(pl.multiple_of((x ^ which) * part, part), part)
+            pick_high[at, slot * tile:(slot + 1) * tile] = high
+            pick_low[at, slot * tile:(slot + 1) * tile] = low
+            in_struct[which] = in_struct[which] | (alive & (anc == 2 * z + (x ^ which)))
+    grown = dot3((pick_high[...], pick_low[...]), (f_high[...], f_low[...]), NN)
+    product[...] = dot3(halves(grown), (d_high[...], d_low[...]), NT)
+    for which in range(2):
+        at = pl.ds(pl.multiple_of((x ^ which) * part, part), part)
+        for flip in range(2):
+            lanes = pl.ds(pl.multiple_of((c ^ flip) * half, half), half)
+            panel_out[2 * which + flip][...] = jnp.where(in_struct[which], -product[at, lanes], 0.0)
+    for step in range(4):
+        wide = 2 * width
+        w_out[step][...] = product[:, pl.ds(pl.multiple_of((z ^ step) * wide, wide), wide)]
+
+
+def scaled_kernel(tile, slots, place, f_high, f_low, d_high, d_low, s_high, s_low, base, own_high, own_low):
+    z, c = place[0], place[2]
+    part = tile // 2
+    half = f_high.shape[1] // 2
+    wide = base.shape[0]
+    for slot in range(slots):
+        at = pl.ds(pl.multiple_of(slot * tile + c * part, part), part)
+        own_high[slot * part:(slot + 1) * part, :] = f_high[at, :]
+        own_low[slot * part:(slot + 1) * part, :] = f_low[at, :]
+    scaled = dot3((own_high[...], own_low[...]), (d_high[...], d_low[...]), NT)
+    s_high[...], s_low[...] = halves(scaled)
+    at = pl.ds(pl.multiple_of(z * wide, wide), wide)
+    base[...] = dot3(
+        (d_high[at, :half], d_low[at, :half]), (d_high[:, :half], d_low[:, :half]), NT
+    )
+
+
+def diag_kernel(tile, slots, structure, live, place, w0, w1, w2, w3, s_high, s_low, base, *refs):
+    outs = refs[:4]
+    w_all, pick_high, pick_low, total = refs[4:]
+    z, x, c = place[0], place[1], place[2]
+    part = tile // 2
+    half = outs[0].shape[1]
+    width = outs[0].shape[0]
+    for step, piece in enumerate((w0, w1, w2, w3)):
+        w_all[pl.ds(pl.multiple_of((z ^ step) * tile, tile), tile), :] = piece[...]
+    for slot in range(slots):
+        value = w_all[pl.ds(pl.multiple_of(structure[x, slot] * part, part), part), :]
+        high, low = halves(jnp.where(slot < live[x], value, 0.0))
+        pick_high[slot * part:(slot + 1) * part, :] = high
+        pick_low[slot * part:(slot + 1) * part, :] = low
+    total[...] = base[...] + dot3((pick_high[...], pick_low[...]), (s_high[...], s_low[...]), TN)
+    for which in range(2):
+        at = pl.ds(pl.multiple_of((x ^ which) * width, width), width)
+        for flip in range(2):
+            lanes = pl.ds(pl.multiple_of((c ^ flip) * half, half), half)
+            outs[2 * which + flip][...] = total[at, lanes]
+
+
+def last_kernel(place, *refs):
+    panel = refs[:4]
+    diag = refs[4:8]
+    panel_out, diag_out = refs[8:]
+    x, c = place[1], place[2]
+    half = panel[0].shape[1]
+    part = panel[0].shape[0]
+    width = diag[0].shape[0]
+    blocks = half // 128
+    for which in range(2):
+        member = x ^ which
+        total = diag[2 * which][...] + diag[2 * which + 1][...]
+        for block in range(blocks):
+            lanes = slice(block * 128, (block + 1) * 128)
+            at = pl.ds(2 * block + member, width, stride=2 * blocks)
+            diag_out[at, :] = total[:, lanes]
+            for flip in range(2):
+                first = (c ^ flip) * (part * 2 * blocks) + 2 * block + member
+                panel_out[pl.ds(first, part, stride=2 * blocks), :] = panel[2 * which + flip][:, lanes]
+
+
+def many_rows(ancestor_cov, panel_factor, diag_inverse, structure, live_counts):
     tile_rows = ancestor_cov.shape[0]
     local_blocks = ancestor_cov.shape[1]
     col_count = lax.axis_size("col")
@@ -71,6 +229,127 @@
     return (panel_cov, diag_cov)
 
 
+def local(ancestor_cov, panel_factor, diag_inverse, structure, live_counts):
+    rows = lax.axis_size("row")
+    if rows != 8:
+        return many_rows(ancestor_cov, panel_factor, diag_inverse, structure, live_counts)
+    tile = ancestor_cov.shape[0]
+    local_blocks = ancestor_cov.shape[1]
+    share, _, half = panel_factor.shape
+    whole, _, width = diag_inverse.shape
+    slots = structure.shape[1]
+    col = lax.axis_index("col")
+    row = lax.axis_index("row")
+    place = jnp.stack([row // 2, row % 2, col]).astype(jnp.int32)
+    smem = pl.BlockSpec(memory_space=pltpu.SMEM)
+    vmem = pl.BlockSpec(memory_space=pltpu.VMEM)
+
+    def like(*shape, dtype=F32):
+        return jax.ShapeDtypeStruct(shape, dtype)
+
+    def call(kernel, name, outs, scalars, arrays, scratch=()):
+        return pl.pallas_call(
+            kernel,
+            out_shape=outs,
+            in_specs=[smem] * len(scalars) + [vmem] * len(arrays),
+            out_specs=[vmem] * len(outs),
+            scratch_shapes=list(scratch),
+            compiler_params=pltpu.CompilerParams(vmem_limit_bytes=VMEM_LIMIT),
+            name=name,
+        )(*scalars, *arrays)
+
+    def move(value, z_step, x_step, flip):
+        pairs = [
+            (r * 2 + c, (r ^ (2 * z_step + x_step)) * 2 + (c ^ flip))
+            for r in range(rows)
+            for c in range(2)
+        ]
+        return lax.ppermute(value, ("row", "col"), pairs)
+
+    factor_lines = (
+        panel_factor.reshape(share, 2, half // 128, 128).transpose(0, 2, 1, 3).reshape(-1, 128)
+    )
+    bundle = share + width
+    own, send = call(
+        pack_kernel,
+        "pack",
+        [like(bundle, half)] * 2,
+        [place],
+        [factor_lines, diag_inverse.transpose(1, 2, 0)],
+    )
+    near = move(send, 0, 1, 0)
+    own_far = move(own, 2, 0, 0)
+    own_side = move(own, 1, 0, 0)
+    c_own = ancestor_cov.reshape(2, -1, 128)
+    c_near = move(c_own, 0, 1, 0)
+    near_far = move(near, 2, 0, 0)
+    near_side = move(near, 1, 0, 0)
+    opposite = move(jnp.concatenate([own_far, near_far]), 1, 0, 0)
+    c_both = jnp.stack([c_own, c_near], axis=1)
+    c_keep = lax.dynamic_index_in_dim(c_both, col, 0, keepdims=False)
+    c_got = move(lax.dynamic_index_in_dim(c_both, 1 - col, 0, keepdims=False), 0, 0, 1)
+    theirs = [
+        move(jnp.concatenate([own, near]), 0, 0, 1),
+        move(jnp.concatenate([own_far, near_far, own_side, near_side]), 0, 0, 1),
+        move(opposite, 0, 0, 1),
+    ]
+    mine = [own, near, own_far, near_far, own_side, near_side, opposite]
+    part = tile // 2
+    outs = call(
+        functools.partial(product_kernel, share, tile, slots),
+        "products",
+        [like(part, half)] * 4
+        + [like(tile, 2 * width)] * 4
+        + [like(slots * tile, whole, dtype=BF16)] * 2
+        + [like(whole, whole, dtype=BF16)] * 2,
+        [structure, live_counts, place],
+        [c_keep, c_got] + mine + theirs,
+        [
+            pltpu.VMEM((tile, slots * tile), BF16),
+            pltpu.VMEM((tile, slots * tile), BF16),
+            pltpu.VMEM((tile, whole), F32),
+        ],
+    )
+    panel, w, split = outs[:4], outs[4:8], outs[8:]
+    w = [w[0]] + [move(w[step], step, 0, 0) for step in range(1, 4)]
+    steps = ((0, 0), (0, 1), (1, 0), (1, 1))
+    panel = [panel[0]] + [move(v, 0, *s) for v, s in zip(panel[1:], steps[1:])]
+    scaled = call(
+        functools.partial(scaled_kernel, tile, slots),
+        "scaled",
+        [like(slots * part, whole, dtype=BF16)] * 2 + [like(2 * width, whole)],
+        [place],
+        split,
+        [pltpu.VMEM((slots * part, whole), BF16)] * 2,
+    )
+    diag = call(
+        functools.partial(diag_kernel, tile, slots),
+        "diag_block",
+        [like(width, half)] * 4,
+        [structure, live_counts, place],
+        w + list(scaled),
+        [
+            pltpu.VMEM((rows * part, 2 * width), F32),
+            pltpu.VMEM((slots * part, 2 * width), BF16),
+            pltpu.VMEM((slots * part, 2 * width), BF16),
+            pltpu.VMEM((2 * width, whole), F32),
+        ],
+    )
+    diag = [diag[0]] + [move(v, 0, *s) for v, s in zip(diag[1:], steps[1:])]
+    panel_lines, diag_lines = call(
+        last_kernel,
+        "outputs",
+        [like(tile * 2 * half // 128, 128), like(width * 2 * half // 128, 128)],
+        [place],
+        panel + diag,
+    )
+
+    def unfold(value, count):
+        return value.reshape(count, half // 128, 2, 128).transpose(0, 2, 1, 3).reshape(count, 2, half)
+
+    return unfold(panel_lines, tile), unfold(diag_lines, width)
+
+
 def solution(mesh):
     placed = (
         P(("mp", "row"), None, "col", None),

time: 249 us -> 58.4 us (0.23)
  waiting for transfers between devices: 197 us -> 22 us
  starting transfers between devices: 0.2 us -> 26.5 us
  local copies, waits for them, and re-layouts: 17 us -> 1.9 us
  between operations: 15.3 us -> 0.77 us
  matrix products: 12.7 us -> 0 us
  Pallas kernels: 0 us -> 6.64 us
  other arithmetic: 4.18 us -> 0.2 us
    all_gather x2 -> x0, waiting for transfers between devices: 104 us -> none  [the longest x1 52.7 us: local(): arrived = lax.all_gather(factor_rows, 'row', axis=0, tiled=True)]
    reduce_scatter x1 -> x0, waiting for transfers between devices: 60.9 us -> none  [local(): lax.psum_scatter(jnp.einsum('tsi,tsn->isn', owned, product_half, precisio...]
    psum x2 -> x0, waiting for transfers between devices: 31.9 us -> none  [the longest x1 18.6 us: local(): factor_rows = lax.psum(factor_term, 'col')]
    ppermute x0 -> x20, starting transfers between devices: none -> 26.5 us  [move(): return lax.ppermute(value, ('row', 'col'), pairs)]
    ppermute x0 -> x20, waiting for transfers between devices: none -> 22 us  [move(): return lax.ppermute(value, ('row', 'col'), pairs)]
    dot_general x5 -> x0, matrix products: 12.7 us -> none  [the longest x2 5.67 us: local(): jnp.dot(sig_cols, weighted, precision=lax.Precision.HIGHEST, preferred_el...]
    gather x4 -> x0, local copies, waits for them, and re-layouts: 7.01 us -> none  [the longest x2 3.85 us: local(): sig_cols = jnp.take(flat_cov, column_index, axis=1)]
    pallas_call x0 -> x5, Pallas kernels: none -> 6.64 us  [call(): pl.pallas_call(kernel, out_shape=outs, in_specs=[smem] * len(scalars) + [...]
  transfers between devices with their start and end apart: 5 -> 20, of which waited for: 5 -> 9; matrix products, arithmetic and copies ran while one was open for 6% -> 0% of each run, Pallas kernels for 0% -> 4%
where the time goes in v3:
time: 58.4 us; the launch traced here: 58.1 us
  starting transfers between devices  26.5 us (45%)
  waiting for transfers between devices  22 us (38%)
  Pallas kernels  6.64 us (11%)
  local copies, waits for them, and re-layouts  1.9 us (3%)
  between operations  0.77 us (1%)
    ppermute x20, starting transfers between devices, move(): return lax.ppermute(value, ('row', 'col'), pairs)  26.5 us
    ppermute x20, waiting for transfers between devices, move(): return lax.ppermute(value, ('row', 'col'), pairs)  22 us
    pallas_call x5, Pallas kernels, call(): pl.pallas_call(kernel, out_shape=outs, in_specs=[smem] * len(scalars) + [...  6.64 us
    unnamed x10, local copies, waits for them, and re-layouts  1.9 us
  transfers between devices with their start and end apart: 20, of which 9 were waited for; matrix products, arithmetic and copies ran while one was open for 0% of the time, Pallas kernels for 4%

profile of v3, /device:TPU:1, one launch (start us, length us, event | category | flops | bytes accessed | tf_op | source)
XLA Modules:
  0.0 58.1 jit_solution(8016181833199087137)
XLA Ops:
  3.2 2.1 %collective-permute-start.2 = (f32[160,256]{1,0:T(8,128)S(1)}, f32[160,256]{1,0:T(8,128)S(1)}, u32[]{:S(2)}, u32[]{:S(2)}) collective-permute-start(f32[160,256]{1,0:T(8,128)S(1)} %get-tuple-element.26), channel_id=1, source_target_pairs={{0,2},{1,3},{2,0},{3,1},{4,6},{5,7},{6,4},{7,5},{8,10},{9,11},{10,... | collective-permute-start | bytes 491528 | tf_op jit(solution)/shard_map/ppermute | solution.py:267
  5.3 2.3 %collective-permute-start.3 = (f32[160,256]{1,0:T(8,128)S(1)}, f32[160,256]{1,0:T(8,128)S(1)}, u32[]{:S(2)}, u32[]{:S(2)}) collective-permute-start(f32[160,256]{1,0:T(8,128)S(1)} %get-tuple-element.25.refs_5_), channel_id=1, source_target_pairs={{0,8},{1,9},{2,10},{3,11},{4,12},{5,13},{6,14},{7,15},{8,0},{9,1},... | collective-permute-start | bytes 491528 | tf_op jit(solution)/shard_map/ppermute | solution.py:267
  7.6 1.6 %collective-permute-done.2.refs_6_ = f32[160,256]{1,0:T(8,128)S(1)} collective-permute-done((f32[160,256]{1,0:T(8,128)S(1)}, f32[160,256]{1,0:T(8,128)S(1)}, u32[]{:S(2)}, u32[]{:S(2)}) %collective-permute-start.2) | collective-permute-done | bytes 163872 | tf_op jit(solution)/shard_map/ppermute | solution.py:267
  9.2 2.2 %collective-permute-start.4 = (f32[160,256]{1,0:T(8,128)S(1)}, f32[160,256]{1,0:T(8,128)S(1)}, u32[]{:S(2)}, u32[]{:S(2)}) collective-permute-start(f32[160,256]{1,0:T(8,128)S(1)} %collective-permute-done.2.refs_6_), channel_id=1, source_target_pairs={{0,8},{1,9},{2,10},{3,11},{4,12},{5,13},{6,14},{7,15},{8,0},{9,1},... | collective-permute-start | bytes 491528 | tf_op jit(solution)/shard_map/ppermute | solution.py:267
  11.5 1.3 %collective-permute-start.5 = (f32[160,256]{1,0:T(8,128)S(1)}, f32[160,256]{1,0:T(8,128)S(1)}, u32[]{:S(2)}, u32[]{:S(2)}) collective-permute-start(f32[160,256]{1,0:T(8,128)S(1)} %get-tuple-element.25.refs_5_), channel_id=1, source_target_pairs={{0,4},{1,5},{2,6},{3,7},{4,0},{5,1},{6,2},{7,3},{8,12},{9,13},{10,... | collective-permute-start | bytes 491528 | tf_op jit(solution)/shard_map/ppermute | solution.py:267
  12.9 4.2 %collective-permute-done.3.refs_7_ = f32[160,256]{1,0:T(8,128)S(1)} collective-permute-done((f32[160,256]{1,0:T(8,128)S(1)}, f32[160,256]{1,0:T(8,128)S(1)}, u32[]{:S(2)}, u32[]{:S(2)}) %collective-permute-start.3) | collective-permute-done | bytes 163872 | tf_op jit(solution)/shard_map/ppermute | solution.py:267
  17.2 4.6 %collective-permute-done.4.refs_8_ = f32[160,256]{1,0:T(8,128)S(1)} collective-permute-done((f32[160,256]{1,0:T(8,128)S(1)}, f32[160,256]{1,0:T(8,128)S(1)}, u32[]{:S(2)}, u32[]{:S(2)}) %collective-permute-start.4) | collective-permute-done | bytes 163872 | tf_op jit(solution)/shard_map/ppermute | solution.py:267
  21.8 1.5 %collective-permute-start.7 = (f32[320,256]{1,0:T(8,128)S(1)}, f32[320,256]{1,0:T(8,128)S(1)}, u32[]{:S(2)}, u32[]{:S(2)}) collective-permute-start(f32[320,256]{1,0:T(8,128)S(1)} %pad_maximum_fusion.1), channel_id=1, source_target_pairs={{0,4},{1,5},{2,6},{3,7},{4,0},{5,1},{6,2},{7,3},{8,12},{9,13},{10,... | collective-permute-start | bytes 983048 | tf_op jit(solution)/shard_map/ppermute | solution.py:267
  23.3 1.8 %collective-permute-done.6.refs_10_ = f32[160,256]{1,0:T(8,128)S(1)} collective-permute-done((f32[160,256]{1,0:T(8,128)S(1)}, f32[160,256]{1,0:T(8,128)S(1)}, u32[]{:S(2)}, u32[]{:S(2)}) %collective-permute-start.6) | collective-permute-done | bytes 163872 | tf_op jit(solution)/shard_map/ppermute | solution.py:267
  25.2 3.9 %collective-permute-start.9 = (f32[640,256]{1,0:T(8,128)S(1)}, f32[640,256]{1,0:T(8,128)S(1)}, u32[]{:S(2)}, u32[]{:S(2)}) collective-permute-start(f32[640,256]{1,0:T(8,128)S(1)} %pad_maximum_fusion), channel_id=1, source_target_pairs={{0,1},{1,0},{2,3},{3,2},{4,5},{5,4},{6,7},{7,6},{8,9},{9,8},{10,11... | collective-permute-start | bytes 1966088 | tf_op jit(solution)/shard_map/ppermute | solution.py:267
  29.7 2.4 %collective-permute-done.7.refs_11_ = f32[320,256]{1,0:T(8,128)S(1)} collective-permute-done((f32[320,256]{1,0:T(8,128)S(1)}, f32[320,256]{1,0:T(8,128)S(1)}, u32[]{:S(2)}, u32[]{:S(2)}) %collective-permute-start.7) | collective-permute-done | bytes 327712 | tf_op jit(solution)/shard_map/ppermute | solution.py:267
  32.1 2.1 %collective-permute-start.10 = (f32[320,256]{1,0:T(8,128)S(1)}, f32[320,256]{1,0:T(8,128)S(1)}, u32[]{:S(2)}, u32[]{:S(2)}) collective-permute-start(f32[320,256]{1,0:T(8,128)S(1)} %collective-permute-done.7.refs_11_), channel_id=1, source_target_pairs={{0,1},{1,0},{2,3},{3,2},{4,5},{5,4},{6,7},{7,6},{8,9},{9,8},{10,11... | collective-permute-start | bytes 983048 | tf_op jit(solution)/shard_map/ppermute | solution.py:267
  34.3 2.7 %collective-permute-done = f32[2,256,128]{2,1,0:T(8,128)S(1)} collective-permute-done((f32[2,256,128]{2,1,0:T(8,128)S(1)}, f32[2,256,128]{2,1,0:T(8,128)S(1)}, u32[]{:S(2)}, u32[]{:S(2)}) %collective-permute-start) | collective-permute-done | bytes 262176 | tf_op jit(solution)/shard_map/ppermute | solution.py:267
  38.0 1.2 %collective-permute-done.1.refs_4_ = f32[2,256,128]{2,1,0:T(8,128)S(1)} collective-permute-done((f32[2,256,128]{2,1,0:T(8,128)S(1)}, f32[2,256,128]{2,1,0:T(8,128)S(1)}, u32[]{:S(2)}, u32[]{:S(2)}) %collective-permute-start.1) | collective-permute-done | bytes 262176 | tf_op jit(solution)/shard_map/ppermute | solution.py:267
  39.1 2.2 %products.1 = (f32[64,256]{1,0:T(8,128)S(1)}, f32[64,256]{1,0:T(8,128)S(1)}, f32[64,256]{1,0:T(8,128)S(1)}, f32[64,256]{1,0:T(8,128)S(1)}, f32[128,128]{1,0:T(8,...) custom-call(s32[2,6]{1,0:T(2,128)S(1)} %copy-done.2, ...), custom_call_target="tpu_custom_call" | custom-call | tf_op jit(solution)/shard_map/products/pallas_call | solution.py:251
  41.4 1.1 %collective-permute-start.15 = (f32[128,128]{1,0:T(8,128)S(1)}, f32[128,128]{1,0:T(8,128)S(1)}, u32[]{:S(2)}, u32[]{:S(2)}) collective-permute-start(f32[128,128]{1,0:T(8,128)S(1)} %get-tuple-element.33), channel_id=1, source_target_pairs={{0,8},{1,9},{2,10},{3,11},{4,12},{5,13},{6,14},{7,15},{8,0},{9,1},... | collective-permute-start | bytes 196616 | tf_op jit(solution)/shard_map/ppermute | solution.py:267
  42.5 2.4 %collective-permute-start.16 = (f32[128,128]{1,0:T(8,128)S(1)}, f32[128,128]{1,0:T(8,128)S(1)}, u32[]{:S(2)}, u32[]{:S(2)}) collective-permute-start(f32[128,128]{1,0:T(8,128)S(1)} %get-tuple-element.34), channel_id=1, source_target_pairs={{0,12},{1,13},{2,14},{3,15},{4,8},{5,9},{6,10},{7,11},{8,4},{9,5},... | collective-permute-start | bytes 196616 | tf_op jit(solution)/shard_map/ppermute | solution.py:267
  44.9 1.2 %collective-permute-start.11 = (f32[64,256]{1,0:T(8,128)S(1)}, f32[64,256]{1,0:T(8,128)S(1)}, u32[]{:S(2)}, u32[]{:S(2)}) collective-permute-start(f32[64,256]{1,0:T(8,128)S(1)} %get-tuple-element.28), channel_id=1, source_target_pairs={{0,1},{1,0},{2,3},{3,2},{4,5},{5,4},{6,7},{7,6},{8,9},{9,8},{10,11... | collective-permute-start | bytes 196616 | tf_op jit(solution)/shard_map/ppermute | solution.py:267
  46.4 1.5 %scaled.1 = (bf16[384,512]{1,0:T(8,128)(2,1)S(1)}, bf16[384,512]{1,0:T(8,128)(2,1)S(1)}, f32[128,512]{1,0:T(8,128)S(1)}) custom-call(s32[3]{0:T(128)S(1)} %pad_add_fusion.place.refs_2_, bf16[768,512]{1,0:T(8,128)(2,1)S(1)} %get-tuple-element.35.f_high, bf16[768,512]{1,0:T(8,128)(2,1)S(1)} %get-tuple-element.36.f_low, ...), custom_call_target="tpu_custom_call" | custom-call | tf_op jit(solution)/shard_map/scaled/pallas_call | solution.py:251
  47.9 1.5 %collective-permute-start.13 = (f32[64,256]{1,0:T(8,128)S(1)}, f32[64,256]{1,0:T(8,128)S(1)}, u32[]{:S(2)}, u32[]{:S(2)}) collective-permute-start(f32[64,256]{1,0:T(8,128)S(1)} %get-tuple-element.30), channel_id=1, source_target_pairs={{0,3},{1,2},{2,1},{3,0},{4,7},{5,6},{6,5},{7,4},{8,11},{9,10},{10,... | collective-permute-start | bytes 196616 | tf_op jit(solution)/shard_map/ppermute | solution.py:267
  52.0 1.2 %collective-permute-start.19 = (f32[64,256]{1,0:T(8,128)S(1)}, f32[64,256]{1,0:T(8,128)S(1)}, u32[]{:S(2)}, u32[]{:S(2)}) collective-permute-start(f32[64,256]{1,0:T(8,128)S(1)} %get-tuple-element.45), channel_id=1, source_target_pairs={{0,3},{1,2},{2,1},{3,0},{4,7},{5,6},{6,5},{7,4},{8,11},{9,10},{10,... | collective-permute-start | bytes 196616 | tf_op jit(solution)/shard_map/ppermute | solution.py:267
  53.2 1.9 %collective-permute-done.18.refs_6_ = f32[64,256]{1,0:T(8,128)S(1)} collective-permute-done((f32[64,256]{1,0:T(8,128)S(1)}, f32[64,256]{1,0:T(8,128)S(1)}, u32[]{:S(2)}, u32[]{:S(2)}) %collective-permute-start.18) | collective-permute-done | bytes 65568 | tf_op jit(solution)/shard_map/ppermute | solution.py:267
  55.2 1.6 %collective-permute-done.19.refs_7_ = f32[64,256]{1,0:T(8,128)S(1)} collective-permute-done((f32[64,256]{1,0:T(8,128)S(1)}, f32[64,256]{1,0:T(8,128)S(1)}, u32[]{:S(2)}, u32[]{:S(2)}) %collective-permute-start.19) | collective-permute-done | bytes 65568 | tf_op jit(solution)/shard_map/ppermute | solution.py:267
  56.7 1.3 %outputs.1 = (f32[512,128]{1,0:T(8,128)}, f32[256,128]{1,0:T(8,128)}) custom-call(s32[3]{0:T(128)S(1)} %pad_add_fusion.place.refs_2_, f32[64,256]{1,0:T(8,128)S(1)} %get-tuple-element.27.refs_0_, f32[64,256]{1,0:T(8,128)S(1)} %collective-permute-done.11.refs_1_, f32[64,256]{1,0:T(8,128)S(1)} %collective-permute-done.12.refs_2_, ...), custom_call_target="tpu_custom_call" | custom-call | tf_op jit(solution)/shard_map/outputs/pallas_call | solution.py:251
  (36 shorter events, 7.2 us)
Async XLA Ops:
  0.7 1.0 %copy-start = (f32[512,2,64]{0,2,1:T(8,128)S(1)}, f32[512,2,64]{0,2,1:T(8,128)}, u32[]{:S(2)}) copy-start(f32[512,2,64]{0,2,1:T(8,128)} %param.7) | copy-start | bytes 786436
  3.2 6.0 %collective-permute-start.2 = (f32[160,256]{1,0:T(8,128)S(1)}, f32[160,256]{1,0:T(8,128)S(1)}, u32[]{:S(2)}, u32[]{:S(2)}) collective-permute-start(f32[160,256]{1,0:T(8,128)S(1)} %get-tuple-element.26), channel_id=1, source_target_pairs={{0,2},{1,3},{2,0},{3,1},{4,6},{5,7},{6,4},{7,5},{8,10},{9,11},{10,... | collective-permute-start | bytes 491528 | tf_op jit(solution)/shard_map/ppermute | solution.py:267
  5.3 11.9 %collective-permute-start.3 = (f32[160,256]{1,0:T(8,128)S(1)}, f32[160,256]{1,0:T(8,128)S(1)}, u32[]{:S(2)}, u32[]{:S(2)}) collective-permute-start(f32[160,256]{1,0:T(8,128)S(1)} %get-tuple-element.25.refs_5_), channel_id=1, source_target_pairs={{0,8},{1,9},{2,10},{3,11},{4,12},{5,13},{6,14},{7,15},{8,0},{9,1},... | collective-permute-start | bytes 491528 | tf_op jit(solution)/shard_map/ppermute | solution.py:267
  9.2 12.6 %collective-permute-start.4 = (f32[160,256]{1,0:T(8,128)S(1)}, f32[160,256]{1,0:T(8,128)S(1)}, u32[]{:S(2)}, u32[]{:S(2)}) collective-permute-start(f32[160,256]{1,0:T(8,128)S(1)} %collective-permute-done.2.refs_6_), channel_id=1, source_target_pairs={{0,8},{1,9},{2,10},{3,11},{4,12},{5,13},{6,14},{7,15},{8,0},{9,1},... | collective-permute-start | bytes 491528 | tf_op jit(solution)/shard_map/ppermute | solution.py:267
  11.5 11.9 %collective-permute-start.5 = (f32[160,256]{1,0:T(8,128)S(1)}, f32[160,256]{1,0:T(8,128)S(1)}, u32[]{:S(2)}, u32[]{:S(2)}) collective-permute-start(f32[160,256]{1,0:T(8,128)S(1)} %get-tuple-element.25.refs_5_), channel_id=1, source_target_pairs={{0,4},{1,5},{2,6},{3,7},{4,0},{5,1},{6,2},{7,3},{8,12},{9,13},{10,... | collective-permute-start | bytes 491528 | tf_op jit(solution)/shard_map/ppermute | solution.py:267
  12.8 12.4 %collective-permute-start.6 = (f32[160,256]{1,0:T(8,128)S(1)}, f32[160,256]{1,0:T(8,128)S(1)}, u32[]{:S(2)}, u32[]{:S(2)}) collective-permute-start(f32[160,256]{1,0:T(8,128)S(1)} %collective-permute-done.2.refs_6_), channel_id=1, source_target_pairs={{0,4},{1,5},{2,6},{3,7},{4,0},{5,1},{6,2},{7,3},{8,12},{9,13},{10,... | collective-permute-start | bytes 491528 | tf_op jit(solution)/shard_map/ppermute | solution.py:267
  21.8 7.3 %copy-start.4 = (f32[128,4,1,128]{3,2,1,0:T(1,128)S(1)}, f32[128,4,1,128]{3,2,1,0:T(1,128)}, u32[]{:S(2)}) copy-start(f32[128,4,1,128]{3,2,1,0:T(1,128)} %param.5) | copy-start | bytes 786436
  21.8 10.3 %collective-permute-start.7 = (f32[320,256]{1,0:T(8,128)S(1)}, f32[320,256]{1,0:T(8,128)S(1)}, u32[]{:S(2)}, u32[]{:S(2)}) collective-permute-start(f32[320,256]{1,0:T(8,128)S(1)} %pad_maximum_fusion.1), channel_id=1, source_target_pairs={{0,4},{1,5},{2,6},{3,7},{4,0},{5,1},{6,2},{7,3},{8,12},{9,13},{10,... | collective-permute-start | bytes 983048 | tf_op jit(solution)/shard_map/ppermute | solution.py:267
  25.2 14.0 %collective-permute-start.9 = (f32[640,256]{1,0:T(8,128)S(1)}, f32[640,256]{1,0:T(8,128)S(1)}, u32[]{:S(2)}, u32[]{:S(2)}) collective-permute-start(f32[640,256]{1,0:T(8,128)S(1)} %pad_maximum_fusion), channel_id=1, source_target_pairs={{0,1},{1,0},{2,3},{3,2},{4,5},{5,4},{6,7},{7,6},{8,9},{9,8},{10,11... | collective-permute-start | bytes 1966088 | tf_op jit(solution)/shard_map/ppermute | solution.py:267
  29.1 7.9 %collective-permute-start = (f32[2,256,128]{2,1,0:T(8,128)S(1)}, f32[2,256,128]{2,1,0:T(8,128)S(1)}, u32[]{:S(2)}, u32[]{:S(2)}) collective-permute-start(f32[2,256,128]{2,1,0:T(8,128)S(1)} %bitcast.30), channel_id=1, source_target_pairs={{0,2},{1,3},{2,0},{3,1},{4,6},{5,7},{6,4},{7,5},{8,10},{9,11},{10,... | collective-permute-start | bytes 786440 | tf_op jit(solution)/shard_map/ppermute | solution.py:267
  29.3 8.6 %collective-permute-start.8 = (f32[320,256]{1,0:T(8,128)S(1)}, f32[320,256]{1,0:T(8,128)S(1)}, u32[]{:S(2)}, u32[]{:S(2)}) collective-permute-start(f32[320,256]{1,0:T(8,128)S(1)} %pad_maximum_fusion.2), channel_id=1, source_target_pairs={{0,1},{1,0},{2,3},{3,2},{4,5},{5,4},{6,7},{7,6},{8,9},{9,8},{10,11... | collective-permute-start | bytes 983048 | tf_op jit(solution)/shard_map/ppermute | solution.py:267
  32.1 7.0 %collective-permute-start.10 = (f32[320,256]{1,0:T(8,128)S(1)}, f32[320,256]{1,0:T(8,128)S(1)}, u32[]{:S(2)}, u32[]{:S(2)}) collective-permute-start(f32[320,256]{1,0:T(8,128)S(1)} %collective-permute-done.7.refs_11_), channel_id=1, source_target_pairs={{0,1},{1,0},{2,3},{3,2},{4,5},{5,4},{6,7},{7,6},{8,9},{9,8},{10,11... | collective-permute-start | bytes 983048 | tf_op jit(solution)/shard_map/ppermute | solution.py:267
  37.0 2.1 %copy-start.2 = (s32[2,6]{1,0:T(2,128)S(1)}, s32[2,6]{1,0:T(2,128)}, u32[]{:S(2)}) copy-start(s32[2,6]{1,0:T(2,128)} %structure.1) | copy-start | bytes 148
  37.0 2.1 %copy-start.3 = (s32[2]{0:T(128)S(1)}, s32[2]{0:T(128)}, u32[]{:S(2)}) copy-start(s32[2]{0:T(128)} %live.1) | copy-start | bytes 28
  37.0 2.1 %collective-permute-start.1 = (f32[2,256,128]{2,1,0:T(8,128)S(1)}, f32[2,256,128]{2,1,0:T(8,128)S(1)}, u32[]{:S(2)}, u32[]{:S(2)}) collective-permute-start(f32[2,256,128]{2,1,0:T(8,128)S(1)} %get-tuple-element.48), channel_id=1, source_target_pairs={{0,1},{1,0},{2,3},{3,2},{4,5},{5,4},{6,7},{7,6},{8,9},{9,8},{10,11... | collective-permute-start | bytes 786440 | tf_op jit(solution)/shard_map/ppermute | solution.py:267
  41.3 6.6 %collective-permute-start.14 = (f32[128,128]{1,0:T(8,128)S(1)}, f32[128,128]{1,0:T(8,128)S(1)}, u32[]{:S(2)}, u32[]{:S(2)}) collective-permute-start(f32[128,128]{1,0:T(8,128)S(1)} %get-tuple-element.32), channel_id=1, source_target_pairs={{0,4},{1,5},{2,6},{3,7},{4,0},{5,1},{6,2},{7,3},{8,12},{9,13},{10,... | collective-permute-start | bytes 196616 | tf_op jit(solution)/shard_map/ppermute | solution.py:267
  41.4 8.0 %collective-permute-start.15 = (f32[128,128]{1,0:T(8,128)S(1)}, f32[128,128]{1,0:T(8,128)S(1)}, u32[]{:S(2)}, u32[]{:S(2)}) collective-permute-start(f32[128,128]{1,0:T(8,128)S(1)} %get-tuple-element.33), channel_id=1, source_target_pairs={{0,8},{1,9},{2,10},{3,11},{4,12},{5,13},{6,14},{7,15},{8,0},{9,1},... | collective-permute-start | bytes 196616 | tf_op jit(solution)/shard_map/ppermute | solution.py:267
  42.5 6.9 %collective-permute-start.16 = (f32[128,128]{1,0:T(8,128)S(1)}, f32[128,128]{1,0:T(8,128)S(1)}, u32[]{:S(2)}, u32[]{:S(2)}) collective-permute-start(f32[128,128]{1,0:T(8,128)S(1)} %get-tuple-element.34), channel_id=1, source_target_pairs={{0,12},{1,13},{2,14},{3,15},{4,8},{5,9},{6,10},{7,11},{8,4},{9,5},... | collective-permute-start | bytes 196616 | tf_op jit(solution)/shard_map/ppermute | solution.py:267
  44.9 7.0 %collective-permute-start.11 = (f32[64,256]{1,0:T(8,128)S(1)}, f32[64,256]{1,0:T(8,128)S(1)}, u32[]{:S(2)}, u32[]{:S(2)}) collective-permute-start(f32[64,256]{1,0:T(8,128)S(1)} %get-tuple-element.28), channel_id=1, source_target_pairs={{0,1},{1,0},{2,3},{3,2},{4,5},{5,4},{6,7},{7,6},{8,9},{9,8},{10,11... | collective-permute-start | bytes 196616 | tf_op jit(solution)/shard_map/ppermute | solution.py:267
  46.2 7.0 %collective-permute-start.12 = (f32[64,256]{1,0:T(8,128)S(1)}, f32[64,256]{1,0:T(8,128)S(1)}, u32[]{:S(2)}, u32[]{:S(2)}) collective-permute-start(f32[64,256]{1,0:T(8,128)S(1)} %get-tuple-element.29), channel_id=1, source_target_pairs={{0,2},{1,3},{2,0},{3,1},{4,6},{5,7},{6,4},{7,5},{8,10},{9,11},{10,... | collective-permute-start | bytes 196616 | tf_op jit(solution)/shard_map/ppermute | solution.py:267
  47.9 5.3 %collective-permute-start.13 = (f32[64,256]{1,0:T(8,128)S(1)}, f32[64,256]{1,0:T(8,128)S(1)}, u32[]{:S(2)}, u32[]{:S(2)}) collective-permute-start(f32[64,256]{1,0:T(8,128)S(1)} %get-tuple-element.30), channel_id=1, source_target_pairs={{0,3},{1,2},{2,1},{3,0},{4,7},{5,6},{6,5},{7,4},{8,11},{9,10},{10,... | collective-permute-start | bytes 196616 | tf_op jit(solution)/shard_map/ppermute | solution.py:267
  50.4 2.8 %collective-permute-start.17 = (f32[64,256]{1,0:T(8,128)S(1)}, f32[64,256]{1,0:T(8,128)S(1)}, u32[]{:S(2)}, u32[]{:S(2)}) collective-permute-start(f32[64,256]{1,0:T(8,128)S(1)} %get-tuple-element.43), channel_id=1, source_target_pairs={{0,1},{1,0},{2,3},{3,2},{4,5},{5,4},{6,7},{7,6},{8,9},{9,8},{10,11... | collective-permute-start | bytes 196616 | tf_op jit(solution)/shard_map/ppermute | solution.py:267
  51.5 3.7 %collective-permute-start.18 = (f32[64,256]{1,0:T(8,128)S(1)}, f32[64,256]{1,0:T(8,128)S(1)}, u32[]{:S(2)}, u32[]{:S(2)}) collective-permute-start(f32[64,256]{1,0:T(8,128)S(1)} %get-tuple-element.44), channel_id=1, source_target_pairs={{0,2},{1,3},{2,0},{3,1},{4,6},{5,7},{6,4},{7,5},{8,10},{9,11},{10,... | collective-permute-start | bytes 196616 | tf_op jit(solution)/shard_map/ppermute | solution.py:267
  52.0 4.8 %collective-permute-start.19 = (f32[64,256]{1,0:T(8,128)S(1)}, f32[64,256]{1,0:T(8,128)S(1)}, u32[]{:S(2)}, u32[]{:S(2)}) collective-permute-start(f32[64,256]{1,0:T(8,128)S(1)} %get-tuple-element.45), channel_id=1, source_target_pairs={{0,3},{1,2},{2,1},{3,0},{4,7},{5,6},{6,5},{7,4},{8,11},{9,10},{10,... | collective-permute-start | bytes 196616 | tf_op jit(solution)/shard_map/ppermute | solution.py:267
  (1 other events, 0.9 us)

commit v4 on v0

--- a/solution.py
+++ b/solution.py
@@ -1,10 +1,209 @@
+import functools
+
 import jax
 import jax.numpy as jnp
 from jax import lax
+from jax.experimental import pallas as pl
+from jax.experimental.pallas import tpu as pltpu
 from jax.sharding import PartitionSpec as P
 
-
-def local(ancestor_cov, panel_factor, diag_inverse, structure, live_counts):
+F32 = jnp.float32
+BF16 = jnp.bfloat16
+NT = (((1,), (1,)), ((), ()))
+NN = (((1,), (0,)), ((), ()))
+TN = (((0,), (0,)), ((), ()))
+VMEM_LIMIT = 20 * 1024 * 1024
+
+
+def halves(value):
+    high = value.astype(BF16)
+    low = (value - high.astype(F32)).astype(BF16)
+    return high, low
+
+
+def dot3(left, right, dims):
+    left_high, left_low = left
+    right_high, right_low = right
+
+    def one(a, b):
+        return lax.dot_general(a, b, dims, preferred_element_type=F32)
+
+    return one(left_high, right_low) + one(left_low, right_high) + one(left_high, right_high)
+
+
+def split(value, high, low, at):
+    high[at], low[at] = halves(value)
+
+
+def pack_kernel(place, factor, inverse, own, send, lines, sem):
+    x = place[1]
+    c = place[2]
+    half = own.shape[1]
+    width = inverse.shape[1]
+    share = own.shape[0] - width
+    blocks = half // 128
+    lanes = pl.ds(pl.multiple_of(c * half, half), half)
+    copies = [pltpu.make_async_copy(factor, lines, sem.at[0])]
+    for index, (out, member) in enumerate(((own, x), (send, 1 - x))):
+        copies.append(
+            pltpu.make_async_copy(
+                inverse.at[member, :, lanes], out.at[pl.ds(share, width), :], sem.at[1 + index]
+            )
+        )
+    for copy in copies:
+        copy.start()
+    copies[0].wait()
+    for out, member in ((own, x), (send, 1 - x)):
+        for block in range(blocks):
+            at = pl.ds(2 * block + member, share, stride=2 * blocks)
+            out[:share, block * 128:(block + 1) * 128] = lines[at, :]
+    copies[1].wait()
+    copies[2].wait()
+
+
+def early_kernel(share, tile, slots, structure, live, place, c_own, c_near, c_sib, *refs):
+    mine = refs[:6]
+    theirs = refs[6]
+    grown, last_high, last_low, f_high, f_low, d_high, d_low, pick = refs[7:]
+    z, x, c = place[0], place[1], place[2]
+    half = theirs.shape[1]
+    block = mine[0].shape[0]
+    width = block - share
+    for index in range(6):
+        source = 2 * (z ^ (0, 2, 1)[index // 2]) + (x ^ (index % 2))
+        f_at = pl.ds(pl.multiple_of(source * share, share), share)
+        d_at = pl.ds(pl.multiple_of(source * width, width), width)
+        for first, value in ((0, mine[index]), (half, theirs.at[index * block:(index + 1) * block, :])):
+            lanes = slice(first, first + half)
+            split(value[:share, :], f_high, f_low, (f_at, lanes))
+            split(value[share:, :], d_high, d_low, (d_at, lanes))
+    far = 2 * (z ^ 3) * share
+    f_at = pl.ds(pl.multiple_of(far, 2 * share), 2 * share)
+    f_high[f_at, :] = jnp.zeros((2 * share, 2 * half), BF16)
+    f_low[f_at, :] = jnp.zeros((2 * share, 2 * half), BF16)
+    blocks = c_own.shape[0] // tile
+    for slot in range(slots):
+        anc = structure[x, slot]
+        rows = pl.ds(anc // 2, tile, stride=blocks)
+        other = pl.ds(c_own.shape[0] + anc // 2, tile, stride=blocks)
+        for which, (here, there) in enumerate(((c_own, rows), (c_near, other))):
+            value = jnp.where(anc % 2 == c, here[rows, :], c_sib[there, :])
+            at = pl.ds(pl.multiple_of((x ^ which) * tile, tile), tile)
+            pick[at, slot * tile:(slot + 1) * tile] = jnp.where(slot < live[x], value, 0.0)
+    picked = pick[...]
+    grown[...] = dot3(halves(picked), (f_high[...], f_low[...]), NN)
+    total = slots * tile
+    turned = pltpu.roll(picked, total - far, 1)
+    last_high[...], last_low[...] = halves(turned[:, :last_high.shape[1]])
+
+
+def product_kernel(share, tile, slots, structure, live, place, *refs):
+    grown, last_high, last_low, d_high, d_low, mine, theirs = refs[:7]
+    panel_out = refs[7:9]
+    w_out = refs[9:13]
+    ff_high, ff_low, fd_high, fd_low = refs[13:17]
+    product = refs[17]
+    z, x, c = place[0], place[1], place[2]
+    half = mine.shape[1]
+    block = mine.shape[0] // 2
+    width = block - share
+    for which in range(2):
+        first = which * block
+        f_at = pl.ds(pl.multiple_of((x ^ which) * share, share), share)
+        d_at = pl.ds(pl.multiple_of((x ^ which) * width, width), width)
+        for lane, value in ((0, mine), (half, theirs)):
+            lanes = slice(lane, lane + half)
+            split(value[first:first + share, :], ff_high, ff_low, (f_at, lanes))
+            split(value[first + share:first + block, :], fd_high, fd_low, (d_at, lanes))
+    wide = 2 * width
+    depth = 2 * share
+    last = (last_high[:, :depth], last_low[:, :depth])
+    value = grown[...] + dot3(last, (ff_high[...], ff_low[...]), NN)
+    value = halves(value)
+    product[...] = dot3(value, (d_high[...], d_low[...]), NT)
+    far = pl.ds(pl.multiple_of((z ^ 3) * wide, wide), wide)
+    product[:, far] = dot3(value, (fd_high[...], fd_low[...]), NT)
+    lanes = pl.ds(pl.multiple_of(c * half, half), half)
+    for which in range(2):
+        at = pl.ds(pl.multiple_of((x ^ which) * tile, tile), tile)
+        used = False
+        for slot in range(slots):
+            used = used | ((slot < live[x]) & (structure[x, slot] == 2 * z + (x ^ which)))
+        panel_out[which][...] = jnp.where(used, -product[at, lanes], 0.0)
+    low_lane = lax.broadcasted_iota(jnp.int32, (tile, wide), 1) < width
+    for step in range(4):
+        columns = pl.ds(pl.multiple_of((z ^ step) * wide, wide), wide)
+        first = product[:tile, columns]
+        second = product[tile:, columns]
+        left = jnp.where(c == 0, first, pltpu.roll(first, width, 1))
+        right = jnp.where(c == 0, pltpu.roll(second, width, 1), second)
+        w_out[step][...] = jnp.where(low_lane, left, right)
+
+
+def scaled_kernel(share, place, *refs):
+    f_high, f_low, d_high, d_low, ff_high, ff_low, fd_high, fd_low = refs[:8]
+    s_high, s_low, base, all_f_high, all_f_low, all_d_high, all_d_low = refs[8:]
+    z, c = place[0], place[2]
+    wide = fd_high.shape[0]
+    width = wide // 2
+    depth = 2 * share
+    f_at = pl.ds(pl.multiple_of((z ^ 3) * depth, depth), depth)
+    d_at = pl.ds(pl.multiple_of((z ^ 3) * wide, wide), wide)
+    for whole, early, late, at in (
+        (all_f_high, f_high, ff_high, f_at),
+        (all_f_low, f_low, ff_low, f_at),
+        (all_d_high, d_high, fd_high, d_at),
+        (all_d_low, d_low, fd_low, d_at),
+    ):
+        whole[...] = early[...]
+        whole[at, :] = late[...]
+    inverse = (all_d_high[...], all_d_low[...])
+    scaled = dot3((all_f_high[...], all_f_low[...]), inverse, NT)
+    s_high[...], s_low[...] = halves(scaled)
+    at = pl.ds(pl.multiple_of((2 * z + c) * width, width), width)
+    base[...] = dot3((all_d_high[at, :], all_d_low[at, :]), inverse, NT)
+
+
+def diag_kernel(tile, slots, structure, live, place, w0, w1, w2, w3, s_high, s_low, base, *refs):
+    keep, cross, w_all, pick_high, pick_low, total = refs
+    z, x = place[0], place[1]
+    half = keep.shape[1]
+    width = keep.shape[0]
+    for step, piece in enumerate((w0, w1, w2, w3)):
+        w_all[z ^ step] = piece[...]
+    for slot in range(slots):
+        anc = structure[x, slot]
+        value = w_all[anc // 2]
+        value = jnp.where(anc % 2 == 0, value, pltpu.roll(value, width, 1))
+        at = slice(slot * tile, (slot + 1) * tile)
+        split(jnp.where(slot < live[x], value, 0.0), pick_high, pick_low, (at, slice(None)))
+    picked = (pick_high[...], pick_low[...])
+    total[...] = base[...] + dot3(picked, (s_high[...], s_low[...]), TN)[:width]
+    keep[...] = total[:, pl.ds(pl.multiple_of(x * half, half), half)]
+    cross[...] = total[:, pl.ds(pl.multiple_of((1 - x) * half, half), half)]
+
+
+def lines_kernel(place, mine, other, out):
+    x = place[1]
+    blocks = mine.shape[1] // 128
+    for member, value in ((x, mine), (1 - x, other)):
+        for block in range(blocks):
+            at = pl.ds(2 * block + member, mine.shape[0], stride=2 * blocks)
+            out[at, :] = value[:, block * 128:(block + 1) * 128]
+
+
+def diag_lines_kernel(place, keep, met, far, out):
+    x, c = place[1], place[2]
+    blocks = keep.shape[1] // 128
+    mine = jnp.where(c == x, keep[...], met[...])
+    other = jnp.where(c == x, met[...], far[...])
+    for member, value in ((x, mine), (1 - x, other)):
+        for block in range(blocks):
+            at = pl.ds(2 * block + member, keep.shape[0], stride=2 * blocks)
+            out[at, :] = value[:, block * 128:(block + 1) * 128]
+
+
+def many_rows(ancestor_cov, panel_factor, diag_inverse, structure, live_counts):
     tile_rows = ancestor_cov.shape[0]
     local_blocks = ancestor_cov.shape[1]
     col_count = lax.axis_size("col")
@@ -71,6 +270,135 @@
     return (panel_cov, diag_cov)
 
 
+def local(ancestor_cov, panel_factor, diag_inverse, structure, live_counts):
+    rows = lax.axis_size("row")
+    if rows != 8:
+        return many_rows(ancestor_cov, panel_factor, diag_inverse, structure, live_counts)
+    tile = ancestor_cov.shape[0]
+    share, _, half = panel_factor.shape
+    whole, _, width = diag_inverse.shape
+    slots = structure.shape[1]
+    col = lax.axis_index("col")
+    row = lax.axis_index("row")
+    place = jnp.stack([row // 2, row % 2, col]).astype(jnp.int32)
+    smem = pl.BlockSpec(memory_space=pltpu.SMEM)
+    vmem = pl.BlockSpec(memory_space=pltpu.VMEM)
+
+    def like(*shape, dtype=F32):
+        return jax.ShapeDtypeStruct(shape, dtype)
+
+    def call(kernel, name, outs, scalars, arrays, scratch=(), space=vmem, limit=VMEM_LIMIT):
+        return pl.pallas_call(
+            kernel,
+            out_shape=outs,
+            in_specs=[smem] * len(scalars) + [space] * len(arrays),
+            out_specs=[vmem] * len(outs),
+            scratch_shapes=list(scratch),
+            compiler_params=pltpu.CompilerParams(vmem_limit_bytes=limit),
+            name=name,
+        )(*scalars, *arrays)
+
+    def send_to(value, target):
+        pairs = []
+        for r in range(rows):
+            for c in range(2):
+                to = target(r // 2, r % 2, c)
+                if to is not None:
+                    pairs.append((r * 2 + c, (to[0] * 2 + to[1]) * 2 + to[2]))
+        return lax.ppermute(value, ("row", "col"), pairs)
+
+    def move(value, z_step, x_step, flip):
+        return send_to(value, lambda z, x, c: (z ^ z_step, x ^ x_step, c ^ flip))
+
+    factor_lines = (
+        panel_factor.reshape(share, 2, half // 128, 128).transpose(0, 2, 1, 3).reshape(-1, 128)
+    )
+    bundle = share + width
+    own, send = call(
+        pack_kernel,
+        "pack",
+        [like(bundle, half)] * 2,
+        [place],
+        [factor_lines, diag_inverse.transpose(1, 2, 0)],
+        [pltpu.VMEM(factor_lines.shape, F32), pltpu.SemaphoreType.DMA((3,))],
+        pl.BlockSpec(memory_space=pl.ANY),
+        60 * 1024 * 1024,
+    )
+    c_own = ancestor_cov.reshape(-1, 128)
+    own_side = move(own, 1, 0, 0)
+    near = move(send, 0, 1, 0)
+    own_far = move(own, 2, 0, 0)
+    c_near = move(c_own, 0, 1, 0)
+    near_far = move(near, 2, 0, 0)
+    near_side = move(near, 1, 0, 0)
+    own_far, near_far, c_near = lax.optimization_barrier((own_far, near_far, c_near))
+    opposite = move(jnp.concatenate([own_far, near_far]), 1, 0, 0)
+    c_sib = move(jnp.concatenate([c_own, c_near]), 0, 0, 1)
+    mine = [own, near, own_far, near_far, own_side, near_side]
+    theirs = move(jnp.concatenate(mine), 0, 0, 1)
+    split_f = [like(slots * tile, whole, dtype=BF16)] * 2
+    split_d = [like(whole, whole, dtype=BF16)] * 2
+    grown, last_high, last_low, f_high, f_low, d_high, d_low = call(
+        functools.partial(early_kernel, share, tile, slots),
+        "early",
+        [like(2 * tile, whole)] + [like(2 * tile, 256, dtype=BF16)] * 2 + split_f + split_d,
+        [structure, live_counts, place],
+        [c_own, c_near, c_sib] + mine + [theirs],
+        [pltpu.VMEM((2 * tile, slots * tile), F32)],
+    )
+    opposite, grown = lax.optimization_barrier((opposite, grown))
+    opposite_theirs = move(opposite, 0, 0, 1)
+    outs = call(
+        functools.partial(product_kernel, share, tile, slots),
+        "products",
+        [like(tile, half)] * 2
+        + [like(tile, 2 * width)] * 4
+        + [like(2 * share, whole, dtype=BF16)] * 2
+        + [like(2 * width, whole, dtype=BF16)] * 2,
+        [structure, live_counts, place],
+        [grown, last_high, last_low, d_high, d_low, opposite, opposite_theirs],
+        [pltpu.VMEM((2 * tile, whole), F32)],
+    )
+    panel, w, late = outs[:2], outs[2:6], outs[6:]
+    w = [w[0]] + [move(w[step], step, 0, 0) for step in range(1, 4)]
+    panel_got = move(panel[1], 0, 1, 0)
+    s_high, s_low, base = call(
+        functools.partial(scaled_kernel, share),
+        "scaled",
+        split_f + [like(width, whole)],
+        [place],
+        [f_high, f_low, d_high, d_low, *late],
+        [pltpu.VMEM(s.shape, BF16) for s in split_f + split_d],
+    )
+    keep, cross = call(
+        functools.partial(diag_kernel, tile, slots),
+        "diag_block",
+        [like(width, half)] * 2,
+        [structure, live_counts, place],
+        [*w, s_high, s_low, base],
+        [
+            pltpu.VMEM((rows // 2, tile, 2 * width), F32),
+            pltpu.VMEM((slots * tile, 2 * width), BF16),
+            pltpu.VMEM((slots * tile, 2 * width), BF16),
+            pltpu.VMEM((width, whole), F32),
+        ],
+    )
+    met = send_to(cross, lambda z, x, c: (z, x, 1 - c) if c == x else (z, 1 - x, c))
+    far = send_to(keep, lambda z, x, c: None if c == x else (z, 1 - x, 1 - c))
+    lines = 2 * half // 128
+    (panel_lines,) = call(
+        lines_kernel, "panel_lines", [like(tile * lines, 128)], [place], [panel[0], panel_got]
+    )
+    (diag_lines,) = call(
+        diag_lines_kernel, "diag_lines", [like(width * lines, 128)], [place], [keep, met, far]
+    )
+
+    def unfold(value, count):
+        return value.reshape(count, half // 128, 2, 128).transpose(0, 2, 1, 3).reshape(count, 2, half)
+
+    return unfold(panel_lines, tile), unfold(diag_lines, width)
+
+
 def solution(mesh):
     placed = (
         P(("mp", "row"), None, "col", None),

time: 249 us -> 58.2 us (0.23)
  waiting for transfers between devices: 197 us -> 17.8 us
  starting transfers between devices: 0.2 us -> 25.2 us
  local copies, waits for them, and re-layouts: 17 us -> 1.02 us
  between operations: 15.3 us -> 0.84 us
  matrix products: 12.7 us -> 0 us
  Pallas kernels: 0 us -> 12.6 us
  other arithmetic: 4.18 us -> 0.64 us
    all_gather x2 -> x0, waiting for transfers between devices: 104 us -> none  [the longest x1 52.7 us: local(): arrived = lax.all_gather(factor_rows, 'row', axis=0, tiled=True)]
    reduce_scatter x1 -> x0, waiting for transfers between devices: 60.9 us -> none  [local(): lax.psum_scatter(jnp.einsum('tsi,tsn->isn', owned, product_half, precisio...]
    psum x2 -> x0, waiting for transfers between devices: 31.9 us -> none  [the longest x1 18.6 us: local(): factor_rows = lax.psum(factor_term, 'col')]
    ppermute x0 -> x16, starting transfers between devices: none -> 25.2 us  [send_to(): return lax.ppermute(value, ('row', 'col'), pairs)]
    ppermute x0 -> x16, waiting for transfers between devices: none -> 17.8 us  [send_to(): return lax.ppermute(value, ('row', 'col'), pairs)]
    dot_general x5 -> x0, matrix products: 12.7 us -> none  [the longest x2 5.67 us: local(): jnp.dot(sig_cols, weighted, precision=lax.Precision.HIGHEST, preferred_el...]
    pallas_call x0 -> x7, Pallas kernels: none -> 12.6 us  [call(): pl.pallas_call(kernel, out_shape=outs, in_specs=[smem] * len(scalars) + [...]
    gather x4 -> x0, local copies, waits for them, and re-layouts: 7.01 us -> none  [the longest x2 3.85 us: local(): sig_cols = jnp.take(flat_cov, column_index, axis=1)]
  transfers between devices with their start and end apart: 5 -> 16, of which waited for: 5 -> 9; matrix products, arithmetic and copies ran while one was open for 6% -> 2% of each run, Pallas kernels for 0% -> 12%
where the time goes in v4:
time: 58.2 us; the launch traced here: 58.1 us
  starting transfers between devices  25.2 us (43%)
  waiting for transfers between devices  17.8 us (31%)
  Pallas kernels  12.6 us (22%)
  local copies, waits for them, and re-layouts  1.02 us (2%)
  between operations  0.84 us (1%)
  other arithmetic  0.64 us (1%)
    ppermute x16, starting transfers between devices, send_to(): return lax.ppermute(value, ('row', 'col'), pairs)  25.2 us
    ppermute x16, waiting for transfers between devices, send_to(): return lax.ppermute(value, ('row', 'col'), pairs)  17.8 us
    pallas_call x7, Pallas kernels, call(): pl.pallas_call(kernel, out_shape=outs, in_specs=[smem] * len(scalars) + [...  12.6 us
  transfers between devices with their start and end apart: 16, of which 9 were waited for; matrix products, arithmetic and copies ran while one was open for 2% of the time, Pallas kernels for 12%

profile of v4, /device:TPU:1, one launch (start us, length us, event | category | flops | bytes accessed | tf_op | source)
XLA Modules:
  0.0 58.1 jit_solution(18266887665263588434)
XLA Ops:
  1.2 2.4 %pack.1 = (f32[160,256]{1,0:T(8,128)}, f32[160,256]{1,0:T(8,128)}) custom-call(s32[3]{0:T(128)} %pad_add_fusion.place, f32[384,128]{1,0:T(8,128)} %bitcast.25, f32[2,64,512]{2,1,0:T(8,128)} %bitcast.24), custom_call_target="tpu_custom_call" | custom-call | tf_op jit(solution)/shard_map/pack/pallas_call | solution.py:291
  3.6 2.1 %collective-permute-start.1 = (f32[160,256]{1,0:T(8,128)}, f32[160,256]{1,0:T(8,128)S(1)}, u32[]{:S(2)}, u32[]{:S(2)}) collective-permute-start(f32[160,256]{1,0:T(8,128)} %get-tuple-element.32), channel_id=1, source_target_pairs={{0,2},{1,3},{2,0},{3,1},{4,6},{5,7},{6,4},{7,5},{8,10},{9,11},{10,... | collective-permute-start | bytes 491528 | tf_op jit(solution)/shard_map/ppermute | solution.py:308
  5.8 2.5 %collective-permute-start = (f32[160,256]{1,0:T(8,128)}, f32[160,256]{1,0:T(8,128)S(1)}, u32[]{:S(2)}, u32[]{:S(2)}) collective-permute-start(f32[160,256]{1,0:T(8,128)} %get-tuple-element.31.refs_0_), channel_id=1, source_target_pairs={{0,8},{1,9},{2,10},{3,11},{4,12},{5,13},{6,14},{7,15},{8,0},{9,1},... | collective-permute-start | bytes 491528 | tf_op jit(solution)/shard_map/ppermute | solution.py:308
  8.3 1.3 %collective-permute-start.6 = (f32[160,256]{1,0:T(8,128)}, f32[160,256]{1,0:T(8,128)S(1)}, u32[]{:S(2)}, u32[]{:S(2)}) collective-permute-start(f32[160,256]{1,0:T(8,128)} %get-tuple-element.31.refs_0_), channel_id=1, source_target_pairs={{0,4},{1,5},{2,6},{3,7},{4,0},{5,1},{6,2},{7,3},{8,12},{9,13},{10,... | collective-permute-start | bytes 491528 | tf_op jit(solution)/shard_map/ppermute | solution.py:308
  9.9 2.2 %collective-permute-start.2 = (f32[160,256]{1,0:T(8,128)S(1)}, f32[160,256]{1,0:T(8,128)S(1)}, u32[]{:S(2)}, u32[]{:S(2)}) collective-permute-start(f32[160,256]{1,0:T(8,128)S(1)} %collective-permute-done.1.refs_1_), channel_id=1, source_target_pairs={{0,8},{1,9},{2,10},{3,11},{4,12},{5,13},{6,14},{7,15},{8,0},{9,1},... | collective-permute-start | bytes 491528 | tf_op jit(solution)/shard_map/ppermute | solution.py:308
  13.0 1.4 %collective-permute-start.7 = (f32[160,256]{1,0:T(8,128)S(1)}, f32[160,256]{1,0:T(8,128)S(1)}, u32[]{:S(2)}, u32[]{:S(2)}) collective-permute-start(f32[160,256]{1,0:T(8,128)S(1)} %collective-permute-done.1.refs_1_), channel_id=1, source_target_pairs={{0,4},{1,5},{2,6},{3,7},{4,0},{5,1},{6,2},{7,3},{8,12},{9,13},{10,... | collective-permute-start | bytes 491528 | tf_op jit(solution)/shard_map/ppermute | solution.py:308
  15.5 6.5 %collective-permute-done.2.refs_3_ = f32[160,256]{1,0:T(8,128)S(1)} collective-permute-done((f32[160,256]{1,0:T(8,128)S(1)}, f32[160,256]{1,0:T(8,128)S(1)}, u32[]{:S(2)}, u32[]{:S(2)}) %collective-permute-start.2) | collective-permute-done | bytes 163872 | tf_op jit(solution)/shard_map/ppermute | solution.py:308
  22.1 2.4 %collective-permute-start.8 = (f32[960,256]{1,0:T(8,128)S(1)}, f32[960,256]{1,0:T(8,128)S(1)}, u32[]{:S(2)}, u32[]{:S(2)}) collective-permute-start(f32[960,256]{1,0:T(8,128)S(1)} %constant_dynamic-update-slice_fusion), channel_id=1, source_target_pairs={{0,1},{1,0},{2,3},{3,2},{4,5},{5,4},{6,7},{7,6},{8,9},{9,8},{10,11... | collective-permute-start | bytes 2949128 | tf_op jit(solution)/shard_map/ppermute | solution.py:308
  24.8 1.2 %collective-permute-start.4 = (f32[320,256]{1,0:T(8,128)S(1)}, f32[320,256]{1,0:T(8,128)S(1)}, u32[]{:S(2)}, u32[]{:S(2)}) collective-permute-start(f32[320,256]{1,0:T(8,128)S(1)} %pad_maximum_fusion.1), channel_id=1, source_target_pairs={{0,4},{1,5},{2,6},{3,7},{4,0},{5,1},{6,2},{7,3},{8,12},{9,13},{10,... | collective-permute-start | bytes 983048 | tf_op jit(solution)/shard_map/ppermute | solution.py:308
  26.0 1.5 %collective-permute-done.5.c_sib = f32[1024,128]{1,0:T(8,128)S(1)} collective-permute-done((f32[1024,128]{1,0:T(8,128)S(1)}, f32[1024,128]{1,0:T(8,128)S(1)}, u32[]{:S(2)}, u32[]{:S(2)}) %collective-permute-start.5) | collective-permute-done | bytes 524320 | tf_op jit(solution)/shard_map/ppermute | solution.py:308
  27.5 1.9 %early.1 = (f32[256,512]{1,0:T(8,128)S(1)}, bf16[256,256]{1,0:T(8,128)(2,1)S(1)}, bf16[256,256]{1,0:T(8,128)(2,1)S(1)}, bf16[768,512]{1,0:T(8,128)(2,1)S(1)}, bf...) custom-call(s32[2,6]{1,0:T(2,128)S(1)} %copy-done.3, s32[2]{0:T(128)S(1)} %copy-done.4, ...), custom_call_target="tpu_custom_call" | custom-call | tf_op jit(solution)/shard_map/early/pallas_call | solution.py:291
  29.5 4.1 %collective-permute-done.4.refs_5_ = f32[320,256]{1,0:T(8,128)S(1)} collective-permute-done((f32[320,256]{1,0:T(8,128)S(1)}, f32[320,256]{1,0:T(8,128)S(1)}, u32[]{:S(2)}, u32[]{:S(2)}) %collective-permute-start.4) | collective-permute-done | bytes 327712 | tf_op jit(solution)/shard_map/ppermute | solution.py:308
  33.6 1.3 %collective-permute-start.9 = (f32[320,256]{1,0:T(8,128)S(1)}, f32[320,256]{1,0:T(8,128)S(1)}, u32[]{:S(2)}, u32[]{:S(2)}) collective-permute-start(f32[320,256]{1,0:T(8,128)S(1)} %collective-permute-done.4.refs_5_), channel_id=1, source_target_pairs={{0,1},{1,0},{2,3},{3,2},{4,5},{5,4},{6,7},{7,6},{8,9},{9,8},{10,11... | collective-permute-start | bytes 983048 | tf_op jit(solution)/shard_map/ppermute | solution.py:308
  35.0 1.3 %collective-permute-done.9.refs_6_ = f32[320,256]{1,0:T(8,128)S(1)} collective-permute-done((f32[320,256]{1,0:T(8,128)S(1)}, f32[320,256]{1,0:T(8,128)S(1)}, u32[]{:S(2)}, u32[]{:S(2)}) %collective-permute-start.9) | collective-permute-done | bytes 327712 | tf_op jit(solution)/shard_map/ppermute | solution.py:308
  36.2 2.1 %products.1 = (f32[128,256]{1,0:T(8,128)S(1)}, f32[128,256]{1,0:T(8,128)S(1)}, f32[128,128]{1,0:T(8,128)S(1)}, f32[128,128]{1,0:T(8,128)S(1)}, f32[128,128]{1,0:...) custom-call(s32[2,6]{1,0:T(2,128)S(1)} %copy-done.3, ...), custom_call_target="tpu_custom_call" | custom-call | tf_op jit(solution)/shard_map/products/pallas_call | solution.py:291
  38.3 1.2 %collective-permute-start.11 = (f32[128,128]{1,0:T(8,128)S(1)}, f32[128,128]{1,0:T(8,128)S(1)}, u32[]{:S(2)}, u32[]{:S(2)}) collective-permute-start(f32[128,128]{1,0:T(8,128)S(1)} %get-tuple-element.46), channel_id=1, source_target_pairs={{0,4},{1,5},{2,6},{3,7},{4,0},{5,1},{6,2},{7,3},{8,12},{9,13},{10,... | collective-permute-start | bytes 196616 | tf_op jit(solution)/shard_map/ppermute | solution.py:308
  39.5 2.2 %collective-permute-start.12 = (f32[128,128]{1,0:T(8,128)S(1)}, f32[128,128]{1,0:T(8,128)S(1)}, u32[]{:S(2)}, u32[]{:S(2)}) collective-permute-start(f32[128,128]{1,0:T(8,128)S(1)} %get-tuple-element.47), channel_id=1, source_target_pairs={{0,8},{1,9},{2,10},{3,11},{4,12},{5,13},{6,14},{7,15},{8,0},{9,1},... | collective-permute-start | bytes 196616 | tf_op jit(solution)/shard_map/ppermute | solution.py:308
  41.9 1.3 %collective-permute-start.10 = (f32[128,256]{1,0:T(8,128)S(1)}, f32[128,256]{1,0:T(8,128)S(1)}, u32[]{:S(2)}, u32[]{:S(2)}) collective-permute-start(f32[128,256]{1,0:T(8,128)S(1)} %get-tuple-element.44), channel_id=1, source_target_pairs={{0,2},{1,3},{2,0},{3,1},{4,6},{5,7},{6,4},{7,5},{8,10},{9,11},{10,... | collective-permute-start | bytes 393224 | tf_op jit(solution)/shard_map/ppermute | solution.py:308
  43.2 2.4 %scaled.1 = (bf16[768,512]{1,0:T(8,128)(2,1)S(1)}, bf16[768,512]{1,0:T(8,128)(2,1)S(1)}, f32[64,512]{1,0:T(8,128)S(1)}) custom-call(s32[3]{0:T(128)S(1)} %copy-done.2, bf16[768,512]{1,0:T(8,128)(2,1)S(1)} %get-tuple-element.49.refs_0_, bf16[768,512]{1,0:T(8,128)(2,1)S(1)} %get-tuple-element.50.refs_1_, ...), custom_call_target="tpu_custom_call" | custom-call | tf_op jit(solution)/shard_map/scaled/pallas_call | solution.py:291
  46.7 1.3 %diag_block.1 = (f32[64,256]{1,0:T(8,128)S(1)}, f32[64,256]{1,0:T(8,128)S(1)}) custom-call(s32[2,6]{1,0:T(2,128)S(1)} %copy-done.3, s32[2]{0:T(128)S(1)} %copy-done.4, s32[3]{0:T(128)S(1)} %copy-done.2, f32[128,128]{1,0:T(8,128)S(1)} %get-tuple-element.45.w0, f32[128,128]{1,0:T(8,128)S(1)} %collective-permute-done.11.w1, ...), custom_call_target="tpu_custom_call" | custom-call | tf_op jit(solution)/shard_map/diag_block/pallas_call | solution.py:291
  48.0 1.2 %collective-permute-start.14 = (f32[64,256]{1,0:T(8,128)S(1)}, f32[64,256]{1,0:T(8,128)S(1)}, u32[]{:S(2)}, u32[]{:S(2)}) collective-permute-start(f32[64,256]{1,0:T(8,128)S(1)} %get-tuple-element.59), channel_id=1, source_target_pairs={{0,1},{1,3},{2,0},{3,2},{4,5},{5,7},{6,4},{7,6},{8,9},{9,11},{10,8... | collective-permute-start | bytes 196616 | tf_op jit(solution)/shard_map/ppermute | solution.py:308
  49.2 4.4 %collective-permute-start.15 = (f32[64,256]{1,0:T(8,128)S(1)}, f32[64,256]{1,0:T(8,128)S(1)}, u32[]{:S(2)}, u32[]{:S(2)}) collective-permute-start(f32[64,256]{1,0:T(8,128)S(1)} %get-tuple-element.58.keep), channel_id=1, source_target_pairs={{1,2},{2,1},{5,6},{6,5},{9,10},{10,9},{13,14},{14,13},{17,18},{18,... | collective-permute-start | bytes 196616 | tf_op jit(solution)/shard_map/ppermute | solution.py:308
  53.6 1.9 %collective-permute-done.15.far = f32[64,256]{1,0:T(8,128)S(1)} collective-permute-done((f32[64,256]{1,0:T(8,128)S(1)}, f32[64,256]{1,0:T(8,128)S(1)}, u32[]{:S(2)}, u32[]{:S(2)}) %collective-permute-start.15) | collective-permute-done | bytes 65568 | tf_op jit(solution)/shard_map/ppermute | solution.py:308
  56.8 1.3 %panel_lines.1 = f32[512,128]{1,0:T(8,128)} custom-call(s32[3]{0:T(128)S(1)} %copy-done.2, f32[128,256]{1,0:T(8,128)S(1)} %get-tuple-element.43.mine, f32[128,256]{1,0:T(8,128)S(1)} %collective-permute-done.10.other), custom_call_target="tpu_custom_call" | custom-call | tf_op jit(solution)/shard_map/panel_lines/pallas_call | solution.py:291
  (34 shorter events, 5.7 us)
Async XLA Ops:
  0.6 5.1 %copy-start = (f32[128,4,1,128]{3,2,1,0:T(1,128)S(1)}, f32[128,4,1,128]{3,2,1,0:T(1,128)}, u32[]{:S(2)}) copy-start(f32[128,4,1,128]{3,2,1,0:T(1,128)} %param.5) | copy-start | bytes 786436
  3.6 6.2 %collective-permute-start.1 = (f32[160,256]{1,0:T(8,128)}, f32[160,256]{1,0:T(8,128)S(1)}, u32[]{:S(2)}, u32[]{:S(2)}) collective-permute-start(f32[160,256]{1,0:T(8,128)} %get-tuple-element.32), channel_id=1, source_target_pairs={{0,2},{1,3},{2,0},{3,1},{4,6},{5,7},{6,4},{7,5},{8,10},{9,11},{10,... | collective-permute-start | bytes 491528 | tf_op jit(solution)/shard_map/ppermute | solution.py:308
  5.7 9.8 %collective-permute-start.3 = (f32[512,128]{1,0:T(8,128)S(1)}, f32[512,128]{1,0:T(8,128)S(1)}, u32[]{:S(2)}, u32[]{:S(2)}) collective-permute-start(f32[512,128]{1,0:T(8,128)S(1)} %bitcast.20), channel_id=1, source_target_pairs={{0,2},{1,3},{2,0},{3,1},{4,6},{5,7},{6,4},{7,5},{8,10},{9,11},{10,... | collective-permute-start | bytes 786440 | tf_op jit(solution)/shard_map/ppermute | solution.py:308
  5.8 9.2 %collective-permute-start = (f32[160,256]{1,0:T(8,128)}, f32[160,256]{1,0:T(8,128)S(1)}, u32[]{:S(2)}, u32[]{:S(2)}) collective-permute-start(f32[160,256]{1,0:T(8,128)} %get-tuple-element.31.refs_0_), channel_id=1, source_target_pairs={{0,8},{1,9},{2,10},{3,11},{4,12},{5,13},{6,14},{7,15},{8,0},{9,1},... | collective-permute-start | bytes 491528 | tf_op jit(solution)/shard_map/ppermute | solution.py:308
  8.3 13.8 %collective-permute-start.6 = (f32[160,256]{1,0:T(8,128)}, f32[160,256]{1,0:T(8,128)S(1)}, u32[]{:S(2)}, u32[]{:S(2)}) collective-permute-start(f32[160,256]{1,0:T(8,128)} %get-tuple-element.31.refs_0_), channel_id=1, source_target_pairs={{0,4},{1,5},{2,6},{3,7},{4,0},{5,1},{6,2},{7,3},{8,12},{9,13},{10,... | collective-permute-start | bytes 491528 | tf_op jit(solution)/shard_map/ppermute | solution.py:308
  9.9 12.2 %collective-permute-start.2 = (f32[160,256]{1,0:T(8,128)S(1)}, f32[160,256]{1,0:T(8,128)S(1)}, u32[]{:S(2)}, u32[]{:S(2)}) collective-permute-start(f32[160,256]{1,0:T(8,128)S(1)} %collective-permute-done.1.refs_1_), channel_id=1, source_target_pairs={{0,8},{1,9},{2,10},{3,11},{4,12},{5,13},{6,14},{7,15},{8,0},{9,1},... | collective-permute-start | bytes 491528 | tf_op jit(solution)/shard_map/ppermute | solution.py:308
  13.0 9.1 %collective-permute-start.7 = (f32[160,256]{1,0:T(8,128)S(1)}, f32[160,256]{1,0:T(8,128)S(1)}, u32[]{:S(2)}, u32[]{:S(2)}) collective-permute-start(f32[160,256]{1,0:T(8,128)S(1)} %collective-permute-done.1.refs_1_), channel_id=1, source_target_pairs={{0,4},{1,5},{2,6},{3,7},{4,0},{5,1},{6,2},{7,3},{8,12},{9,13},{10,... | collective-permute-start | bytes 491528 | tf_op jit(solution)/shard_map/ppermute | solution.py:308
  22.1 5.4 %collective-permute-start.8 = (f32[960,256]{1,0:T(8,128)S(1)}, f32[960,256]{1,0:T(8,128)S(1)}, u32[]{:S(2)}, u32[]{:S(2)}) collective-permute-start(f32[960,256]{1,0:T(8,128)S(1)} %constant_dynamic-update-slice_fusion), channel_id=1, source_target_pairs={{0,1},{1,0},{2,3},{3,2},{4,5},{5,4},{6,7},{7,6},{8,9},{9,8},{10,11... | collective-permute-start | bytes 2949128 | tf_op jit(solution)/shard_map/ppermute | solution.py:308
  24.6 2.9 %copy-start.1 = (f32[160,256]{1,0:T(8,128)S(1)}, f32[160,256]{1,0:T(8,128)}, u32[]{:S(2)}) copy-start(f32[160,256]{1,0:T(8,128)} %get-tuple-element.31.refs_0_) | copy-start | bytes 491524
  24.6 2.9 %copy-start.2 = (s32[3]{0:T(128)S(1)}, s32[3]{0:T(128)}, u32[]{:S(2)}) copy-start(s32[3]{0:T(128)} %pad_add_fusion.place) | copy-start | bytes 40
  24.6 2.9 %copy-start.3 = (s32[2,6]{1,0:T(2,128)S(1)}, s32[2,6]{1,0:T(2,128)}, u32[]{:S(2)}) copy-start(s32[2,6]{1,0:T(2,128)} %structure.5) | copy-start | bytes 148
  24.6 2.9 %copy-start.4 = (s32[2]{0:T(128)S(1)}, s32[2]{0:T(128)}, u32[]{:S(2)}) copy-start(s32[2]{0:T(128)} %live.5) | copy-start | bytes 28
  24.7 2.9 %collective-permute-start.5 = (f32[1024,128]{1,0:T(8,128)S(1)}, f32[1024,128]{1,0:T(8,128)S(1)}, u32[]{:S(2)}, u32[]{:S(2)}) collective-permute-start(f32[1024,128]{1,0:T(8,128)S(1)} %pad_maximum_fusion), channel_id=1, source_target_pairs={{0,1},{1,0},{2,3},{3,2},{4,5},{5,4},{6,7},{7,6},{8,9},{9,8},{10,11... | collective-permute-start | bytes 1572872 | tf_op jit(solution)/shard_map/ppermute | solution.py:308
  24.8 8.9 %collective-permute-start.4 = (f32[320,256]{1,0:T(8,128)S(1)}, f32[320,256]{1,0:T(8,128)S(1)}, u32[]{:S(2)}, u32[]{:S(2)}) collective-permute-start(f32[320,256]{1,0:T(8,128)S(1)} %pad_maximum_fusion.1), channel_id=1, source_target_pairs={{0,4},{1,5},{2,6},{3,7},{4,0},{5,1},{6,2},{7,3},{8,12},{9,13},{10,... | collective-permute-start | bytes 983048 | tf_op jit(solution)/shard_map/ppermute | solution.py:308
  33.6 2.6 %collective-permute-start.9 = (f32[320,256]{1,0:T(8,128)S(1)}, f32[320,256]{1,0:T(8,128)S(1)}, u32[]{:S(2)}, u32[]{:S(2)}) collective-permute-start(f32[320,256]{1,0:T(8,128)S(1)} %collective-permute-done.4.refs_5_), channel_id=1, source_target_pairs={{0,1},{1,0},{2,3},{3,2},{4,5},{5,4},{6,7},{7,6},{8,9},{9,8},{10,11... | collective-permute-start | bytes 983048 | tf_op jit(solution)/shard_map/ppermute | solution.py:308
  38.3 7.3 %collective-permute-start.11 = (f32[128,128]{1,0:T(8,128)S(1)}, f32[128,128]{1,0:T(8,128)S(1)}, u32[]{:S(2)}, u32[]{:S(2)}) collective-permute-start(f32[128,128]{1,0:T(8,128)S(1)} %get-tuple-element.46), channel_id=1, source_target_pairs={{0,4},{1,5},{2,6},{3,7},{4,0},{5,1},{6,2},{7,3},{8,12},{9,13},{10,... | collective-permute-start | bytes 196616 | tf_op jit(solution)/shard_map/ppermute | solution.py:308
  39.5 6.1 %collective-permute-start.12 = (f32[128,128]{1,0:T(8,128)S(1)}, f32[128,128]{1,0:T(8,128)S(1)}, u32[]{:S(2)}, u32[]{:S(2)}) collective-permute-start(f32[128,128]{1,0:T(8,128)S(1)} %get-tuple-element.47), channel_id=1, source_target_pairs={{0,8},{1,9},{2,10},{3,11},{4,12},{5,13},{6,14},{7,15},{8,0},{9,1},... | collective-permute-start | bytes 196616 | tf_op jit(solution)/shard_map/ppermute | solution.py:308
  41.7 5.0 %collective-permute-start.13 = (f32[128,128]{1,0:T(8,128)S(1)}, f32[128,128]{1,0:T(8,128)S(1)}, u32[]{:S(2)}, u32[]{:S(2)}) collective-permute-start(f32[128,128]{1,0:T(8,128)S(1)} %get-tuple-element.48), channel_id=1, source_target_pairs={{0,12},{1,13},{2,14},{3,15},{4,8},{5,9},{6,10},{7,11},{8,4},{9,5},... | collective-permute-start | bytes 196616 | tf_op jit(solution)/shard_map/ppermute | solution.py:308
  41.9 14.9 %collective-permute-start.10 = (f32[128,256]{1,0:T(8,128)S(1)}, f32[128,256]{1,0:T(8,128)S(1)}, u32[]{:S(2)}, u32[]{:S(2)}) collective-permute-start(f32[128,256]{1,0:T(8,128)S(1)} %get-tuple-element.44), channel_id=1, source_target_pairs={{0,2},{1,3},{2,0},{3,1},{4,6},{5,7},{6,4},{7,5},{8,10},{9,11},{10,... | collective-permute-start | bytes 393224 | tf_op jit(solution)/shard_map/ppermute | solution.py:308
  48.0 5.6 %collective-permute-start.14 = (f32[64,256]{1,0:T(8,128)S(1)}, f32[64,256]{1,0:T(8,128)S(1)}, u32[]{:S(2)}, u32[]{:S(2)}) collective-permute-start(f32[64,256]{1,0:T(8,128)S(1)} %get-tuple-element.59), channel_id=1, source_target_pairs={{0,1},{1,3},{2,0},{3,2},{4,5},{5,7},{6,4},{7,6},{8,9},{9,11},{10,8... | collective-permute-start | bytes 196616 | tf_op jit(solution)/shard_map/ppermute | solution.py:308
  49.2 6.3 %collective-permute-start.15 = (f32[64,256]{1,0:T(8,128)S(1)}, f32[64,256]{1,0:T(8,128)S(1)}, u32[]{:S(2)}, u32[]{:S(2)}) collective-permute-start(f32[64,256]{1,0:T(8,128)S(1)} %get-tuple-element.58.keep), channel_id=1, source_target_pairs={{1,2},{2,1},{5,6},{6,5},{9,10},{10,9},{13,14},{14,13},{17,18},{18,... | collective-permute-start | bytes 196616 | tf_op jit(solution)/shard_map/ppermute | solution.py:308

commit v5 on v4

--- a/solution.py
+++ b/solution.py
@@ -13,6 +13,7 @@
 NN = (((1,), (0,)), ((), ()))
 TN = (((0,), (0,)), ((), ()))
 VMEM_LIMIT = 20 * 1024 * 1024
+PACK_LIMIT = 60 * 1024 * 1024
 
 
 def halves(value):
@@ -35,65 +36,85 @@
     high[at], low[at] = halves(value)
 
 
-def pack_kernel(place, factor, inverse, own, send, lines, sem):
-    x = place[1]
-    c = place[2]
-    half = own.shape[1]
-    width = inverse.shape[1]
-    share = own.shape[0] - width
-    blocks = half // 128
-    lanes = pl.ds(pl.multiple_of(c * half, half), half)
-    copies = [pltpu.make_async_copy(factor, lines, sem.at[0])]
-    for index, (out, member) in enumerate(((own, x), (send, 1 - x))):
-        copies.append(
-            pltpu.make_async_copy(
-                inverse.at[member, :, lanes], out.at[pl.ds(share, width), :], sem.at[1 + index]
-            )
-        )
+def pack_kernel(factor, inverse, cov, own, send, near, lines, held, sem):
+    x = lax.axis_index("row") % 2
+    c = lax.axis_index("col")
+    width = held.shape[1]
+    blocks = held.shape[2] // 128
+    block = own.shape[0] // blocks
+    share = block - width
+    lanes = pl.ds(pl.multiple_of(c * held.shape[2], held.shape[2]), held.shape[2])
+    copies = [
+        pltpu.make_async_copy(factor, lines, sem.at[0]),
+        pltpu.make_async_copy(inverse.at[:, :, lanes], held, sem.at[1]),
+        pltpu.make_async_copy(cov, near.at[pl.ds(own.shape[0], cov.shape[0]), :], sem.at[2]),
+    ]
     for copy in copies:
         copy.start()
     copies[0].wait()
-    for out, member in ((own, x), (send, 1 - x)):
-        for block in range(blocks):
-            at = pl.ds(2 * block + member, share, stride=2 * blocks)
-            out[:share, block * 128:(block + 1) * 128] = lines[at, :]
     copies[1].wait()
+    for outs, member in (((own,), x), ((send, near), 1 - x)):
+        for b in range(blocks):
+            rows = lines[pl.ds(2 * b + member, share, stride=2 * blocks), :]
+            cols = held[member, :, b * 128:(b + 1) * 128]
+            for out in outs:
+                out[b * block:b * block + share, :] = rows
+                out[b * block + share:(b + 1) * block, :] = cols
     copies[2].wait()
 
 
-def early_kernel(share, tile, slots, structure, live, place, c_own, c_near, c_sib, *refs):
-    mine = refs[:6]
-    theirs = refs[6]
-    grown, last_high, last_low, f_high, f_low, d_high, d_low, pick = refs[7:]
+def early_kernel(share, tile, slots, structure, live, place, c_own, *refs):
+    mine = refs[:7]
+    theirs = refs[7]
+    grown, last_high, last_low, f_high, f_low, d_high, d_low, pick = refs[8:]
     z, x, c = place[0], place[1], place[2]
-    half = theirs.shape[1]
-    block = mine[0].shape[0]
+    size = mine[0].shape[0]
+    whole = d_high.shape[0]
+    half = whole // 2
+    lane_blocks = half // 128
+    block = size // lane_blocks
     width = block - share
-    for index in range(6):
-        source = 2 * (z ^ (0, 2, 1)[index // 2]) + (x ^ (index % 2))
+    near_x = 1 - x
+    sources = (
+        2 * z + x,
+        2 * (z ^ 2) + x,
+        2 * (z ^ 2) + near_x,
+        2 * (z ^ 1) + x,
+        2 * (z ^ 1) + near_x,
+        2 * (z ^ 3) + x,
+        2 * z + near_x,
+    )
+    for index, source in enumerate(sources):
         f_at = pl.ds(pl.multiple_of(source * share, share), share)
         d_at = pl.ds(pl.multiple_of(source * width, width), width)
-        for first, value in ((0, mine[index]), (half, theirs.at[index * block:(index + 1) * block, :])):
-            lanes = slice(first, first + half)
-            split(value[:share, :], f_high, f_low, (f_at, lanes))
-            split(value[share:, :], d_high, d_low, (d_at, lanes))
-    far = 2 * (z ^ 3) * share
-    f_at = pl.ds(pl.multiple_of(far, 2 * share), 2 * share)
-    f_high[f_at, :] = jnp.zeros((2 * share, 2 * half), BF16)
-    f_low[f_at, :] = jnp.zeros((2 * share, 2 * half), BF16)
+        for first, ref, start in ((0, mine[index], 0), (half, theirs, index * size)):
+            for b in range(lane_blocks):
+                lanes = slice(first + b * 128, first + (b + 1) * 128)
+                top = start + b * block
+                split(ref[top:top + share, :], f_high, f_low, (f_at, lanes))
+                split(ref[top + share:top + block, :], d_high, d_low, (d_at, lanes))
+    last = (2 * (z ^ 3) + near_x) * share
+    f_at = pl.ds(pl.multiple_of(last, share), share)
+    f_high[f_at, :] = jnp.zeros((share, whole), BF16)
+    f_low[f_at, :] = jnp.zeros((share, whole), BF16)
+    d_at = pl.ds(pl.multiple_of((2 * (z ^ 3) + near_x) * width, width), width)
+    d_high[d_at, :] = jnp.zeros((width, whole), BF16)
+    d_low[d_at, :] = jnp.zeros((width, whole), BF16)
     blocks = c_own.shape[0] // tile
     for slot in range(slots):
         anc = structure[x, slot]
-        rows = pl.ds(anc // 2, tile, stride=blocks)
-        other = pl.ds(c_own.shape[0] + anc // 2, tile, stride=blocks)
-        for which, (here, there) in enumerate(((c_own, rows), (c_near, other))):
-            value = jnp.where(anc % 2 == c, here[rows, :], c_sib[there, :])
+        for which, (here, start, offset) in enumerate(
+            ((c_own, 0, 7 * size + c_own.shape[0]), (mine[6], size, 7 * size))
+        ):
+            here_at = pl.ds(start + anc // 2, tile, stride=blocks)
+            there_at = pl.ds(offset + anc // 2, tile, stride=blocks)
+            value = jnp.where(anc % 2 == c, here[here_at, :], theirs[there_at, :])
             at = pl.ds(pl.multiple_of((x ^ which) * tile, tile), tile)
             pick[at, slot * tile:(slot + 1) * tile] = jnp.where(slot < live[x], value, 0.0)
     picked = pick[...]
     grown[...] = dot3(halves(picked), (f_high[...], f_low[...]), NN)
     total = slots * tile
-    turned = pltpu.roll(picked, total - far, 1)
+    turned = pltpu.roll(picked, total - last, 1)
     last_high[...], last_low[...] = halves(turned[:, :last_high.shape[1]])
 
 
@@ -104,24 +125,25 @@
     ff_high, ff_low, fd_high, fd_low = refs[13:17]
     product = refs[17]
     z, x, c = place[0], place[1], place[2]
-    half = mine.shape[1]
-    block = mine.shape[0] // 2
-    width = block - share
-    for which in range(2):
-        first = which * block
-        f_at = pl.ds(pl.multiple_of((x ^ which) * share, share), share)
-        d_at = pl.ds(pl.multiple_of((x ^ which) * width, width), width)
-        for lane, value in ((0, mine), (half, theirs)):
-            lanes = slice(lane, lane + half)
-            split(value[first:first + share, :], ff_high, ff_low, (f_at, lanes))
-            split(value[first + share:first + block, :], fd_high, fd_low, (d_at, lanes))
-    wide = 2 * width
-    depth = 2 * share
-    last = (last_high[:, :depth], last_low[:, :depth])
+    wide = fd_high.shape[0]
+    width = wide // 2
+    half = d_high.shape[0] // 2
+    lane_blocks = half // 128
+    block = share + width
+    far = pl.ds(pl.multiple_of((z ^ 3) * wide, wide), wide)
+    fd_high[...] = d_high[far, :]
+    fd_low[...] = d_low[far, :]
+    d_at = pl.ds(pl.multiple_of((1 - x) * width, width), width)
+    for first, ref in ((0, mine), (half, theirs)):
+        for b in range(lane_blocks):
+            lanes = slice(first + b * 128, first + (b + 1) * 128)
+            top = b * block
+            split(ref[top:top + share, :], ff_high, ff_low, (slice(None), lanes))
+            split(ref[top + share:top + block, :], fd_high, fd_low, (d_at, lanes))
+    last = (last_high[:, :share], last_low[:, :share])
     value = grown[...] + dot3(last, (ff_high[...], ff_low[...]), NN)
     value = halves(value)
     product[...] = dot3(value, (d_high[...], d_low[...]), NT)
-    far = pl.ds(pl.multiple_of((z ^ 3) * wide, wide), wide)
     product[:, far] = dot3(value, (fd_high[...], fd_low[...]), NT)
     lanes = pl.ds(pl.multiple_of(c * half, half), half)
     for which in range(2):
@@ -143,11 +165,10 @@
 def scaled_kernel(share, place, *refs):
     f_high, f_low, d_high, d_low, ff_high, ff_low, fd_high, fd_low = refs[:8]
     s_high, s_low, base, all_f_high, all_f_low, all_d_high, all_d_low = refs[8:]
-    z, c = place[0], place[2]
+    z, x, c = place[0], place[1], place[2]
     wide = fd_high.shape[0]
     width = wide // 2
-    depth = 2 * share
-    f_at = pl.ds(pl.multiple_of((z ^ 3) * depth, depth), depth)
+    f_at = pl.ds(pl.multiple_of((2 * (z ^ 3) + 1 - x) * share, share), share)
     d_at = pl.ds(pl.multiple_of((z ^ 3) * wide, wide), wide)
     for whole, early, late, at in (
         (all_f_high, f_high, ff_high, f_at),
@@ -313,50 +334,52 @@
     factor_lines = (
         panel_factor.reshape(share, 2, half // 128, 128).transpose(0, 2, 1, 3).reshape(-1, 128)
     )
-    bundle = share + width
-    own, send = call(
+    c_own = ancestor_cov.reshape(-1, 128)
+    bundle = (share + width) * half // 128
+    own, send, send_near = call(
         pack_kernel,
         "pack",
-        [like(bundle, half)] * 2,
-        [place],
-        [factor_lines, diag_inverse.transpose(1, 2, 0)],
-        [pltpu.VMEM(factor_lines.shape, F32), pltpu.SemaphoreType.DMA((3,))],
+        [like(bundle, 128)] * 2 + [like(bundle + c_own.shape[0], 128)],
+        [],
+        [factor_lines, diag_inverse.transpose(1, 2, 0), c_own],
+        [
+            pltpu.VMEM(factor_lines.shape, F32),
+            pltpu.VMEM((2, width, half), F32),
+            pltpu.SemaphoreType.DMA((3,)),
+        ],
         pl.BlockSpec(memory_space=pl.ANY),
-        60 * 1024 * 1024,
-    )
-    c_own = ancestor_cov.reshape(-1, 128)
+        PACK_LIMIT,
+    )
+    own_far = move(own, 2, 0, 0)
+    near_far = move(send, 2, 1, 0)
     own_side = move(own, 1, 0, 0)
-    near = move(send, 0, 1, 0)
-    own_far = move(own, 2, 0, 0)
-    c_near = move(c_own, 0, 1, 0)
-    near_far = move(near, 2, 0, 0)
-    near_side = move(near, 1, 0, 0)
-    own_far, near_far, c_near = lax.optimization_barrier((own_far, near_far, c_near))
-    opposite = move(jnp.concatenate([own_far, near_far]), 1, 0, 0)
-    c_sib = move(jnp.concatenate([c_own, c_near]), 0, 0, 1)
-    mine = [own, near, own_far, near_far, own_side, near_side]
-    theirs = move(jnp.concatenate(mine), 0, 0, 1)
+    near_side = move(send, 1, 1, 0)
+    near = move(send_near, 0, 1, 0)
+    own_opposite = move(own_far, 1, 0, 0)
+    near_opposite = move(near_far, 1, 0, 0)
+    mine = [own, own_far, near_far, own_side, near_side, own_opposite, near]
+    theirs = move(jnp.concatenate([*mine, c_own]), 0, 0, 1)
     split_f = [like(slots * tile, whole, dtype=BF16)] * 2
     split_d = [like(whole, whole, dtype=BF16)] * 2
     grown, last_high, last_low, f_high, f_low, d_high, d_low = call(
         functools.partial(early_kernel, share, tile, slots),
         "early",
-        [like(2 * tile, whole)] + [like(2 * tile, 256, dtype=BF16)] * 2 + split_f + split_d,
+        [like(2 * tile, whole)] + [like(2 * tile, 128, dtype=BF16)] * 2 + split_f + split_d,
         [structure, live_counts, place],
-        [c_own, c_near, c_sib] + mine + [theirs],
+        [c_own, *mine, theirs],
         [pltpu.VMEM((2 * tile, slots * tile), F32)],
     )
-    opposite, grown = lax.optimization_barrier((opposite, grown))
-    opposite_theirs = move(opposite, 0, 0, 1)
+    near_opposite, grown = lax.optimization_barrier((near_opposite, grown))
+    opposite_theirs = move(near_opposite, 0, 0, 1)
     outs = call(
         functools.partial(product_kernel, share, tile, slots),
         "products",
         [like(tile, half)] * 2
         + [like(tile, 2 * width)] * 4
-        + [like(2 * share, whole, dtype=BF16)] * 2
+        + [like(share, whole, dtype=BF16)] * 2
         + [like(2 * width, whole, dtype=BF16)] * 2,
         [structure, live_counts, place],
-        [grown, last_high, last_low, d_high, d_low, opposite, opposite_theirs],
+        [grown, last_high, last_low, d_high, d_low, near_opposite, opposite_theirs],
         [pltpu.VMEM((2 * tile, whole), F32)],
     )
     panel, w, late = outs[:2], outs[2:6], outs[6:]
@@ -386,9 +409,11 @@
     met = send_to(cross, lambda z, x, c: (z, x, 1 - c) if c == x else (z, 1 - x, c))
     far = send_to(keep, lambda z, x, c: None if c == x else (z, 1 - x, 1 - c))
     lines = 2 * half // 128
+    panel_got, keep = lax.optimization_barrier((panel_got, keep))
     (panel_lines,) = call(
         lines_kernel, "panel_lines", [like(tile * lines, 128)], [place], [panel[0], panel_got]
     )
+    panel_lines, keep = lax.optimization_barrier((panel_lines, keep))
     (diag_lines,) = call(
         diag_lines_kernel, "diag_lines", [like(width * lines, 128)], [place], [keep, met, far]
     )

time: 58.2 us -> 59 us (1.014)
  local copies, waits for them, and re-layouts: 1.02 us -> 6.49 us
  waiting for transfers between devices: 17.8 us -> 15.7 us
  starting transfers between devices: 25.2 us -> 23.5 us
    unnamed x15, local copies, waits for them, and re-layouts: 1 us -> 5.77 us
    ppermute x16 -> x15, waiting for transfers between devices: 17.8 us -> 15.7 us  [send_to(): return lax.ppermute(value, ('row', 'col'), pairs)]
    ppermute x16 -> x15, starting transfers between devices: 25.2 us -> 23.5 us  [send_to(): return lax.ppermute(value, ('row', 'col'), pairs)]
    concatenate x1, local copies, waits for them, and re-layouts: 0.01 us -> 0.72 us  [local(): theirs = move(jnp.concatenate([*mine, c_own]), 0, 0, 1)]
  transfers between devices with their start and end apart: 16 -> 15, of which waited for: 9 -> 9; matrix products, arithmetic and copies ran while one was open for 2% -> 9% of each run, Pallas kernels for 12% -> 12%
where the time goes in v5:
time: 59 us; the launch traced here: 58.8 us
  starting transfers between devices  23.5 us (40%)
  waiting for transfers between devices  15.7 us (27%)
  Pallas kernels  12.3 us (21%)
  local copies, waits for them, and re-layouts  6.49 us (11%)
  between operations  0.73 us (1%)
    ppermute x15, starting transfers between devices, send_to(): return lax.ppermute(value, ('row', 'col'), pairs)  23.5 us
    ppermute x15, waiting for transfers between devices, send_to(): return lax.ppermute(value, ('row', 'col'), pairs)  15.7 us
    pallas_call x7, Pallas kernels, call(): pl.pallas_call(kernel, out_shape=outs, in_specs=[smem] * len(scalars) + [...  12.3 us
    unnamed x15, local copies, waits for them, and re-layouts  5.77 us
  transfers between devices with their start and end apart: 15, of which 9 were waited for; matrix products, arithmetic and copies ran while one was open for 9% of the time, Pallas kernels for 12%

profile of v5, /device:TPU:1, one launch (start us, length us, event | category | flops | bytes accessed | tf_op | source)
XLA Modules:
  0.0 58.8 jit_solution(10009971527009612259)
XLA Ops:
  0.6 2.1 %pack.1 = (f32[320,128]{1,0:T(8,128)}, f32[320,128]{1,0:T(8,128)}, f32[832,128]{1,0:T(8,128)}) custom-call(f32[384,128]{1,0:T(8,128)} %bitcast.25, f32[2,64,512]{2,1,0:T(8,128)} %bitcast.24, f32[512,128]{1,0:T(8,128)} %bitcast.20), custom_call_target="tpu_custom_call" | custom-call | tf_op jit(solution)/shard_map/pack/pallas_call | solution.py:312
  2.7 3.2 %collective-permute-start.2 = (f32[320,128]{1,0:T(8,128)}, f32[320,128]{1,0:T(8,128)S(1)}, u32[]{:S(2)}, u32[]{:S(2)}) collective-permute-start(f32[320,128]{1,0:T(8,128)} %get-tuple-element.34.refs_0_), channel_id=1, source_target_pairs={{0,8},{1,9},{2,10},{3,11},{4,12},{5,13},{6,14},{7,15},{8,0},{9,1},... | collective-permute-start | bytes 491528 | tf_op jit(solution)/shard_map/ppermute | solution.py:329
  5.9 1.3 %collective-permute-start.3 = (f32[320,128]{1,0:T(8,128)}, f32[320,128]{1,0:T(8,128)S(1)}, u32[]{:S(2)}, u32[]{:S(2)}) collective-permute-start(f32[320,128]{1,0:T(8,128)} %get-tuple-element.34.refs_0_), channel_id=1, source_target_pairs={{0,4},{1,5},{2,6},{3,7},{4,0},{5,1},{6,2},{7,3},{8,12},{9,13},{10,... | collective-permute-start | bytes 491528 | tf_op jit(solution)/shard_map/ppermute | solution.py:329
  7.2 1.0 %collective-permute-start = (f32[320,128]{1,0:T(8,128)}, f32[320,128]{1,0:T(8,128)S(1)}, u32[]{:S(2)}, u32[]{:S(2)}) collective-permute-start(f32[320,128]{1,0:T(8,128)} %get-tuple-element.33), channel_id=1, source_target_pairs={{0,10},{1,11},{2,8},{3,9},{4,14},{5,15},{6,12},{7,13},{8,2},{9,3},... | collective-permute-start | bytes 491528 | tf_op jit(solution)/shard_map/ppermute | solution.py:329
  8.4 1.2 %collective-permute-start.6 = (f32[832,128]{1,0:T(8,128)}, f32[832,128]{1,0:T(8,128)S(1)}, u32[]{:S(2)}, u32[]{:S(2)}) collective-permute-start(f32[832,128]{1,0:T(8,128)} %get-tuple-element.35), channel_id=1, source_target_pairs={{0,2},{1,3},{2,0},{3,1},{4,6},{5,7},{6,4},{7,5},{8,10},{9,11},{10,... | collective-permute-start | bytes 1277960 | tf_op jit(solution)/shard_map/ppermute | solution.py:329
  9.6 1.6 %constant_dynamic-update-slice_fusion.7 = f32[3264,128]{1,0:T(8,128)} fusion(f32[320,128]{1,0:T(8,128)} %get-tuple-element.34.refs_0_), kind=kLoop, calls=%fused_computation.7 | loop fusion | bytes 327680
  11.2 2.4 %collective-permute-done.2.refs_1_ = f32[320,128]{1,0:T(8,128)S(1)} collective-permute-done((f32[320,128]{1,0:T(8,128)}, f32[320,128]{1,0:T(8,128)S(1)}, u32[]{:S(2)}, u32[]{:S(2)}) %collective-permute-start.2) | collective-permute-done | bytes 163872 | tf_op jit(solution)/shard_map/ppermute | solution.py:329
  13.6 1.9 %collective-permute-start.5 = (f32[320,128]{1,0:T(8,128)S(1)}, f32[320,128]{1,0:T(8,128)S(1)}, u32[]{:S(2)}, u32[]{:S(2)}) collective-permute-start(f32[320,128]{1,0:T(8,128)S(1)} %collective-permute-done.2.refs_1_), channel_id=1, source_target_pairs={{0,4},{1,5},{2,6},{3,7},{4,0},{5,1},{6,2},{7,3},{8,12},{9,13},{10,... | collective-permute-start | bytes 491528 | tf_op jit(solution)/shard_map/ppermute | solution.py:329
  16.1 5.2 %collective-permute-done.refs_2_ = f32[320,128]{1,0:T(8,128)S(1)} collective-permute-done((f32[320,128]{1,0:T(8,128)}, f32[320,128]{1,0:T(8,128)S(1)}, u32[]{:S(2)}, u32[]{:S(2)}) %collective-permute-start) | collective-permute-done | bytes 163872 | tf_op jit(solution)/shard_map/ppermute | solution.py:329
  24.6 1.1 %collective-permute-done.6.refs_6_ = f32[832,128]{1,0:T(8,128)S(1)} collective-permute-done((f32[832,128]{1,0:T(8,128)}, f32[832,128]{1,0:T(8,128)S(1)}, u32[]{:S(2)}, u32[]{:S(2)}) %collective-permute-start.6) | collective-permute-done | bytes 426016 | tf_op jit(solution)/shard_map/ppermute | solution.py:329
  27.2 2.1 %collective-permute-start.7 = (f32[3264,128]{1,0:T(8,128)}, f32[3264,128]{1,0:T(8,128)S(1)}, u32[]{:S(2)}, u32[]{:S(2)}) collective-permute-start(f32[3264,128]{1,0:T(8,128)} %constant_dynamic-update-slice_fusion), channel_id=1, source_target_pairs={{0,1},{1,0},{2,3},{3,2},{4,5},{5,4},{6,7},{7,6},{8,9},{9,8},{10,11... | collective-permute-start | bytes 5013512 | tf_op jit(solution)/shard_map/ppermute | solution.py:329
  29.4 1.3 %collective-permute-start.1 = (f32[320,128]{1,0:T(8,128)S(1)}, f32[320,128]{1,0:T(8,128)S(1)}, u32[]{:S(2)}, u32[]{:S(2)}) collective-permute-start(f32[320,128]{1,0:T(8,128)S(1)} %collective-permute-done.refs_2_), channel_id=1, source_target_pairs={{0,4},{1,5},{2,6},{3,7},{4,0},{5,1},{6,2},{7,3},{8,12},{9,13},{10,... | collective-permute-start | bytes 491528 | tf_op jit(solution)/shard_map/ppermute | solution.py:329
  30.7 2.0 %collective-permute-done.7.refs_7_ = f32[3264,128]{1,0:T(8,128)S(1)} collective-permute-done((f32[3264,128]{1,0:T(8,128)}, f32[3264,128]{1,0:T(8,128)S(1)}, u32[]{:S(2)}, u32[]{:S(2)}) %collective-permute-start.7) | collective-permute-done | bytes 1671200 | tf_op jit(solution)/shard_map/ppermute | solution.py:329
  32.8 2.0 %early.1 = (f32[256,512]{1,0:T(8,128)S(1)}, bf16[256,128]{1,0:T(8,128)(2,1)S(1)}, bf16[256,128]{1,0:T(8,128)(2,1)S(1)}, bf16[768,512]{1,0:T(8,128)(2,1)S(1)}, bf...) custom-call(s32[2,6]{1,0:T(2,128)S(1)} %copy-done.2, s32[2]{0:T(128)S(1)} %copy-done.3, ...), custom_call_target="tpu_custom_call" | custom-call | tf_op jit(solution)/shard_map/early/pallas_call | solution.py:312
  36.0 1.0 %collective-permute-done.8.refs_6_ = f32[320,128]{1,0:T(8,128)S(1)} collective-permute-done((f32[320,128]{1,0:T(8,128)S(1)}, f32[320,128]{1,0:T(8,128)S(1)}, u32[]{:S(2)}, u32[]{:S(2)}) %collective-permute-start.8) | collective-permute-done | bytes 163872 | tf_op jit(solution)/shard_map/ppermute | solution.py:329
  37.0 2.1 %products.1 = (f32[128,256]{1,0:T(8,128)S(1)}, f32[128,256]{1,0:T(8,128)S(1)}, f32[128,128]{1,0:T(8,128)S(1)}, f32[128,128]{1,0:T(8,128)S(1)}, f32[128,128]{1,0:...) custom-call(s32[2,6]{1,0:T(2,128)S(1)} %copy-done.2, ...), custom_call_target="tpu_custom_call" | custom-call | tf_op jit(solution)/shard_map/products/pallas_call | solution.py:312
  39.1 1.4 %collective-permute-start.10 = (f32[128,128]{1,0:T(8,128)S(1)}, f32[128,128]{1,0:T(8,128)S(1)}, u32[]{:S(2)}, u32[]{:S(2)}) collective-permute-start(f32[128,128]{1,0:T(8,128)S(1)} %get-tuple-element.46), channel_id=1, source_target_pairs={{0,4},{1,5},{2,6},{3,7},{4,0},{5,1},{6,2},{7,3},{8,12},{9,13},{10,... | collective-permute-start | bytes 196616 | tf_op jit(solution)/shard_map/ppermute | solution.py:329
  40.4 2.2 %collective-permute-start.11 = (f32[128,128]{1,0:T(8,128)S(1)}, f32[128,128]{1,0:T(8,128)S(1)}, u32[]{:S(2)}, u32[]{:S(2)}) collective-permute-start(f32[128,128]{1,0:T(8,128)S(1)} %get-tuple-element.47), channel_id=1, source_target_pairs={{0,8},{1,9},{2,10},{3,11},{4,12},{5,13},{6,14},{7,15},{8,0},{9,1},... | collective-permute-start | bytes 196616 | tf_op jit(solution)/shard_map/ppermute | solution.py:329
  43.8 2.4 %scaled.1 = (bf16[768,512]{1,0:T(8,128)(2,1)S(1)}, bf16[768,512]{1,0:T(8,128)(2,1)S(1)}, f32[64,512]{1,0:T(8,128)S(1)}) custom-call(s32[3]{0:T(128)S(1)} %pad_add_fusion.place, bf16[768,512]{1,0:T(8,128)(2,1)S(1)} %get-tuple-element.49.refs_0_, bf16[768,512]{1,0:T(8,128)(2,1)S(1)} %get-tuple-element.50.refs_1_, ...), custom_call_target="tpu_custom_call" | custom-call | tf_op jit(solution)/shard_map/scaled/pallas_call | solution.py:312
  46.3 2.3 %collective-permute-done.12.w3 = f32[128,128]{1,0:T(8,128)S(1)} collective-permute-done((f32[128,128]{1,0:T(8,128)S(1)}, f32[128,128]{1,0:T(8,128)S(1)}, u32[]{:S(2)}, u32[]{:S(2)}) %collective-permute-start.12) | collective-permute-done | bytes 65568 | tf_op jit(solution)/shard_map/ppermute | solution.py:329
  48.6 1.3 %diag_block.1 = (f32[64,256]{1,0:T(8,128)S(1)}, f32[64,256]{1,0:T(8,128)S(1)}) custom-call(s32[2,6]{1,0:T(2,128)S(1)} %copy-done.2, s32[2]{0:T(128)S(1)} %copy-done.3, s32[3]{0:T(128)S(1)} %pad_add_fusion.place, f32[128,128]{1,0:T(8,128)S(1)} %get-tuple-element.45.w0, f32[128,128]{1,0:T(8,128)S(1)} %collective-permute-done.10.w1, ...), custom_call_target="tpu_custom_call" | custom-call | tf_op jit(solution)/shard_map/diag_block/pallas_call | solution.py:312
  50.5 5.2 %collective-permute-start.14 = (f32[64,256]{1,0:T(8,128)S(1)}, f32[64,256]{1,0:T(8,128)S(1)}, u32[]{:S(2)}, u32[]{:S(2)}) collective-permute-start(f32[64,256]{1,0:T(8,128)S(1)} %get-tuple-element.62.keep), channel_id=1, source_target_pairs={{1,2},{2,1},{5,6},{6,5},{9,10},{10,9},{13,14},{14,13},{17,18},{18,... | collective-permute-start | bytes 196616 | tf_op jit(solution)/shard_map/ppermute | solution.py:329
  55.7 1.3 %panel_lines.1 = f32[512,128]{1,0:T(8,128)} custom-call(s32[3]{0:T(128)S(1)} %pad_add_fusion.place, f32[128,256]{1,0:T(8,128)S(1)} %get-tuple-element.43.mine, f32[128,256]{1,0:T(8,128)S(1)} %collective-permute-done.9.other), custom_call_target="tpu_custom_call" | custom-call | tf_op jit(solution)/shard_map/panel_lines/pallas_call | solution.py:312
  57.6 1.2 %diag_lines.1 = f32[256,128]{1,0:T(8,128)} custom-call(s32[3]{0:T(128)S(1)} %pad_add_fusion.place, f32[64,256]{1,0:T(8,128)S(1)} %get-tuple-element.62.keep, f32[64,256]{1,0:T(8,128)S(1)} %collective-permute-done.13.met, f32[64,256]{1,0:T(8,128)S(1)} %collective-permute-done.14.far), custom_call_target="tpu_custom_call" | custom-call | tf_op jit(solution)/shard_map/diag_lines/pallas_call | solution.py:312
  (30 shorter events, 9.3 us)
Async XLA Ops:
  0.6 25.9 %copy-start = (f32[128,4,1,128]{3,2,1,0:T(1,128)S(1)}, f32[128,4,1,128]{3,2,1,0:T(1,128)}, u32[]{:S(2)}) copy-start(f32[128,4,1,128]{3,2,1,0:T(1,128)} %param.5) | copy-start | bytes 786436
  2.7 10.9 %collective-permute-start.2 = (f32[320,128]{1,0:T(8,128)}, f32[320,128]{1,0:T(8,128)S(1)}, u32[]{:S(2)}, u32[]{:S(2)}) collective-permute-start(f32[320,128]{1,0:T(8,128)} %get-tuple-element.34.refs_0_), channel_id=1, source_target_pairs={{0,8},{1,9},{2,10},{3,11},{4,12},{5,13},{6,14},{7,15},{8,0},{9,1},... | collective-permute-start | bytes 491528 | tf_op jit(solution)/shard_map/ppermute | solution.py:329
  5.9 16.1 %collective-permute-start.3 = (f32[320,128]{1,0:T(8,128)}, f32[320,128]{1,0:T(8,128)S(1)}, u32[]{:S(2)}, u32[]{:S(2)}) collective-permute-start(f32[320,128]{1,0:T(8,128)} %get-tuple-element.34.refs_0_), channel_id=1, source_target_pairs={{0,4},{1,5},{2,6},{3,7},{4,0},{5,1},{6,2},{7,3},{8,12},{9,13},{10,... | collective-permute-start | bytes 491528 | tf_op jit(solution)/shard_map/ppermute | solution.py:329
  7.2 14.1 %collective-permute-start = (f32[320,128]{1,0:T(8,128)}, f32[320,128]{1,0:T(8,128)S(1)}, u32[]{:S(2)}, u32[]{:S(2)}) collective-permute-start(f32[320,128]{1,0:T(8,128)} %get-tuple-element.33), channel_id=1, source_target_pairs={{0,10},{1,11},{2,8},{3,9},{4,14},{5,15},{6,12},{7,13},{8,2},{9,3},... | collective-permute-start | bytes 491528 | tf_op jit(solution)/shard_map/ppermute | solution.py:329
  8.2 14.4 %collective-permute-start.4 = (f32[320,128]{1,0:T(8,128)}, f32[320,128]{1,0:T(8,128)S(1)}, u32[]{:S(2)}, u32[]{:S(2)}) collective-permute-start(f32[320,128]{1,0:T(8,128)} %get-tuple-element.33), channel_id=1, source_target_pairs={{0,6},{1,7},{2,4},{3,5},{4,2},{5,3},{6,0},{7,1},{8,14},{9,15},{10,... | collective-permute-start | bytes 491528 | tf_op jit(solution)/shard_map/ppermute | solution.py:329
  8.4 24.4 %copy-start.1 = (f32[320,128]{1,0:T(8,128)S(1)}, f32[320,128]{1,0:T(8,128)}, u32[]{:S(2)}) copy-start(f32[320,128]{1,0:T(8,128)} %get-tuple-element.34.refs_0_) | copy-start | bytes 491524
  8.4 24.4 %copy-start.2 = (s32[2,6]{1,0:T(2,128)S(1)}, s32[2,6]{1,0:T(2,128)}, u32[]{:S(2)}) copy-start(s32[2,6]{1,0:T(2,128)} %structure.5) | copy-start | bytes 148
  8.4 24.4 %copy-start.3 = (s32[2]{0:T(128)S(1)}, s32[2]{0:T(128)}, u32[]{:S(2)}) copy-start(s32[2]{0:T(128)} %live.5) | copy-start | bytes 28
  8.4 17.3 %collective-permute-start.6 = (f32[832,128]{1,0:T(8,128)}, f32[832,128]{1,0:T(8,128)S(1)}, u32[]{:S(2)}, u32[]{:S(2)}) collective-permute-start(f32[832,128]{1,0:T(8,128)} %get-tuple-element.35), channel_id=1, source_target_pairs={{0,2},{1,3},{2,0},{3,1},{4,6},{5,7},{6,4},{7,5},{8,10},{9,11},{10,... | collective-permute-start | bytes 1277960 | tf_op jit(solution)/shard_map/ppermute | solution.py:329
  13.6 10.3 %collective-permute-start.5 = (f32[320,128]{1,0:T(8,128)S(1)}, f32[320,128]{1,0:T(8,128)S(1)}, u32[]{:S(2)}, u32[]{:S(2)}) collective-permute-start(f32[320,128]{1,0:T(8,128)S(1)} %collective-permute-done.2.refs_1_), channel_id=1, source_target_pairs={{0,4},{1,5},{2,6},{3,7},{4,0},{5,1},{6,2},{7,3},{8,12},{9,13},{10,... | collective-permute-start | bytes 491528 | tf_op jit(solution)/shard_map/ppermute | solution.py:329
  27.2 5.5 %collective-permute-start.7 = (f32[3264,128]{1,0:T(8,128)}, f32[3264,128]{1,0:T(8,128)S(1)}, u32[]{:S(2)}, u32[]{:S(2)}) collective-permute-start(f32[3264,128]{1,0:T(8,128)} %constant_dynamic-update-slice_fusion), channel_id=1, source_target_pairs={{0,1},{1,0},{2,3},{3,2},{4,5},{5,4},{6,7},{7,6},{8,9},{9,8},{10,11... | collective-permute-start | bytes 5013512 | tf_op jit(solution)/shard_map/ppermute | solution.py:329
  29.4 5.8 %collective-permute-start.1 = (f32[320,128]{1,0:T(8,128)S(1)}, f32[320,128]{1,0:T(8,128)S(1)}, u32[]{:S(2)}, u32[]{:S(2)}) collective-permute-start(f32[320,128]{1,0:T(8,128)S(1)} %collective-permute-done.refs_2_), channel_id=1, source_target_pairs={{0,4},{1,5},{2,6},{3,7},{4,0},{5,1},{6,2},{7,3},{8,12},{9,13},{10,... | collective-permute-start | bytes 491528 | tf_op jit(solution)/shard_map/ppermute | solution.py:329
  35.2 1.8 %collective-permute-start.8 = (f32[320,128]{1,0:T(8,128)S(1)}, f32[320,128]{1,0:T(8,128)S(1)}, u32[]{:S(2)}, u32[]{:S(2)}) collective-permute-start(f32[320,128]{1,0:T(8,128)S(1)} %collective-permute-done.1.refs_5_), channel_id=1, source_target_pairs={{0,1},{1,0},{2,3},{3,2},{4,5},{5,4},{6,7},{7,6},{8,9},{9,8},{10,11... | collective-permute-start | bytes 491528 | tf_op jit(solution)/shard_map/ppermute | solution.py:329
  39.1 7.2 %collective-permute-start.10 = (f32[128,128]{1,0:T(8,128)S(1)}, f32[128,128]{1,0:T(8,128)S(1)}, u32[]{:S(2)}, u32[]{:S(2)}) collective-permute-start(f32[128,128]{1,0:T(8,128)S(1)} %get-tuple-element.46), channel_id=1, source_target_pairs={{0,4},{1,5},{2,6},{3,7},{4,0},{5,1},{6,2},{7,3},{8,12},{9,13},{10,... | collective-permute-start | bytes 196616 | tf_op jit(solution)/shard_map/ppermute | solution.py:329
  40.4 5.8 %collective-permute-start.11 = (f32[128,128]{1,0:T(8,128)S(1)}, f32[128,128]{1,0:T(8,128)S(1)}, u32[]{:S(2)}, u32[]{:S(2)}) collective-permute-start(f32[128,128]{1,0:T(8,128)S(1)} %get-tuple-element.47), channel_id=1, source_target_pairs={{0,8},{1,9},{2,10},{3,11},{4,12},{5,13},{6,14},{7,15},{8,0},{9,1},... | collective-permute-start | bytes 196616 | tf_op jit(solution)/shard_map/ppermute | solution.py:329
  42.7 13.0 %collective-permute-start.9 = (f32[128,256]{1,0:T(8,128)S(1)}, f32[128,256]{1,0:T(8,128)S(1)}, u32[]{:S(2)}, u32[]{:S(2)}) collective-permute-start(f32[128,256]{1,0:T(8,128)S(1)} %get-tuple-element.44), channel_id=1, source_target_pairs={{0,2},{1,3},{2,0},{3,1},{4,6},{5,7},{6,4},{7,5},{8,10},{9,11},{10,... | collective-permute-start | bytes 393224 | tf_op jit(solution)/shard_map/ppermute | solution.py:329
  43.6 5.0 %collective-permute-start.12 = (f32[128,128]{1,0:T(8,128)S(1)}, f32[128,128]{1,0:T(8,128)S(1)}, u32[]{:S(2)}, u32[]{:S(2)}) collective-permute-start(f32[128,128]{1,0:T(8,128)S(1)} %get-tuple-element.48), channel_id=1, source_target_pairs={{0,12},{1,13},{2,14},{3,15},{4,8},{5,9},{6,10},{7,11},{8,4},{9,5},... | collective-permute-start | bytes 196616 | tf_op jit(solution)/shard_map/ppermute | solution.py:329
  49.8 7.1 %collective-permute-start.13 = (f32[64,256]{1,0:T(8,128)S(1)}, f32[64,256]{1,0:T(8,128)S(1)}, u32[]{:S(2)}, u32[]{:S(2)}) collective-permute-start(f32[64,256]{1,0:T(8,128)S(1)} %get-tuple-element.63), channel_id=1, source_target_pairs={{0,1},{1,3},{2,0},{3,2},{4,5},{5,7},{6,4},{7,6},{8,9},{9,11},{10,8... | collective-permute-start | bytes 196616 | tf_op jit(solution)/shard_map/ppermute | solution.py:329
  50.5 7.2 %collective-permute-start.14 = (f32[64,256]{1,0:T(8,128)S(1)}, f32[64,256]{1,0:T(8,128)S(1)}, u32[]{:S(2)}, u32[]{:S(2)}) collective-permute-start(f32[64,256]{1,0:T(8,128)S(1)} %get-tuple-element.62.keep), channel_id=1, source_target_pairs={{1,2},{2,1},{5,6},{6,5},{9,10},{10,9},{13,14},{14,13},{17,18},{18,... | collective-permute-start | bytes 196616 | tf_op jit(solution)/shard_map/ppermute | solution.py:329

commit v6 on v5

--- a/solution.py
+++ b/solution.py
@@ -13,7 +13,6 @@
 NN = (((1,), (0,)), ((), ()))
 TN = (((0,), (0,)), ((), ()))
 VMEM_LIMIT = 20 * 1024 * 1024
-PACK_LIMIT = 60 * 1024 * 1024
 
 
 def halves(value):
@@ -341,14 +340,16 @@
         "pack",
         [like(bundle, 128)] * 2 + [like(bundle + c_own.shape[0], 128)],
         [],
-        [factor_lines, diag_inverse.transpose(1, 2, 0), c_own],
+        [
+            pltpu.with_memory_space_constraint(v, pltpu.HBM)
+            for v in (factor_lines, diag_inverse.transpose(1, 2, 0), c_own)
+        ],
         [
             pltpu.VMEM(factor_lines.shape, F32),
             pltpu.VMEM((2, width, half), F32),
             pltpu.SemaphoreType.DMA((3,)),
         ],
-        pl.BlockSpec(memory_space=pl.ANY),
-        PACK_LIMIT,
+        pl.BlockSpec(memory_space=pltpu.HBM),
     )
     own_far = move(own, 2, 0, 0)
     near_far = move(send, 2, 1, 0)
@@ -384,7 +385,6 @@
     )
     panel, w, late = outs[:2], outs[2:6], outs[6:]
     w = [w[0]] + [move(w[step], step, 0, 0) for step in range(1, 4)]
-    panel_got = move(panel[1], 0, 1, 0)
     s_high, s_low, base = call(
         functools.partial(scaled_kernel, share),
         "scaled",
@@ -393,6 +393,8 @@
         [f_high, f_low, d_high, d_low, *late],
         [pltpu.VMEM(s.shape, BF16) for s in split_f + split_d],
     )
+    panel_send, w[1] = lax.optimization_barrier((panel[1], w[1]))
+    panel_got = move(panel_send, 0, 1, 0)
     keep, cross = call(
         functools.partial(diag_kernel, tile, slots),
         "diag_block",

time: 59 us -> 56.8 us (0.963)
  Pallas kernels: 12.3 us -> 11.4 us
  local copies, waits for them, and re-layouts: 6.49 us -> 5.59 us
    unnamed x15 -> x13, local copies, waits for them, and re-layouts: 5.77 us -> 4.86 us
    pallas_call x7, Pallas kernels: 12.3 us -> 11.4 us  [call(): pl.pallas_call(kernel, out_shape=outs, in_specs=[smem] * len(scalars) + [...]
  transfers between devices with their start and end apart: 15 -> 15, of which waited for: 9 -> 9; matrix products, arithmetic and copies ran while one was open for 9% -> 7% of each run, Pallas kernels for 12% -> 12%
where the time goes in v6:
time: 56.8 us; the launch traced here: 56.6 us
  starting transfers between devices  23.2 us (41%)
  waiting for transfers between devices  15.6 us (27%)
  Pallas kernels  11.4 us (20%)
  local copies, waits for them, and re-layouts  5.59 us (10%)
  between operations  0.72 us (1%)
    ppermute x15, starting transfers between devices, send_to(): return lax.ppermute(value, ('row', 'col'), pairs)  23.2 us
    ppermute x15, waiting for transfers between devices, send_to(): return lax.ppermute(value, ('row', 'col'), pairs)  15.6 us
    pallas_call x7, Pallas kernels, call(): pl.pallas_call(kernel, out_shape=outs, in_specs=[smem] * len(scalars) + [...  11.4 us
    unnamed x13, local copies, waits for them, and re-layouts  4.86 us
  transfers between devices with their start and end apart: 15, of which 9 were waited for; matrix products, arithmetic and copies ran while one was open for 7% of the time, Pallas kernels for 12%

profile of v6, /device:TPU:1, one launch (start us, length us, event | category | flops | bytes accessed | tf_op | source)
XLA Modules:
  0.0 56.6 jit_solution(11624773846111884198)
XLA Ops:
  0.6 1.2 %pack.1 = (f32[320,128]{1,0:T(8,128)S(1)}, f32[320,128]{1,0:T(8,128)S(1)}, f32[832,128]{1,0:T(8,128)S(1)}) custom-call(f32[384,128]{1,0:T(8,128)} %bitcast.25, f32[2,64,512]{2,1,0:T(8,128)} %bitcast.24, f32[512,128]{1,0:T(8,128)} %bitcast.20), custom_call_target="tpu_custom_call" | custom-call | tf_op jit(solution)/shard_map/pack/pallas_call | solution.py:311
  1.8 3.2 %collective-permute-start.2 = (f32[320,128]{1,0:T(8,128)S(1)}, f32[320,128]{1,0:T(8,128)S(1)}, u32[]{:S(2)}, u32[]{:S(2)}) collective-permute-start(f32[320,128]{1,0:T(8,128)S(1)} %get-tuple-element.36.refs_0_), channel_id=1, source_target_pairs={{0,8},{1,9},{2,10},{3,11},{4,12},{5,13},{6,14},{7,15},{8,0},{9,1},... | collective-permute-start | bytes 491528 | tf_op jit(solution)/shard_map/ppermute | solution.py:328
  5.0 1.3 %collective-permute-start.3 = (f32[320,128]{1,0:T(8,128)S(1)}, f32[320,128]{1,0:T(8,128)S(1)}, u32[]{:S(2)}, u32[]{:S(2)}) collective-permute-start(f32[320,128]{1,0:T(8,128)S(1)} %get-tuple-element.36.refs_0_), channel_id=1, source_target_pairs={{0,4},{1,5},{2,6},{3,7},{4,0},{5,1},{6,2},{7,3},{8,12},{9,13},{10,... | collective-permute-start | bytes 491528 | tf_op jit(solution)/shard_map/ppermute | solution.py:328
  6.3 1.0 %collective-permute-start = (f32[320,128]{1,0:T(8,128)S(1)}, f32[320,128]{1,0:T(8,128)S(1)}, u32[]{:S(2)}, u32[]{:S(2)}) collective-permute-start(f32[320,128]{1,0:T(8,128)S(1)} %get-tuple-element.35), channel_id=1, source_target_pairs={{0,10},{1,11},{2,8},{3,9},{4,14},{5,15},{6,12},{7,13},{8,2},{9,3},... | collective-permute-start | bytes 491528 | tf_op jit(solution)/shard_map/ppermute | solution.py:328
  7.5 1.2 %collective-permute-start.6 = (f32[832,128]{1,0:T(8,128)S(1)}, f32[832,128]{1,0:T(8,128)S(1)}, u32[]{:S(2)}, u32[]{:S(2)}) collective-permute-start(f32[832,128]{1,0:T(8,128)S(1)} %get-tuple-element.37), channel_id=1, source_target_pairs={{0,2},{1,3},{2,0},{3,1},{4,6},{5,7},{6,4},{7,5},{8,10},{9,11},{10,... | collective-permute-start | bytes 1277960 | tf_op jit(solution)/shard_map/ppermute | solution.py:328
  9.4 3.1 %collective-permute-done.2.refs_1_ = f32[320,128]{1,0:T(8,128)S(1)} collective-permute-done((f32[320,128]{1,0:T(8,128)S(1)}, f32[320,128]{1,0:T(8,128)S(1)}, u32[]{:S(2)}, u32[]{:S(2)}) %collective-permute-start.2) | collective-permute-done | bytes 163872 | tf_op jit(solution)/shard_map/ppermute | solution.py:328
  12.5 1.8 %collective-permute-start.5 = (f32[320,128]{1,0:T(8,128)S(1)}, f32[320,128]{1,0:T(8,128)S(1)}, u32[]{:S(2)}, u32[]{:S(2)}) collective-permute-start(f32[320,128]{1,0:T(8,128)S(1)} %collective-permute-done.2.refs_1_), channel_id=1, source_target_pairs={{0,4},{1,5},{2,6},{3,7},{4,0},{5,1},{6,2},{7,3},{8,12},{9,13},{10,... | collective-permute-start | bytes 491528 | tf_op jit(solution)/shard_map/ppermute | solution.py:328
  14.9 5.3 %collective-permute-done.refs_2_ = f32[320,128]{1,0:T(8,128)S(1)} collective-permute-done((f32[320,128]{1,0:T(8,128)S(1)}, f32[320,128]{1,0:T(8,128)S(1)}, u32[]{:S(2)}, u32[]{:S(2)}) %collective-permute-start) | collective-permute-done | bytes 163872 | tf_op jit(solution)/shard_map/ppermute | solution.py:328
  23.5 1.1 %collective-permute-done.6.refs_6_ = f32[832,128]{1,0:T(8,128)S(1)} collective-permute-done((f32[832,128]{1,0:T(8,128)S(1)}, f32[832,128]{1,0:T(8,128)S(1)}, u32[]{:S(2)}, u32[]{:S(2)}) %collective-permute-start.6) | collective-permute-done | bytes 426016 | tf_op jit(solution)/shard_map/ppermute | solution.py:328
  26.2 2.1 %collective-permute-start.7 = (f32[3264,128]{1,0:T(8,128)}, f32[3264,128]{1,0:T(8,128)S(1)}, u32[]{:S(2)}, u32[]{:S(2)}) collective-permute-start(f32[3264,128]{1,0:T(8,128)} %constant_dynamic-update-slice_fusion), channel_id=1, source_target_pairs={{0,1},{1,0},{2,3},{3,2},{4,5},{5,4},{6,7},{7,6},{8,9},{9,8},{10,11... | collective-permute-start | bytes 5013512 | tf_op jit(solution)/shard_map/ppermute | solution.py:328
  28.3 1.3 %collective-permute-start.1 = (f32[320,128]{1,0:T(8,128)S(1)}, f32[320,128]{1,0:T(8,128)S(1)}, u32[]{:S(2)}, u32[]{:S(2)}) collective-permute-start(f32[320,128]{1,0:T(8,128)S(1)} %collective-permute-done.refs_2_), channel_id=1, source_target_pairs={{0,4},{1,5},{2,6},{3,7},{4,0},{5,1},{6,2},{7,3},{8,12},{9,13},{10,... | collective-permute-start | bytes 491528 | tf_op jit(solution)/shard_map/ppermute | solution.py:328
  29.6 2.0 %collective-permute-done.7.refs_7_ = f32[3264,128]{1,0:T(8,128)S(1)} collective-permute-done((f32[3264,128]{1,0:T(8,128)}, f32[3264,128]{1,0:T(8,128)S(1)}, u32[]{:S(2)}, u32[]{:S(2)}) %collective-permute-start.7) | collective-permute-done | bytes 1671200 | tf_op jit(solution)/shard_map/ppermute | solution.py:328
  31.7 2.0 %early.1 = (f32[256,512]{1,0:T(8,128)S(1)}, bf16[256,128]{1,0:T(8,128)(2,1)S(1)}, bf16[256,128]{1,0:T(8,128)(2,1)S(1)}, bf16[768,512]{1,0:T(8,128)(2,1)S(1)}, bf...) custom-call(s32[2,6]{1,0:T(2,128)S(1)} %copy-done.1, s32[2]{0:T(128)S(1)} %copy-done.2, ...), custom_call_target="tpu_custom_call" | custom-call | tf_op jit(solution)/shard_map/early/pallas_call | solution.py:311
  34.9 1.0 %collective-permute-done.8.refs_6_ = f32[320,128]{1,0:T(8,128)S(1)} collective-permute-done((f32[320,128]{1,0:T(8,128)S(1)}, f32[320,128]{1,0:T(8,128)S(1)}, u32[]{:S(2)}, u32[]{:S(2)}) %collective-permute-start.8) | collective-permute-done | bytes 163872 | tf_op jit(solution)/shard_map/ppermute | solution.py:328
  35.9 2.1 %products.1 = (f32[128,256]{1,0:T(8,128)S(1)}, f32[128,256]{1,0:T(8,128)S(1)}, f32[128,128]{1,0:T(8,128)S(1)}, f32[128,128]{1,0:T(8,128)S(1)}, f32[128,128]{1,0:...) custom-call(s32[2,6]{1,0:T(2,128)S(1)} %copy-done.1, ...), custom_call_target="tpu_custom_call" | custom-call | tf_op jit(solution)/shard_map/products/pallas_call | solution.py:311
  38.0 1.4 %collective-permute-start.9 = (f32[128,128]{1,0:T(8,128)S(1)}, f32[128,128]{1,0:T(8,128)S(1)}, u32[]{:S(2)}, u32[]{:S(2)}) collective-permute-start(f32[128,128]{1,0:T(8,128)S(1)} %get-tuple-element.47), channel_id=1, source_target_pairs={{0,4},{1,5},{2,6},{3,7},{4,0},{5,1},{6,2},{7,3},{8,12},{9,13},{10,... | collective-permute-start | bytes 196616 | tf_op jit(solution)/shard_map/ppermute | solution.py:328
  39.3 2.2 %collective-permute-start.11 = (f32[128,128]{1,0:T(8,128)S(1)}, f32[128,128]{1,0:T(8,128)S(1)}, u32[]{:S(2)}, u32[]{:S(2)}) collective-permute-start(f32[128,128]{1,0:T(8,128)S(1)} %get-tuple-element.51), channel_id=1, source_target_pairs={{0,8},{1,9},{2,10},{3,11},{4,12},{5,13},{6,14},{7,15},{8,0},{9,1},... | collective-permute-start | bytes 196616 | tf_op jit(solution)/shard_map/ppermute | solution.py:328
  41.6 1.2 %collective-permute-start.10 = (f32[128,256]{1,0:T(8,128)S(1)}, f32[128,256]{1,0:T(8,128)S(1)}, u32[]{:S(2)}, u32[]{:S(2)}) collective-permute-start(f32[128,256]{1,0:T(8,128)S(1)} %get-tuple-element.48), channel_id=1, source_target_pairs={{0,2},{1,3},{2,0},{3,1},{4,6},{5,7},{6,4},{7,5},{8,10},{9,11},{10,... | collective-permute-start | bytes 393224 | tf_op jit(solution)/shard_map/ppermute | solution.py:328
  42.8 2.4 %scaled.1 = (bf16[768,512]{1,0:T(8,128)(2,1)S(1)}, bf16[768,512]{1,0:T(8,128)(2,1)S(1)}, f32[64,512]{1,0:T(8,128)S(1)}) custom-call(s32[3]{0:T(128)S(1)} %pad_add_fusion.place, bf16[768,512]{1,0:T(8,128)(2,1)S(1)} %get-tuple-element.53.refs_0_, bf16[768,512]{1,0:T(8,128)(2,1)S(1)} %get-tuple-element.54.refs_1_, ...), custom_call_target="tpu_custom_call" | custom-call | tf_op jit(solution)/shard_map/scaled/pallas_call | solution.py:311
  45.2 1.4 %collective-permute-done.12.w3 = f32[128,128]{1,0:T(8,128)S(1)} collective-permute-done((f32[128,128]{1,0:T(8,128)S(1)}, f32[128,128]{1,0:T(8,128)S(1)}, u32[]{:S(2)}, u32[]{:S(2)}) %collective-permute-start.12) | collective-permute-done | bytes 65568 | tf_op jit(solution)/shard_map/ppermute | solution.py:328
  46.6 1.3 %diag_block.1 = (f32[64,256]{1,0:T(8,128)S(1)}, f32[64,256]{1,0:T(8,128)S(1)}) custom-call(s32[2,6]{1,0:T(2,128)S(1)} %copy-done.1, s32[2]{0:T(128)S(1)} %copy-done.2, s32[3]{0:T(128)S(1)} %pad_add_fusion.place, f32[128,128]{1,0:T(8,128)S(1)} %get-tuple-element.49.w0, f32[128,128]{1,0:T(8,128)S(1)} %collective-permute-done.9.w1, ...), custom_call_target="tpu_custom_call" | custom-call | tf_op jit(solution)/shard_map/diag_block/pallas_call | solution.py:311
  48.7 4.8 %collective-permute-start.14 = (f32[64,256]{1,0:T(8,128)S(1)}, f32[64,256]{1,0:T(8,128)S(1)}, u32[]{:S(2)}, u32[]{:S(2)}) collective-permute-start(f32[64,256]{1,0:T(8,128)S(1)} %get-tuple-element.66.keep), channel_id=1, source_target_pairs={{1,2},{2,1},{5,6},{6,5},{9,10},{10,9},{13,14},{14,13},{17,18},{18,... | collective-permute-start | bytes 196616 | tf_op jit(solution)/shard_map/ppermute | solution.py:328
  53.5 1.3 %panel_lines.1 = f32[512,128]{1,0:T(8,128)} custom-call(s32[3]{0:T(128)S(1)} %pad_add_fusion.place, f32[128,256]{1,0:T(8,128)S(1)} %get-tuple-element.45.mine, f32[128,256]{1,0:T(8,128)S(1)} %collective-permute-done.10.other), custom_call_target="tpu_custom_call" | custom-call | tf_op jit(solution)/shard_map/panel_lines/pallas_call | solution.py:311
  55.4 1.2 %diag_lines.1 = f32[256,128]{1,0:T(8,128)} custom-call(s32[3]{0:T(128)S(1)} %pad_add_fusion.place, f32[64,256]{1,0:T(8,128)S(1)} %get-tuple-element.66.keep, f32[64,256]{1,0:T(8,128)S(1)} %collective-permute-done.13.met, f32[64,256]{1,0:T(8,128)S(1)} %collective-permute-done.14.far), custom_call_target="tpu_custom_call" | custom-call | tf_op jit(solution)/shard_map/diag_lines/pallas_call | solution.py:311
  (28 shorter events, 9.1 us)
Async XLA Ops:
  0.6 24.8 %copy-start = (f32[128,4,1,128]{3,2,1,0:T(1,128)S(1)}, f32[128,4,1,128]{3,2,1,0:T(1,128)}, u32[]{:S(2)}) copy-start(f32[128,4,1,128]{3,2,1,0:T(1,128)} %param.5) | copy-start | bytes 786436
  1.8 10.6 %collective-permute-start.2 = (f32[320,128]{1,0:T(8,128)S(1)}, f32[320,128]{1,0:T(8,128)S(1)}, u32[]{:S(2)}, u32[]{:S(2)}) collective-permute-start(f32[320,128]{1,0:T(8,128)S(1)} %get-tuple-element.36.refs_0_), channel_id=1, source_target_pairs={{0,8},{1,9},{2,10},{3,11},{4,12},{5,13},{6,14},{7,15},{8,0},{9,1},... | collective-permute-start | bytes 491528 | tf_op jit(solution)/shard_map/ppermute | solution.py:328
  5.0 15.9 %collective-permute-start.3 = (f32[320,128]{1,0:T(8,128)S(1)}, f32[320,128]{1,0:T(8,128)S(1)}, u32[]{:S(2)}, u32[]{:S(2)}) collective-permute-start(f32[320,128]{1,0:T(8,128)S(1)} %get-tuple-element.36.refs_0_), channel_id=1, source_target_pairs={{0,4},{1,5},{2,6},{3,7},{4,0},{5,1},{6,2},{7,3},{8,12},{9,13},{10,... | collective-permute-start | bytes 491528 | tf_op jit(solution)/shard_map/ppermute | solution.py:328
  6.3 13.9 %collective-permute-start = (f32[320,128]{1,0:T(8,128)S(1)}, f32[320,128]{1,0:T(8,128)S(1)}, u32[]{:S(2)}, u32[]{:S(2)}) collective-permute-start(f32[320,128]{1,0:T(8,128)S(1)} %get-tuple-element.35), channel_id=1, source_target_pairs={{0,10},{1,11},{2,8},{3,9},{4,14},{5,15},{6,12},{7,13},{8,2},{9,3},... | collective-permute-start | bytes 491528 | tf_op jit(solution)/shard_map/ppermute | solution.py:328
  7.3 14.2 %collective-permute-start.4 = (f32[320,128]{1,0:T(8,128)S(1)}, f32[320,128]{1,0:T(8,128)S(1)}, u32[]{:S(2)}, u32[]{:S(2)}) collective-permute-start(f32[320,128]{1,0:T(8,128)S(1)} %get-tuple-element.35), channel_id=1, source_target_pairs={{0,6},{1,7},{2,4},{3,5},{4,2},{5,3},{6,0},{7,1},{8,14},{9,15},{10,... | collective-permute-start | bytes 491528 | tf_op jit(solution)/shard_map/ppermute | solution.py:328
  7.5 24.2 %copy-start.1 = (s32[2,6]{1,0:T(2,128)S(1)}, s32[2,6]{1,0:T(2,128)}, u32[]{:S(2)}) copy-start(s32[2,6]{1,0:T(2,128)} %structure.5) | copy-start | bytes 148
  7.5 24.2 %copy-start.2 = (s32[2]{0:T(128)S(1)}, s32[2]{0:T(128)}, u32[]{:S(2)}) copy-start(s32[2]{0:T(128)} %live.5) | copy-start | bytes 28
  7.5 17.1 %collective-permute-start.6 = (f32[832,128]{1,0:T(8,128)S(1)}, f32[832,128]{1,0:T(8,128)S(1)}, u32[]{:S(2)}, u32[]{:S(2)}) collective-permute-start(f32[832,128]{1,0:T(8,128)S(1)} %get-tuple-element.37), channel_id=1, source_target_pairs={{0,2},{1,3},{2,0},{3,1},{4,6},{5,7},{6,4},{7,5},{8,10},{9,11},{10,... | collective-permute-start | bytes 1277960 | tf_op jit(solution)/shard_map/ppermute | solution.py:328
  12.5 10.3 %collective-permute-start.5 = (f32[320,128]{1,0:T(8,128)S(1)}, f32[320,128]{1,0:T(8,128)S(1)}, u32[]{:S(2)}, u32[]{:S(2)}) collective-permute-start(f32[320,128]{1,0:T(8,128)S(1)} %collective-permute-done.2.refs_1_), channel_id=1, source_target_pairs={{0,4},{1,5},{2,6},{3,7},{4,0},{5,1},{6,2},{7,3},{8,12},{9,13},{10,... | collective-permute-start | bytes 491528 | tf_op jit(solution)/shard_map/ppermute | solution.py:328
  26.2 5.5 %collective-permute-start.7 = (f32[3264,128]{1,0:T(8,128)}, f32[3264,128]{1,0:T(8,128)S(1)}, u32[]{:S(2)}, u32[]{:S(2)}) collective-permute-start(f32[3264,128]{1,0:T(8,128)} %constant_dynamic-update-slice_fusion), channel_id=1, source_target_pairs={{0,1},{1,0},{2,3},{3,2},{4,5},{5,4},{6,7},{7,6},{8,9},{9,8},{10,11... | collective-permute-start | bytes 5013512 | tf_op jit(solution)/shard_map/ppermute | solution.py:328
  28.3 5.8 %collective-permute-start.1 = (f32[320,128]{1,0:T(8,128)S(1)}, f32[320,128]{1,0:T(8,128)S(1)}, u32[]{:S(2)}, u32[]{:S(2)}) collective-permute-start(f32[320,128]{1,0:T(8,128)S(1)} %collective-permute-done.refs_2_), channel_id=1, source_target_pairs={{0,4},{1,5},{2,6},{3,7},{4,0},{5,1},{6,2},{7,3},{8,12},{9,13},{10,... | collective-permute-start | bytes 491528 | tf_op jit(solution)/shard_map/ppermute | solution.py:328
  34.1 1.8 %collective-permute-start.8 = (f32[320,128]{1,0:T(8,128)S(1)}, f32[320,128]{1,0:T(8,128)S(1)}, u32[]{:S(2)}, u32[]{:S(2)}) collective-permute-start(f32[320,128]{1,0:T(8,128)S(1)} %collective-permute-done.1.refs_5_), channel_id=1, source_target_pairs={{0,1},{1,0},{2,3},{3,2},{4,5},{5,4},{6,7},{7,6},{8,9},{9,8},{10,11... | collective-permute-start | bytes 491528 | tf_op jit(solution)/shard_map/ppermute | solution.py:328
  38.0 3.6 %collective-permute-start.9 = (f32[128,128]{1,0:T(8,128)S(1)}, f32[128,128]{1,0:T(8,128)S(1)}, u32[]{:S(2)}, u32[]{:S(2)}) collective-permute-start(f32[128,128]{1,0:T(8,128)S(1)} %get-tuple-element.47), channel_id=1, source_target_pairs={{0,4},{1,5},{2,6},{3,7},{4,0},{5,1},{6,2},{7,3},{8,12},{9,13},{10,... | collective-permute-start | bytes 196616 | tf_op jit(solution)/shard_map/ppermute | solution.py:328
  39.3 5.8 %collective-permute-start.11 = (f32[128,128]{1,0:T(8,128)S(1)}, f32[128,128]{1,0:T(8,128)S(1)}, u32[]{:S(2)}, u32[]{:S(2)}) collective-permute-start(f32[128,128]{1,0:T(8,128)S(1)} %get-tuple-element.51), channel_id=1, source_target_pairs={{0,8},{1,9},{2,10},{3,11},{4,12},{5,13},{6,14},{7,15},{8,0},{9,1},... | collective-permute-start | bytes 196616 | tf_op jit(solution)/shard_map/ppermute | solution.py:328
  41.6 5.0 %collective-permute-start.12 = (f32[128,128]{1,0:T(8,128)S(1)}, f32[128,128]{1,0:T(8,128)S(1)}, u32[]{:S(2)}, u32[]{:S(2)}) collective-permute-start(f32[128,128]{1,0:T(8,128)S(1)} %get-tuple-element.52), channel_id=1, source_target_pairs={{0,12},{1,13},{2,14},{3,15},{4,8},{5,9},{6,10},{7,11},{8,4},{9,5},... | collective-permute-start | bytes 196616 | tf_op jit(solution)/shard_map/ppermute | solution.py:328
  41.6 11.9 %collective-permute-start.10 = (f32[128,256]{1,0:T(8,128)S(1)}, f32[128,256]{1,0:T(8,128)S(1)}, u32[]{:S(2)}, u32[]{:S(2)}) collective-permute-start(f32[128,256]{1,0:T(8,128)S(1)} %get-tuple-element.48), channel_id=1, source_target_pairs={{0,2},{1,3},{2,0},{3,1},{4,6},{5,7},{6,4},{7,5},{8,10},{9,11},{10,... | collective-permute-start | bytes 393224 | tf_op jit(solution)/shard_map/ppermute | solution.py:328
  47.9 6.9 %collective-permute-start.13 = (f32[64,256]{1,0:T(8,128)S(1)}, f32[64,256]{1,0:T(8,128)S(1)}, u32[]{:S(2)}, u32[]{:S(2)}) collective-permute-start(f32[64,256]{1,0:T(8,128)S(1)} %get-tuple-element.67), channel_id=1, source_target_pairs={{0,1},{1,3},{2,0},{3,2},{4,5},{5,7},{6,4},{7,6},{8,9},{9,11},{10,8... | collective-permute-start | bytes 196616 | tf_op jit(solution)/shard_map/ppermute | solution.py:328
  48.7 6.7 %collective-permute-start.14 = (f32[64,256]{1,0:T(8,128)S(1)}, f32[64,256]{1,0:T(8,128)S(1)}, u32[]{:S(2)}, u32[]{:S(2)}) collective-permute-start(f32[64,256]{1,0:T(8,128)S(1)} %get-tuple-element.66.keep), channel_id=1, source_target_pairs={{1,2},{2,1},{5,6},{6,5},{9,10},{10,9},{13,14},{14,13},{17,18},{18,... | collective-permute-start | bytes 196616 | tf_op jit(solution)/shard_map/ppermute | solution.py:328

commit v7 on v6

--- a/solution.py
+++ b/solution.py
@@ -35,7 +35,7 @@
     high[at], low[at] = halves(value)
 
 
-def pack_kernel(factor, inverse, cov, own, send, near, lines, held, sem):
+def pack_kernel(factor, inverse, own, send, lines, held, sem):
     x = lax.axis_index("row") % 2
     c = lax.axis_index("col")
     width = held.shape[1]
@@ -46,26 +46,23 @@
     copies = [
         pltpu.make_async_copy(factor, lines, sem.at[0]),
         pltpu.make_async_copy(inverse.at[:, :, lanes], held, sem.at[1]),
-        pltpu.make_async_copy(cov, near.at[pl.ds(own.shape[0], cov.shape[0]), :], sem.at[2]),
     ]
     for copy in copies:
         copy.start()
-    copies[0].wait()
-    copies[1].wait()
-    for outs, member in (((own,), x), ((send, near), 1 - x)):
+    for copy in copies:
+        copy.wait()
+    for out, member in ((own, x), (send, 1 - x)):
         for b in range(blocks):
             rows = lines[pl.ds(2 * b + member, share, stride=2 * blocks), :]
             cols = held[member, :, b * 128:(b + 1) * 128]
-            for out in outs:
-                out[b * block:b * block + share, :] = rows
-                out[b * block + share:(b + 1) * block, :] = cols
-    copies[2].wait()
+            out[b * block:b * block + share, :] = rows
+            out[b * block + share:(b + 1) * block, :] = cols
 
 
 def early_kernel(share, tile, slots, structure, live, place, c_own, *refs):
     mine = refs[:7]
-    theirs = refs[7]
-    grown, last_high, last_low, f_high, f_low, d_high, d_low, pick = refs[8:]
+    theirs, near_theirs, c_sib, c_near, c_near_sib = refs[7:12]
+    grown, last_high, last_low, f_high, f_low, d_high, d_low, pick = refs[12:]
     z, x, c = place[0], place[1], place[2]
     size = mine[0].shape[0]
     whole = d_high.shape[0]
@@ -86,7 +83,8 @@
     for index, source in enumerate(sources):
         f_at = pl.ds(pl.multiple_of(source * share, share), share)
         d_at = pl.ds(pl.multiple_of(source * width, width), width)
-        for first, ref, start in ((0, mine[index], 0), (half, theirs, index * size)):
+        there = (theirs, index * size) if index < 6 else (near_theirs, 0)
+        for first, (ref, start) in ((0, (mine[index], 0)), (half, there)):
             for b in range(lane_blocks):
                 lanes = slice(first + b * 128, first + (b + 1) * 128)
                 top = start + b * block
@@ -102,12 +100,9 @@
     blocks = c_own.shape[0] // tile
     for slot in range(slots):
         anc = structure[x, slot]
-        for which, (here, start, offset) in enumerate(
-            ((c_own, 0, 7 * size + c_own.shape[0]), (mine[6], size, 7 * size))
-        ):
-            here_at = pl.ds(start + anc // 2, tile, stride=blocks)
-            there_at = pl.ds(offset + anc // 2, tile, stride=blocks)
-            value = jnp.where(anc % 2 == c, here[here_at, :], theirs[there_at, :])
+        rows = pl.ds(anc // 2, tile, stride=blocks)
+        for which, (here, there) in enumerate(((c_own, c_sib), (c_near, c_near_sib))):
+            value = jnp.where(anc % 2 == c, here[rows, :], there[rows, :])
             at = pl.ds(pl.multiple_of((x ^ which) * tile, tile), tile)
             pick[at, slot * tile:(slot + 1) * tile] = jnp.where(slot < live[x], value, 0.0)
     picked = pick[...]
@@ -335,19 +330,19 @@
     )
     c_own = ancestor_cov.reshape(-1, 128)
     bundle = (share + width) * half // 128
-    own, send, send_near = call(
+    own, send = call(
         pack_kernel,
         "pack",
-        [like(bundle, 128)] * 2 + [like(bundle + c_own.shape[0], 128)],
+        [like(bundle, 128)] * 2,
         [],
         [
             pltpu.with_memory_space_constraint(v, pltpu.HBM)
-            for v in (factor_lines, diag_inverse.transpose(1, 2, 0), c_own)
+            for v in (factor_lines, diag_inverse.transpose(1, 2, 0))
         ],
         [
             pltpu.VMEM(factor_lines.shape, F32),
             pltpu.VMEM((2, width, half), F32),
-            pltpu.SemaphoreType.DMA((3,)),
+            pltpu.SemaphoreType.DMA((2,)),
         ],
         pl.BlockSpec(memory_space=pltpu.HBM),
     )
@@ -355,11 +350,21 @@
     near_far = move(send, 2, 1, 0)
     own_side = move(own, 1, 0, 0)
     near_side = move(send, 1, 1, 0)
-    near = move(send_near, 0, 1, 0)
+    near = move(send, 0, 1, 0)
+    c_near = move(c_own, 0, 1, 0)
+    own_far, near = lax.optimization_barrier((own_far, near))
     own_opposite = move(own_far, 1, 0, 0)
+    near_far, c_near = lax.optimization_barrier((near_far, c_near))
     near_opposite = move(near_far, 1, 0, 0)
-    mine = [own, own_far, near_far, own_side, near_side, own_opposite, near]
-    theirs = move(jnp.concatenate([*mine, c_own]), 0, 0, 1)
+    mine = [own, own_far, near_far, own_side, near_side, own_opposite]
+    theirs = [
+        move(jnp.concatenate(mine), 0, 0, 1),
+        move(near, 0, 0, 1),
+        move(c_own, 0, 0, 1),
+        move(c_near, 0, 0, 1),
+    ]
+    near_opposite, c_first = lax.optimization_barrier((near_opposite, c_own))
+    opposite_theirs = move(near_opposite, 0, 0, 1)
     split_f = [like(slots * tile, whole, dtype=BF16)] * 2
     split_d = [like(whole, whole, dtype=BF16)] * 2
     grown, last_high, last_low, f_high, f_low, d_high, d_low = call(
@@ -367,11 +372,9 @@
         "early",
         [like(2 * tile, whole)] + [like(2 * tile, 128, dtype=BF16)] * 2 + split_f + split_d,
         [structure, live_counts, place],
-        [c_own, *mine, theirs],
+        [c_first, *mine, near, *theirs[:3], c_near, theirs[3]],
         [pltpu.VMEM((2 * tile, slots * tile), F32)],
     )
-    near_opposite, grown = lax.optimization_barrier((near_opposite, grown))
-    opposite_theirs = move(near_opposite, 0, 0, 1)
     outs = call(
         functools.partial(product_kernel, share, tile, slots),
         "products",

time: 56.8 us -> 59.4 us (1.046)
  starting transfers between devices: 23.2 us -> 25.4 us
  local copies, waits for them, and re-layouts: 5.59 us -> 4.68 us
  waiting for transfers between devices: 15.6 us -> 16.5 us
    ppermute x15 -> x19, starting transfers between devices: 23.2 us -> 25.4 us  [send_to(): return lax.ppermute(value, ('row', 'col'), pairs)]
    ppermute x15 -> x19, waiting for transfers between devices: 15.6 us -> 16.5 us  [send_to(): return lax.ppermute(value, ('row', 'col'), pairs)]
    unnamed x13 -> x11, local copies, waits for them, and re-layouts: 4.86 us -> 4 us
  transfers between devices with their start and end apart: 15 -> 19, of which waited for: 9 -> 7; matrix products, arithmetic and copies ran while one was open for 7% -> 6% of each run, Pallas kernels for 12% -> 12%
where the time goes in v7:
time: 59.4 us; the launch traced here: 59.2 us
  starting transfers between devices  25.4 us (43%)
  waiting for transfers between devices  16.5 us (28%)
  Pallas kernels  11.7 us (20%)
  local copies, waits for them, and re-layouts  4.68 us (8%)
  between operations  0.74 us (1%)
    ppermute x19, starting transfers between devices, send_to(): return lax.ppermute(value, ('row', 'col'), pairs)  25.4 us
    ppermute x19, waiting for transfers between devices, send_to(): return lax.ppermute(value, ('row', 'col'), pairs)  16.5 us
    pallas_call x7, Pallas kernels, call(): pl.pallas_call(kernel, out_shape=outs, in_specs=[smem] * len(scalars) + [...  11.7 us
    unnamed x11, local copies, waits for them, and re-layouts  4 us
  transfers between devices with their start and end apart: 19, of which 7 were waited for; matrix products, arithmetic and copies ran while one was open for 6% of the time, Pallas kernels for 12%

profile of v7, /device:TPU:1, one launch (start us, length us, event | category | flops | bytes accessed | tf_op | source)
XLA Modules:
  0.0 59.2 jit_solution(9373381161167029754)
XLA Ops:
  0.6 1.1 %pack.1 = (f32[320,128]{1,0:T(8,128)S(1)}, f32[320,128]{1,0:T(8,128)S(1)}) custom-call(f32[384,128]{1,0:T(8,128)} %bitcast.25, f32[2,64,512]{2,1,0:T(8,128)} %bitcast.23), custom_call_target="tpu_custom_call" | custom-call | tf_op jit(solution)/shard_map/pack/pallas_call | solution.py:306
  1.7 3.2 %collective-permute-start.3 = (f32[320,128]{1,0:T(8,128)S(1)}, f32[320,128]{1,0:T(8,128)S(1)}, u32[]{:S(2)}, u32[]{:S(2)}) collective-permute-start(f32[320,128]{1,0:T(8,128)S(1)} %get-tuple-element.41.refs_0_), channel_id=1, source_target_pairs={{0,8},{1,9},{2,10},{3,11},{4,12},{5,13},{6,14},{7,15},{8,0},{9,1},... | collective-permute-start | bytes 491528 | tf_op jit(solution)/shard_map/ppermute | solution.py:323
  4.9 1.2 %collective-permute-start.4 = (f32[320,128]{1,0:T(8,128)S(1)}, f32[320,128]{1,0:T(8,128)S(1)}, u32[]{:S(2)}, u32[]{:S(2)}) collective-permute-start(f32[320,128]{1,0:T(8,128)S(1)} %get-tuple-element.38), channel_id=1, source_target_pairs={{0,2},{1,3},{2,0},{3,1},{4,6},{5,7},{6,4},{7,5},{8,10},{9,11},{10,... | collective-permute-start | bytes 491528 | tf_op jit(solution)/shard_map/ppermute | solution.py:323
  6.4 1.0 %collective-permute-start = (f32[320,128]{1,0:T(8,128)S(1)}, f32[320,128]{1,0:T(8,128)S(1)}, u32[]{:S(2)}, u32[]{:S(2)}) collective-permute-start(f32[320,128]{1,0:T(8,128)S(1)} %get-tuple-element.38), channel_id=1, source_target_pairs={{0,10},{1,11},{2,8},{3,9},{4,14},{5,15},{6,12},{7,13},{8,2},{9,3},... | collective-permute-start | bytes 491528 | tf_op jit(solution)/shard_map/ppermute | solution.py:323
  7.4 1.3 %collective-permute-start.5 = (f32[320,128]{1,0:T(8,128)S(1)}, f32[320,128]{1,0:T(8,128)S(1)}, u32[]{:S(2)}, u32[]{:S(2)}) collective-permute-start(f32[320,128]{1,0:T(8,128)S(1)} %get-tuple-element.41.refs_0_), channel_id=1, source_target_pairs={{0,4},{1,5},{2,6},{3,7},{4,0},{5,1},{6,2},{7,3},{8,12},{9,13},{10,... | collective-permute-start | bytes 491528 | tf_op jit(solution)/shard_map/ppermute | solution.py:323
  9.4 5.0 %collective-permute-done.3.refs_1_ = f32[320,128]{1,0:T(8,128)S(1)} collective-permute-done((f32[320,128]{1,0:T(8,128)S(1)}, f32[320,128]{1,0:T(8,128)S(1)}, u32[]{:S(2)}, u32[]{:S(2)}) %collective-permute-start.3) | collective-permute-done | bytes 163872 | tf_op jit(solution)/shard_map/ppermute | solution.py:323
  14.4 3.6 %collective-permute-start.6 = (f32[320,128]{1,0:T(8,128)S(1)}, f32[320,128]{1,0:T(8,128)S(1)}, u32[]{:S(2)}, u32[]{:S(2)}) collective-permute-start(f32[320,128]{1,0:T(8,128)S(1)} %get-tuple-element.38), channel_id=1, source_target_pairs={{0,6},{1,7},{2,4},{3,5},{4,2},{5,3},{6,0},{7,1},{8,14},{9,15},{10,... | collective-permute-start | bytes 491528 | tf_op jit(solution)/shard_map/ppermute | solution.py:323
  18.0 0.7 %constant_dynamic-update-slice_fusion.4 = f32[1920,128]{1,0:T(8,128)} fusion(f32[1920,128]{1,0:T(8,128)} %constant_dynamic-update-slice_fusion.5, f32[320,128]{1,0:T(8,128)S(1)} %collective-permute-done.3.refs_1_), kind=kLoop, calls=%fused_computation.4 | loop fusion | bytes 327680
  18.7 1.4 %collective-permute-done.refs_2_ = f32[320,128]{1,0:T(8,128)S(1)} collective-permute-done((f32[320,128]{1,0:T(8,128)S(1)}, f32[320,128]{1,0:T(8,128)S(1)}, u32[]{:S(2)}, u32[]{:S(2)}) %collective-permute-start) | collective-permute-done | bytes 163872 | tf_op jit(solution)/shard_map/ppermute | solution.py:323
  20.1 0.7 %constant_dynamic-update-slice_fusion.3 = f32[1920,128]{1,0:T(8,128)} fusion(f32[1920,128]{1,0:T(8,128)} %constant_dynamic-update-slice_fusion.4, f32[320,128]{1,0:T(8,128)S(1)} %collective-permute-done.refs_2_), kind=kLoop, calls=%fused_computation.3 | loop fusion | bytes 327680
  20.8 0.7 %constant_dynamic-update-slice_fusion.2 = f32[1920,128]{1,0:T(8,128)} fusion(f32[1920,128]{1,0:T(8,128)} %constant_dynamic-update-slice_fusion.3, f32[320,128]{1,0:T(8,128)S(1)} %collective-permute-done.5.refs_3_), kind=kLoop, calls=%fused_computation.2 | loop fusion | bytes 327680
  21.5 2.3 %collective-permute-done.6.refs_4_ = f32[320,128]{1,0:T(8,128)S(1)} collective-permute-done((f32[320,128]{1,0:T(8,128)S(1)}, f32[320,128]{1,0:T(8,128)S(1)}, u32[]{:S(2)}, u32[]{:S(2)}) %collective-permute-start.6) | collective-permute-done | bytes 163872 | tf_op jit(solution)/shard_map/ppermute | solution.py:323
  25.8 2.6 %collective-permute-start.8 = (f32[1920,128]{1,0:T(8,128)}, f32[1920,128]{1,0:T(8,128)S(1)}, u32[]{:S(2)}, u32[]{:S(2)}) collective-permute-start(f32[1920,128]{1,0:T(8,128)} %constant_dynamic-update-slice_fusion), channel_id=1, source_target_pairs={{0,1},{1,0},{2,3},{3,2},{4,5},{5,4},{6,7},{7,6},{8,9},{9,8},{10,11... | collective-permute-start | bytes 2949128 | tf_op jit(solution)/shard_map/ppermute | solution.py:323
  29.6 4.6 %collective-permute-done.2.refs_5_ = f32[320,128]{1,0:T(8,128)S(1)} collective-permute-done((f32[320,128]{1,0:T(8,128)S(1)}, f32[320,128]{1,0:T(8,128)S(1)}, u32[]{:S(2)}, u32[]{:S(2)}) %collective-permute-start.2) | collective-permute-done | bytes 163872 | tf_op jit(solution)/shard_map/ppermute | solution.py:323
  34.2 0.8 %collective-permute-start.12 = (f32[320,128]{1,0:T(8,128)S(1)}, f32[320,128]{1,0:T(8,128)S(1)}, u32[]{:S(2)}, u32[]{:S(2)}) collective-permute-start(f32[320,128]{1,0:T(8,128)S(1)} %collective-permute-done.2.refs_5_), channel_id=1, source_target_pairs={{0,1},{1,0},{2,3},{3,2},{4,5},{5,4},{6,7},{7,6},{8,9},{9,8},{10,11... | collective-permute-start | bytes 491528 | tf_op jit(solution)/shard_map/ppermute | solution.py:323
  35.7 2.4 %early.1 = (f32[256,512]{1,0:T(8,128)S(1)}, bf16[256,128]{1,0:T(8,128)(2,1)S(1)}, bf16[256,128]{1,0:T(8,128)(2,1)S(1)}, bf16[768,512]{1,0:T(8,128)(2,1)S(1)}, bf...) custom-call(s32[2,6]{1,0:T(2,128)S(1)} %copy-done.1, s32[2]{0:T(128)S(1)} %copy-done.2, ...), custom_call_target="tpu_custom_call" | custom-call | tf_op jit(solution)/shard_map/early/pallas_call | solution.py:306
  38.1 2.1 %products.1 = (f32[128,256]{1,0:T(8,128)S(1)}, f32[128,256]{1,0:T(8,128)S(1)}, f32[128,128]{1,0:T(8,128)S(1)}, f32[128,128]{1,0:T(8,128)S(1)}, f32[128,128]{1,0:...) custom-call(s32[2,6]{1,0:T(2,128)S(1)} %copy-done.1, ...), custom_call_target="tpu_custom_call" | custom-call | tf_op jit(solution)/shard_map/products/pallas_call | solution.py:306
  40.7 3.8 %collective-permute-start.15 = (f32[128,128]{1,0:T(8,128)S(1)}, f32[128,128]{1,0:T(8,128)S(1)}, u32[]{:S(2)}, u32[]{:S(2)}) collective-permute-start(f32[128,128]{1,0:T(8,128)S(1)} %get-tuple-element.57), channel_id=1, source_target_pairs={{0,8},{1,9},{2,10},{3,11},{4,12},{5,13},{6,14},{7,15},{8,0},{9,1},... | collective-permute-start | bytes 196616 | tf_op jit(solution)/shard_map/ppermute | solution.py:323
  45.1 2.4 %scaled.1 = (bf16[768,512]{1,0:T(8,128)(2,1)S(1)}, bf16[768,512]{1,0:T(8,128)(2,1)S(1)}, f32[64,512]{1,0:T(8,128)S(1)}) custom-call(s32[3]{0:T(128)S(1)} %pad_add_fusion.place, bf16[768,512]{1,0:T(8,128)(2,1)S(1)} %get-tuple-element.59.refs_0_, bf16[768,512]{1,0:T(8,128)(2,1)S(1)} %get-tuple-element.60.refs_1_, ...), custom_call_target="tpu_custom_call" | custom-call | tf_op jit(solution)/shard_map/scaled/pallas_call | solution.py:306
  47.6 2.0 %collective-permute-done.16.w3 = f32[128,128]{1,0:T(8,128)S(1)} collective-permute-done((f32[128,128]{1,0:T(8,128)S(1)}, f32[128,128]{1,0:T(8,128)S(1)}, u32[]{:S(2)}, u32[]{:S(2)}) %collective-permute-start.16) | collective-permute-done | bytes 65568 | tf_op jit(solution)/shard_map/ppermute | solution.py:323
  49.5 1.3 %diag_block.1 = (f32[64,256]{1,0:T(8,128)S(1)}, f32[64,256]{1,0:T(8,128)S(1)}) custom-call(s32[2,6]{1,0:T(2,128)S(1)} %copy-done.1, s32[2]{0:T(128)S(1)} %copy-done.2, s32[3]{0:T(128)S(1)} %pad_add_fusion.place, f32[128,128]{1,0:T(8,128)S(1)} %get-tuple-element.55.w0, f32[128,128]{1,0:T(8,128)S(1)} %collective-permute-done.13.w1, ...), custom_call_target="tpu_custom_call" | custom-call | tf_op jit(solution)/shard_map/diag_block/pallas_call | solution.py:306
  51.2 4.8 %collective-permute-start.18 = (f32[64,256]{1,0:T(8,128)S(1)}, f32[64,256]{1,0:T(8,128)S(1)}, u32[]{:S(2)}, u32[]{:S(2)}) collective-permute-start(f32[64,256]{1,0:T(8,128)S(1)} %get-tuple-element.72.keep), channel_id=1, source_target_pairs={{1,2},{2,1},{5,6},{6,5},{9,10},{10,9},{13,14},{14,13},{17,18},{18,... | collective-permute-start | bytes 196616 | tf_op jit(solution)/shard_map/ppermute | solution.py:323
  56.0 1.3 %panel_lines.1 = f32[512,128]{1,0:T(8,128)} custom-call(s32[3]{0:T(128)S(1)} %pad_add_fusion.place, f32[128,256]{1,0:T(8,128)S(1)} %get-tuple-element.51.mine, f32[128,256]{1,0:T(8,128)S(1)} %collective-permute-done.14.other), custom_call_target="tpu_custom_call" | custom-call | tf_op jit(solution)/shard_map/panel_lines/pallas_call | solution.py:306
  58.0 1.2 %diag_lines.1 = f32[256,128]{1,0:T(8,128)} custom-call(s32[3]{0:T(128)S(1)} %pad_add_fusion.place, f32[64,256]{1,0:T(8,128)S(1)} %get-tuple-element.72.keep, f32[64,256]{1,0:T(8,128)S(1)} %collective-permute-done.17.met, f32[64,256]{1,0:T(8,128)S(1)} %collective-permute-done.18.far), custom_call_target="tpu_custom_call" | custom-call | tf_op jit(solution)/shard_map/diag_lines/pallas_call | solution.py:306
  (34 shorter events, 7.1 us)
Async XLA Ops:
  0.6 5.5 %copy-start = (f32[128,4,1,128]{3,2,1,0:T(1,128)S(1)}, f32[128,4,1,128]{3,2,1,0:T(1,128)}, u32[]{:S(2)}) copy-start(f32[128,4,1,128]{3,2,1,0:T(1,128)} %param.5) | copy-start | bytes 786436
  1.7 12.6 %collective-permute-start.3 = (f32[320,128]{1,0:T(8,128)S(1)}, f32[320,128]{1,0:T(8,128)S(1)}, u32[]{:S(2)}, u32[]{:S(2)}) collective-permute-start(f32[320,128]{1,0:T(8,128)S(1)} %get-tuple-element.41.refs_0_), channel_id=1, source_target_pairs={{0,8},{1,9},{2,10},{3,11},{4,12},{5,13},{6,14},{7,15},{8,0},{9,1},... | collective-permute-start | bytes 491528 | tf_op jit(solution)/shard_map/ppermute | solution.py:323
  4.9 13.1 %collective-permute-start.4 = (f32[320,128]{1,0:T(8,128)S(1)}, f32[320,128]{1,0:T(8,128)S(1)}, u32[]{:S(2)}, u32[]{:S(2)}) collective-permute-start(f32[320,128]{1,0:T(8,128)S(1)} %get-tuple-element.38), channel_id=1, source_target_pairs={{0,2},{1,3},{2,0},{3,1},{4,6},{5,7},{6,4},{7,5},{8,10},{9,11},{10,... | collective-permute-start | bytes 491528 | tf_op jit(solution)/shard_map/ppermute | solution.py:323
  6.2 13.9 %collective-permute-start.1 = (f32[512,128]{1,0:T(8,128)S(1)}, f32[512,128]{1,0:T(8,128)S(1)}, u32[]{:S(2)}, u32[]{:S(2)}) collective-permute-start(f32[512,128]{1,0:T(8,128)S(1)} %bitcast.20), channel_id=1, source_target_pairs={{0,2},{1,3},{2,0},{3,1},{4,6},{5,7},{6,4},{7,5},{8,10},{9,11},{10,... | collective-permute-start | bytes 786440 | tf_op jit(solution)/shard_map/ppermute | solution.py:323
  6.4 13.7 %collective-permute-start = (f32[320,128]{1,0:T(8,128)S(1)}, f32[320,128]{1,0:T(8,128)S(1)}, u32[]{:S(2)}, u32[]{:S(2)}) collective-permute-start(f32[320,128]{1,0:T(8,128)S(1)} %get-tuple-element.38), channel_id=1, source_target_pairs={{0,10},{1,11},{2,8},{3,9},{4,14},{5,15},{6,12},{7,13},{8,2},{9,3},... | collective-permute-start | bytes 491528 | tf_op jit(solution)/shard_map/ppermute | solution.py:323
  7.4 13.4 %collective-permute-start.5 = (f32[320,128]{1,0:T(8,128)S(1)}, f32[320,128]{1,0:T(8,128)S(1)}, u32[]{:S(2)}, u32[]{:S(2)}) collective-permute-start(f32[320,128]{1,0:T(8,128)S(1)} %get-tuple-element.41.refs_0_), channel_id=1, source_target_pairs={{0,4},{1,5},{2,6},{3,7},{4,0},{5,1},{6,2},{7,3},{8,12},{9,13},{10,... | collective-permute-start | bytes 491528 | tf_op jit(solution)/shard_map/ppermute | solution.py:323
  14.4 9.5 %collective-permute-start.6 = (f32[320,128]{1,0:T(8,128)S(1)}, f32[320,128]{1,0:T(8,128)S(1)}, u32[]{:S(2)}, u32[]{:S(2)}) collective-permute-start(f32[320,128]{1,0:T(8,128)S(1)} %get-tuple-element.38), channel_id=1, source_target_pairs={{0,6},{1,7},{2,4},{3,5},{4,2},{5,3},{6,0},{7,1},{8,14},{9,15},{10,... | collective-permute-start | bytes 491528 | tf_op jit(solution)/shard_map/ppermute | solution.py:323
  18.0 7.1 %collective-permute-start.7 = (f32[320,128]{1,0:T(8,128)S(1)}, f32[320,128]{1,0:T(8,128)S(1)}, u32[]{:S(2)}, u32[]{:S(2)}) collective-permute-start(f32[320,128]{1,0:T(8,128)S(1)} %collective-permute-done.3.refs_1_), channel_id=1, source_target_pairs={{0,4},{1,5},{2,6},{3,7},{4,0},{5,1},{6,2},{7,3},{8,12},{9,13},{10,... | collective-permute-start | bytes 491528 | tf_op jit(solution)/shard_map/ppermute | solution.py:323
  25.8 9.3 %collective-permute-start.8 = (f32[1920,128]{1,0:T(8,128)}, f32[1920,128]{1,0:T(8,128)S(1)}, u32[]{:S(2)}, u32[]{:S(2)}) collective-permute-start(f32[1920,128]{1,0:T(8,128)} %constant_dynamic-update-slice_fusion), channel_id=1, source_target_pairs={{0,1},{1,0},{2,3},{3,2},{4,5},{5,4},{6,7},{7,6},{8,9},{9,8},{10,11... | collective-permute-start | bytes 2949128 | tf_op jit(solution)/shard_map/ppermute | solution.py:323
  28.4 5.8 %collective-permute-start.2 = (f32[320,128]{1,0:T(8,128)S(1)}, f32[320,128]{1,0:T(8,128)S(1)}, u32[]{:S(2)}, u32[]{:S(2)}) collective-permute-start(f32[320,128]{1,0:T(8,128)S(1)} %collective-permute-done.refs_2_), channel_id=1, source_target_pairs={{0,4},{1,5},{2,6},{3,7},{4,0},{5,1},{6,2},{7,3},{8,12},{9,13},{10,... | collective-permute-start | bytes 491528 | tf_op jit(solution)/shard_map/ppermute | solution.py:323
  28.8 6.2 %collective-permute-start.10 = (f32[512,128]{1,0:T(8,128)S(1)}, f32[512,128]{1,0:T(8,128)S(1)}, u32[]{:S(2)}, u32[]{:S(2)}) collective-permute-start(f32[512,128]{1,0:T(8,128)S(1)} %bitcast.21), channel_id=1, source_target_pairs={{0,1},{1,0},{2,3},{3,2},{4,5},{5,4},{6,7},{7,6},{8,9},{9,8},{10,11... | collective-permute-start | bytes 786440 | tf_op jit(solution)/shard_map/ppermute | solution.py:323
  29.1 6.0 %collective-permute-start.11 = (f32[512,128]{1,0:T(8,128)S(1)}, f32[512,128]{1,0:T(8,128)S(1)}, u32[]{:S(2)}, u32[]{:S(2)}) collective-permute-start(f32[512,128]{1,0:T(8,128)S(1)} %collective-permute-done.1.refs_10_), channel_id=1, source_target_pairs={{0,1},{1,0},{2,3},{3,2},{4,5},{5,4},{6,7},{7,6},{8,9},{9,8},{10,11... | collective-permute-start | bytes 786440 | tf_op jit(solution)/shard_map/ppermute | solution.py:323
  29.3 5.7 %collective-permute-start.9 = (f32[320,128]{1,0:T(8,128)S(1)}, f32[320,128]{1,0:T(8,128)}, u32[]{:S(2)}, u32[]{:S(2)}) collective-permute-start(f32[320,128]{1,0:T(8,128)S(1)} %collective-permute-done.4.refs_6_), channel_id=1, source_target_pairs={{0,1},{1,0},{2,3},{3,2},{4,5},{5,4},{6,7},{7,6},{8,9},{9,8},{10,11... | collective-permute-start | bytes 491528 | tf_op jit(solution)/shard_map/ppermute | solution.py:323
  34.2 3.9 %collective-permute-start.12 = (f32[320,128]{1,0:T(8,128)S(1)}, f32[320,128]{1,0:T(8,128)S(1)}, u32[]{:S(2)}, u32[]{:S(2)}) collective-permute-start(f32[320,128]{1,0:T(8,128)S(1)} %collective-permute-done.2.refs_5_), channel_id=1, source_target_pairs={{0,1},{1,0},{2,3},{3,2},{4,5},{5,4},{6,7},{7,6},{8,9},{9,8},{10,11... | collective-permute-start | bytes 491528 | tf_op jit(solution)/shard_map/ppermute | solution.py:323
  35.0 0.7 %copy-start.1 = (s32[2,6]{1,0:T(2,128)S(1)}, s32[2,6]{1,0:T(2,128)}, u32[]{:S(2)}) copy-start(s32[2,6]{1,0:T(2,128)} %structure.5) | copy-start | bytes 148
  35.0 0.7 %copy-start.2 = (s32[2]{0:T(128)S(1)}, s32[2]{0:T(128)}, u32[]{:S(2)}) copy-start(s32[2]{0:T(128)} %live.5) | copy-start | bytes 28
  40.1 4.4 %collective-permute-start.13 = (f32[128,128]{1,0:T(8,128)S(1)}, f32[128,128]{1,0:T(8,128)S(1)}, u32[]{:S(2)}, u32[]{:S(2)}) collective-permute-start(f32[128,128]{1,0:T(8,128)S(1)} %get-tuple-element.53), channel_id=1, source_target_pairs={{0,4},{1,5},{2,6},{3,7},{4,0},{5,1},{6,2},{7,3},{8,12},{9,13},{10,... | collective-permute-start | bytes 196616 | tf_op jit(solution)/shard_map/ppermute | solution.py:323
  40.7 6.9 %collective-permute-start.15 = (f32[128,128]{1,0:T(8,128)S(1)}, f32[128,128]{1,0:T(8,128)S(1)}, u32[]{:S(2)}, u32[]{:S(2)}) collective-permute-start(f32[128,128]{1,0:T(8,128)S(1)} %get-tuple-element.57), channel_id=1, source_target_pairs={{0,8},{1,9},{2,10},{3,11},{4,12},{5,13},{6,14},{7,15},{8,0},{9,1},... | collective-permute-start | bytes 196616 | tf_op jit(solution)/shard_map/ppermute | solution.py:323
  44.5 5.0 %collective-permute-start.16 = (f32[128,128]{1,0:T(8,128)S(1)}, f32[128,128]{1,0:T(8,128)S(1)}, u32[]{:S(2)}, u32[]{:S(2)}) collective-permute-start(f32[128,128]{1,0:T(8,128)S(1)} %get-tuple-element.58), channel_id=1, source_target_pairs={{0,12},{1,13},{2,14},{3,15},{4,8},{5,9},{6,10},{7,11},{8,4},{9,5},... | collective-permute-start | bytes 196616 | tf_op jit(solution)/shard_map/ppermute | solution.py:323
  44.5 11.5 %collective-permute-start.14 = (f32[128,256]{1,0:T(8,128)S(1)}, f32[128,256]{1,0:T(8,128)S(1)}, u32[]{:S(2)}, u32[]{:S(2)}) collective-permute-start(f32[128,256]{1,0:T(8,128)S(1)} %get-tuple-element.54), channel_id=1, source_target_pairs={{0,2},{1,3},{2,0},{3,1},{4,6},{5,7},{6,4},{7,5},{8,10},{9,11},{10,... | collective-permute-start | bytes 393224 | tf_op jit(solution)/shard_map/ppermute | solution.py:323
  50.8 6.5 %collective-permute-start.17 = (f32[64,256]{1,0:T(8,128)S(1)}, f32[64,256]{1,0:T(8,128)S(1)}, u32[]{:S(2)}, u32[]{:S(2)}) collective-permute-start(f32[64,256]{1,0:T(8,128)S(1)} %get-tuple-element.73), channel_id=1, source_target_pairs={{0,1},{1,3},{2,0},{3,2},{4,5},{5,7},{6,4},{7,6},{8,9},{9,11},{10,8... | collective-permute-start | bytes 196616 | tf_op jit(solution)/shard_map/ppermute | solution.py:323
  51.2 6.7 %collective-permute-start.18 = (f32[64,256]{1,0:T(8,128)S(1)}, f32[64,256]{1,0:T(8,128)S(1)}, u32[]{:S(2)}, u32[]{:S(2)}) collective-permute-start(f32[64,256]{1,0:T(8,128)S(1)} %get-tuple-element.72.keep), channel_id=1, source_target_pairs={{1,2},{2,1},{5,6},{6,5},{9,10},{10,9},{13,14},{14,13},{17,18},{18,... | collective-permute-start | bytes 196616 | tf_op jit(solution)/shard_map/ppermute | solution.py:323

commit v8 on v6

--- a/solution.py
+++ b/solution.py
@@ -13,6 +13,7 @@
 NN = (((1,), (0,)), ((), ()))
 TN = (((0,), (0,)), ((), ()))
 VMEM_LIMIT = 20 * 1024 * 1024
+THERE = ((2, 0), (0, 0), (0, 1), (1, 0), (1, 1), (2, 1))
 
 
 def halves(value):
@@ -64,8 +65,9 @@
 
 def early_kernel(share, tile, slots, structure, live, place, c_own, *refs):
     mine = refs[:7]
-    theirs = refs[7]
-    grown, last_high, last_low, f_high, f_low, d_high, d_low, pick = refs[8:]
+    theirs = refs[7:10]
+    near_theirs, c_sib = refs[10:12]
+    grown, last_high, last_low, f_high, f_low, d_high, d_low, pick = refs[12:]
     z, x, c = place[0], place[1], place[2]
     size = mine[0].shape[0]
     whole = d_high.shape[0]
@@ -86,7 +88,11 @@
     for index, source in enumerate(sources):
         f_at = pl.ds(pl.multiple_of(source * share, share), share)
         d_at = pl.ds(pl.multiple_of(source * width, width), width)
-        for first, ref, start in ((0, mine[index], 0), (half, theirs, index * size)):
+        there = (near_theirs, 0)
+        if index < 6:
+            message, start = THERE[index]
+            there = (theirs[message], start * size)
+        for first, (ref, start) in ((0, (mine[index], 0)), (half, there)):
             for b in range(lane_blocks):
                 lanes = slice(first + b * 128, first + (b + 1) * 128)
                 top = start + b * block
@@ -102,12 +108,11 @@
     blocks = c_own.shape[0] // tile
     for slot in range(slots):
         anc = structure[x, slot]
-        for which, (here, start, offset) in enumerate(
-            ((c_own, 0, 7 * size + c_own.shape[0]), (mine[6], size, 7 * size))
+        for which, (here, there, start) in enumerate(
+            ((c_own, c_sib, 0), (mine[6], near_theirs, size))
         ):
-            here_at = pl.ds(start + anc // 2, tile, stride=blocks)
-            there_at = pl.ds(offset + anc // 2, tile, stride=blocks)
-            value = jnp.where(anc % 2 == c, here[here_at, :], theirs[there_at, :])
+            rows = pl.ds(start + anc // 2, tile, stride=blocks)
+            value = jnp.where(anc % 2 == c, here[rows, :], there[rows, :])
             at = pl.ds(pl.multiple_of((x ^ which) * tile, tile), tile)
             pick[at, slot * tile:(slot + 1) * tile] = jnp.where(slot < live[x], value, 0.0)
     picked = pick[...]
@@ -358,8 +363,16 @@
     near = move(send_near, 0, 1, 0)
     own_opposite = move(own_far, 1, 0, 0)
     near_opposite = move(near_far, 1, 0, 0)
-    mine = [own, own_far, near_far, own_side, near_side, own_opposite, near]
-    theirs = move(jnp.concatenate([*mine, c_own]), 0, 0, 1)
+    mine = [own, own_far, near_far, own_side, near_side, own_opposite]
+    theirs = [
+        move(jnp.concatenate([own_far, near_far]), 0, 0, 1),
+        move(jnp.concatenate([own_side, near_side]), 0, 0, 1),
+        move(jnp.concatenate([own, own_opposite]), 0, 0, 1),
+        move(near, 0, 0, 1),
+        move(c_own, 0, 0, 1),
+    ]
+    near_opposite, c_first = lax.optimization_barrier((near_opposite, c_own))
+    opposite_theirs = move(near_opposite, 0, 0, 1)
     split_f = [like(slots * tile, whole, dtype=BF16)] * 2
     split_d = [like(whole, whole, dtype=BF16)] * 2
     grown, last_high, last_low, f_high, f_low, d_high, d_low = call(
@@ -367,11 +380,9 @@
         "early",
         [like(2 * tile, whole)] + [like(2 * tile, 128, dtype=BF16)] * 2 + split_f + split_d,
         [structure, live_counts, place],
-        [c_own, *mine, theirs],
+        [c_first, *mine, near, *theirs],
         [pltpu.VMEM((2 * tile, slots * tile), F32)],
     )
-    near_opposite, grown = lax.optimization_barrier((near_opposite, grown))
-    opposite_theirs = move(near_opposite, 0, 0, 1)
     outs = call(
         functools.partial(product_kernel, share, tile, slots),
         "products",

time: 56.8 us -> 56.7 us (level)
  local copies, waits for them, and re-layouts: 5.59 us -> 0.01 us
  starting transfers between devices: 23.2 us -> 28.2 us
  other arithmetic: 0.08 us -> 2.32 us
  waiting for transfers between devices: 15.6 us -> 13.4 us
    ppermute x15 -> x19, starting transfers between devices: 23.2 us -> 28.2 us  [send_to(): return lax.ppermute(value, ('row', 'col'), pairs)]
    unnamed x13 -> x6, local copies, waits for them, and re-layouts: 4.86 us -> 0.01 us
    concatenate x0 -> x3, other arithmetic: none -> 2.24 us  [the longest x1 0.75 us: local(): jnp.concatenate([own_far, near_far])]
    ppermute x15 -> x19, waiting for transfers between devices: 15.6 us -> 13.4 us  [send_to(): return lax.ppermute(value, ('row', 'col'), pairs)]
    concatenate x1 -> x0, local copies, waits for them, and re-layouts: 0.73 us -> none  [local(): theirs = move(jnp.concatenate([*mine, c_own]), 0, 0, 1)]
  transfers between devices with their start and end apart: 15 -> 19, of which waited for: 9 -> 6; matrix products, arithmetic and copies ran while one was open for 7% -> 4% of each run, Pallas kernels for 12% -> 12%
where the time goes in v8:
time: 56.7 us; the launch traced here: 56.5 us
  starting transfers between devices  28.2 us (50%)
  waiting for transfers between devices  13.4 us (24%)
  Pallas kernels  11.8 us (21%)
  other arithmetic  2.32 us (4%)
  between operations  0.74 us (1%)
    ppermute x19, starting transfers between devices, send_to(): return lax.ppermute(value, ('row', 'col'), pairs)  28.2 us
    ppermute x19, waiting for transfers between devices, send_to(): return lax.ppermute(value, ('row', 'col'), pairs)  13.4 us
    pallas_call x7, Pallas kernels, call(): pl.pallas_call(kernel, out_shape=outs, in_specs=[smem] * len(scalars) + [...  11.8 us
  transfers between devices with their start and end apart: 19, of which 6 were waited for; matrix products, arithmetic and copies ran while one was open for 4% of the time, Pallas kernels for 12%

profile of v8, /device:TPU:1, one launch (start us, length us, event | category | flops | bytes accessed | tf_op | source)
XLA Modules:
  0.0 56.5 jit_solution(11416299177742425095)
XLA Ops:
  0.6 1.2 %pack.1 = (f32[320,128]{1,0:T(8,128)S(1)}, f32[320,128]{1,0:T(8,128)S(1)}, f32[832,128]{1,0:T(8,128)S(1)}) custom-call(f32[384,128]{1,0:T(8,128)} %bitcast.25, f32[2,64,512]{2,1,0:T(8,128)} %bitcast.24, f32[512,128]{1,0:T(8,128)} %bitcast.20), custom_call_target="tpu_custom_call" | custom-call | tf_op jit(solution)/shard_map/pack/pallas_call | solution.py:316
  1.8 2.1 %collective-permute-start.6 = (f32[832,128]{1,0:T(8,128)S(1)}, f32[832,128]{1,0:T(8,128)S(1)}, u32[]{:S(2)}, u32[]{:S(2)}) collective-permute-start(f32[832,128]{1,0:T(8,128)S(1)} %get-tuple-element.38), channel_id=1, source_target_pairs={{0,2},{1,3},{2,0},{3,1},{4,6},{5,7},{6,4},{7,5},{8,10},{9,11},{10,... | collective-permute-start | bytes 1277960 | tf_op jit(solution)/shard_map/ppermute | solution.py:333
  3.9 2.3 %collective-permute-start.2 = (f32[320,128]{1,0:T(8,128)S(1)}, f32[320,128]{1,0:T(8,128)S(1)}, u32[]{:S(2)}, u32[]{:S(2)}) collective-permute-start(f32[320,128]{1,0:T(8,128)S(1)} %get-tuple-element.37.refs_0_), channel_id=1, source_target_pairs={{0,8},{1,9},{2,10},{3,11},{4,12},{5,13},{6,14},{7,15},{8,0},{9,1},... | collective-permute-start | bytes 491528 | tf_op jit(solution)/shard_map/ppermute | solution.py:333
  6.2 1.3 %collective-permute-start.3 = (f32[320,128]{1,0:T(8,128)S(1)}, f32[320,128]{1,0:T(8,128)S(1)}, u32[]{:S(2)}, u32[]{:S(2)}) collective-permute-start(f32[320,128]{1,0:T(8,128)S(1)} %get-tuple-element.37.refs_0_), channel_id=1, source_target_pairs={{0,4},{1,5},{2,6},{3,7},{4,0},{5,1},{6,2},{7,3},{8,12},{9,13},{10,... | collective-permute-start | bytes 491528 | tf_op jit(solution)/shard_map/ppermute | solution.py:333
  7.6 1.1 %collective-permute-start.4 = (f32[320,128]{1,0:T(8,128)S(1)}, f32[320,128]{1,0:T(8,128)S(1)}, u32[]{:S(2)}, u32[]{:S(2)}) collective-permute-start(f32[320,128]{1,0:T(8,128)S(1)} %get-tuple-element.35), channel_id=1, source_target_pairs={{0,6},{1,7},{2,4},{3,5},{4,2},{5,3},{6,0},{7,1},{8,14},{9,15},{10,... | collective-permute-start | bytes 491528 | tf_op jit(solution)/shard_map/ppermute | solution.py:333
  8.7 8.2 %collective-permute-done.2.refs_1_ = f32[320,128]{1,0:T(8,128)S(1)} collective-permute-done((f32[320,128]{1,0:T(8,128)S(1)}, f32[320,128]{1,0:T(8,128)S(1)}, u32[]{:S(2)}, u32[]{:S(2)}) %collective-permute-start.2) | collective-permute-done | bytes 163872 | tf_op jit(solution)/shard_map/ppermute | solution.py:333
  16.9 2.8 %collective-permute-start.11 = (f32[512,128]{1,0:T(8,128)S(1)}, f32[512,128]{1,0:T(8,128)S(1)}, u32[]{:S(2)}, u32[]{:S(2)}) collective-permute-start(f32[512,128]{1,0:T(8,128)S(1)} %bitcast.21), channel_id=1, source_target_pairs={{0,1},{1,0},{2,3},{3,2},{4,5},{5,4},{6,7},{7,6},{8,9},{9,8},{10,11... | collective-permute-start | bytes 786440 | tf_op jit(solution)/shard_map/ppermute | solution.py:333
  20.4 1.5 %collective-permute-start.5 = (f32[320,128]{1,0:T(8,128)S(1)}, f32[320,128]{1,0:T(8,128)S(1)}, u32[]{:S(2)}, u32[]{:S(2)}) collective-permute-start(f32[320,128]{1,0:T(8,128)S(1)} %collective-permute-done.2.refs_1_), channel_id=1, source_target_pairs={{0,4},{1,5},{2,6},{3,7},{4,0},{5,1},{6,2},{7,3},{8,12},{9,13},{10,... | collective-permute-start | bytes 491528 | tf_op jit(solution)/shard_map/ppermute | solution.py:333
  23.5 1.0 %collective-permute-start.1 = (f32[320,128]{1,0:T(8,128)S(1)}, f32[320,128]{1,0:T(8,128)S(1)}, u32[]{:S(2)}, u32[]{:S(2)}) collective-permute-start(f32[320,128]{1,0:T(8,128)S(1)} %collective-permute-done.refs_2_), channel_id=1, source_target_pairs={{0,4},{1,5},{2,6},{3,7},{4,0},{5,1},{6,2},{7,3},{8,12},{9,13},{10,... | collective-permute-start | bytes 491528 | tf_op jit(solution)/shard_map/ppermute | solution.py:333
  25.2 2.8 %collective-permute-start.8 = (f32[640,128]{1,0:T(8,128)}, f32[640,128]{1,0:T(8,128)S(1)}, u32[]{:S(2)}, u32[]{:S(2)}) collective-permute-start(f32[640,128]{1,0:T(8,128)} %pad_maximum_fusion.1), channel_id=1, source_target_pairs={{0,1},{1,0},{2,3},{3,2},{4,5},{5,4},{6,7},{7,6},{8,9},{9,8},{10,11... | collective-permute-start | bytes 983048 | tf_op jit(solution)/shard_map/ppermute | solution.py:333
  29.7 1.1 %collective-permute-start.9 = (f32[640,128]{1,0:T(8,128)}, f32[640,128]{1,0:T(8,128)S(1)}, u32[]{:S(2)}, u32[]{:S(2)}) collective-permute-start(f32[640,128]{1,0:T(8,128)} %pad_maximum_fusion.2), channel_id=1, source_target_pairs={{0,1},{1,0},{2,3},{3,2},{4,5},{5,4},{6,7},{7,6},{8,9},{9,8},{10,11... | collective-permute-start | bytes 983048 | tf_op jit(solution)/shard_map/ppermute | solution.py:333
  30.9 1.6 %collective-permute-done.9.refs_9_ = f32[640,128]{1,0:T(8,128)S(1)} collective-permute-done((f32[640,128]{1,0:T(8,128)}, f32[640,128]{1,0:T(8,128)S(1)}, u32[]{:S(2)}, u32[]{:S(2)}) %collective-permute-start.9) | collective-permute-done | bytes 327712 | tf_op jit(solution)/shard_map/ppermute | solution.py:333
  32.5 2.0 %early.1 = (f32[256,512]{1,0:T(8,128)S(1)}, bf16[256,128]{1,0:T(8,128)(2,1)S(1)}, bf16[256,128]{1,0:T(8,128)(2,1)S(1)}, bf16[768,512]{1,0:T(8,128)(2,1)S(1)}, bf...) custom-call(s32[2,6]{1,0:T(2,128)S(1)} %copy-done.1, s32[2]{0:T(128)S(1)} %copy-done.2, ...), custom_call_target="tpu_custom_call" | custom-call | tf_op jit(solution)/shard_map/early/pallas_call | solution.py:316
  34.6 2.4 %products.1 = (f32[128,256]{1,0:T(8,128)S(1)}, f32[128,256]{1,0:T(8,128)S(1)}, f32[128,128]{1,0:T(8,128)S(1)}, f32[128,128]{1,0:T(8,128)S(1)}, f32[128,128]{1,0:...) custom-call(s32[2,6]{1,0:T(2,128)S(1)} %copy-done.1, ...), custom_call_target="tpu_custom_call" | custom-call | tf_op jit(solution)/shard_map/products/pallas_call | solution.py:316
  37.0 1.3 %collective-permute-start.13 = (f32[128,128]{1,0:T(8,128)S(1)}, f32[128,128]{1,0:T(8,128)S(1)}, u32[]{:S(2)}, u32[]{:S(2)}) collective-permute-start(f32[128,128]{1,0:T(8,128)S(1)} %get-tuple-element.47), channel_id=1, source_target_pairs={{0,4},{1,5},{2,6},{3,7},{4,0},{5,1},{6,2},{7,3},{8,12},{9,13},{10,... | collective-permute-start | bytes 196616 | tf_op jit(solution)/shard_map/ppermute | solution.py:333
  38.3 3.1 %collective-permute-start.15 = (f32[128,128]{1,0:T(8,128)S(1)}, f32[128,128]{1,0:T(8,128)S(1)}, u32[]{:S(2)}, u32[]{:S(2)}) collective-permute-start(f32[128,128]{1,0:T(8,128)S(1)} %get-tuple-element.51), channel_id=1, source_target_pairs={{0,8},{1,9},{2,10},{3,11},{4,12},{5,13},{6,14},{7,15},{8,0},{9,1},... | collective-permute-start | bytes 196616 | tf_op jit(solution)/shard_map/ppermute | solution.py:333
  41.4 1.2 %collective-permute-start.14 = (f32[128,256]{1,0:T(8,128)S(1)}, f32[128,256]{1,0:T(8,128)S(1)}, u32[]{:S(2)}, u32[]{:S(2)}) collective-permute-start(f32[128,256]{1,0:T(8,128)S(1)} %get-tuple-element.48), channel_id=1, source_target_pairs={{0,2},{1,3},{2,0},{3,1},{4,6},{5,7},{6,4},{7,5},{8,10},{9,11},{10,... | collective-permute-start | bytes 393224 | tf_op jit(solution)/shard_map/ppermute | solution.py:333
  42.6 2.4 %scaled.1 = (bf16[768,512]{1,0:T(8,128)(2,1)S(1)}, bf16[768,512]{1,0:T(8,128)(2,1)S(1)}, f32[64,512]{1,0:T(8,128)S(1)}) custom-call(s32[3]{0:T(128)S(1)} %pad_add_fusion.place, bf16[768,512]{1,0:T(8,128)(2,1)S(1)} %get-tuple-element.53.refs_0_, bf16[768,512]{1,0:T(8,128)(2,1)S(1)} %get-tuple-element.54.refs_1_, ...), custom_call_target="tpu_custom_call" | custom-call | tf_op jit(solution)/shard_map/scaled/pallas_call | solution.py:316
  45.1 1.4 %collective-permute-done.16.w3 = f32[128,128]{1,0:T(8,128)S(1)} collective-permute-done((f32[128,128]{1,0:T(8,128)S(1)}, f32[128,128]{1,0:T(8,128)S(1)}, u32[]{:S(2)}, u32[]{:S(2)}) %collective-permute-start.16) | collective-permute-done | bytes 65568 | tf_op jit(solution)/shard_map/ppermute | solution.py:333
  46.4 1.3 %diag_block.1 = (f32[64,256]{1,0:T(8,128)S(1)}, f32[64,256]{1,0:T(8,128)S(1)}) custom-call(s32[2,6]{1,0:T(2,128)S(1)} %copy-done.1, s32[2]{0:T(128)S(1)} %copy-done.2, s32[3]{0:T(128)S(1)} %pad_add_fusion.place, f32[128,128]{1,0:T(8,128)S(1)} %get-tuple-element.49.w0, f32[128,128]{1,0:T(8,128)S(1)} %collective-permute-done.13.w1, ...), custom_call_target="tpu_custom_call" | custom-call | tf_op jit(solution)/shard_map/diag_block/pallas_call | solution.py:316
  47.7 1.2 %collective-permute-start.17 = (f32[64,256]{1,0:T(8,128)S(1)}, f32[64,256]{1,0:T(8,128)S(1)}, u32[]{:S(2)}, u32[]{:S(2)}) collective-permute-start(f32[64,256]{1,0:T(8,128)S(1)} %get-tuple-element.67), channel_id=1, source_target_pairs={{0,1},{1,3},{2,0},{3,2},{4,5},{5,7},{6,4},{7,6},{8,9},{9,11},{10,8... | collective-permute-start | bytes 196616 | tf_op jit(solution)/shard_map/ppermute | solution.py:333
  48.9 4.4 %collective-permute-start.18 = (f32[64,256]{1,0:T(8,128)S(1)}, f32[64,256]{1,0:T(8,128)S(1)}, u32[]{:S(2)}, u32[]{:S(2)}) collective-permute-start(f32[64,256]{1,0:T(8,128)S(1)} %get-tuple-element.66.keep), channel_id=1, source_target_pairs={{1,2},{2,1},{5,6},{6,5},{9,10},{10,9},{13,14},{14,13},{17,18},{18,... | collective-permute-start | bytes 196616 | tf_op jit(solution)/shard_map/ppermute | solution.py:333
  53.4 1.3 %panel_lines.1 = f32[512,128]{1,0:T(8,128)} custom-call(s32[3]{0:T(128)S(1)} %pad_add_fusion.place, f32[128,256]{1,0:T(8,128)S(1)} %get-tuple-element.45.mine, f32[128,256]{1,0:T(8,128)S(1)} %collective-permute-done.14.other), custom_call_target="tpu_custom_call" | custom-call | tf_op jit(solution)/shard_map/panel_lines/pallas_call | solution.py:316
  55.3 1.2 %diag_lines.1 = f32[256,128]{1,0:T(8,128)} custom-call(s32[3]{0:T(128)S(1)} %pad_add_fusion.place, f32[64,256]{1,0:T(8,128)S(1)} %get-tuple-element.66.keep, f32[64,256]{1,0:T(8,128)S(1)} %collective-permute-done.17.met, f32[64,256]{1,0:T(8,128)S(1)} %collective-permute-done.18.far), custom_call_target="tpu_custom_call" | custom-call | tf_op jit(solution)/shard_map/diag_lines/pallas_call | solution.py:316
  (31 shorter events, 5.3 us)
Async XLA Ops:
  0.6 16.3 %copy-start = (f32[128,4,1,128]{3,2,1,0:T(1,128)S(1)}, f32[128,4,1,128]{3,2,1,0:T(1,128)}, u32[]{:S(2)}) copy-start(f32[128,4,1,128]{3,2,1,0:T(1,128)} %param.5) | copy-start | bytes 786436
  1.8 26.2 %collective-permute-start.6 = (f32[832,128]{1,0:T(8,128)S(1)}, f32[832,128]{1,0:T(8,128)S(1)}, u32[]{:S(2)}, u32[]{:S(2)}) collective-permute-start(f32[832,128]{1,0:T(8,128)S(1)} %get-tuple-element.38), channel_id=1, source_target_pairs={{0,2},{1,3},{2,0},{3,1},{4,6},{5,7},{6,4},{7,5},{8,10},{9,11},{10,... | collective-permute-start | bytes 1277960 | tf_op jit(solution)/shard_map/ppermute | solution.py:333
  3.9 13.0 %collective-permute-start.2 = (f32[320,128]{1,0:T(8,128)S(1)}, f32[320,128]{1,0:T(8,128)S(1)}, u32[]{:S(2)}, u32[]{:S(2)}) collective-permute-start(f32[320,128]{1,0:T(8,128)S(1)} %get-tuple-element.37.refs_0_), channel_id=1, source_target_pairs={{0,8},{1,9},{2,10},{3,11},{4,12},{5,13},{6,14},{7,15},{8,0},{9,1},... | collective-permute-start | bytes 491528 | tf_op jit(solution)/shard_map/ppermute | solution.py:333
  6.2 14.2 %collective-permute-start = (f32[320,128]{1,0:T(8,128)S(1)}, f32[320,128]{1,0:T(8,128)S(1)}, u32[]{:S(2)}, u32[]{:S(2)}) collective-permute-start(f32[320,128]{1,0:T(8,128)S(1)} %get-tuple-element.35), channel_id=1, source_target_pairs={{0,10},{1,11},{2,8},{3,9},{4,14},{5,15},{6,12},{7,13},{8,2},{9,3},... | collective-permute-start | bytes 491528 | tf_op jit(solution)/shard_map/ppermute | solution.py:333
  6.2 16.4 %collective-permute-start.3 = (f32[320,128]{1,0:T(8,128)S(1)}, f32[320,128]{1,0:T(8,128)S(1)}, u32[]{:S(2)}, u32[]{:S(2)}) collective-permute-start(f32[320,128]{1,0:T(8,128)S(1)} %get-tuple-element.37.refs_0_), channel_id=1, source_target_pairs={{0,4},{1,5},{2,6},{3,7},{4,0},{5,1},{6,2},{7,3},{8,12},{9,13},{10,... | collective-permute-start | bytes 491528 | tf_op jit(solution)/shard_map/ppermute | solution.py:333
  7.6 15.9 %collective-permute-start.4 = (f32[320,128]{1,0:T(8,128)S(1)}, f32[320,128]{1,0:T(8,128)S(1)}, u32[]{:S(2)}, u32[]{:S(2)}) collective-permute-start(f32[320,128]{1,0:T(8,128)S(1)} %get-tuple-element.35), channel_id=1, source_target_pairs={{0,6},{1,7},{2,4},{3,5},{4,2},{5,3},{6,0},{7,1},{8,14},{9,15},{10,... | collective-permute-start | bytes 491528 | tf_op jit(solution)/shard_map/ppermute | solution.py:333
  16.9 13.9 %collective-permute-start.11 = (f32[512,128]{1,0:T(8,128)S(1)}, f32[512,128]{1,0:T(8,128)S(1)}, u32[]{:S(2)}, u32[]{:S(2)}) collective-permute-start(f32[512,128]{1,0:T(8,128)S(1)} %bitcast.21), channel_id=1, source_target_pairs={{0,1},{1,0},{2,3},{3,2},{4,5},{5,4},{6,7},{7,6},{8,9},{9,8},{10,11... | collective-permute-start | bytes 786440 | tf_op jit(solution)/shard_map/ppermute | solution.py:333
  20.4 4.8 %collective-permute-start.5 = (f32[320,128]{1,0:T(8,128)S(1)}, f32[320,128]{1,0:T(8,128)S(1)}, u32[]{:S(2)}, u32[]{:S(2)}) collective-permute-start(f32[320,128]{1,0:T(8,128)S(1)} %collective-permute-done.2.refs_1_), channel_id=1, source_target_pairs={{0,4},{1,5},{2,6},{3,7},{4,0},{5,1},{6,2},{7,3},{8,12},{9,13},{10,... | collective-permute-start | bytes 491528 | tf_op jit(solution)/shard_map/ppermute | solution.py:333
  22.7 8.2 %collective-permute-start.7 = (f32[640,128]{1,0:T(8,128)}, f32[640,128]{1,0:T(8,128)S(1)}, u32[]{:S(2)}, u32[]{:S(2)}) collective-permute-start(f32[640,128]{1,0:T(8,128)} %pad_maximum_fusion), channel_id=1, source_target_pairs={{0,1},{1,0},{2,3},{3,2},{4,5},{5,4},{6,7},{7,6},{8,9},{9,8},{10,11... | collective-permute-start | bytes 983048 | tf_op jit(solution)/shard_map/ppermute | solution.py:333
  23.5 6.2 %collective-permute-start.1 = (f32[320,128]{1,0:T(8,128)S(1)}, f32[320,128]{1,0:T(8,128)S(1)}, u32[]{:S(2)}, u32[]{:S(2)}) collective-permute-start(f32[320,128]{1,0:T(8,128)S(1)} %collective-permute-done.refs_2_), channel_id=1, source_target_pairs={{0,4},{1,5},{2,6},{3,7},{4,0},{5,1},{6,2},{7,3},{8,12},{9,13},{10,... | collective-permute-start | bytes 491528 | tf_op jit(solution)/shard_map/ppermute | solution.py:333
  25.2 5.7 %collective-permute-start.8 = (f32[640,128]{1,0:T(8,128)}, f32[640,128]{1,0:T(8,128)S(1)}, u32[]{:S(2)}, u32[]{:S(2)}) collective-permute-start(f32[640,128]{1,0:T(8,128)} %pad_maximum_fusion.1), channel_id=1, source_target_pairs={{0,1},{1,0},{2,3},{3,2},{4,5},{5,4},{6,7},{7,6},{8,9},{9,8},{10,11... | collective-permute-start | bytes 983048 | tf_op jit(solution)/shard_map/ppermute | solution.py:333
  28.1 4.5 %collective-permute-start.10 = (f32[832,128]{1,0:T(8,128)S(1)}, f32[832,128]{1,0:T(8,128)S(1)}, u32[]{:S(2)}, u32[]{:S(2)}) collective-permute-start(f32[832,128]{1,0:T(8,128)S(1)} %collective-permute-done.6.refs_6_), channel_id=1, source_target_pairs={{0,1},{1,0},{2,3},{3,2},{4,5},{5,4},{6,7},{7,6},{8,9},{9,8},{10,11... | collective-permute-start | bytes 1277960 | tf_op jit(solution)/shard_map/ppermute | solution.py:333
  29.7 2.8 %collective-permute-start.9 = (f32[640,128]{1,0:T(8,128)}, f32[640,128]{1,0:T(8,128)S(1)}, u32[]{:S(2)}, u32[]{:S(2)}) collective-permute-start(f32[640,128]{1,0:T(8,128)} %pad_maximum_fusion.2), channel_id=1, source_target_pairs={{0,1},{1,0},{2,3},{3,2},{4,5},{5,4},{6,7},{7,6},{8,9},{9,8},{10,11... | collective-permute-start | bytes 983048 | tf_op jit(solution)/shard_map/ppermute | solution.py:333
  30.8 3.7 %collective-permute-start.12 = (f32[320,128]{1,0:T(8,128)S(1)}, f32[320,128]{1,0:T(8,128)}, u32[]{:S(2)}, u32[]{:S(2)}) collective-permute-start(f32[320,128]{1,0:T(8,128)S(1)} %collective-permute-done.1.refs_5_), channel_id=1, source_target_pairs={{0,1},{1,0},{2,3},{3,2},{4,5},{5,4},{6,7},{7,6},{8,9},{9,8},{10,11... | collective-permute-start | bytes 491528 | tf_op jit(solution)/shard_map/ppermute | solution.py:333
  30.8 1.7 %copy-start.1 = (s32[2,6]{1,0:T(2,128)S(1)}, s32[2,6]{1,0:T(2,128)}, u32[]{:S(2)}) copy-start(s32[2,6]{1,0:T(2,128)} %structure.5) | copy-start | bytes 148
  30.8 1.7 %copy-start.2 = (s32[2]{0:T(128)S(1)}, s32[2]{0:T(128)}, u32[]{:S(2)}) copy-start(s32[2]{0:T(128)} %live.5) | copy-start | bytes 28
  37.0 4.4 %collective-permute-start.13 = (f32[128,128]{1,0:T(8,128)S(1)}, f32[128,128]{1,0:T(8,128)S(1)}, u32[]{:S(2)}, u32[]{:S(2)}) collective-permute-start(f32[128,128]{1,0:T(8,128)S(1)} %get-tuple-element.47), channel_id=1, source_target_pairs={{0,4},{1,5},{2,6},{3,7},{4,0},{5,1},{6,2},{7,3},{8,12},{9,13},{10,... | collective-permute-start | bytes 196616 | tf_op jit(solution)/shard_map/ppermute | solution.py:333
  38.3 6.7 %collective-permute-start.15 = (f32[128,128]{1,0:T(8,128)S(1)}, f32[128,128]{1,0:T(8,128)S(1)}, u32[]{:S(2)}, u32[]{:S(2)}) collective-permute-start(f32[128,128]{1,0:T(8,128)S(1)} %get-tuple-element.51), channel_id=1, source_target_pairs={{0,8},{1,9},{2,10},{3,11},{4,12},{5,13},{6,14},{7,15},{8,0},{9,1},... | collective-permute-start | bytes 196616 | tf_op jit(solution)/shard_map/ppermute | solution.py:333
  41.4 5.0 %collective-permute-start.16 = (f32[128,128]{1,0:T(8,128)S(1)}, f32[128,128]{1,0:T(8,128)S(1)}, u32[]{:S(2)}, u32[]{:S(2)}) collective-permute-start(f32[128,128]{1,0:T(8,128)S(1)} %get-tuple-element.52), channel_id=1, source_target_pairs={{0,12},{1,13},{2,14},{3,15},{4,8},{5,9},{6,10},{7,11},{8,4},{9,5},... | collective-permute-start | bytes 196616 | tf_op jit(solution)/shard_map/ppermute | solution.py:333
  41.4 12.0 %collective-permute-start.14 = (f32[128,256]{1,0:T(8,128)S(1)}, f32[128,256]{1,0:T(8,128)S(1)}, u32[]{:S(2)}, u32[]{:S(2)}) collective-permute-start(f32[128,256]{1,0:T(8,128)S(1)} %get-tuple-element.48), channel_id=1, source_target_pairs={{0,2},{1,3},{2,0},{3,1},{4,6},{5,7},{6,4},{7,5},{8,10},{9,11},{10,... | collective-permute-start | bytes 393224 | tf_op jit(solution)/shard_map/ppermute | solution.py:333
  47.7 6.9 %collective-permute-start.17 = (f32[64,256]{1,0:T(8,128)S(1)}, f32[64,256]{1,0:T(8,128)S(1)}, u32[]{:S(2)}, u32[]{:S(2)}) collective-permute-start(f32[64,256]{1,0:T(8,128)S(1)} %get-tuple-element.67), channel_id=1, source_target_pairs={{0,1},{1,3},{2,0},{3,2},{4,5},{5,7},{6,4},{7,6},{8,9},{9,11},{10,8... | collective-permute-start | bytes 196616 | tf_op jit(solution)/shard_map/ppermute | solution.py:333
  48.9 6.4 %collective-permute-start.18 = (f32[64,256]{1,0:T(8,128)S(1)}, f32[64,256]{1,0:T(8,128)S(1)}, u32[]{:S(2)}, u32[]{:S(2)}) collective-permute-start(f32[64,256]{1,0:T(8,128)S(1)} %get-tuple-element.66.keep), channel_id=1, source_target_pairs={{1,2},{2,1},{5,6},{6,5},{9,10},{10,9},{13,14},{14,13},{17,18},{18,... | collective-permute-start | bytes 196616 | tf_op jit(solution)/shard_map/ppermute | solution.py:333

commit v9 on v8

--- a/solution.py
+++ b/solution.py
@@ -13,7 +13,7 @@
 NN = (((1,), (0,)), ((), ()))
 TN = (((0,), (0,)), ((), ()))
 VMEM_LIMIT = 20 * 1024 * 1024
-THERE = ((2, 0), (0, 0), (0, 1), (1, 0), (1, 1), (2, 1))
+THERE = ((2, 0), (0, 0), (0, 1), (1, 0), (1, 1), (3, 0), (4, 0))
 
 
 def halves(value):
@@ -63,11 +63,14 @@
     copies[2].wait()
 
 
-def early_kernel(share, tile, slots, structure, live, place, c_own, *refs):
-    mine = refs[:7]
-    theirs = refs[7:10]
-    near_theirs, c_sib = refs[10:12]
-    grown, last_high, last_low, f_high, f_low, d_high, d_low, pick = refs[12:]
+def product_kernel(share, tile, slots, structure, live, place, c_own, *refs):
+    mine = refs[:8]
+    theirs = refs[8:13]
+    near_theirs, c_sib = refs[13:15]
+    panel_out = refs[15:17]
+    w_out = refs[17:21]
+    f_high, f_low, d_high, d_low = refs[21:25]
+    pick, product = refs[25:]
     z, x, c = place[0], place[1], place[2]
     size = mine[0].shape[0]
     whole = d_high.shape[0]
@@ -75,6 +78,7 @@
     lane_blocks = half // 128
     block = size // lane_blocks
     width = block - share
+    wide = 2 * width
     near_x = 1 - x
     sources = (
         2 * z + x,
@@ -83,13 +87,24 @@
         2 * (z ^ 1) + x,
         2 * (z ^ 1) + near_x,
         2 * (z ^ 3) + x,
+        2 * (z ^ 3) + near_x,
         2 * z + near_x,
     )
+    blocks = c_own.shape[0] // tile
+    for slot in range(slots):
+        anc = structure[x, slot]
+        for which, (here, there, start) in enumerate(
+            ((c_own, c_sib, 0), (mine[7], near_theirs, size))
+        ):
+            rows = pl.ds(start + anc // 2, tile, stride=blocks)
+            value = jnp.where(anc % 2 == c, here[rows, :], there[rows, :])
+            at = pl.ds(pl.multiple_of((x ^ which) * tile, tile), tile)
+            pick[at, slot * tile:(slot + 1) * tile] = jnp.where(slot < live[x], value, 0.0)
     for index, source in enumerate(sources):
         f_at = pl.ds(pl.multiple_of(source * share, share), share)
         d_at = pl.ds(pl.multiple_of(source * width, width), width)
         there = (near_theirs, 0)
-        if index < 6:
+        if index < 7:
             message, start = THERE[index]
             there = (theirs[message], start * size)
         for first, (ref, start) in ((0, (mine[index], 0)), (half, there)):
@@ -98,57 +113,8 @@
                 top = start + b * block
                 split(ref[top:top + share, :], f_high, f_low, (f_at, lanes))
                 split(ref[top + share:top + block, :], d_high, d_low, (d_at, lanes))
-    last = (2 * (z ^ 3) + near_x) * share
-    f_at = pl.ds(pl.multiple_of(last, share), share)
-    f_high[f_at, :] = jnp.zeros((share, whole), BF16)
-    f_low[f_at, :] = jnp.zeros((share, whole), BF16)
-    d_at = pl.ds(pl.multiple_of((2 * (z ^ 3) + near_x) * width, width), width)
-    d_high[d_at, :] = jnp.zeros((width, whole), BF16)
-    d_low[d_at, :] = jnp.zeros((width, whole), BF16)
-    blocks = c_own.shape[0] // tile
-    for slot in range(slots):
-        anc = structure[x, slot]
-        for which, (here, there, start) in enumerate(
-            ((c_own, c_sib, 0), (mine[6], near_theirs, size))
-        ):
-            rows = pl.ds(start + anc // 2, tile, stride=blocks)
-            value = jnp.where(anc % 2 == c, here[rows, :], there[rows, :])
-            at = pl.ds(pl.multiple_of((x ^ which) * tile, tile), tile)
-            pick[at, slot * tile:(slot + 1) * tile] = jnp.where(slot < live[x], value, 0.0)
-    picked = pick[...]
-    grown[...] = dot3(halves(picked), (f_high[...], f_low[...]), NN)
-    total = slots * tile
-    turned = pltpu.roll(picked, total - last, 1)
-    last_high[...], last_low[...] = halves(turned[:, :last_high.shape[1]])
-
-
-def product_kernel(share, tile, slots, structure, live, place, *refs):
-    grown, last_high, last_low, d_high, d_low, mine, theirs = refs[:7]
-    panel_out = refs[7:9]
-    w_out = refs[9:13]
-    ff_high, ff_low, fd_high, fd_low = refs[13:17]
-    product = refs[17]
-    z, x, c = place[0], place[1], place[2]
-    wide = fd_high.shape[0]
-    width = wide // 2
-    half = d_high.shape[0] // 2
-    lane_blocks = half // 128
-    block = share + width
-    far = pl.ds(pl.multiple_of((z ^ 3) * wide, wide), wide)
-    fd_high[...] = d_high[far, :]
-    fd_low[...] = d_low[far, :]
-    d_at = pl.ds(pl.multiple_of((1 - x) * width, width), width)
-    for first, ref in ((0, mine), (half, theirs)):
-        for b in range(lane_blocks):
-            lanes = slice(first + b * 128, first + (b + 1) * 128)
-            top = b * block
-            split(ref[top:top + share, :], ff_high, ff_low, (slice(None), lanes))
-            split(ref[top + share:top + block, :], fd_high, fd_low, (d_at, lanes))
-    last = (last_high[:, :share], last_low[:, :share])
-    value = grown[...] + dot3(last, (ff_high[...], ff_low[...]), NN)
-    value = halves(value)
-    product[...] = dot3(value, (d_high[...], d_low[...]), NT)
-    product[:, far] = dot3(value, (fd_high[...], fd_low[...]), NT)
+    grown = dot3(halves(pick[...]), (f_high[...], f_low[...]), NN)
+    product[...] = dot3(halves(grown), (d_high[...], d_low[...]), NT)
     lanes = pl.ds(pl.multiple_of(c * half, half), half)
     for which in range(2):
         at = pl.ds(pl.multiple_of((x ^ which) * tile, tile), tile)
@@ -166,27 +132,14 @@
         w_out[step][...] = jnp.where(low_lane, left, right)
 
 
-def scaled_kernel(share, place, *refs):
-    f_high, f_low, d_high, d_low, ff_high, ff_low, fd_high, fd_low = refs[:8]
-    s_high, s_low, base, all_f_high, all_f_low, all_d_high, all_d_low = refs[8:]
-    z, x, c = place[0], place[1], place[2]
-    wide = fd_high.shape[0]
-    width = wide // 2
-    f_at = pl.ds(pl.multiple_of((2 * (z ^ 3) + 1 - x) * share, share), share)
-    d_at = pl.ds(pl.multiple_of((z ^ 3) * wide, wide), wide)
-    for whole, early, late, at in (
-        (all_f_high, f_high, ff_high, f_at),
-        (all_f_low, f_low, ff_low, f_at),
-        (all_d_high, d_high, fd_high, d_at),
-        (all_d_low, d_low, fd_low, d_at),
-    ):
-        whole[...] = early[...]
-        whole[at, :] = late[...]
-    inverse = (all_d_high[...], all_d_low[...])
-    scaled = dot3((all_f_high[...], all_f_low[...]), inverse, NT)
+def scaled_kernel(place, f_high, f_low, d_high, d_low, s_high, s_low, base):
+    z, c = place[0], place[2]
+    width = base.shape[0]
+    inverse = (d_high[...], d_low[...])
+    scaled = dot3((f_high[...], f_low[...]), inverse, NT)
     s_high[...], s_low[...] = halves(scaled)
     at = pl.ds(pl.multiple_of((2 * z + c) * width, width), width)
-    base[...] = dot3((all_d_high[at, :], all_d_low[at, :]), inverse, NT)
+    base[...] = dot3((d_high[at, :], d_low[at, :]), inverse, NT)
 
 
 def diag_kernel(tile, slots, structure, live, place, w0, w1, w2, w3, s_high, s_low, base, *refs):
@@ -363,46 +316,30 @@
     near = move(send_near, 0, 1, 0)
     own_opposite = move(own_far, 1, 0, 0)
     near_opposite = move(near_far, 1, 0, 0)
-    mine = [own, own_far, near_far, own_side, near_side, own_opposite]
+    mine = [own, own_far, near_far, own_side, near_side, own_opposite, near_opposite, near]
     theirs = [
         move(jnp.concatenate([own_far, near_far]), 0, 0, 1),
         move(jnp.concatenate([own_side, near_side]), 0, 0, 1),
-        move(jnp.concatenate([own, own_opposite]), 0, 0, 1),
+        move(own, 0, 0, 1),
+        move(own_opposite, 0, 0, 1),
+        move(near_opposite, 0, 0, 1),
         move(near, 0, 0, 1),
         move(c_own, 0, 0, 1),
     ]
-    near_opposite, c_first = lax.optimization_barrier((near_opposite, c_own))
-    opposite_theirs = move(near_opposite, 0, 0, 1)
     split_f = [like(slots * tile, whole, dtype=BF16)] * 2
     split_d = [like(whole, whole, dtype=BF16)] * 2
-    grown, last_high, last_low, f_high, f_low, d_high, d_low = call(
-        functools.partial(early_kernel, share, tile, slots),
-        "early",
-        [like(2 * tile, whole)] + [like(2 * tile, 128, dtype=BF16)] * 2 + split_f + split_d,
-        [structure, live_counts, place],
-        [c_first, *mine, near, *theirs],
-        [pltpu.VMEM((2 * tile, slots * tile), F32)],
-    )
     outs = call(
         functools.partial(product_kernel, share, tile, slots),
         "products",
-        [like(tile, half)] * 2
-        + [like(tile, 2 * width)] * 4
-        + [like(share, whole, dtype=BF16)] * 2
-        + [like(2 * width, whole, dtype=BF16)] * 2,
+        [like(tile, half)] * 2 + [like(tile, 2 * width)] * 4 + split_f + split_d,
         [structure, live_counts, place],
-        [grown, last_high, last_low, d_high, d_low, near_opposite, opposite_theirs],
-        [pltpu.VMEM((2 * tile, whole), F32)],
-    )
-    panel, w, late = outs[:2], outs[2:6], outs[6:]
+        [c_own, *mine, *theirs],
+        [pltpu.VMEM((2 * tile, slots * tile), F32), pltpu.VMEM((2 * tile, whole), F32)],
+    )
+    panel, w, parts = outs[:2], outs[2:6], outs[6:]
     w = [w[0]] + [move(w[step], step, 0, 0) for step in range(1, 4)]
     s_high, s_low, base = call(
-        functools.partial(scaled_kernel, share),
-        "scaled",
-        split_f + [like(width, whole)],
-        [place],
-        [f_high, f_low, d_high, d_low, *late],
-        [pltpu.VMEM(s.shape, BF16) for s in split_f + split_d],
+        scaled_kernel, "scaled", split_f + [like(width, whole)], [place], parts
     )
     panel_send, w[1] = lax.optimization_barrier((panel[1], w[1]))
     panel_got = move(panel_send, 0, 1, 0)

time: 56.7 us -> 56 us (0.988)
  waiting for transfers between devices: 13.4 us -> 17.2 us
  starting transfers between devices: 28.2 us -> 26 us
  Pallas kernels: 11.8 us -> 10.4 us
  other arithmetic: 2.32 us -> 1.57 us
    ppermute x19 -> x20, waiting for transfers between devices: 13.4 us -> 17.2 us  [send_to(): return lax.ppermute(value, ('row', 'col'), pairs)]
    ppermute x19 -> x20, starting transfers between devices: 28.2 us -> 26 us  [send_to(): return lax.ppermute(value, ('row', 'col'), pairs)]
    pallas_call x7 -> x6, Pallas kernels: 11.8 us -> 10.4 us  [call(): pl.pallas_call(kernel, out_shape=outs, in_specs=[smem] * len(scalars) + [...]
    concatenate x1 -> x0, other arithmetic: 0.75 us -> none  [local(): jnp.concatenate([own, own_opposite])]
  transfers between devices with their start and end apart: 19 -> 20, of which waited for: 6 -> 6; matrix products, arithmetic and copies ran while one was open for 4% -> 3% of each run, Pallas kernels for 12% -> 9%
where the time goes in v9:
time: 56 us; the launch traced here: 55.9 us
  starting transfers between devices  26 us (46%)
  waiting for transfers between devices  17.2 us (31%)
  Pallas kernels  10.4 us (19%)
  other arithmetic  1.57 us (3%)
  between operations  0.73 us (1%)
    ppermute x20, starting transfers between devices, send_to(): return lax.ppermute(value, ('row', 'col'), pairs)  26 us
    ppermute x20, waiting for transfers between devices, send_to(): return lax.ppermute(value, ('row', 'col'), pairs)  17.2 us
    pallas_call x6, Pallas kernels, call(): pl.pallas_call(kernel, out_shape=outs, in_specs=[smem] * len(scalars) + [...  10.4 us
  transfers between devices with their start and end apart: 20, of which 6 were waited for; matrix products, arithmetic and copies ran while one was open for 3% of the time, Pallas kernels for 9%

profile of v9, /device:TPU:1, one launch (start us, length us, event | category | flops | bytes accessed | tf_op | source)
XLA Modules:
  0.0 55.9 jit_solution(14061728046944598014)
XLA Ops:
  0.6 1.2 %pack.1 = (f32[320,128]{1,0:T(8,128)S(1)}, f32[320,128]{1,0:T(8,128)S(1)}, f32[832,128]{1,0:T(8,128)S(1)}) custom-call(f32[384,128]{1,0:T(8,128)} %bitcast.25, f32[2,64,512]{2,1,0:T(8,128)} %bitcast.24, f32[512,128]{1,0:T(8,128)} %bitcast.20), custom_call_target="tpu_custom_call" | custom-call | tf_op jit(solution)/shard_map/pack/pallas_call | solution.py:269
  1.8 2.1 %collective-permute-start.6 = (f32[832,128]{1,0:T(8,128)S(1)}, f32[832,128]{1,0:T(8,128)S(1)}, u32[]{:S(2)}, u32[]{:S(2)}) collective-permute-start(f32[832,128]{1,0:T(8,128)S(1)} %get-tuple-element.28), channel_id=1, source_target_pairs={{0,2},{1,3},{2,0},{3,1},{4,6},{5,7},{6,4},{7,5},{8,10},{9,11},{10,... | collective-permute-start | bytes 1277960 | tf_op jit(solution)/shard_map/ppermute | solution.py:286
  3.9 2.3 %collective-permute-start.1 = (f32[320,128]{1,0:T(8,128)S(1)}, f32[320,128]{1,0:T(8,128)S(1)}, u32[]{:S(2)}, u32[]{:S(2)}) collective-permute-start(f32[320,128]{1,0:T(8,128)S(1)} %get-tuple-element.27), channel_id=1, source_target_pairs={{0,10},{1,11},{2,8},{3,9},{4,14},{5,15},{6,12},{7,13},{8,2},{9,3},... | collective-permute-start | bytes 491528 | tf_op jit(solution)/shard_map/ppermute | solution.py:286
  6.2 2.2 %collective-permute-start.3 = (f32[320,128]{1,0:T(8,128)S(1)}, f32[320,128]{1,0:T(8,128)S(1)}, u32[]{:S(2)}, u32[]{:S(2)}) collective-permute-start(f32[320,128]{1,0:T(8,128)S(1)} %get-tuple-element.27), channel_id=1, source_target_pairs={{0,6},{1,7},{2,4},{3,5},{4,2},{5,3},{6,0},{7,1},{8,14},{9,15},{10,... | collective-permute-start | bytes 491528 | tf_op jit(solution)/shard_map/ppermute | solution.py:286
  8.7 9.1 %collective-permute-done.1.refs_2_ = f32[320,128]{1,0:T(8,128)S(1)} collective-permute-done((f32[320,128]{1,0:T(8,128)S(1)}, f32[320,128]{1,0:T(8,128)S(1)}, u32[]{:S(2)}, u32[]{:S(2)}) %collective-permute-start.1) | collective-permute-done | bytes 163872 | tf_op jit(solution)/shard_map/ppermute | solution.py:286
  17.8 2.8 %collective-permute-start.13 = (f32[512,128]{1,0:T(8,128)S(1)}, f32[512,128]{1,0:T(8,128)S(1)}, u32[]{:S(2)}, u32[]{:S(2)}) collective-permute-start(f32[512,128]{1,0:T(8,128)S(1)} %bitcast.21), channel_id=1, source_target_pairs={{0,1},{1,0},{2,3},{3,2},{4,5},{5,4},{6,7},{7,6},{8,9},{9,8},{10,11... | collective-permute-start | bytes 786440 | tf_op jit(solution)/shard_map/ppermute | solution.py:286
  20.6 1.4 %collective-permute-start.9 = (f32[320,128]{1,0:T(8,128)S(1)}, f32[320,128]{1,0:T(8,128)S(1)}, u32[]{:S(2)}, u32[]{:S(2)}) collective-permute-start(f32[320,128]{1,0:T(8,128)S(1)} %get-tuple-element.26.refs_0_), channel_id=1, source_target_pairs={{0,1},{1,0},{2,3},{3,2},{4,5},{5,4},{6,7},{7,6},{8,9},{9,8},{10,11... | collective-permute-start | bytes 491528 | tf_op jit(solution)/shard_map/ppermute | solution.py:286
  22.0 0.8 %pad_maximum_fusion = f32[640,128]{1,0:T(8,128)} fusion(f32[320,128]{1,0:T(8,128)S(1)} %collective-permute-done.1.refs_2_, f32[320,128]{1,0:T(8,128)S(1)} %collective-permute-done.refs_1_), kind=kLoop, calls=%fused_computation | loop fusion | flops 81920 | bytes 655360 | tf_op jit(solution)/shard_map/concatenate | solution.py:321
  23.1 1.1 %collective-permute-start.4 = (f32[320,128]{1,0:T(8,128)S(1)}, f32[320,128]{1,0:T(8,128)S(1)}, u32[]{:S(2)}, u32[]{:S(2)}) collective-permute-start(f32[320,128]{1,0:T(8,128)S(1)} %collective-permute-done.refs_1_), channel_id=1, source_target_pairs={{0,4},{1,5},{2,6},{3,7},{4,0},{5,1},{6,2},{7,3},{8,12},{9,13},{10,... | collective-permute-start | bytes 491528 | tf_op jit(solution)/shard_map/ppermute | solution.py:286
  26.1 2.5 %collective-permute-done.5.refs_6_ = f32[320,128]{1,0:T(8,128)S(1)} collective-permute-done((f32[320,128]{1,0:T(8,128)S(1)}, f32[320,128]{1,0:T(8,128)S(1)}, u32[]{:S(2)}, u32[]{:S(2)}) %collective-permute-start.5) | collective-permute-done | bytes 163872 | tf_op jit(solution)/shard_map/ppermute | solution.py:286
  28.6 1.2 %collective-permute-start.11 = (f32[320,128]{1,0:T(8,128)S(1)}, f32[320,128]{1,0:T(8,128)S(1)}, u32[]{:S(2)}, u32[]{:S(2)}) collective-permute-start(f32[320,128]{1,0:T(8,128)S(1)} %collective-permute-done.5.refs_6_), channel_id=1, source_target_pairs={{0,1},{1,0},{2,3},{3,2},{4,5},{5,4},{6,7},{7,6},{8,9},{9,8},{10,11... | collective-permute-start | bytes 491528 | tf_op jit(solution)/shard_map/ppermute | solution.py:286
  29.8 2.3 %collective-permute-done.4.refs_5_ = f32[320,128]{1,0:T(8,128)S(1)} collective-permute-done((f32[320,128]{1,0:T(8,128)S(1)}, f32[320,128]{1,0:T(8,128)S(1)}, u32[]{:S(2)}, u32[]{:S(2)}) %collective-permute-start.4) | collective-permute-done | bytes 163872 | tf_op jit(solution)/shard_map/ppermute | solution.py:286
  32.1 0.8 %collective-permute-start.10 = (f32[320,128]{1,0:T(8,128)S(1)}, f32[320,128]{1,0:T(8,128)}, u32[]{:S(2)}, u32[]{:S(2)}) collective-permute-start(f32[320,128]{1,0:T(8,128)S(1)} %collective-permute-done.4.refs_5_), channel_id=1, source_target_pairs={{0,1},{1,0},{2,3},{3,2},{4,5},{5,4},{6,7},{7,6},{8,9},{9,8},{10,11... | collective-permute-start | bytes 491528 | tf_op jit(solution)/shard_map/ppermute | solution.py:286
  33.0 1.1 %collective-permute-done.10.refs_11_ = f32[320,128]{1,0:T(8,128)} collective-permute-done((f32[320,128]{1,0:T(8,128)S(1)}, f32[320,128]{1,0:T(8,128)}, u32[]{:S(2)}, u32[]{:S(2)}) %collective-permute-start.10) | collective-permute-done | bytes 163872 | tf_op jit(solution)/shard_map/ppermute | solution.py:286
  34.1 3.1 %products.1 = (f32[128,256]{1,0:T(8,128)S(1)}, f32[128,256]{1,0:T(8,128)S(1)}, f32[128,128]{1,0:T(8,128)S(1)}, f32[128,128]{1,0:T(8,128)S(1)}, f32[128,128]{1,0:...) custom-call(s32[2,6]{1,0:T(2,128)S(1)} %copy-done.1, ...), custom_call_target="tpu_custom_call" | custom-call | tf_op jit(solution)/shard_map/products/pallas_call | solution.py:269
  37.6 3.2 %collective-permute-start.16 = (f32[128,128]{1,0:T(8,128)S(1)}, f32[128,128]{1,0:T(8,128)S(1)}, u32[]{:S(2)}, u32[]{:S(2)}) collective-permute-start(f32[128,128]{1,0:T(8,128)S(1)} %get-tuple-element.35), channel_id=1, source_target_pairs={{0,8},{1,9},{2,10},{3,11},{4,12},{5,13},{6,14},{7,15},{8,0},{9,1},... | collective-permute-start | bytes 196616 | tf_op jit(solution)/shard_map/ppermute | solution.py:286
  40.8 1.2 %collective-permute-start.15 = (f32[128,256]{1,0:T(8,128)S(1)}, f32[128,256]{1,0:T(8,128)S(1)}, u32[]{:S(2)}, u32[]{:S(2)}) collective-permute-start(f32[128,256]{1,0:T(8,128)S(1)} %get-tuple-element.32), channel_id=1, source_target_pairs={{0,2},{1,3},{2,0},{3,1},{4,6},{5,7},{6,4},{7,5},{8,10},{9,11},{10,... | collective-permute-start | bytes 393224 | tf_op jit(solution)/shard_map/ppermute | solution.py:286
  42.1 2.3 %scaled.1 = (bf16[768,512]{1,0:T(8,128)(2,1)S(1)}, bf16[768,512]{1,0:T(8,128)(2,1)S(1)}, f32[64,512]{1,0:T(8,128)S(1)}) custom-call(s32[3]{0:T(128)S(1)} %pad_add_fusion.place, bf16[768,512]{1,0:T(8,128)(2,1)S(1)} %get-tuple-element.37.f_high, bf16[768,512]{1,0:T(8,128)(2,1)S(1)} %get-tuple-element.38.f_low, bf16[512,512]{1,0:T(8,128)(2,1)S(1)} %get-tuple-element.39.d_high, ...), custom_call_target="tpu_custom_call" | custom-call | tf_op jit(solution)/shard_map/scaled/pallas_call | solution.py:269
  44.4 1.4 %collective-permute-done.17.w3 = f32[128,128]{1,0:T(8,128)S(1)} collective-permute-done((f32[128,128]{1,0:T(8,128)S(1)}, f32[128,128]{1,0:T(8,128)S(1)}, u32[]{:S(2)}, u32[]{:S(2)}) %collective-permute-start.17) | collective-permute-done | bytes 65568 | tf_op jit(solution)/shard_map/ppermute | solution.py:286
  45.8 1.3 %diag_block.1 = (f32[64,256]{1,0:T(8,128)S(1)}, f32[64,256]{1,0:T(8,128)S(1)}) custom-call(s32[2,6]{1,0:T(2,128)S(1)} %copy-done.1, s32[2]{0:T(128)S(1)} %copy-done.2, s32[3]{0:T(128)S(1)} %pad_add_fusion.place, f32[128,128]{1,0:T(8,128)S(1)} %get-tuple-element.33.w0, f32[128,128]{1,0:T(8,128)S(1)} %collective-permute-done.14.w1, ...), custom_call_target="tpu_custom_call" | custom-call | tf_op jit(solution)/shard_map/diag_block/pallas_call | solution.py:269
  47.1 1.2 %collective-permute-start.18 = (f32[64,256]{1,0:T(8,128)S(1)}, f32[64,256]{1,0:T(8,128)S(1)}, u32[]{:S(2)}, u32[]{:S(2)}) collective-permute-start(f32[64,256]{1,0:T(8,128)S(1)} %get-tuple-element.49), channel_id=1, source_target_pairs={{0,1},{1,3},{2,0},{3,2},{4,5},{5,7},{6,4},{7,6},{8,9},{9,11},{10,8... | collective-permute-start | bytes 196616 | tf_op jit(solution)/shard_map/ppermute | solution.py:286
  48.3 4.4 %collective-permute-start.19 = (f32[64,256]{1,0:T(8,128)S(1)}, f32[64,256]{1,0:T(8,128)S(1)}, u32[]{:S(2)}, u32[]{:S(2)}) collective-permute-start(f32[64,256]{1,0:T(8,128)S(1)} %get-tuple-element.48.keep), channel_id=1, source_target_pairs={{1,2},{2,1},{5,6},{6,5},{9,10},{10,9},{13,14},{14,13},{17,18},{18,... | collective-permute-start | bytes 196616 | tf_op jit(solution)/shard_map/ppermute | solution.py:286
  52.7 1.3 %panel_lines.1 = f32[512,128]{1,0:T(8,128)} custom-call(s32[3]{0:T(128)S(1)} %pad_add_fusion.place, f32[128,256]{1,0:T(8,128)S(1)} %get-tuple-element.29.mine, f32[128,256]{1,0:T(8,128)S(1)} %collective-permute-done.15.other), custom_call_target="tpu_custom_call" | custom-call | tf_op jit(solution)/shard_map/panel_lines/pallas_call | solution.py:269
  54.7 1.2 %diag_lines.1 = f32[256,128]{1,0:T(8,128)} custom-call(s32[3]{0:T(128)S(1)} %pad_add_fusion.place, f32[64,256]{1,0:T(8,128)S(1)} %get-tuple-element.48.keep, f32[64,256]{1,0:T(8,128)S(1)} %collective-permute-done.18.met, f32[64,256]{1,0:T(8,128)S(1)} %collective-permute-done.19.far), custom_call_target="tpu_custom_call" | custom-call | tf_op jit(solution)/shard_map/diag_lines/pallas_call | solution.py:269
  (31 shorter events, 3.6 us)
Async XLA Ops:
  0.6 17.2 %copy-start = (f32[128,4,1,128]{3,2,1,0:T(1,128)S(1)}, f32[128,4,1,128]{3,2,1,0:T(1,128)}, u32[]{:S(2)}) copy-start(f32[128,4,1,128]{3,2,1,0:T(1,128)} %param.5) | copy-start | bytes 786436
  1.8 22.4 %collective-permute-start.6 = (f32[832,128]{1,0:T(8,128)S(1)}, f32[832,128]{1,0:T(8,128)S(1)}, u32[]{:S(2)}, u32[]{:S(2)}) collective-permute-start(f32[832,128]{1,0:T(8,128)S(1)} %get-tuple-element.28), channel_id=1, source_target_pairs={{0,2},{1,3},{2,0},{3,1},{4,6},{5,7},{6,4},{7,5},{8,10},{9,11},{10,... | collective-permute-start | bytes 1277960 | tf_op jit(solution)/shard_map/ppermute | solution.py:286
  3.9 13.9 %collective-permute-start.1 = (f32[320,128]{1,0:T(8,128)S(1)}, f32[320,128]{1,0:T(8,128)S(1)}, u32[]{:S(2)}, u32[]{:S(2)}) collective-permute-start(f32[320,128]{1,0:T(8,128)S(1)} %get-tuple-element.27), channel_id=1, source_target_pairs={{0,10},{1,11},{2,8},{3,9},{4,14},{5,15},{6,12},{7,13},{8,2},{9,3},... | collective-permute-start | bytes 491528 | tf_op jit(solution)/shard_map/ppermute | solution.py:286
  6.2 14.4 %collective-permute-start = (f32[320,128]{1,0:T(8,128)S(1)}, f32[320,128]{1,0:T(8,128)S(1)}, u32[]{:S(2)}, u32[]{:S(2)}) collective-permute-start(f32[320,128]{1,0:T(8,128)S(1)} %get-tuple-element.26.refs_0_), channel_id=1, source_target_pairs={{0,8},{1,9},{2,10},{3,11},{4,12},{5,13},{6,14},{7,15},{8,0},{9,1},... | collective-permute-start | bytes 491528 | tf_op jit(solution)/shard_map/ppermute | solution.py:286
  6.2 16.5 %collective-permute-start.3 = (f32[320,128]{1,0:T(8,128)S(1)}, f32[320,128]{1,0:T(8,128)S(1)}, u32[]{:S(2)}, u32[]{:S(2)}) collective-permute-start(f32[320,128]{1,0:T(8,128)S(1)} %get-tuple-element.27), channel_id=1, source_target_pairs={{0,6},{1,7},{2,4},{3,5},{4,2},{5,3},{6,0},{7,1},{8,14},{9,15},{10,... | collective-permute-start | bytes 491528 | tf_op jit(solution)/shard_map/ppermute | solution.py:286
  8.5 14.7 %collective-permute-start.2 = (f32[320,128]{1,0:T(8,128)S(1)}, f32[320,128]{1,0:T(8,128)S(1)}, u32[]{:S(2)}, u32[]{:S(2)}) collective-permute-start(f32[320,128]{1,0:T(8,128)S(1)} %get-tuple-element.26.refs_0_), channel_id=1, source_target_pairs={{0,4},{1,5},{2,6},{3,7},{4,0},{5,1},{6,2},{7,3},{8,12},{9,13},{10,... | collective-permute-start | bytes 491528 | tf_op jit(solution)/shard_map/ppermute | solution.py:286
  17.8 7.8 %collective-permute-start.13 = (f32[512,128]{1,0:T(8,128)S(1)}, f32[512,128]{1,0:T(8,128)S(1)}, u32[]{:S(2)}, u32[]{:S(2)}) collective-permute-start(f32[512,128]{1,0:T(8,128)S(1)} %bitcast.21), channel_id=1, source_target_pairs={{0,1},{1,0},{2,3},{3,2},{4,5},{5,4},{6,7},{7,6},{8,9},{9,8},{10,11... | collective-permute-start | bytes 786440 | tf_op jit(solution)/shard_map/ppermute | solution.py:286
  20.6 4.9 %collective-permute-start.9 = (f32[320,128]{1,0:T(8,128)S(1)}, f32[320,128]{1,0:T(8,128)S(1)}, u32[]{:S(2)}, u32[]{:S(2)}) collective-permute-start(f32[320,128]{1,0:T(8,128)S(1)} %get-tuple-element.26.refs_0_), channel_id=1, source_target_pairs={{0,1},{1,0},{2,3},{3,2},{4,5},{5,4},{6,7},{7,6},{8,9},{9,8},{10,11... | collective-permute-start | bytes 491528 | tf_op jit(solution)/shard_map/ppermute | solution.py:286
  22.8 5.8 %collective-permute-start.5 = (f32[320,128]{1,0:T(8,128)S(1)}, f32[320,128]{1,0:T(8,128)S(1)}, u32[]{:S(2)}, u32[]{:S(2)}) collective-permute-start(f32[320,128]{1,0:T(8,128)S(1)} %collective-permute-done.1.refs_2_), channel_id=1, source_target_pairs={{0,4},{1,5},{2,6},{3,7},{4,0},{5,1},{6,2},{7,3},{8,12},{9,13},{10,... | collective-permute-start | bytes 491528 | tf_op jit(solution)/shard_map/ppermute | solution.py:286
  23.1 9.0 %collective-permute-start.4 = (f32[320,128]{1,0:T(8,128)S(1)}, f32[320,128]{1,0:T(8,128)S(1)}, u32[]{:S(2)}, u32[]{:S(2)}) collective-permute-start(f32[320,128]{1,0:T(8,128)S(1)} %collective-permute-done.refs_1_), channel_id=1, source_target_pairs={{0,4},{1,5},{2,6},{3,7},{4,0},{5,1},{6,2},{7,3},{8,12},{9,13},{10,... | collective-permute-start | bytes 491528 | tf_op jit(solution)/shard_map/ppermute | solution.py:286
  24.3 9.8 %collective-permute-start.12 = (f32[832,128]{1,0:T(8,128)S(1)}, f32[832,128]{1,0:T(8,128)S(1)}, u32[]{:S(2)}, u32[]{:S(2)}) collective-permute-start(f32[832,128]{1,0:T(8,128)S(1)} %collective-permute-done.6.refs_7_), channel_id=1, source_target_pairs={{0,1},{1,0},{2,3},{3,2},{4,5},{5,4},{6,7},{7,6},{8,9},{9,8},{10,11... | collective-permute-start | bytes 1277960 | tf_op jit(solution)/shard_map/ppermute | solution.py:286
  25.6 8.5 %collective-permute-start.8 = (f32[640,128]{1,0:T(8,128)}, f32[640,128]{1,0:T(8,128)S(1)}, u32[]{:S(2)}, u32[]{:S(2)}) collective-permute-start(f32[640,128]{1,0:T(8,128)} %pad_maximum_fusion.1), channel_id=1, source_target_pairs={{0,1},{1,0},{2,3},{3,2},{4,5},{5,4},{6,7},{7,6},{8,9},{9,8},{10,11... | collective-permute-start | bytes 983048 | tf_op jit(solution)/shard_map/ppermute | solution.py:286
  25.6 8.5 %collective-permute-start.7 = (f32[640,128]{1,0:T(8,128)}, f32[640,128]{1,0:T(8,128)S(1)}, u32[]{:S(2)}, u32[]{:S(2)}) collective-permute-start(f32[640,128]{1,0:T(8,128)} %pad_maximum_fusion), channel_id=1, source_target_pairs={{0,1},{1,0},{2,3},{3,2},{4,5},{5,4},{6,7},{7,6},{8,9},{9,8},{10,11... | collective-permute-start | bytes 983048 | tf_op jit(solution)/shard_map/ppermute | solution.py:286
  28.6 4.4 %collective-permute-start.11 = (f32[320,128]{1,0:T(8,128)S(1)}, f32[320,128]{1,0:T(8,128)S(1)}, u32[]{:S(2)}, u32[]{:S(2)}) collective-permute-start(f32[320,128]{1,0:T(8,128)S(1)} %collective-permute-done.5.refs_6_), channel_id=1, source_target_pairs={{0,1},{1,0},{2,3},{3,2},{4,5},{5,4},{6,7},{7,6},{8,9},{9,8},{10,11... | collective-permute-start | bytes 491528 | tf_op jit(solution)/shard_map/ppermute | solution.py:286
  32.1 1.9 %collective-permute-start.10 = (f32[320,128]{1,0:T(8,128)S(1)}, f32[320,128]{1,0:T(8,128)}, u32[]{:S(2)}, u32[]{:S(2)}) collective-permute-start(f32[320,128]{1,0:T(8,128)S(1)} %collective-permute-done.4.refs_5_), channel_id=1, source_target_pairs={{0,1},{1,0},{2,3},{3,2},{4,5},{5,4},{6,7},{7,6},{8,9},{9,8},{10,11... | collective-permute-start | bytes 491528 | tf_op jit(solution)/shard_map/ppermute | solution.py:286
  32.9 1.2 %copy-start.1 = (s32[2,6]{1,0:T(2,128)S(1)}, s32[2,6]{1,0:T(2,128)}, u32[]{:S(2)}) copy-start(s32[2,6]{1,0:T(2,128)} %structure.3) | copy-start | bytes 148
  32.9 1.2 %copy-start.2 = (s32[2]{0:T(128)S(1)}, s32[2]{0:T(128)}, u32[]{:S(2)}) copy-start(s32[2]{0:T(128)} %live.3) | copy-start | bytes 28
  37.2 3.6 %collective-permute-start.14 = (f32[128,128]{1,0:T(8,128)S(1)}, f32[128,128]{1,0:T(8,128)S(1)}, u32[]{:S(2)}, u32[]{:S(2)}) collective-permute-start(f32[128,128]{1,0:T(8,128)S(1)} %get-tuple-element.31), channel_id=1, source_target_pairs={{0,4},{1,5},{2,6},{3,7},{4,0},{5,1},{6,2},{7,3},{8,12},{9,13},{10,... | collective-permute-start | bytes 196616 | tf_op jit(solution)/shard_map/ppermute | solution.py:286
  37.6 6.8 %collective-permute-start.16 = (f32[128,128]{1,0:T(8,128)S(1)}, f32[128,128]{1,0:T(8,128)S(1)}, u32[]{:S(2)}, u32[]{:S(2)}) collective-permute-start(f32[128,128]{1,0:T(8,128)S(1)} %get-tuple-element.35), channel_id=1, source_target_pairs={{0,8},{1,9},{2,10},{3,11},{4,12},{5,13},{6,14},{7,15},{8,0},{9,1},... | collective-permute-start | bytes 196616 | tf_op jit(solution)/shard_map/ppermute | solution.py:286
  40.8 5.0 %collective-permute-start.17 = (f32[128,128]{1,0:T(8,128)S(1)}, f32[128,128]{1,0:T(8,128)S(1)}, u32[]{:S(2)}, u32[]{:S(2)}) collective-permute-start(f32[128,128]{1,0:T(8,128)S(1)} %get-tuple-element.36), channel_id=1, source_target_pairs={{0,12},{1,13},{2,14},{3,15},{4,8},{5,9},{6,10},{7,11},{8,4},{9,5},... | collective-permute-start | bytes 196616 | tf_op jit(solution)/shard_map/ppermute | solution.py:286
  40.8 11.9 %collective-permute-start.15 = (f32[128,256]{1,0:T(8,128)S(1)}, f32[128,256]{1,0:T(8,128)S(1)}, u32[]{:S(2)}, u32[]{:S(2)}) collective-permute-start(f32[128,256]{1,0:T(8,128)S(1)} %get-tuple-element.32), channel_id=1, source_target_pairs={{0,2},{1,3},{2,0},{3,1},{4,6},{5,7},{6,4},{7,5},{8,10},{9,11},{10,... | collective-permute-start | bytes 393224 | tf_op jit(solution)/shard_map/ppermute | solution.py:286
  47.1 6.9 %collective-permute-start.18 = (f32[64,256]{1,0:T(8,128)S(1)}, f32[64,256]{1,0:T(8,128)S(1)}, u32[]{:S(2)}, u32[]{:S(2)}) collective-permute-start(f32[64,256]{1,0:T(8,128)S(1)} %get-tuple-element.49), channel_id=1, source_target_pairs={{0,1},{1,3},{2,0},{3,2},{4,5},{5,7},{6,4},{7,6},{8,9},{9,11},{10,8... | collective-permute-start | bytes 196616 | tf_op jit(solution)/shard_map/ppermute | solution.py:286
  48.3 6.3 %collective-permute-start.19 = (f32[64,256]{1,0:T(8,128)S(1)}, f32[64,256]{1,0:T(8,128)S(1)}, u32[]{:S(2)}, u32[]{:S(2)}) collective-permute-start(f32[64,256]{1,0:T(8,128)S(1)} %get-tuple-element.48.keep), channel_id=1, source_target_pairs={{1,2},{2,1},{5,6},{6,5},{9,10},{10,9},{13,14},{14,13},{17,18},{18,... | collective-permute-start | bytes 196616 | tf_op jit(solution)/shard_map/ppermute | solution.py:286

commit v10 on v9

--- a/solution.py
+++ b/solution.py
@@ -13,7 +13,7 @@
 NN = (((1,), (0,)), ((), ()))
 TN = (((0,), (0,)), ((), ()))
 VMEM_LIMIT = 20 * 1024 * 1024
-THERE = ((2, 0), (0, 0), (0, 1), (1, 0), (1, 1), (3, 0), (4, 0))
+THERE = ((2, 0), (0, 0), (0, 1), (1, 0), (1, 1), (3, 0), (3, 1))
 
 
 def halves(value):
@@ -65,12 +65,12 @@
 
 def product_kernel(share, tile, slots, structure, live, place, c_own, *refs):
     mine = refs[:8]
-    theirs = refs[8:13]
-    near_theirs, c_sib = refs[13:15]
-    panel_out = refs[15:17]
-    w_out = refs[17:21]
-    f_high, f_low, d_high, d_low = refs[21:25]
-    pick, product = refs[25:]
+    theirs = refs[8:12]
+    near_theirs, c_sib = refs[12:14]
+    panel_out = refs[14:16]
+    w_out = refs[16:20]
+    f_high, f_low, d_high, d_low = refs[20:24]
+    pick, product = refs[24:]
     z, x, c = place[0], place[1], place[2]
     size = mine[0].shape[0]
     whole = d_high.shape[0]
@@ -315,16 +315,18 @@
     near_side = move(send, 1, 1, 0)
     near = move(send_near, 0, 1, 0)
     own_opposite = move(own_far, 1, 0, 0)
+    near_far, near = lax.optimization_barrier((near_far, near))
     near_opposite = move(near_far, 1, 0, 0)
+    c_sib = move(c_own, 0, 0, 1)
+    near_in, c_sib = lax.optimization_barrier((near, c_sib))
     mine = [own, own_far, near_far, own_side, near_side, own_opposite, near_opposite, near]
     theirs = [
         move(jnp.concatenate([own_far, near_far]), 0, 0, 1),
         move(jnp.concatenate([own_side, near_side]), 0, 0, 1),
         move(own, 0, 0, 1),
-        move(own_opposite, 0, 0, 1),
-        move(near_opposite, 0, 0, 1),
-        move(near, 0, 0, 1),
-        move(c_own, 0, 0, 1),
+        move(jnp.concatenate([own_opposite, near_opposite]), 0, 0, 1),
+        move(near_in, 0, 0, 1),
+        c_sib,
     ]
     split_f = [like(slots * tile, whole, dtype=BF16)] * 2
     split_d = [like(whole, whole, dtype=BF16)] * 2

time: 56 us -> 56 us (level)
  waiting for transfers between devices: 17.2 us -> 15.3 us
  starting transfers between devices: 26 us -> 27.2 us
  other arithmetic: 1.57 us -> 2.3 us
    ppermute x20 -> x19, waiting for transfers between devices: 17.2 us -> 15.3 us  [send_to(): return lax.ppermute(value, ('row', 'col'), pairs)]
    ppermute x20 -> x19, starting transfers between devices: 26 us -> 27.2 us  [send_to(): return lax.ppermute(value, ('row', 'col'), pairs)]
    concatenate x0 -> x1, other arithmetic: none -> 0.74 us  [local(): jnp.concatenate([own_opposite, near_opposite])]
  transfers between devices with their start and end apart: 20 -> 19, of which waited for: 6 -> 6; matrix products, arithmetic and copies ran while one was open for 3% -> 4% of each run, Pallas kernels for 9% -> 9%
where the time goes in v10:
time: 56 us; the launch traced here: 55.8 us
  starting transfers between devices  27.2 us (49%)
  waiting for transfers between devices  15.3 us (27%)
  Pallas kernels  10.4 us (19%)
  other arithmetic  2.3 us (4%)
  between operations  0.71 us (1%)
    ppermute x19, starting transfers between devices, send_to(): return lax.ppermute(value, ('row', 'col'), pairs)  27.2 us
    ppermute x19, waiting for transfers between devices, send_to(): return lax.ppermute(value, ('row', 'col'), pairs)  15.3 us
    pallas_call x6, Pallas kernels, call(): pl.pallas_call(kernel, out_shape=outs, in_specs=[smem] * len(scalars) + [...  10.4 us
  transfers between devices with their start and end apart: 19, of which 6 were waited for; matrix products, arithmetic and copies ran while one was open for 4% of the time, Pallas kernels for 9%

profile of v10, /device:TPU:1, one launch (start us, length us, event | category | flops | bytes accessed | tf_op | source)
XLA Modules:
  0.0 55.8 jit_solution(16955430344467771753)
XLA Ops:
  0.6 1.2 %pack.1 = (f32[320,128]{1,0:T(8,128)S(1)}, f32[320,128]{1,0:T(8,128)S(1)}, f32[832,128]{1,0:T(8,128)S(1)}) custom-call(f32[384,128]{1,0:T(8,128)} %bitcast.25, f32[2,64,512]{2,1,0:T(8,128)} %bitcast.24, f32[512,128]{1,0:T(8,128)} %bitcast.20), custom_call_target="tpu_custom_call" | custom-call | tf_op jit(solution)/shard_map/pack/pallas_call | solution.py:269
  1.8 2.1 %collective-permute-start.2 = (f32[832,128]{1,0:T(8,128)S(1)}, f32[832,128]{1,0:T(8,128)S(1)}, u32[]{:S(2)}, u32[]{:S(2)}) collective-permute-start(f32[832,128]{1,0:T(8,128)S(1)} %get-tuple-element.32), channel_id=1, source_target_pairs={{0,2},{1,3},{2,0},{3,1},{4,6},{5,7},{6,4},{7,5},{8,10},{9,11},{10,... | collective-permute-start | bytes 1277960 | tf_op jit(solution)/shard_map/ppermute | solution.py:286
  3.9 2.3 %collective-permute-start.1 = (f32[320,128]{1,0:T(8,128)S(1)}, f32[320,128]{1,0:T(8,128)S(1)}, u32[]{:S(2)}, u32[]{:S(2)}) collective-permute-start(f32[320,128]{1,0:T(8,128)S(1)} %get-tuple-element.31), channel_id=1, source_target_pairs={{0,10},{1,11},{2,8},{3,9},{4,14},{5,15},{6,12},{7,13},{8,2},{9,3},... | collective-permute-start | bytes 491528 | tf_op jit(solution)/shard_map/ppermute | solution.py:286
  6.2 2.2 %collective-permute-start.4 = (f32[320,128]{1,0:T(8,128)S(1)}, f32[320,128]{1,0:T(8,128)S(1)}, u32[]{:S(2)}, u32[]{:S(2)}) collective-permute-start(f32[320,128]{1,0:T(8,128)S(1)} %get-tuple-element.31), channel_id=1, source_target_pairs={{0,6},{1,7},{2,4},{3,5},{4,2},{5,3},{6,0},{7,1},{8,14},{9,15},{10,... | collective-permute-start | bytes 491528 | tf_op jit(solution)/shard_map/ppermute | solution.py:286
  8.7 9.1 %collective-permute-done.1.refs_2_ = f32[320,128]{1,0:T(8,128)S(1)} collective-permute-done((f32[320,128]{1,0:T(8,128)S(1)}, f32[320,128]{1,0:T(8,128)S(1)}, u32[]{:S(2)}, u32[]{:S(2)}) %collective-permute-start.1) | collective-permute-done | bytes 163872 | tf_op jit(solution)/shard_map/ppermute | solution.py:286
  17.8 2.8 %collective-permute-start.11 = (f32[512,128]{1,0:T(8,128)S(1)}, f32[512,128]{1,0:T(8,128)S(1)}, u32[]{:S(2)}, u32[]{:S(2)}) collective-permute-start(f32[512,128]{1,0:T(8,128)S(1)} %bitcast.21), channel_id=1, source_target_pairs={{0,1},{1,0},{2,3},{3,2},{4,5},{5,4},{6,7},{7,6},{8,9},{9,8},{10,11... | collective-permute-start | bytes 786440 | tf_op jit(solution)/shard_map/ppermute | solution.py:286
  20.6 1.3 %collective-permute-start.5 = (f32[320,128]{1,0:T(8,128)S(1)}, f32[320,128]{1,0:T(8,128)S(1)}, u32[]{:S(2)}, u32[]{:S(2)}) collective-permute-start(f32[320,128]{1,0:T(8,128)S(1)} %collective-permute-done.refs_1_), channel_id=1, source_target_pairs={{0,4},{1,5},{2,6},{3,7},{4,0},{5,1},{6,2},{7,3},{8,12},{9,13},{10,... | collective-permute-start | bytes 491528 | tf_op jit(solution)/shard_map/ppermute | solution.py:286
  22.1 0.7 %pad_maximum_fusion.1 = f32[640,128]{1,0:T(8,128)} fusion(f32[320,128]{1,0:T(8,128)S(1)} %collective-permute-done.4.refs_4_, f32[320,128]{1,0:T(8,128)S(1)} %collective-permute-done.3.refs_3_), kind=kLoop, calls=%fused_computation.1 | loop fusion | flops 81920 | bytes 655360 | tf_op jit(solution)/shard_map/concatenate | solution.py:325
  22.9 2.0 %collective-permute-start.8 = (f32[640,128]{1,0:T(8,128)}, f32[640,128]{1,0:T(8,128)S(1)}, u32[]{:S(2)}, u32[]{:S(2)}) collective-permute-start(f32[640,128]{1,0:T(8,128)} %pad_maximum_fusion.1), channel_id=1, source_target_pairs={{0,1},{1,0},{2,3},{3,2},{4,5},{5,4},{6,7},{7,6},{8,9},{9,8},{10,11... | collective-permute-start | bytes 983048 | tf_op jit(solution)/shard_map/ppermute | solution.py:286
  24.8 0.7 %pad_maximum_fusion = f32[640,128]{1,0:T(8,128)} fusion(f32[320,128]{1,0:T(8,128)S(1)} %collective-permute-done.1.refs_2_, f32[320,128]{1,0:T(8,128)S(1)} %collective-permute-done.refs_1_), kind=kLoop, calls=%fused_computation | loop fusion | flops 81920 | bytes 655360 | tf_op jit(solution)/shard_map/concatenate | solution.py:324
  26.1 2.4 %collective-permute-done.6.refs_6_ = f32[320,128]{1,0:T(8,128)S(1)} collective-permute-done((f32[320,128]{1,0:T(8,128)S(1)}, f32[320,128]{1,0:T(8,128)S(1)}, u32[]{:S(2)}, u32[]{:S(2)}) %collective-permute-start.6) | collective-permute-done | bytes 163872 | tf_op jit(solution)/shard_map/ppermute | solution.py:286
  29.2 2.3 %collective-permute-start.10 = (f32[640,128]{1,0:T(8,128)}, f32[640,128]{1,0:T(8,128)S(1)}, u32[]{:S(2)}, u32[]{:S(2)}) collective-permute-start(f32[640,128]{1,0:T(8,128)} %pad_maximum_fusion.2), channel_id=1, source_target_pairs={{0,1},{1,0},{2,3},{3,2},{4,5},{5,4},{6,7},{7,6},{8,9},{9,8},{10,11... | collective-permute-start | bytes 983048 | tf_op jit(solution)/shard_map/ppermute | solution.py:286
  31.6 1.4 %collective-permute-done.9.refs_10_ = f32[320,128]{1,0:T(8,128)} collective-permute-done((f32[320,128]{1,0:T(8,128)S(1)}, f32[320,128]{1,0:T(8,128)}, u32[]{:S(2)}, u32[]{:S(2)}) %collective-permute-start.9) | collective-permute-done | bytes 163872 | tf_op jit(solution)/shard_map/ppermute | solution.py:286
  33.2 3.1 %products.1 = (f32[128,256]{1,0:T(8,128)S(1)}, f32[128,256]{1,0:T(8,128)S(1)}, f32[128,128]{1,0:T(8,128)S(1)}, f32[128,128]{1,0:T(8,128)S(1)}, f32[128,128]{1,0:...) custom-call(s32[2,6]{1,0:T(2,128)S(1)} %copy-done.1, ...), custom_call_target="tpu_custom_call" | custom-call | tf_op jit(solution)/shard_map/products/pallas_call | solution.py:269
  36.3 1.3 %collective-permute-start.13 = (f32[128,128]{1,0:T(8,128)S(1)}, f32[128,128]{1,0:T(8,128)S(1)}, u32[]{:S(2)}, u32[]{:S(2)}) collective-permute-start(f32[128,128]{1,0:T(8,128)S(1)} %get-tuple-element.39), channel_id=1, source_target_pairs={{0,4},{1,5},{2,6},{3,7},{4,0},{5,1},{6,2},{7,3},{8,12},{9,13},{10,... | collective-permute-start | bytes 196616 | tf_op jit(solution)/shard_map/ppermute | solution.py:286
  37.6 3.1 %collective-permute-start.15 = (f32[128,128]{1,0:T(8,128)S(1)}, f32[128,128]{1,0:T(8,128)S(1)}, u32[]{:S(2)}, u32[]{:S(2)}) collective-permute-start(f32[128,128]{1,0:T(8,128)S(1)} %get-tuple-element.43), channel_id=1, source_target_pairs={{0,8},{1,9},{2,10},{3,11},{4,12},{5,13},{6,14},{7,15},{8,0},{9,1},... | collective-permute-start | bytes 196616 | tf_op jit(solution)/shard_map/ppermute | solution.py:286
  40.7 1.2 %collective-permute-start.14 = (f32[128,256]{1,0:T(8,128)S(1)}, f32[128,256]{1,0:T(8,128)S(1)}, u32[]{:S(2)}, u32[]{:S(2)}) collective-permute-start(f32[128,256]{1,0:T(8,128)S(1)} %get-tuple-element.40), channel_id=1, source_target_pairs={{0,2},{1,3},{2,0},{3,1},{4,6},{5,7},{6,4},{7,5},{8,10},{9,11},{10,... | collective-permute-start | bytes 393224 | tf_op jit(solution)/shard_map/ppermute | solution.py:286
  41.9 2.4 %scaled.1 = (bf16[768,512]{1,0:T(8,128)(2,1)S(1)}, bf16[768,512]{1,0:T(8,128)(2,1)S(1)}, f32[64,512]{1,0:T(8,128)S(1)}) custom-call(s32[3]{0:T(128)S(1)} %pad_add_fusion.place, bf16[768,512]{1,0:T(8,128)(2,1)S(1)} %get-tuple-element.45.f_high, bf16[768,512]{1,0:T(8,128)(2,1)S(1)} %get-tuple-element.46.f_low, bf16[512,512]{1,0:T(8,128)(2,1)S(1)} %get-tuple-element.47.d_high, ...), custom_call_target="tpu_custom_call" | custom-call | tf_op jit(solution)/shard_map/scaled/pallas_call | solution.py:269
  44.3 1.4 %collective-permute-done.16.w3 = f32[128,128]{1,0:T(8,128)S(1)} collective-permute-done((f32[128,128]{1,0:T(8,128)S(1)}, f32[128,128]{1,0:T(8,128)S(1)}, u32[]{:S(2)}, u32[]{:S(2)}) %collective-permute-start.16) | collective-permute-done | bytes 65568 | tf_op jit(solution)/shard_map/ppermute | solution.py:286
  45.7 1.3 %diag_block.1 = (f32[64,256]{1,0:T(8,128)S(1)}, f32[64,256]{1,0:T(8,128)S(1)}) custom-call(s32[2,6]{1,0:T(2,128)S(1)} %copy-done.1, s32[2]{0:T(128)S(1)} %copy-done.2, s32[3]{0:T(128)S(1)} %pad_add_fusion.place, f32[128,128]{1,0:T(8,128)S(1)} %get-tuple-element.41.w0, f32[128,128]{1,0:T(8,128)S(1)} %collective-permute-done.13.w1, ...), custom_call_target="tpu_custom_call" | custom-call | tf_op jit(solution)/shard_map/diag_block/pallas_call | solution.py:269
  47.0 1.2 %collective-permute-start.17 = (f32[64,256]{1,0:T(8,128)S(1)}, f32[64,256]{1,0:T(8,128)S(1)}, u32[]{:S(2)}, u32[]{:S(2)}) collective-permute-start(f32[64,256]{1,0:T(8,128)S(1)} %get-tuple-element.57), channel_id=1, source_target_pairs={{0,1},{1,3},{2,0},{3,2},{4,5},{5,7},{6,4},{7,6},{8,9},{9,11},{10,8... | collective-permute-start | bytes 196616 | tf_op jit(solution)/shard_map/ppermute | solution.py:286
  48.2 4.4 %collective-permute-start.18 = (f32[64,256]{1,0:T(8,128)S(1)}, f32[64,256]{1,0:T(8,128)S(1)}, u32[]{:S(2)}, u32[]{:S(2)}) collective-permute-start(f32[64,256]{1,0:T(8,128)S(1)} %get-tuple-element.56.keep), channel_id=1, source_target_pairs={{1,2},{2,1},{5,6},{6,5},{9,10},{10,9},{13,14},{14,13},{17,18},{18,... | collective-permute-start | bytes 196616 | tf_op jit(solution)/shard_map/ppermute | solution.py:286
  52.7 1.3 %panel_lines.1 = f32[512,128]{1,0:T(8,128)} custom-call(s32[3]{0:T(128)S(1)} %pad_add_fusion.place, f32[128,256]{1,0:T(8,128)S(1)} %get-tuple-element.37.mine, f32[128,256]{1,0:T(8,128)S(1)} %collective-permute-done.14.other), custom_call_target="tpu_custom_call" | custom-call | tf_op jit(solution)/shard_map/panel_lines/pallas_call | solution.py:269
  54.6 1.2 %diag_lines.1 = f32[256,128]{1,0:T(8,128)} custom-call(s32[3]{0:T(128)S(1)} %pad_add_fusion.place, f32[64,256]{1,0:T(8,128)S(1)} %get-tuple-element.56.keep, f32[64,256]{1,0:T(8,128)S(1)} %collective-permute-done.17.met, f32[64,256]{1,0:T(8,128)S(1)} %collective-permute-done.18.far), custom_call_target="tpu_custom_call" | custom-call | tf_op jit(solution)/shard_map/diag_lines/pallas_call | solution.py:269
  (30 shorter events, 2.6 us)
Async XLA Ops:
  0.6 17.2 %copy-start = (f32[128,4,1,128]{3,2,1,0:T(1,128)S(1)}, f32[128,4,1,128]{3,2,1,0:T(1,128)}, u32[]{:S(2)}) copy-start(f32[128,4,1,128]{3,2,1,0:T(1,128)} %param.5) | copy-start | bytes 786436
  1.8 20.1 %collective-permute-start.2 = (f32[832,128]{1,0:T(8,128)S(1)}, f32[832,128]{1,0:T(8,128)S(1)}, u32[]{:S(2)}, u32[]{:S(2)}) collective-permute-start(f32[832,128]{1,0:T(8,128)S(1)} %get-tuple-element.32), channel_id=1, source_target_pairs={{0,2},{1,3},{2,0},{3,1},{4,6},{5,7},{6,4},{7,5},{8,10},{9,11},{10,... | collective-permute-start | bytes 1277960 | tf_op jit(solution)/shard_map/ppermute | solution.py:286
  3.9 13.9 %collective-permute-start.1 = (f32[320,128]{1,0:T(8,128)S(1)}, f32[320,128]{1,0:T(8,128)S(1)}, u32[]{:S(2)}, u32[]{:S(2)}) collective-permute-start(f32[320,128]{1,0:T(8,128)S(1)} %get-tuple-element.31), channel_id=1, source_target_pairs={{0,10},{1,11},{2,8},{3,9},{4,14},{5,15},{6,12},{7,13},{8,2},{9,3},... | collective-permute-start | bytes 491528 | tf_op jit(solution)/shard_map/ppermute | solution.py:286
  6.2 14.4 %collective-permute-start = (f32[320,128]{1,0:T(8,128)S(1)}, f32[320,128]{1,0:T(8,128)S(1)}, u32[]{:S(2)}, u32[]{:S(2)}) collective-permute-start(f32[320,128]{1,0:T(8,128)S(1)} %get-tuple-element.30.refs_0_), channel_id=1, source_target_pairs={{0,8},{1,9},{2,10},{3,11},{4,12},{5,13},{6,14},{7,15},{8,0},{9,1},... | collective-permute-start | bytes 491528 | tf_op jit(solution)/shard_map/ppermute | solution.py:286
  6.2 15.9 %collective-permute-start.4 = (f32[320,128]{1,0:T(8,128)S(1)}, f32[320,128]{1,0:T(8,128)S(1)}, u32[]{:S(2)}, u32[]{:S(2)}) collective-permute-start(f32[320,128]{1,0:T(8,128)S(1)} %get-tuple-element.31), channel_id=1, source_target_pairs={{0,6},{1,7},{2,4},{3,5},{4,2},{5,3},{6,0},{7,1},{8,14},{9,15},{10,... | collective-permute-start | bytes 491528 | tf_op jit(solution)/shard_map/ppermute | solution.py:286
  8.5 13.6 %collective-permute-start.3 = (f32[320,128]{1,0:T(8,128)S(1)}, f32[320,128]{1,0:T(8,128)S(1)}, u32[]{:S(2)}, u32[]{:S(2)}) collective-permute-start(f32[320,128]{1,0:T(8,128)S(1)} %get-tuple-element.30.refs_0_), channel_id=1, source_target_pairs={{0,4},{1,5},{2,6},{3,7},{4,0},{5,1},{6,2},{7,3},{8,12},{9,13},{10,... | collective-permute-start | bytes 491528 | tf_op jit(solution)/shard_map/ppermute | solution.py:286
  17.8 7.0 %collective-permute-start.11 = (f32[512,128]{1,0:T(8,128)S(1)}, f32[512,128]{1,0:T(8,128)S(1)}, u32[]{:S(2)}, u32[]{:S(2)}) collective-permute-start(f32[512,128]{1,0:T(8,128)S(1)} %bitcast.21), channel_id=1, source_target_pairs={{0,1},{1,0},{2,3},{3,2},{4,5},{5,4},{6,7},{7,6},{8,9},{9,8},{10,11... | collective-permute-start | bytes 786440 | tf_op jit(solution)/shard_map/ppermute | solution.py:286
  20.6 5.4 %collective-permute-start.5 = (f32[320,128]{1,0:T(8,128)S(1)}, f32[320,128]{1,0:T(8,128)S(1)}, u32[]{:S(2)}, u32[]{:S(2)}) collective-permute-start(f32[320,128]{1,0:T(8,128)S(1)} %collective-permute-done.refs_1_), channel_id=1, source_target_pairs={{0,4},{1,5},{2,6},{3,7},{4,0},{5,1},{6,2},{7,3},{8,12},{9,13},{10,... | collective-permute-start | bytes 491528 | tf_op jit(solution)/shard_map/ppermute | solution.py:286
  21.9 6.6 %collective-permute-start.6 = (f32[320,128]{1,0:T(8,128)S(1)}, f32[320,128]{1,0:T(8,128)S(1)}, u32[]{:S(2)}, u32[]{:S(2)}) collective-permute-start(f32[320,128]{1,0:T(8,128)S(1)} %collective-permute-done.1.refs_2_), channel_id=1, source_target_pairs={{0,4},{1,5},{2,6},{3,7},{4,0},{5,1},{6,2},{7,3},{8,12},{9,13},{10,... | collective-permute-start | bytes 491528 | tf_op jit(solution)/shard_map/ppermute | solution.py:286
  22.9 10.2 %collective-permute-start.8 = (f32[640,128]{1,0:T(8,128)}, f32[640,128]{1,0:T(8,128)S(1)}, u32[]{:S(2)}, u32[]{:S(2)}) collective-permute-start(f32[640,128]{1,0:T(8,128)} %pad_maximum_fusion.1), channel_id=1, source_target_pairs={{0,1},{1,0},{2,3},{3,2},{4,5},{5,4},{6,7},{7,6},{8,9},{9,8},{10,11... | collective-permute-start | bytes 983048 | tf_op jit(solution)/shard_map/ppermute | solution.py:286
  25.6 7.5 %collective-permute-start.7 = (f32[640,128]{1,0:T(8,128)}, f32[640,128]{1,0:T(8,128)S(1)}, u32[]{:S(2)}, u32[]{:S(2)}) collective-permute-start(f32[640,128]{1,0:T(8,128)} %pad_maximum_fusion), channel_id=1, source_target_pairs={{0,1},{1,0},{2,3},{3,2},{4,5},{5,4},{6,7},{7,6},{8,9},{9,8},{10,11... | collective-permute-start | bytes 983048 | tf_op jit(solution)/shard_map/ppermute | solution.py:286
  25.6 7.5 %collective-permute-start.12 = (f32[832,128]{1,0:T(8,128)S(1)}, f32[832,128]{1,0:T(8,128)S(1)}, u32[]{:S(2)}, u32[]{:S(2)}) collective-permute-start(f32[832,128]{1,0:T(8,128)S(1)} %collective-permute-done.2.refs_7_), channel_id=1, source_target_pairs={{0,1},{1,0},{2,3},{3,2},{4,5},{5,4},{6,7},{7,6},{8,9},{9,8},{10,11... | collective-permute-start | bytes 1277960 | tf_op jit(solution)/shard_map/ppermute | solution.py:286
  29.2 4.0 %collective-permute-start.10 = (f32[640,128]{1,0:T(8,128)}, f32[640,128]{1,0:T(8,128)S(1)}, u32[]{:S(2)}, u32[]{:S(2)}) collective-permute-start(f32[640,128]{1,0:T(8,128)} %pad_maximum_fusion.2), channel_id=1, source_target_pairs={{0,1},{1,0},{2,3},{3,2},{4,5},{5,4},{6,7},{7,6},{8,9},{9,8},{10,11... | collective-permute-start | bytes 983048 | tf_op jit(solution)/shard_map/ppermute | solution.py:286
  31.5 1.5 %collective-permute-start.9 = (f32[320,128]{1,0:T(8,128)S(1)}, f32[320,128]{1,0:T(8,128)}, u32[]{:S(2)}, u32[]{:S(2)}) collective-permute-start(f32[320,128]{1,0:T(8,128)S(1)} %get-tuple-element.30.refs_0_), channel_id=1, source_target_pairs={{0,1},{1,0},{2,3},{3,2},{4,5},{5,4},{6,7},{7,6},{8,9},{9,8},{10,11... | collective-permute-start | bytes 491528 | tf_op jit(solution)/shard_map/ppermute | solution.py:286
  31.5 1.7 %copy-start.1 = (s32[2,6]{1,0:T(2,128)S(1)}, s32[2,6]{1,0:T(2,128)}, u32[]{:S(2)}) copy-start(s32[2,6]{1,0:T(2,128)} %structure.3) | copy-start | bytes 148
  31.5 1.7 %copy-start.2 = (s32[2]{0:T(128)S(1)}, s32[2]{0:T(128)}, u32[]{:S(2)}) copy-start(s32[2]{0:T(128)} %live.3) | copy-start | bytes 28
  36.3 4.4 %collective-permute-start.13 = (f32[128,128]{1,0:T(8,128)S(1)}, f32[128,128]{1,0:T(8,128)S(1)}, u32[]{:S(2)}, u32[]{:S(2)}) collective-permute-start(f32[128,128]{1,0:T(8,128)S(1)} %get-tuple-element.39), channel_id=1, source_target_pairs={{0,4},{1,5},{2,6},{3,7},{4,0},{5,1},{6,2},{7,3},{8,12},{9,13},{10,... | collective-permute-start | bytes 196616 | tf_op jit(solution)/shard_map/ppermute | solution.py:286
  37.6 6.7 %collective-permute-start.15 = (f32[128,128]{1,0:T(8,128)S(1)}, f32[128,128]{1,0:T(8,128)S(1)}, u32[]{:S(2)}, u32[]{:S(2)}) collective-permute-start(f32[128,128]{1,0:T(8,128)S(1)} %get-tuple-element.43), channel_id=1, source_target_pairs={{0,8},{1,9},{2,10},{3,11},{4,12},{5,13},{6,14},{7,15},{8,0},{9,1},... | collective-permute-start | bytes 196616 | tf_op jit(solution)/shard_map/ppermute | solution.py:286
  40.7 5.0 %collective-permute-start.16 = (f32[128,128]{1,0:T(8,128)S(1)}, f32[128,128]{1,0:T(8,128)S(1)}, u32[]{:S(2)}, u32[]{:S(2)}) collective-permute-start(f32[128,128]{1,0:T(8,128)S(1)} %get-tuple-element.44), channel_id=1, source_target_pairs={{0,12},{1,13},{2,14},{3,15},{4,8},{5,9},{6,10},{7,11},{8,4},{9,5},... | collective-permute-start | bytes 196616 | tf_op jit(solution)/shard_map/ppermute | solution.py:286
  40.7 11.9 %collective-permute-start.14 = (f32[128,256]{1,0:T(8,128)S(1)}, f32[128,256]{1,0:T(8,128)S(1)}, u32[]{:S(2)}, u32[]{:S(2)}) collective-permute-start(f32[128,256]{1,0:T(8,128)S(1)} %get-tuple-element.40), channel_id=1, source_target_pairs={{0,2},{1,3},{2,0},{3,1},{4,6},{5,7},{6,4},{7,5},{8,10},{9,11},{10,... | collective-permute-start | bytes 393224 | tf_op jit(solution)/shard_map/ppermute | solution.py:286
  47.0 6.9 %collective-permute-start.17 = (f32[64,256]{1,0:T(8,128)S(1)}, f32[64,256]{1,0:T(8,128)S(1)}, u32[]{:S(2)}, u32[]{:S(2)}) collective-permute-start(f32[64,256]{1,0:T(8,128)S(1)} %get-tuple-element.57), channel_id=1, source_target_pairs={{0,1},{1,3},{2,0},{3,2},{4,5},{5,7},{6,4},{7,6},{8,9},{9,11},{10,8... | collective-permute-start | bytes 196616 | tf_op jit(solution)/shard_map/ppermute | solution.py:286
  48.2 6.3 %collective-permute-start.18 = (f32[64,256]{1,0:T(8,128)S(1)}, f32[64,256]{1,0:T(8,128)S(1)}, u32[]{:S(2)}, u32[]{:S(2)}) collective-permute-start(f32[64,256]{1,0:T(8,128)S(1)} %get-tuple-element.56.keep), channel_id=1, source_target_pairs={{1,2},{2,1},{5,6},{6,5},{9,10},{10,9},{13,14},{14,13},{17,18},{18,... | collective-permute-start | bytes 196616 | tf_op jit(solution)/shard_map/ppermute | solution.py:286

commit v11 on v10

--- a/solution.py
+++ b/solution.py
@@ -12,7 +12,7 @@
 NT = (((1,), (1,)), ((), ()))
 NN = (((1,), (0,)), ((), ()))
 TN = (((0,), (0,)), ((), ()))
-VMEM_LIMIT = 20 * 1024 * 1024
+VMEM_LIMIT = 10 * 1024 * 1024
 THERE = ((2, 0), (0, 0), (0, 1), (1, 0), (1, 1), (3, 0), (3, 1))
 
 

time: 56 us -> 56 us (level)
  no operation moved by 1% of the time
where the time goes in v11:
time: 56 us; the launch traced here: 55.8 us
  starting transfers between devices  27.2 us (49%)
  waiting for transfers between devices  15.3 us (27%)
  Pallas kernels  10.4 us (19%)
  other arithmetic  2.3 us (4%)
  between operations  0.71 us (1%)
    ppermute x19, starting transfers between devices, send_to(): return lax.ppermute(value, ('row', 'col'), pairs)  27.2 us
    ppermute x19, waiting for transfers between devices, send_to(): return lax.ppermute(value, ('row', 'col'), pairs)  15.3 us
    pallas_call x6, Pallas kernels, call(): pl.pallas_call(kernel, out_shape=outs, in_specs=[smem] * len(scalars) + [...  10.4 us
  transfers between devices with their start and end apart: 19, of which 6 were waited for; matrix products, arithmetic and copies ran while one was open for 4% of the time, Pallas kernels for 9%

profile of v11, /device:TPU:1, one launch (start us, length us, event | category | flops | bytes accessed | tf_op | source)
XLA Modules:
  0.0 55.8 jit_solution(17850666307219025999)
XLA Ops:
  0.6 1.2 %pack.1 = (f32[320,128]{1,0:T(8,128)S(1)}, f32[320,128]{1,0:T(8,128)S(1)}, f32[832,128]{1,0:T(8,128)S(1)}) custom-call(f32[384,128]{1,0:T(8,128)} %bitcast.25, f32[2,64,512]{2,1,0:T(8,128)} %bitcast.24, f32[512,128]{1,0:T(8,128)} %bitcast.20), custom_call_target="tpu_custom_call" | custom-call | tf_op jit(solution)/shard_map/pack/pallas_call | solution.py:269
  1.8 2.1 %collective-permute-start.2 = (f32[832,128]{1,0:T(8,128)S(1)}, f32[832,128]{1,0:T(8,128)S(1)}, u32[]{:S(2)}, u32[]{:S(2)}) collective-permute-start(f32[832,128]{1,0:T(8,128)S(1)} %get-tuple-element.32), channel_id=1, source_target_pairs={{0,2},{1,3},{2,0},{3,1},{4,6},{5,7},{6,4},{7,5},{8,10},{9,11},{10,... | collective-permute-start | bytes 1277960 | tf_op jit(solution)/shard_map/ppermute | solution.py:286
  3.9 2.3 %collective-permute-start.1 = (f32[320,128]{1,0:T(8,128)S(1)}, f32[320,128]{1,0:T(8,128)S(1)}, u32[]{:S(2)}, u32[]{:S(2)}) collective-permute-start(f32[320,128]{1,0:T(8,128)S(1)} %get-tuple-element.31), channel_id=1, source_target_pairs={{0,10},{1,11},{2,8},{3,9},{4,14},{5,15},{6,12},{7,13},{8,2},{9,3},... | collective-permute-start | bytes 491528 | tf_op jit(solution)/shard_map/ppermute | solution.py:286
  6.2 2.2 %collective-permute-start.4 = (f32[320,128]{1,0:T(8,128)S(1)}, f32[320,128]{1,0:T(8,128)S(1)}, u32[]{:S(2)}, u32[]{:S(2)}) collective-permute-start(f32[320,128]{1,0:T(8,128)S(1)} %get-tuple-element.31), channel_id=1, source_target_pairs={{0,6},{1,7},{2,4},{3,5},{4,2},{5,3},{6,0},{7,1},{8,14},{9,15},{10,... | collective-permute-start | bytes 491528 | tf_op jit(solution)/shard_map/ppermute | solution.py:286
  8.7 9.1 %collective-permute-done.1.refs_2_ = f32[320,128]{1,0:T(8,128)S(1)} collective-permute-done((f32[320,128]{1,0:T(8,128)S(1)}, f32[320,128]{1,0:T(8,128)S(1)}, u32[]{:S(2)}, u32[]{:S(2)}) %collective-permute-start.1) | collective-permute-done | bytes 163872 | tf_op jit(solution)/shard_map/ppermute | solution.py:286
  17.8 2.8 %collective-permute-start.11 = (f32[512,128]{1,0:T(8,128)S(1)}, f32[512,128]{1,0:T(8,128)S(1)}, u32[]{:S(2)}, u32[]{:S(2)}) collective-permute-start(f32[512,128]{1,0:T(8,128)S(1)} %bitcast.21), channel_id=1, source_target_pairs={{0,1},{1,0},{2,3},{3,2},{4,5},{5,4},{6,7},{7,6},{8,9},{9,8},{10,11... | collective-permute-start | bytes 786440 | tf_op jit(solution)/shard_map/ppermute | solution.py:286
  20.6 1.3 %collective-permute-start.5 = (f32[320,128]{1,0:T(8,128)S(1)}, f32[320,128]{1,0:T(8,128)S(1)}, u32[]{:S(2)}, u32[]{:S(2)}) collective-permute-start(f32[320,128]{1,0:T(8,128)S(1)} %collective-permute-done.refs_1_), channel_id=1, source_target_pairs={{0,4},{1,5},{2,6},{3,7},{4,0},{5,1},{6,2},{7,3},{8,12},{9,13},{10,... | collective-permute-start | bytes 491528 | tf_op jit(solution)/shard_map/ppermute | solution.py:286
  22.1 0.7 %pad_maximum_fusion.1 = f32[640,128]{1,0:T(8,128)} fusion(f32[320,128]{1,0:T(8,128)S(1)} %collective-permute-done.4.refs_4_, f32[320,128]{1,0:T(8,128)S(1)} %collective-permute-done.3.refs_3_), kind=kLoop, calls=%fused_computation.1 | loop fusion | flops 81920 | bytes 655360 | tf_op jit(solution)/shard_map/concatenate | solution.py:325
  22.9 2.0 %collective-permute-start.8 = (f32[640,128]{1,0:T(8,128)}, f32[640,128]{1,0:T(8,128)S(1)}, u32[]{:S(2)}, u32[]{:S(2)}) collective-permute-start(f32[640,128]{1,0:T(8,128)} %pad_maximum_fusion.1), channel_id=1, source_target_pairs={{0,1},{1,0},{2,3},{3,2},{4,5},{5,4},{6,7},{7,6},{8,9},{9,8},{10,11... | collective-permute-start | bytes 983048 | tf_op jit(solution)/shard_map/ppermute | solution.py:286
  24.8 0.7 %pad_maximum_fusion = f32[640,128]{1,0:T(8,128)} fusion(f32[320,128]{1,0:T(8,128)S(1)} %collective-permute-done.1.refs_2_, f32[320,128]{1,0:T(8,128)S(1)} %collective-permute-done.refs_1_), kind=kLoop, calls=%fused_computation | loop fusion | flops 81920 | bytes 655360 | tf_op jit(solution)/shard_map/concatenate | solution.py:324
  26.1 2.4 %collective-permute-done.6.refs_6_ = f32[320,128]{1,0:T(8,128)S(1)} collective-permute-done((f32[320,128]{1,0:T(8,128)S(1)}, f32[320,128]{1,0:T(8,128)S(1)}, u32[]{:S(2)}, u32[]{:S(2)}) %collective-permute-start.6) | collective-permute-done | bytes 163872 | tf_op jit(solution)/shard_map/ppermute | solution.py:286
  29.2 2.3 %collective-permute-start.10 = (f32[640,128]{1,0:T(8,128)}, f32[640,128]{1,0:T(8,128)S(1)}, u32[]{:S(2)}, u32[]{:S(2)}) collective-permute-start(f32[640,128]{1,0:T(8,128)} %pad_maximum_fusion.2), channel_id=1, source_target_pairs={{0,1},{1,0},{2,3},{3,2},{4,5},{5,4},{6,7},{7,6},{8,9},{9,8},{10,11... | collective-permute-start | bytes 983048 | tf_op jit(solution)/shard_map/ppermute | solution.py:286
  31.6 1.4 %collective-permute-done.9.refs_10_ = f32[320,128]{1,0:T(8,128)} collective-permute-done((f32[320,128]{1,0:T(8,128)S(1)}, f32[320,128]{1,0:T(8,128)}, u32[]{:S(2)}, u32[]{:S(2)}) %collective-permute-start.9) | collective-permute-done | bytes 163872 | tf_op jit(solution)/shard_map/ppermute | solution.py:286
  33.2 3.1 %products.1 = (f32[128,256]{1,0:T(8,128)S(1)}, f32[128,256]{1,0:T(8,128)S(1)}, f32[128,128]{1,0:T(8,128)S(1)}, f32[128,128]{1,0:T(8,128)S(1)}, f32[128,128]{1,0:...) custom-call(s32[2,6]{1,0:T(2,128)S(1)} %copy-done.1, ...), custom_call_target="tpu_custom_call" | custom-call | tf_op jit(solution)/shard_map/products/pallas_call | solution.py:269
  36.3 1.3 %collective-permute-start.13 = (f32[128,128]{1,0:T(8,128)S(1)}, f32[128,128]{1,0:T(8,128)S(1)}, u32[]{:S(2)}, u32[]{:S(2)}) collective-permute-start(f32[128,128]{1,0:T(8,128)S(1)} %get-tuple-element.39), channel_id=1, source_target_pairs={{0,4},{1,5},{2,6},{3,7},{4,0},{5,1},{6,2},{7,3},{8,12},{9,13},{10,... | collective-permute-start | bytes 196616 | tf_op jit(solution)/shard_map/ppermute | solution.py:286
  37.6 3.1 %collective-permute-start.15 = (f32[128,128]{1,0:T(8,128)S(1)}, f32[128,128]{1,0:T(8,128)S(1)}, u32[]{:S(2)}, u32[]{:S(2)}) collective-permute-start(f32[128,128]{1,0:T(8,128)S(1)} %get-tuple-element.43), channel_id=1, source_target_pairs={{0,8},{1,9},{2,10},{3,11},{4,12},{5,13},{6,14},{7,15},{8,0},{9,1},... | collective-permute-start | bytes 196616 | tf_op jit(solution)/shard_map/ppermute | solution.py:286
  40.7 1.2 %collective-permute-start.14 = (f32[128,256]{1,0:T(8,128)S(1)}, f32[128,256]{1,0:T(8,128)S(1)}, u32[]{:S(2)}, u32[]{:S(2)}) collective-permute-start(f32[128,256]{1,0:T(8,128)S(1)} %get-tuple-element.40), channel_id=1, source_target_pairs={{0,2},{1,3},{2,0},{3,1},{4,6},{5,7},{6,4},{7,5},{8,10},{9,11},{10,... | collective-permute-start | bytes 393224 | tf_op jit(solution)/shard_map/ppermute | solution.py:286
  41.9 2.4 %scaled.1 = (bf16[768,512]{1,0:T(8,128)(2,1)S(1)}, bf16[768,512]{1,0:T(8,128)(2,1)S(1)}, f32[64,512]{1,0:T(8,128)S(1)}) custom-call(s32[3]{0:T(128)S(1)} %pad_add_fusion.place, bf16[768,512]{1,0:T(8,128)(2,1)S(1)} %get-tuple-element.45.f_high, bf16[768,512]{1,0:T(8,128)(2,1)S(1)} %get-tuple-element.46.f_low, bf16[512,512]{1,0:T(8,128)(2,1)S(1)} %get-tuple-element.47.d_high, ...), custom_call_target="tpu_custom_call" | custom-call | tf_op jit(solution)/shard_map/scaled/pallas_call | solution.py:269
  44.3 1.4 %collective-permute-done.16.w3 = f32[128,128]{1,0:T(8,128)S(1)} collective-permute-done((f32[128,128]{1,0:T(8,128)S(1)}, f32[128,128]{1,0:T(8,128)S(1)}, u32[]{:S(2)}, u32[]{:S(2)}) %collective-permute-start.16) | collective-permute-done | bytes 65568 | tf_op jit(solution)/shard_map/ppermute | solution.py:286
  45.7 1.3 %diag_block.1 = (f32[64,256]{1,0:T(8,128)S(1)}, f32[64,256]{1,0:T(8,128)S(1)}) custom-call(s32[2,6]{1,0:T(2,128)S(1)} %copy-done.1, s32[2]{0:T(128)S(1)} %copy-done.2, s32[3]{0:T(128)S(1)} %pad_add_fusion.place, f32[128,128]{1,0:T(8,128)S(1)} %get-tuple-element.41.w0, f32[128,128]{1,0:T(8,128)S(1)} %collective-permute-done.13.w1, ...), custom_call_target="tpu_custom_call" | custom-call | tf_op jit(solution)/shard_map/diag_block/pallas_call | solution.py:269
  47.0 1.2 %collective-permute-start.17 = (f32[64,256]{1,0:T(8,128)S(1)}, f32[64,256]{1,0:T(8,128)S(1)}, u32[]{:S(2)}, u32[]{:S(2)}) collective-permute-start(f32[64,256]{1,0:T(8,128)S(1)} %get-tuple-element.57), channel_id=1, source_target_pairs={{0,1},{1,3},{2,0},{3,2},{4,5},{5,7},{6,4},{7,6},{8,9},{9,11},{10,8... | collective-permute-start | bytes 196616 | tf_op jit(solution)/shard_map/ppermute | solution.py:286
  48.2 4.4 %collective-permute-start.18 = (f32[64,256]{1,0:T(8,128)S(1)}, f32[64,256]{1,0:T(8,128)S(1)}, u32[]{:S(2)}, u32[]{:S(2)}) collective-permute-start(f32[64,256]{1,0:T(8,128)S(1)} %get-tuple-element.56.keep), channel_id=1, source_target_pairs={{1,2},{2,1},{5,6},{6,5},{9,10},{10,9},{13,14},{14,13},{17,18},{18,... | collective-permute-start | bytes 196616 | tf_op jit(solution)/shard_map/ppermute | solution.py:286
  52.7 1.3 %panel_lines.1 = f32[512,128]{1,0:T(8,128)} custom-call(s32[3]{0:T(128)S(1)} %pad_add_fusion.place, f32[128,256]{1,0:T(8,128)S(1)} %get-tuple-element.37.mine, f32[128,256]{1,0:T(8,128)S(1)} %collective-permute-done.14.other), custom_call_target="tpu_custom_call" | custom-call | tf_op jit(solution)/shard_map/panel_lines/pallas_call | solution.py:269
  54.6 1.2 %diag_lines.1 = f32[256,128]{1,0:T(8,128)} custom-call(s32[3]{0:T(128)S(1)} %pad_add_fusion.place, f32[64,256]{1,0:T(8,128)S(1)} %get-tuple-element.56.keep, f32[64,256]{1,0:T(8,128)S(1)} %collective-permute-done.17.met, f32[64,256]{1,0:T(8,128)S(1)} %collective-permute-done.18.far), custom_call_target="tpu_custom_call" | custom-call | tf_op jit(solution)/shard_map/diag_lines/pallas_call | solution.py:269
  (30 shorter events, 2.6 us)
Async XLA Ops:
  0.6 17.2 %copy-start = (f32[128,4,1,128]{3,2,1,0:T(1,128)S(1)}, f32[128,4,1,128]{3,2,1,0:T(1,128)}, u32[]{:S(2)}) copy-start(f32[128,4,1,128]{3,2,1,0:T(1,128)} %param.5) | copy-start | bytes 786436
  1.8 20.1 %collective-permute-start.2 = (f32[832,128]{1,0:T(8,128)S(1)}, f32[832,128]{1,0:T(8,128)S(1)}, u32[]{:S(2)}, u32[]{:S(2)}) collective-permute-start(f32[832,128]{1,0:T(8,128)S(1)} %get-tuple-element.32), channel_id=1, source_target_pairs={{0,2},{1,3},{2,0},{3,1},{4,6},{5,7},{6,4},{7,5},{8,10},{9,11},{10,... | collective-permute-start | bytes 1277960 | tf_op jit(solution)/shard_map/ppermute | solution.py:286
  3.9 13.9 %collective-permute-start.1 = (f32[320,128]{1,0:T(8,128)S(1)}, f32[320,128]{1,0:T(8,128)S(1)}, u32[]{:S(2)}, u32[]{:S(2)}) collective-permute-start(f32[320,128]{1,0:T(8,128)S(1)} %get-tuple-element.31), channel_id=1, source_target_pairs={{0,10},{1,11},{2,8},{3,9},{4,14},{5,15},{6,12},{7,13},{8,2},{9,3},... | collective-permute-start | bytes 491528 | tf_op jit(solution)/shard_map/ppermute | solution.py:286
  6.2 14.4 %collective-permute-start = (f32[320,128]{1,0:T(8,128)S(1)}, f32[320,128]{1,0:T(8,128)S(1)}, u32[]{:S(2)}, u32[]{:S(2)}) collective-permute-start(f32[320,128]{1,0:T(8,128)S(1)} %get-tuple-element.30.refs_0_), channel_id=1, source_target_pairs={{0,8},{1,9},{2,10},{3,11},{4,12},{5,13},{6,14},{7,15},{8,0},{9,1},... | collective-permute-start | bytes 491528 | tf_op jit(solution)/shard_map/ppermute | solution.py:286
  6.2 15.9 %collective-permute-start.4 = (f32[320,128]{1,0:T(8,128)S(1)}, f32[320,128]{1,0:T(8,128)S(1)}, u32[]{:S(2)}, u32[]{:S(2)}) collective-permute-start(f32[320,128]{1,0:T(8,128)S(1)} %get-tuple-element.31), channel_id=1, source_target_pairs={{0,6},{1,7},{2,4},{3,5},{4,2},{5,3},{6,0},{7,1},{8,14},{9,15},{10,... | collective-permute-start | bytes 491528 | tf_op jit(solution)/shard_map/ppermute | solution.py:286
  8.5 13.6 %collective-permute-start.3 = (f32[320,128]{1,0:T(8,128)S(1)}, f32[320,128]{1,0:T(8,128)S(1)}, u32[]{:S(2)}, u32[]{:S(2)}) collective-permute-start(f32[320,128]{1,0:T(8,128)S(1)} %get-tuple-element.30.refs_0_), channel_id=1, source_target_pairs={{0,4},{1,5},{2,6},{3,7},{4,0},{5,1},{6,2},{7,3},{8,12},{9,13},{10,... | collective-permute-start | bytes 491528 | tf_op jit(solution)/shard_map/ppermute | solution.py:286
  17.8 7.0 %collective-permute-start.11 = (f32[512,128]{1,0:T(8,128)S(1)}, f32[512,128]{1,0:T(8,128)S(1)}, u32[]{:S(2)}, u32[]{:S(2)}) collective-permute-start(f32[512,128]{1,0:T(8,128)S(1)} %bitcast.21), channel_id=1, source_target_pairs={{0,1},{1,0},{2,3},{3,2},{4,5},{5,4},{6,7},{7,6},{8,9},{9,8},{10,11... | collective-permute-start | bytes 786440 | tf_op jit(solution)/shard_map/ppermute | solution.py:286
  20.6 5.4 %collective-permute-start.5 = (f32[320,128]{1,0:T(8,128)S(1)}, f32[320,128]{1,0:T(8,128)S(1)}, u32[]{:S(2)}, u32[]{:S(2)}) collective-permute-start(f32[320,128]{1,0:T(8,128)S(1)} %collective-permute-done.refs_1_), channel_id=1, source_target_pairs={{0,4},{1,5},{2,6},{3,7},{4,0},{5,1},{6,2},{7,3},{8,12},{9,13},{10,... | collective-permute-start | bytes 491528 | tf_op jit(solution)/shard_map/ppermute | solution.py:286
  21.9 6.6 %collective-permute-start.6 = (f32[320,128]{1,0:T(8,128)S(1)}, f32[320,128]{1,0:T(8,128)S(1)}, u32[]{:S(2)}, u32[]{:S(2)}) collective-permute-start(f32[320,128]{1,0:T(8,128)S(1)} %collective-permute-done.1.refs_2_), channel_id=1, source_target_pairs={{0,4},{1,5},{2,6},{3,7},{4,0},{5,1},{6,2},{7,3},{8,12},{9,13},{10,... | collective-permute-start | bytes 491528 | tf_op jit(solution)/shard_map/ppermute | solution.py:286
  22.9 10.2 %collective-permute-start.8 = (f32[640,128]{1,0:T(8,128)}, f32[640,128]{1,0:T(8,128)S(1)}, u32[]{:S(2)}, u32[]{:S(2)}) collective-permute-start(f32[640,128]{1,0:T(8,128)} %pad_maximum_fusion.1), channel_id=1, source_target_pairs={{0,1},{1,0},{2,3},{3,2},{4,5},{5,4},{6,7},{7,6},{8,9},{9,8},{10,11... | collective-permute-start | bytes 983048 | tf_op jit(solution)/shard_map/ppermute | solution.py:286
  25.6 7.5 %collective-permute-start.7 = (f32[640,128]{1,0:T(8,128)}, f32[640,128]{1,0:T(8,128)S(1)}, u32[]{:S(2)}, u32[]{:S(2)}) collective-permute-start(f32[640,128]{1,0:T(8,128)} %pad_maximum_fusion), channel_id=1, source_target_pairs={{0,1},{1,0},{2,3},{3,2},{4,5},{5,4},{6,7},{7,6},{8,9},{9,8},{10,11... | collective-permute-start | bytes 983048 | tf_op jit(solution)/shard_map/ppermute | solution.py:286
  25.6 7.5 %collective-permute-start.12 = (f32[832,128]{1,0:T(8,128)S(1)}, f32[832,128]{1,0:T(8,128)S(1)}, u32[]{:S(2)}, u32[]{:S(2)}) collective-permute-start(f32[832,128]{1,0:T(8,128)S(1)} %collective-permute-done.2.refs_7_), channel_id=1, source_target_pairs={{0,1},{1,0},{2,3},{3,2},{4,5},{5,4},{6,7},{7,6},{8,9},{9,8},{10,11... | collective-permute-start | bytes 1277960 | tf_op jit(solution)/shard_map/ppermute | solution.py:286
  29.2 4.0 %collective-permute-start.10 = (f32[640,128]{1,0:T(8,128)}, f32[640,128]{1,0:T(8,128)S(1)}, u32[]{:S(2)}, u32[]{:S(2)}) collective-permute-start(f32[640,128]{1,0:T(8,128)} %pad_maximum_fusion.2), channel_id=1, source_target_pairs={{0,1},{1,0},{2,3},{3,2},{4,5},{5,4},{6,7},{7,6},{8,9},{9,8},{10,11... | collective-permute-start | bytes 983048 | tf_op jit(solution)/shard_map/ppermute | solution.py:286
  31.5 1.5 %collective-permute-start.9 = (f32[320,128]{1,0:T(8,128)S(1)}, f32[320,128]{1,0:T(8,128)}, u32[]{:S(2)}, u32[]{:S(2)}) collective-permute-start(f32[320,128]{1,0:T(8,128)S(1)} %get-tuple-element.30.refs_0_), channel_id=1, source_target_pairs={{0,1},{1,0},{2,3},{3,2},{4,5},{5,4},{6,7},{7,6},{8,9},{9,8},{10,11... | collective-permute-start | bytes 491528 | tf_op jit(solution)/shard_map/ppermute | solution.py:286
  31.5 1.7 %copy-start.1 = (s32[2,6]{1,0:T(2,128)S(1)}, s32[2,6]{1,0:T(2,128)}, u32[]{:S(2)}) copy-start(s32[2,6]{1,0:T(2,128)} %structure.3) | copy-start | bytes 148
  31.5 1.7 %copy-start.2 = (s32[2]{0:T(128)S(1)}, s32[2]{0:T(128)}, u32[]{:S(2)}) copy-start(s32[2]{0:T(128)} %live.3) | copy-start | bytes 28
  36.3 4.4 %collective-permute-start.13 = (f32[128,128]{1,0:T(8,128)S(1)}, f32[128,128]{1,0:T(8,128)S(1)}, u32[]{:S(2)}, u32[]{:S(2)}) collective-permute-start(f32[128,128]{1,0:T(8,128)S(1)} %get-tuple-element.39), channel_id=1, source_target_pairs={{0,4},{1,5},{2,6},{3,7},{4,0},{5,1},{6,2},{7,3},{8,12},{9,13},{10,... | collective-permute-start | bytes 196616 | tf_op jit(solution)/shard_map/ppermute | solution.py:286
  37.6 6.7 %collective-permute-start.15 = (f32[128,128]{1,0:T(8,128)S(1)}, f32[128,128]{1,0:T(8,128)S(1)}, u32[]{:S(2)}, u32[]{:S(2)}) collective-permute-start(f32[128,128]{1,0:T(8,128)S(1)} %get-tuple-element.43), channel_id=1, source_target_pairs={{0,8},{1,9},{2,10},{3,11},{4,12},{5,13},{6,14},{7,15},{8,0},{9,1},... | collective-permute-start | bytes 196616 | tf_op jit(solution)/shard_map/ppermute | solution.py:286
  40.7 5.0 %collective-permute-start.16 = (f32[128,128]{1,0:T(8,128)S(1)}, f32[128,128]{1,0:T(8,128)S(1)}, u32[]{:S(2)}, u32[]{:S(2)}) collective-permute-start(f32[128,128]{1,0:T(8,128)S(1)} %get-tuple-element.44), channel_id=1, source_target_pairs={{0,12},{1,13},{2,14},{3,15},{4,8},{5,9},{6,10},{7,11},{8,4},{9,5},... | collective-permute-start | bytes 196616 | tf_op jit(solution)/shard_map/ppermute | solution.py:286
  40.7 11.9 %collective-permute-start.14 = (f32[128,256]{1,0:T(8,128)S(1)}, f32[128,256]{1,0:T(8,128)S(1)}, u32[]{:S(2)}, u32[]{:S(2)}) collective-permute-start(f32[128,256]{1,0:T(8,128)S(1)} %get-tuple-element.40), channel_id=1, source_target_pairs={{0,2},{1,3},{2,0},{3,1},{4,6},{5,7},{6,4},{7,5},{8,10},{9,11},{10,... | collective-permute-start | bytes 393224 | tf_op jit(solution)/shard_map/ppermute | solution.py:286
  47.0 6.9 %collective-permute-start.17 = (f32[64,256]{1,0:T(8,128)S(1)}, f32[64,256]{1,0:T(8,128)S(1)}, u32[]{:S(2)}, u32[]{:S(2)}) collective-permute-start(f32[64,256]{1,0:T(8,128)S(1)} %get-tuple-element.57), channel_id=1, source_target_pairs={{0,1},{1,3},{2,0},{3,2},{4,5},{5,7},{6,4},{7,6},{8,9},{9,11},{10,8... | collective-permute-start | bytes 196616 | tf_op jit(solution)/shard_map/ppermute | solution.py:286
  48.2 6.3 %collective-permute-start.18 = (f32[64,256]{1,0:T(8,128)S(1)}, f32[64,256]{1,0:T(8,128)S(1)}, u32[]{:S(2)}, u32[]{:S(2)}) collective-permute-start(f32[64,256]{1,0:T(8,128)S(1)} %get-tuple-element.56.keep), channel_id=1, source_target_pairs={{1,2},{2,1},{5,6},{6,5},{9,10},{10,9},{13,14},{14,13},{17,18},{18,... | collective-permute-start | bytes 196616 | tf_op jit(solution)/shard_map/ppermute | solution.py:286

commit v12 on v10

--- a/solution.py
+++ b/solution.py
@@ -315,9 +315,9 @@
     near_side = move(send, 1, 1, 0)
     near = move(send_near, 0, 1, 0)
     own_opposite = move(own_far, 1, 0, 0)
-    near_far, near = lax.optimization_barrier((near_far, near))
+    c_sib = move(c_own, 0, 0, 1)
+    near_far, c_sib = lax.optimization_barrier((near_far, c_sib))
     near_opposite = move(near_far, 1, 0, 0)
-    c_sib = move(c_own, 0, 0, 1)
     near_in, c_sib = lax.optimization_barrier((near, c_sib))
     mine = [own, own_far, near_far, own_side, near_side, own_opposite, near_opposite, near]
     theirs = [

time: 56 us -> 56.7 us (1.012)
  waiting for transfers between devices: 15.3 us -> 19.1 us
  starting transfers between devices: 27.2 us -> 24 us
    ppermute x19, waiting for transfers between devices: 15.3 us -> 19.1 us  [send_to(): return lax.ppermute(value, ('row', 'col'), pairs)]
    ppermute x19, starting transfers between devices: 27.2 us -> 24 us  [send_to(): return lax.ppermute(value, ('row', 'col'), pairs)]
  transfers between devices with their start and end apart: 19 -> 19, of which waited for: 6 -> 8; matrix products, arithmetic and copies ran while one was open for 4% -> 4% of each run, Pallas kernels for 9% -> 9%
where the time goes in v12:
time: 56.7 us; the launch traced here: 56.5 us
  starting transfers between devices  24 us (42%)
  waiting for transfers between devices  19.1 us (34%)
  Pallas kernels  10.4 us (18%)
  other arithmetic  2.3 us (4%)
  between operations  0.72 us (1%)
    ppermute x19, starting transfers between devices, send_to(): return lax.ppermute(value, ('row', 'col'), pairs)  24 us
    ppermute x19, waiting for transfers between devices, send_to(): return lax.ppermute(value, ('row', 'col'), pairs)  19.1 us
    pallas_call x6, Pallas kernels, call(): pl.pallas_call(kernel, out_shape=outs, in_specs=[smem] * len(scalars) + [...  10.4 us
  transfers between devices with their start and end apart: 19, of which 8 were waited for; matrix products, arithmetic and copies ran while one was open for 4% of the time, Pallas kernels for 9%

profile of v12, /device:TPU:1, one launch (start us, length us, event | category | flops | bytes accessed | tf_op | source)
XLA Modules:
  0.0 56.5 jit_solution(6038320728946199834)
XLA Ops:
  0.6 1.2 %pack.1 = (f32[320,128]{1,0:T(8,128)S(1)}, f32[320,128]{1,0:T(8,128)S(1)}, f32[832,128]{1,0:T(8,128)S(1)}) custom-call(f32[384,128]{1,0:T(8,128)} %bitcast.25, f32[2,64,512]{2,1,0:T(8,128)} %bitcast.24, f32[512,128]{1,0:T(8,128)} %bitcast.20), custom_call_target="tpu_custom_call" | custom-call | tf_op jit(solution)/shard_map/pack/pallas_call | solution.py:269
  1.8 4.1 %collective-permute-start.1 = (f32[320,128]{1,0:T(8,128)S(1)}, f32[320,128]{1,0:T(8,128)S(1)}, u32[]{:S(2)}, u32[]{:S(2)}) collective-permute-start(f32[320,128]{1,0:T(8,128)S(1)} %get-tuple-element.31), channel_id=1, source_target_pairs={{0,10},{1,11},{2,8},{3,9},{4,14},{5,15},{6,12},{7,13},{8,2},{9,3},... | collective-permute-start | bytes 491528 | tf_op jit(solution)/shard_map/ppermute | solution.py:286
  6.0 1.0 %collective-permute-start.2 = (f32[512,128]{1,0:T(8,128)S(1)}, f32[512,128]{1,0:T(8,128)S(1)}, u32[]{:S(2)}, u32[]{:S(2)}) collective-permute-start(f32[512,128]{1,0:T(8,128)S(1)} %bitcast.21), channel_id=1, source_target_pairs={{0,1},{1,0},{2,3},{3,2},{4,5},{5,4},{6,7},{7,6},{8,9},{9,8},{10,11... | collective-permute-start | bytes 786440 | tf_op jit(solution)/shard_map/ppermute | solution.py:286
  7.2 2.3 %collective-permute-start.4 = (f32[320,128]{1,0:T(8,128)S(1)}, f32[320,128]{1,0:T(8,128)S(1)}, u32[]{:S(2)}, u32[]{:S(2)}) collective-permute-start(f32[320,128]{1,0:T(8,128)S(1)} %get-tuple-element.31), channel_id=1, source_target_pairs={{0,6},{1,7},{2,4},{3,5},{4,2},{5,3},{6,0},{7,1},{8,14},{9,15},{10,... | collective-permute-start | bytes 491528 | tf_op jit(solution)/shard_map/ppermute | solution.py:286
  9.5 7.4 %collective-permute-done.1.refs_2_ = f32[320,128]{1,0:T(8,128)S(1)} collective-permute-done((f32[320,128]{1,0:T(8,128)S(1)}, f32[320,128]{1,0:T(8,128)S(1)}, u32[]{:S(2)}, u32[]{:S(2)}) %collective-permute-start.1) | collective-permute-done | bytes 163872 | tf_op jit(solution)/shard_map/ppermute | solution.py:286
  16.8 1.3 %collective-permute-start.3 = (f32[320,128]{1,0:T(8,128)S(1)}, f32[320,128]{1,0:T(8,128)S(1)}, u32[]{:S(2)}, u32[]{:S(2)}) collective-permute-start(f32[320,128]{1,0:T(8,128)S(1)} %get-tuple-element.30.refs_0_), channel_id=1, source_target_pairs={{0,4},{1,5},{2,6},{3,7},{4,0},{5,1},{6,2},{7,3},{8,12},{9,13},{10,... | collective-permute-start | bytes 491528 | tf_op jit(solution)/shard_map/ppermute | solution.py:286
  18.1 2.0 %collective-permute-done.refs_1_ = f32[320,128]{1,0:T(8,128)S(1)} collective-permute-done((f32[320,128]{1,0:T(8,128)S(1)}, f32[320,128]{1,0:T(8,128)S(1)}, u32[]{:S(2)}, u32[]{:S(2)}) %collective-permute-start) | collective-permute-done | bytes 163872 | tf_op jit(solution)/shard_map/ppermute | solution.py:286
  20.2 1.5 %collective-permute-start.5 = (f32[320,128]{1,0:T(8,128)S(1)}, f32[320,128]{1,0:T(8,128)S(1)}, u32[]{:S(2)}, u32[]{:S(2)}) collective-permute-start(f32[320,128]{1,0:T(8,128)S(1)} %collective-permute-done.refs_1_), channel_id=1, source_target_pairs={{0,4},{1,5},{2,6},{3,7},{4,0},{5,1},{6,2},{7,3},{8,12},{9,13},{10,... | collective-permute-start | bytes 491528 | tf_op jit(solution)/shard_map/ppermute | solution.py:286
  21.7 2.2 %collective-permute-done.3.refs_3_ = f32[320,128]{1,0:T(8,128)S(1)} collective-permute-done((f32[320,128]{1,0:T(8,128)S(1)}, f32[320,128]{1,0:T(8,128)S(1)}, u32[]{:S(2)}, u32[]{:S(2)}) %collective-permute-start.3) | collective-permute-done | bytes 163872 | tf_op jit(solution)/shard_map/ppermute | solution.py:286
  23.9 0.7 %pad_maximum_fusion.1 = f32[640,128]{1,0:T(8,128)} fusion(f32[320,128]{1,0:T(8,128)S(1)} %collective-permute-done.4.refs_4_, f32[320,128]{1,0:T(8,128)S(1)} %collective-permute-done.3.refs_3_), kind=kLoop, calls=%fused_computation.1 | loop fusion | flops 81920 | bytes 655360 | tf_op jit(solution)/shard_map/concatenate | solution.py:325
  24.6 2.2 %collective-permute-start.9 = (f32[640,128]{1,0:T(8,128)}, f32[640,128]{1,0:T(8,128)S(1)}, u32[]{:S(2)}, u32[]{:S(2)}) collective-permute-start(f32[640,128]{1,0:T(8,128)} %pad_maximum_fusion.1), channel_id=1, source_target_pairs={{0,1},{1,0},{2,3},{3,2},{4,5},{5,4},{6,7},{7,6},{8,9},{9,8},{10,11... | collective-permute-start | bytes 983048 | tf_op jit(solution)/shard_map/ppermute | solution.py:286
  26.8 0.7 %pad_maximum_fusion = f32[640,128]{1,0:T(8,128)} fusion(f32[320,128]{1,0:T(8,128)S(1)} %collective-permute-done.1.refs_2_, f32[320,128]{1,0:T(8,128)S(1)} %collective-permute-done.refs_1_), kind=kLoop, calls=%fused_computation | loop fusion | flops 81920 | bytes 655360 | tf_op jit(solution)/shard_map/concatenate | solution.py:324
  28.1 2.8 %collective-permute-done.6.refs_6_ = f32[320,128]{1,0:T(8,128)S(1)} collective-permute-done((f32[320,128]{1,0:T(8,128)S(1)}, f32[320,128]{1,0:T(8,128)S(1)}, u32[]{:S(2)}, u32[]{:S(2)}) %collective-permute-start.6) | collective-permute-done | bytes 163872 | tf_op jit(solution)/shard_map/ppermute | solution.py:286
  30.9 0.7 %pad_maximum_fusion.2 = f32[640,128]{1,0:T(8,128)} fusion(f32[320,128]{1,0:T(8,128)S(1)} %collective-permute-done.6.refs_6_, f32[320,128]{1,0:T(8,128)S(1)} %collective-permute-done.5.refs_5_), kind=kLoop, calls=%fused_computation.2 | loop fusion | flops 81920 | bytes 655360 | tf_op jit(solution)/shard_map/concatenate | solution.py:327
  31.7 1.3 %collective-permute-start.11 = (f32[640,128]{1,0:T(8,128)}, f32[640,128]{1,0:T(8,128)S(1)}, u32[]{:S(2)}, u32[]{:S(2)}) collective-permute-start(f32[640,128]{1,0:T(8,128)} %pad_maximum_fusion.2), channel_id=1, source_target_pairs={{0,1},{1,0},{2,3},{3,2},{4,5},{5,4},{6,7},{7,6},{8,9},{9,8},{10,11... | collective-permute-start | bytes 983048 | tf_op jit(solution)/shard_map/ppermute | solution.py:286
  33.1 1.4 %collective-permute-done.10.refs_10_ = f32[320,128]{1,0:T(8,128)} collective-permute-done((f32[320,128]{1,0:T(8,128)S(1)}, f32[320,128]{1,0:T(8,128)}, u32[]{:S(2)}, u32[]{:S(2)}) %collective-permute-start.10) | collective-permute-done | bytes 163872 | tf_op jit(solution)/shard_map/ppermute | solution.py:286
  34.7 3.1 %products.1 = (f32[128,256]{1,0:T(8,128)S(1)}, f32[128,256]{1,0:T(8,128)S(1)}, f32[128,128]{1,0:T(8,128)S(1)}, f32[128,128]{1,0:T(8,128)S(1)}, f32[128,128]{1,0:...) custom-call(s32[2,6]{1,0:T(2,128)S(1)} %copy-done.1, ...), custom_call_target="tpu_custom_call" | custom-call | tf_op jit(solution)/shard_map/products/pallas_call | solution.py:269
  37.9 3.6 %collective-permute-start.15 = (f32[128,128]{1,0:T(8,128)S(1)}, f32[128,128]{1,0:T(8,128)S(1)}, u32[]{:S(2)}, u32[]{:S(2)}) collective-permute-start(f32[128,128]{1,0:T(8,128)S(1)} %get-tuple-element.43), channel_id=1, source_target_pairs={{0,8},{1,9},{2,10},{3,11},{4,12},{5,13},{6,14},{7,15},{8,0},{9,1},... | collective-permute-start | bytes 196616 | tf_op jit(solution)/shard_map/ppermute | solution.py:286
  41.8 2.4 %scaled.1 = (bf16[768,512]{1,0:T(8,128)(2,1)S(1)}, bf16[768,512]{1,0:T(8,128)(2,1)S(1)}, f32[64,512]{1,0:T(8,128)S(1)}) custom-call(s32[3]{0:T(128)S(1)} %pad_add_fusion.place, bf16[768,512]{1,0:T(8,128)(2,1)S(1)} %get-tuple-element.45.f_high, bf16[768,512]{1,0:T(8,128)(2,1)S(1)} %get-tuple-element.46.f_low, bf16[512,512]{1,0:T(8,128)(2,1)S(1)} %get-tuple-element.47.d_high, ...), custom_call_target="tpu_custom_call" | custom-call | tf_op jit(solution)/shard_map/scaled/pallas_call | solution.py:269
  44.1 2.3 %collective-permute-done.16.w3 = f32[128,128]{1,0:T(8,128)S(1)} collective-permute-done((f32[128,128]{1,0:T(8,128)S(1)}, f32[128,128]{1,0:T(8,128)S(1)}, u32[]{:S(2)}, u32[]{:S(2)}) %collective-permute-start.16) | collective-permute-done | bytes 65568 | tf_op jit(solution)/shard_map/ppermute | solution.py:286
  46.5 1.3 %diag_block.1 = (f32[64,256]{1,0:T(8,128)S(1)}, f32[64,256]{1,0:T(8,128)S(1)}) custom-call(s32[2,6]{1,0:T(2,128)S(1)} %copy-done.1, s32[2]{0:T(128)S(1)} %copy-done.2, s32[3]{0:T(128)S(1)} %pad_add_fusion.place, f32[128,128]{1,0:T(8,128)S(1)} %get-tuple-element.41.w0, f32[128,128]{1,0:T(8,128)S(1)} %collective-permute-done.13.w1, ...), custom_call_target="tpu_custom_call" | custom-call | tf_op jit(solution)/shard_map/diag_block/pallas_call | solution.py:269
  48.1 5.3 %collective-permute-start.18 = (f32[64,256]{1,0:T(8,128)S(1)}, f32[64,256]{1,0:T(8,128)S(1)}, u32[]{:S(2)}, u32[]{:S(2)}) collective-permute-start(f32[64,256]{1,0:T(8,128)S(1)} %get-tuple-element.56.keep), channel_id=1, source_target_pairs={{1,2},{2,1},{5,6},{6,5},{9,10},{10,9},{13,14},{14,13},{17,18},{18,... | collective-permute-start | bytes 196616 | tf_op jit(solution)/shard_map/ppermute | solution.py:286
  53.4 1.3 %panel_lines.1 = f32[512,128]{1,0:T(8,128)} custom-call(s32[3]{0:T(128)S(1)} %pad_add_fusion.place, f32[128,256]{1,0:T(8,128)S(1)} %get-tuple-element.37.mine, f32[128,256]{1,0:T(8,128)S(1)} %collective-permute-done.14.other), custom_call_target="tpu_custom_call" | custom-call | tf_op jit(solution)/shard_map/panel_lines/pallas_call | solution.py:269
  55.3 1.2 %diag_lines.1 = f32[256,128]{1,0:T(8,128)} custom-call(s32[3]{0:T(128)S(1)} %pad_add_fusion.place, f32[64,256]{1,0:T(8,128)S(1)} %get-tuple-element.56.keep, f32[64,256]{1,0:T(8,128)S(1)} %collective-permute-done.17.met, f32[64,256]{1,0:T(8,128)S(1)} %collective-permute-done.18.far), custom_call_target="tpu_custom_call" | custom-call | tf_op jit(solution)/shard_map/diag_lines/pallas_call | solution.py:269
  (30 shorter events, 2.4 us)
Async XLA Ops:
  0.6 5.3 %copy-start = (f32[128,4,1,128]{3,2,1,0:T(1,128)S(1)}, f32[128,4,1,128]{3,2,1,0:T(1,128)}, u32[]{:S(2)}) copy-start(f32[128,4,1,128]{3,2,1,0:T(1,128)} %param.5) | copy-start | bytes 786436
  1.8 15.0 %collective-permute-start.1 = (f32[320,128]{1,0:T(8,128)S(1)}, f32[320,128]{1,0:T(8,128)S(1)}, u32[]{:S(2)}, u32[]{:S(2)}) collective-permute-start(f32[320,128]{1,0:T(8,128)S(1)} %get-tuple-element.31), channel_id=1, source_target_pairs={{0,10},{1,11},{2,8},{3,9},{4,14},{5,15},{6,12},{7,13},{8,2},{9,3},... | collective-permute-start | bytes 491528 | tf_op jit(solution)/shard_map/ppermute | solution.py:286
  6.0 15.7 %collective-permute-start.2 = (f32[512,128]{1,0:T(8,128)S(1)}, f32[512,128]{1,0:T(8,128)S(1)}, u32[]{:S(2)}, u32[]{:S(2)}) collective-permute-start(f32[512,128]{1,0:T(8,128)S(1)} %bitcast.21), channel_id=1, source_target_pairs={{0,1},{1,0},{2,3},{3,2},{4,5},{5,4},{6,7},{7,6},{8,9},{9,8},{10,11... | collective-permute-start | bytes 786440 | tf_op jit(solution)/shard_map/ppermute | solution.py:286
  6.9 20.7 %collective-permute-start.7 = (f32[832,128]{1,0:T(8,128)S(1)}, f32[832,128]{1,0:T(8,128)S(1)}, u32[]{:S(2)}, u32[]{:S(2)}) collective-permute-start(f32[832,128]{1,0:T(8,128)S(1)} %get-tuple-element.33), channel_id=1, source_target_pairs={{0,2},{1,3},{2,0},{3,1},{4,6},{5,7},{6,4},{7,5},{8,10},{9,11},{10,... | collective-permute-start | bytes 1277960 | tf_op jit(solution)/shard_map/ppermute | solution.py:286
  7.2 13.0 %collective-permute-start = (f32[320,128]{1,0:T(8,128)S(1)}, f32[320,128]{1,0:T(8,128)S(1)}, u32[]{:S(2)}, u32[]{:S(2)}) collective-permute-start(f32[320,128]{1,0:T(8,128)S(1)} %get-tuple-element.30.refs_0_), channel_id=1, source_target_pairs={{0,8},{1,9},{2,10},{3,11},{4,12},{5,13},{6,14},{7,15},{8,0},{9,1},... | collective-permute-start | bytes 491528 | tf_op jit(solution)/shard_map/ppermute | solution.py:286
  7.2 14.5 %collective-permute-start.4 = (f32[320,128]{1,0:T(8,128)S(1)}, f32[320,128]{1,0:T(8,128)S(1)}, u32[]{:S(2)}, u32[]{:S(2)}) collective-permute-start(f32[320,128]{1,0:T(8,128)S(1)} %get-tuple-element.31), channel_id=1, source_target_pairs={{0,6},{1,7},{2,4},{3,5},{4,2},{5,3},{6,0},{7,1},{8,14},{9,15},{10,... | collective-permute-start | bytes 491528 | tf_op jit(solution)/shard_map/ppermute | solution.py:286
  16.8 7.1 %collective-permute-start.3 = (f32[320,128]{1,0:T(8,128)S(1)}, f32[320,128]{1,0:T(8,128)S(1)}, u32[]{:S(2)}, u32[]{:S(2)}) collective-permute-start(f32[320,128]{1,0:T(8,128)S(1)} %get-tuple-element.30.refs_0_), channel_id=1, source_target_pairs={{0,4},{1,5},{2,6},{3,7},{4,0},{5,1},{6,2},{7,3},{8,12},{9,13},{10,... | collective-permute-start | bytes 491528 | tf_op jit(solution)/shard_map/ppermute | solution.py:286
  20.2 7.9 %collective-permute-start.5 = (f32[320,128]{1,0:T(8,128)S(1)}, f32[320,128]{1,0:T(8,128)S(1)}, u32[]{:S(2)}, u32[]{:S(2)}) collective-permute-start(f32[320,128]{1,0:T(8,128)S(1)} %collective-permute-done.refs_1_), channel_id=1, source_target_pairs={{0,4},{1,5},{2,6},{3,7},{4,0},{5,1},{6,2},{7,3},{8,12},{9,13},{10,... | collective-permute-start | bytes 491528 | tf_op jit(solution)/shard_map/ppermute | solution.py:286
  21.6 9.3 %collective-permute-start.6 = (f32[320,128]{1,0:T(8,128)S(1)}, f32[320,128]{1,0:T(8,128)S(1)}, u32[]{:S(2)}, u32[]{:S(2)}) collective-permute-start(f32[320,128]{1,0:T(8,128)S(1)} %collective-permute-done.1.refs_2_), channel_id=1, source_target_pairs={{0,4},{1,5},{2,6},{3,7},{4,0},{5,1},{6,2},{7,3},{8,12},{9,13},{10,... | collective-permute-start | bytes 491528 | tf_op jit(solution)/shard_map/ppermute | solution.py:286
  24.6 9.9 %collective-permute-start.9 = (f32[640,128]{1,0:T(8,128)}, f32[640,128]{1,0:T(8,128)S(1)}, u32[]{:S(2)}, u32[]{:S(2)}) collective-permute-start(f32[640,128]{1,0:T(8,128)} %pad_maximum_fusion.1), channel_id=1, source_target_pairs={{0,1},{1,0},{2,3},{3,2},{4,5},{5,4},{6,7},{7,6},{8,9},{9,8},{10,11... | collective-permute-start | bytes 983048 | tf_op jit(solution)/shard_map/ppermute | solution.py:286
  27.6 6.9 %collective-permute-start.8 = (f32[640,128]{1,0:T(8,128)}, f32[640,128]{1,0:T(8,128)S(1)}, u32[]{:S(2)}, u32[]{:S(2)}) collective-permute-start(f32[640,128]{1,0:T(8,128)} %pad_maximum_fusion), channel_id=1, source_target_pairs={{0,1},{1,0},{2,3},{3,2},{4,5},{5,4},{6,7},{7,6},{8,9},{9,8},{10,11... | collective-permute-start | bytes 983048 | tf_op jit(solution)/shard_map/ppermute | solution.py:286
  27.6 7.1 %collective-permute-start.12 = (f32[832,128]{1,0:T(8,128)S(1)}, f32[832,128]{1,0:T(8,128)S(1)}, u32[]{:S(2)}, u32[]{:S(2)}) collective-permute-start(f32[832,128]{1,0:T(8,128)S(1)} %collective-permute-done.7.refs_7_), channel_id=1, source_target_pairs={{0,1},{1,0},{2,3},{3,2},{4,5},{5,4},{6,7},{7,6},{8,9},{9,8},{10,11... | collective-permute-start | bytes 1277960 | tf_op jit(solution)/shard_map/ppermute | solution.py:286
  31.7 3.0 %collective-permute-start.11 = (f32[640,128]{1,0:T(8,128)}, f32[640,128]{1,0:T(8,128)S(1)}, u32[]{:S(2)}, u32[]{:S(2)}) collective-permute-start(f32[640,128]{1,0:T(8,128)} %pad_maximum_fusion.2), channel_id=1, source_target_pairs={{0,1},{1,0},{2,3},{3,2},{4,5},{5,4},{6,7},{7,6},{8,9},{9,8},{10,11... | collective-permute-start | bytes 983048 | tf_op jit(solution)/shard_map/ppermute | solution.py:286
  33.0 1.5 %collective-permute-start.10 = (f32[320,128]{1,0:T(8,128)S(1)}, f32[320,128]{1,0:T(8,128)}, u32[]{:S(2)}, u32[]{:S(2)}) collective-permute-start(f32[320,128]{1,0:T(8,128)S(1)} %get-tuple-element.30.refs_0_), channel_id=1, source_target_pairs={{0,1},{1,0},{2,3},{3,2},{4,5},{5,4},{6,7},{7,6},{8,9},{9,8},{10,11... | collective-permute-start | bytes 491528 | tf_op jit(solution)/shard_map/ppermute | solution.py:286
  33.0 1.7 %copy-start.1 = (s32[2,6]{1,0:T(2,128)S(1)}, s32[2,6]{1,0:T(2,128)}, u32[]{:S(2)}) copy-start(s32[2,6]{1,0:T(2,128)} %structure.3) | copy-start | bytes 148
  33.0 1.7 %copy-start.2 = (s32[2]{0:T(128)S(1)}, s32[2]{0:T(128)}, u32[]{:S(2)}) copy-start(s32[2]{0:T(128)} %live.3) | copy-start | bytes 28
  37.8 3.7 %collective-permute-start.13 = (f32[128,128]{1,0:T(8,128)S(1)}, f32[128,128]{1,0:T(8,128)S(1)}, u32[]{:S(2)}, u32[]{:S(2)}) collective-permute-start(f32[128,128]{1,0:T(8,128)S(1)} %get-tuple-element.39), channel_id=1, source_target_pairs={{0,4},{1,5},{2,6},{3,7},{4,0},{5,1},{6,2},{7,3},{8,12},{9,13},{10,... | collective-permute-start | bytes 196616 | tf_op jit(solution)/shard_map/ppermute | solution.py:286
  37.9 6.3 %collective-permute-start.15 = (f32[128,128]{1,0:T(8,128)S(1)}, f32[128,128]{1,0:T(8,128)S(1)}, u32[]{:S(2)}, u32[]{:S(2)}) collective-permute-start(f32[128,128]{1,0:T(8,128)S(1)} %get-tuple-element.43), channel_id=1, source_target_pairs={{0,8},{1,9},{2,10},{3,11},{4,12},{5,13},{6,14},{7,15},{8,0},{9,1},... | collective-permute-start | bytes 196616 | tf_op jit(solution)/shard_map/ppermute | solution.py:286
  41.4 5.0 %collective-permute-start.16 = (f32[128,128]{1,0:T(8,128)S(1)}, f32[128,128]{1,0:T(8,128)S(1)}, u32[]{:S(2)}, u32[]{:S(2)}) collective-permute-start(f32[128,128]{1,0:T(8,128)S(1)} %get-tuple-element.44), channel_id=1, source_target_pairs={{0,12},{1,13},{2,14},{3,15},{4,8},{5,9},{6,10},{7,11},{8,4},{9,5},... | collective-permute-start | bytes 196616 | tf_op jit(solution)/shard_map/ppermute | solution.py:286
  41.5 11.9 %collective-permute-start.14 = (f32[128,256]{1,0:T(8,128)S(1)}, f32[128,256]{1,0:T(8,128)S(1)}, u32[]{:S(2)}, u32[]{:S(2)}) collective-permute-start(f32[128,256]{1,0:T(8,128)S(1)} %get-tuple-element.40), channel_id=1, source_target_pairs={{0,2},{1,3},{2,0},{3,1},{4,6},{5,7},{6,4},{7,5},{8,10},{9,11},{10,... | collective-permute-start | bytes 393224 | tf_op jit(solution)/shard_map/ppermute | solution.py:286
  47.8 6.9 %collective-permute-start.17 = (f32[64,256]{1,0:T(8,128)S(1)}, f32[64,256]{1,0:T(8,128)S(1)}, u32[]{:S(2)}, u32[]{:S(2)}) collective-permute-start(f32[64,256]{1,0:T(8,128)S(1)} %get-tuple-element.57), channel_id=1, source_target_pairs={{0,1},{1,3},{2,0},{3,2},{4,5},{5,7},{6,4},{7,6},{8,9},{9,11},{10,8... | collective-permute-start | bytes 196616 | tf_op jit(solution)/shard_map/ppermute | solution.py:286
  48.1 7.3 %collective-permute-start.18 = (f32[64,256]{1,0:T(8,128)S(1)}, f32[64,256]{1,0:T(8,128)S(1)}, u32[]{:S(2)}, u32[]{:S(2)}) collective-permute-start(f32[64,256]{1,0:T(8,128)S(1)} %get-tuple-element.56.keep), channel_id=1, source_target_pairs={{1,2},{2,1},{5,6},{6,5},{9,10},{10,9},{13,14},{14,13},{17,18},{18,... | collective-permute-start | bytes 196616 | tf_op jit(solution)/shard_map/ppermute | solution.py:286

commit v13 on v10

--- a/solution.py
+++ b/solution.py
@@ -13,7 +13,7 @@
 NN = (((1,), (0,)), ((), ()))
 TN = (((0,), (0,)), ((), ()))
 VMEM_LIMIT = 20 * 1024 * 1024
-THERE = ((2, 0), (0, 0), (0, 1), (1, 0), (1, 1), (3, 0), (3, 1))
+THERE = ((2, 0), (0, 0), (0, 1), (1, 0), (1, 1), (3, 0), (2, 1))
 
 
 def halves(value):
@@ -315,7 +315,6 @@
     near_side = move(send, 1, 1, 0)
     near = move(send_near, 0, 1, 0)
     own_opposite = move(own_far, 1, 0, 0)
-    near_far, near = lax.optimization_barrier((near_far, near))
     near_opposite = move(near_far, 1, 0, 0)
     c_sib = move(c_own, 0, 0, 1)
     near_in, c_sib = lax.optimization_barrier((near, c_sib))
@@ -323,8 +322,8 @@
     theirs = [
         move(jnp.concatenate([own_far, near_far]), 0, 0, 1),
         move(jnp.concatenate([own_side, near_side]), 0, 0, 1),
-        move(own, 0, 0, 1),
-        move(jnp.concatenate([own_opposite, near_opposite]), 0, 0, 1),
+        move(jnp.concatenate([own, near_opposite]), 0, 0, 1),
+        move(own_opposite, 0, 0, 1),
         move(near_in, 0, 0, 1),
         c_sib,
     ]

time: 56 us -> 53.7 us (0.959)
  waiting for transfers between devices: 15.3 us -> 10.1 us
  starting transfers between devices: 27.2 us -> 30 us
    ppermute x19, waiting for transfers between devices: 15.3 us -> 10.1 us  [send_to(): return lax.ppermute(value, ('row', 'col'), pairs)]
    ppermute x19, starting transfers between devices: 27.2 us -> 30 us  [send_to(): return lax.ppermute(value, ('row', 'col'), pairs)]
  transfers between devices with their start and end apart: 19 -> 19, of which waited for: 6 -> 7; matrix products, arithmetic and copies ran while one was open for 4% -> 4% of each run, Pallas kernels for 9% -> 9%
where the time goes in v13:
time: 53.7 us; the launch traced here: 53.5 us
  starting transfers between devices  30 us (56%)
  Pallas kernels  10.4 us (19%)
  waiting for transfers between devices  10.1 us (19%)
  other arithmetic  2.3 us (4%)
  between operations  0.74 us (1%)
    ppermute x19, starting transfers between devices, send_to(): return lax.ppermute(value, ('row', 'col'), pairs)  30 us
    pallas_call x6, Pallas kernels, call(): pl.pallas_call(kernel, out_shape=outs, in_specs=[smem] * len(scalars) + [...  10.4 us
    ppermute x19, waiting for transfers between devices, send_to(): return lax.ppermute(value, ('row', 'col'), pairs)  10.1 us
  transfers between devices with their start and end apart: 19, of which 7 were waited for; matrix products, arithmetic and copies ran while one was open for 4% of the time, Pallas kernels for 9%

profile of v13, /device:TPU:1, one launch (start us, length us, event | category | flops | bytes accessed | tf_op | source)
XLA Modules:
  0.0 53.5 jit_solution(16653547686784257830)
XLA Ops:
  0.6 1.2 %pack.1 = (f32[320,128]{1,0:T(8,128)S(1)}, f32[320,128]{1,0:T(8,128)S(1)}, f32[832,128]{1,0:T(8,128)S(1)}) custom-call(f32[384,128]{1,0:T(8,128)} %bitcast.25, f32[2,64,512]{2,1,0:T(8,128)} %bitcast.24, f32[512,128]{1,0:T(8,128)} %bitcast.20), custom_call_target="tpu_custom_call" | custom-call | tf_op jit(solution)/shard_map/pack/pallas_call | solution.py:269
  1.8 3.1 %collective-permute-start.3 = (f32[320,128]{1,0:T(8,128)S(1)}, f32[320,128]{1,0:T(8,128)S(1)}, u32[]{:S(2)}, u32[]{:S(2)}) collective-permute-start(f32[320,128]{1,0:T(8,128)S(1)} %get-tuple-element.29), channel_id=1, source_target_pairs={{0,6},{1,7},{2,4},{3,5},{4,2},{5,3},{6,0},{7,1},{8,14},{9,15},{10,... | collective-permute-start | bytes 491528 | tf_op jit(solution)/shard_map/ppermute | solution.py:286
  5.2 3.2 %collective-permute-start.1 = (f32[320,128]{1,0:T(8,128)S(1)}, f32[320,128]{1,0:T(8,128)S(1)}, u32[]{:S(2)}, u32[]{:S(2)}) collective-permute-start(f32[320,128]{1,0:T(8,128)S(1)} %get-tuple-element.29), channel_id=1, source_target_pairs={{0,10},{1,11},{2,8},{3,9},{4,14},{5,15},{6,12},{7,13},{8,2},{9,3},... | collective-permute-start | bytes 491528 | tf_op jit(solution)/shard_map/ppermute | solution.py:286
  8.9 1.9 %collective-permute-start.11 = (f32[512,128]{1,0:T(8,128)S(1)}, f32[512,128]{1,0:T(8,128)S(1)}, u32[]{:S(2)}, u32[]{:S(2)}) collective-permute-start(f32[512,128]{1,0:T(8,128)S(1)} %bitcast.21), channel_id=1, source_target_pairs={{0,1},{1,0},{2,3},{3,2},{4,5},{5,4},{6,7},{7,6},{8,9},{9,8},{10,11... | collective-permute-start | bytes 786440 | tf_op jit(solution)/shard_map/ppermute | solution.py:286
  10.7 2.1 %collective-permute-done.1.refs_2_ = f32[320,128]{1,0:T(8,128)S(1)} collective-permute-done((f32[320,128]{1,0:T(8,128)S(1)}, f32[320,128]{1,0:T(8,128)S(1)}, u32[]{:S(2)}, u32[]{:S(2)}) %collective-permute-start.1) | collective-permute-done | bytes 163872 | tf_op jit(solution)/shard_map/ppermute | solution.py:286
  12.9 1.7 %collective-permute-start.5 = (f32[320,128]{1,0:T(8,128)S(1)}, f32[320,128]{1,0:T(8,128)S(1)}, u32[]{:S(2)}, u32[]{:S(2)}) collective-permute-start(f32[320,128]{1,0:T(8,128)S(1)} %collective-permute-done.1.refs_2_), channel_id=1, source_target_pairs={{0,4},{1,5},{2,6},{3,7},{4,0},{5,1},{6,2},{7,3},{8,12},{9,13},{10,... | collective-permute-start | bytes 491528 | tf_op jit(solution)/shard_map/ppermute | solution.py:286
  14.9 0.7 %pad_maximum_fusion.1 = f32[640,128]{1,0:T(8,128)} fusion(f32[320,128]{1,0:T(8,128)S(1)} %collective-permute-done.3.refs_4_, f32[320,128]{1,0:T(8,128)S(1)} %collective-permute-done.2.refs_3_), kind=kLoop, calls=%fused_computation.1 | loop fusion | flops 81920 | bytes 655360 | tf_op jit(solution)/shard_map/concatenate | solution.py:324
  15.6 4.7 %collective-permute-start.8 = (f32[640,128]{1,0:T(8,128)}, f32[640,128]{1,0:T(8,128)S(1)}, u32[]{:S(2)}, u32[]{:S(2)}) collective-permute-start(f32[640,128]{1,0:T(8,128)} %pad_maximum_fusion.1), channel_id=1, source_target_pairs={{0,1},{1,0},{2,3},{3,2},{4,5},{5,4},{6,7},{7,6},{8,9},{9,8},{10,11... | collective-permute-start | bytes 983048 | tf_op jit(solution)/shard_map/ppermute | solution.py:286
  20.3 0.7 %pad_maximum_fusion = f32[640,128]{1,0:T(8,128)} fusion(f32[320,128]{1,0:T(8,128)S(1)} %collective-permute-done.1.refs_2_, f32[320,128]{1,0:T(8,128)S(1)} %collective-permute-done.refs_1_), kind=kLoop, calls=%fused_computation | loop fusion | flops 81920 | bytes 655360 | tf_op jit(solution)/shard_map/concatenate | solution.py:323
  21.1 4.0 %collective-permute-start.7 = (f32[640,128]{1,0:T(8,128)}, f32[640,128]{1,0:T(8,128)S(1)}, u32[]{:S(2)}, u32[]{:S(2)}) collective-permute-start(f32[640,128]{1,0:T(8,128)} %pad_maximum_fusion), channel_id=1, source_target_pairs={{0,1},{1,0},{2,3},{3,2},{4,5},{5,4},{6,7},{7,6},{8,9},{9,8},{10,11... | collective-permute-start | bytes 983048 | tf_op jit(solution)/shard_map/ppermute | solution.py:286
  25.4 0.7 %pad_maximum_fusion.2 = f32[640,128]{1,0:T(8,128)} fusion(f32[320,128]{1,0:T(8,128)S(1)} %collective-permute-done.5.refs_6_, f32[320,128]{1,0:T(8,128)S(1)} %get-tuple-element.28.refs_0_), kind=kLoop, calls=%fused_computation.2 | loop fusion | flops 81920 | bytes 655360 | tf_op jit(solution)/shard_map/concatenate | solution.py:325
  26.4 4.5 %collective-permute-done.4.refs_5_ = f32[320,128]{1,0:T(8,128)S(1)} collective-permute-done((f32[320,128]{1,0:T(8,128)S(1)}, f32[320,128]{1,0:T(8,128)S(1)}, u32[]{:S(2)}, u32[]{:S(2)}) %collective-permute-start.4) | collective-permute-done | bytes 163872 | tf_op jit(solution)/shard_map/ppermute | solution.py:286
  30.9 0.8 %collective-permute-start.10 = (f32[320,128]{1,0:T(8,128)S(1)}, f32[320,128]{1,0:T(8,128)}, u32[]{:S(2)}, u32[]{:S(2)}) collective-permute-start(f32[320,128]{1,0:T(8,128)S(1)} %collective-permute-done.4.refs_5_), channel_id=1, source_target_pairs={{0,1},{1,0},{2,3},{3,2},{4,5},{5,4},{6,7},{7,6},{8,9},{9,8},{10,11... | collective-permute-start | bytes 491528 | tf_op jit(solution)/shard_map/ppermute | solution.py:286
  31.8 1.1 %collective-permute-done.10.refs_11_ = f32[320,128]{1,0:T(8,128)} collective-permute-done((f32[320,128]{1,0:T(8,128)S(1)}, f32[320,128]{1,0:T(8,128)}, u32[]{:S(2)}, u32[]{:S(2)}) %collective-permute-start.10) | collective-permute-done | bytes 163872 | tf_op jit(solution)/shard_map/ppermute | solution.py:286
  32.9 3.1 %products.1 = (f32[128,256]{1,0:T(8,128)S(1)}, f32[128,256]{1,0:T(8,128)S(1)}, f32[128,128]{1,0:T(8,128)S(1)}, f32[128,128]{1,0:T(8,128)S(1)}, f32[128,128]{1,0:...) custom-call(s32[2,6]{1,0:T(2,128)S(1)} %copy-done.1, ...), custom_call_target="tpu_custom_call" | custom-call | tf_op jit(solution)/shard_map/products/pallas_call | solution.py:269
  36.1 2.3 %collective-permute-start.15 = (f32[128,128]{1,0:T(8,128)S(1)}, f32[128,128]{1,0:T(8,128)S(1)}, u32[]{:S(2)}, u32[]{:S(2)}) collective-permute-start(f32[128,128]{1,0:T(8,128)S(1)} %get-tuple-element.39), channel_id=1, source_target_pairs={{0,8},{1,9},{2,10},{3,11},{4,12},{5,13},{6,14},{7,15},{8,0},{9,1},... | collective-permute-start | bytes 196616 | tf_op jit(solution)/shard_map/ppermute | solution.py:286
  38.5 1.2 %collective-permute-start.16 = (f32[128,128]{1,0:T(8,128)S(1)}, f32[128,128]{1,0:T(8,128)S(1)}, u32[]{:S(2)}, u32[]{:S(2)}) collective-permute-start(f32[128,128]{1,0:T(8,128)S(1)} %get-tuple-element.40), channel_id=1, source_target_pairs={{0,12},{1,13},{2,14},{3,15},{4,8},{5,9},{6,10},{7,11},{8,4},{9,5},... | collective-permute-start | bytes 196616 | tf_op jit(solution)/shard_map/ppermute | solution.py:286
  39.9 2.3 %scaled.1 = (bf16[768,512]{1,0:T(8,128)(2,1)S(1)}, bf16[768,512]{1,0:T(8,128)(2,1)S(1)}, f32[64,512]{1,0:T(8,128)S(1)}) custom-call(s32[3]{0:T(128)S(1)} %pad_add_fusion.place, bf16[768,512]{1,0:T(8,128)(2,1)S(1)} %get-tuple-element.41.f_high, bf16[768,512]{1,0:T(8,128)(2,1)S(1)} %get-tuple-element.42.f_low, bf16[512,512]{1,0:T(8,128)(2,1)S(1)} %get-tuple-element.43.d_high, ...), custom_call_target="tpu_custom_call" | custom-call | tf_op jit(solution)/shard_map/scaled/pallas_call | solution.py:269
  42.2 1.1 %collective-permute-done.16.w3 = f32[128,128]{1,0:T(8,128)S(1)} collective-permute-done((f32[128,128]{1,0:T(8,128)S(1)}, f32[128,128]{1,0:T(8,128)S(1)}, u32[]{:S(2)}, u32[]{:S(2)}) %collective-permute-start.16) | collective-permute-done | bytes 65568 | tf_op jit(solution)/shard_map/ppermute | solution.py:286
  43.4 1.3 %diag_block.1 = (f32[64,256]{1,0:T(8,128)S(1)}, f32[64,256]{1,0:T(8,128)S(1)}) custom-call(s32[2,6]{1,0:T(2,128)S(1)} %copy-done.1, s32[2]{0:T(128)S(1)} %copy-done.2, s32[3]{0:T(128)S(1)} %pad_add_fusion.place, f32[128,128]{1,0:T(8,128)S(1)} %get-tuple-element.37.w0, f32[128,128]{1,0:T(8,128)S(1)} %collective-permute-done.13.w1, ...), custom_call_target="tpu_custom_call" | custom-call | tf_op jit(solution)/shard_map/diag_block/pallas_call | solution.py:269
  44.9 5.5 %collective-permute-start.18 = (f32[64,256]{1,0:T(8,128)S(1)}, f32[64,256]{1,0:T(8,128)S(1)}, u32[]{:S(2)}, u32[]{:S(2)}) collective-permute-start(f32[64,256]{1,0:T(8,128)S(1)} %get-tuple-element.52.keep), channel_id=1, source_target_pairs={{1,2},{2,1},{5,6},{6,5},{9,10},{10,9},{13,14},{14,13},{17,18},{18,... | collective-permute-start | bytes 196616 | tf_op jit(solution)/shard_map/ppermute | solution.py:286
  50.4 1.3 %panel_lines.1 = f32[512,128]{1,0:T(8,128)} custom-call(s32[3]{0:T(128)S(1)} %pad_add_fusion.place, f32[128,256]{1,0:T(8,128)S(1)} %get-tuple-element.33.mine, f32[128,256]{1,0:T(8,128)S(1)} %collective-permute-done.14.other), custom_call_target="tpu_custom_call" | custom-call | tf_op jit(solution)/shard_map/panel_lines/pallas_call | solution.py:269
  51.7 0.6 %collective-permute-done.18.far = f32[64,256]{1,0:T(8,128)S(1)} collective-permute-done((f32[64,256]{1,0:T(8,128)S(1)}, f32[64,256]{1,0:T(8,128)S(1)}, u32[]{:S(2)}, u32[]{:S(2)}) %collective-permute-start.18) | collective-permute-done | bytes 65568 | tf_op jit(solution)/shard_map/ppermute | solution.py:286
  52.3 1.2 %diag_lines.1 = f32[256,128]{1,0:T(8,128)} custom-call(s32[3]{0:T(128)S(1)} %pad_add_fusion.place, f32[64,256]{1,0:T(8,128)S(1)} %get-tuple-element.52.keep, f32[64,256]{1,0:T(8,128)S(1)} %collective-permute-done.17.met, f32[64,256]{1,0:T(8,128)S(1)} %collective-permute-done.18.far), custom_call_target="tpu_custom_call" | custom-call | tf_op jit(solution)/shard_map/diag_lines/pallas_call | solution.py:269
  (30 shorter events, 2.3 us)
Async XLA Ops:
  0.6 8.2 %copy-start = (f32[128,4,1,128]{3,2,1,0:T(1,128)S(1)}, f32[128,4,1,128]{3,2,1,0:T(1,128)}, u32[]{:S(2)}) copy-start(f32[128,4,1,128]{3,2,1,0:T(1,128)} %param.5) | copy-start | bytes 786436
  1.8 7.0 %collective-permute-start.3 = (f32[320,128]{1,0:T(8,128)S(1)}, f32[320,128]{1,0:T(8,128)S(1)}, u32[]{:S(2)}, u32[]{:S(2)}) collective-permute-start(f32[320,128]{1,0:T(8,128)S(1)} %get-tuple-element.29), channel_id=1, source_target_pairs={{0,6},{1,7},{2,4},{3,5},{4,2},{5,3},{6,0},{7,1},{8,14},{9,15},{10,... | collective-permute-start | bytes 491528 | tf_op jit(solution)/shard_map/ppermute | solution.py:286
  4.9 20.2 %collective-permute-start.6 = (f32[832,128]{1,0:T(8,128)S(1)}, f32[832,128]{1,0:T(8,128)S(1)}, u32[]{:S(2)}, u32[]{:S(2)}) collective-permute-start(f32[832,128]{1,0:T(8,128)S(1)} %get-tuple-element.30), channel_id=1, source_target_pairs={{0,2},{1,3},{2,0},{3,1},{4,6},{5,7},{6,4},{7,5},{8,10},{9,11},{10,... | collective-permute-start | bytes 1277960 | tf_op jit(solution)/shard_map/ppermute | solution.py:286
  5.2 7.7 %collective-permute-start.1 = (f32[320,128]{1,0:T(8,128)S(1)}, f32[320,128]{1,0:T(8,128)S(1)}, u32[]{:S(2)}, u32[]{:S(2)}) collective-permute-start(f32[320,128]{1,0:T(8,128)S(1)} %get-tuple-element.29), channel_id=1, source_target_pairs={{0,10},{1,11},{2,8},{3,9},{4,14},{5,15},{6,12},{7,13},{8,2},{9,3},... | collective-permute-start | bytes 491528 | tf_op jit(solution)/shard_map/ppermute | solution.py:286
  8.4 6.5 %collective-permute-start.2 = (f32[320,128]{1,0:T(8,128)S(1)}, f32[320,128]{1,0:T(8,128)S(1)}, u32[]{:S(2)}, u32[]{:S(2)}) collective-permute-start(f32[320,128]{1,0:T(8,128)S(1)} %get-tuple-element.28.refs_0_), channel_id=1, source_target_pairs={{0,4},{1,5},{2,6},{3,7},{4,0},{5,1},{6,2},{7,3},{8,12},{9,13},{10,... | collective-permute-start | bytes 491528 | tf_op jit(solution)/shard_map/ppermute | solution.py:286
  8.6 11.7 %collective-permute-start = (f32[320,128]{1,0:T(8,128)S(1)}, f32[320,128]{1,0:T(8,128)S(1)}, u32[]{:S(2)}, u32[]{:S(2)}) collective-permute-start(f32[320,128]{1,0:T(8,128)S(1)} %get-tuple-element.28.refs_0_), channel_id=1, source_target_pairs={{0,8},{1,9},{2,10},{3,11},{4,12},{5,13},{6,14},{7,15},{8,0},{9,1},... | collective-permute-start | bytes 491528 | tf_op jit(solution)/shard_map/ppermute | solution.py:286
  8.9 16.2 %collective-permute-start.11 = (f32[512,128]{1,0:T(8,128)S(1)}, f32[512,128]{1,0:T(8,128)S(1)}, u32[]{:S(2)}, u32[]{:S(2)}) collective-permute-start(f32[512,128]{1,0:T(8,128)S(1)} %bitcast.21), channel_id=1, source_target_pairs={{0,1},{1,0},{2,3},{3,2},{4,5},{5,4},{6,7},{7,6},{8,9},{9,8},{10,11... | collective-permute-start | bytes 786440 | tf_op jit(solution)/shard_map/ppermute | solution.py:286
  12.9 12.6 %collective-permute-start.5 = (f32[320,128]{1,0:T(8,128)S(1)}, f32[320,128]{1,0:T(8,128)S(1)}, u32[]{:S(2)}, u32[]{:S(2)}) collective-permute-start(f32[320,128]{1,0:T(8,128)S(1)} %collective-permute-done.1.refs_2_), channel_id=1, source_target_pairs={{0,4},{1,5},{2,6},{3,7},{4,0},{5,1},{6,2},{7,3},{8,12},{9,13},{10,... | collective-permute-start | bytes 491528 | tf_op jit(solution)/shard_map/ppermute | solution.py:286
  15.6 17.2 %collective-permute-start.8 = (f32[640,128]{1,0:T(8,128)}, f32[640,128]{1,0:T(8,128)S(1)}, u32[]{:S(2)}, u32[]{:S(2)}) collective-permute-start(f32[640,128]{1,0:T(8,128)} %pad_maximum_fusion.1), channel_id=1, source_target_pairs={{0,1},{1,0},{2,3},{3,2},{4,5},{5,4},{6,7},{7,6},{8,9},{9,8},{10,11... | collective-permute-start | bytes 983048 | tf_op jit(solution)/shard_map/ppermute | solution.py:286
  21.1 11.8 %collective-permute-start.7 = (f32[640,128]{1,0:T(8,128)}, f32[640,128]{1,0:T(8,128)S(1)}, u32[]{:S(2)}, u32[]{:S(2)}) collective-permute-start(f32[640,128]{1,0:T(8,128)} %pad_maximum_fusion), channel_id=1, source_target_pairs={{0,1},{1,0},{2,3},{3,2},{4,5},{5,4},{6,7},{7,6},{8,9},{9,8},{10,11... | collective-permute-start | bytes 983048 | tf_op jit(solution)/shard_map/ppermute | solution.py:286
  25.1 5.8 %collective-permute-start.4 = (f32[320,128]{1,0:T(8,128)S(1)}, f32[320,128]{1,0:T(8,128)S(1)}, u32[]{:S(2)}, u32[]{:S(2)}) collective-permute-start(f32[320,128]{1,0:T(8,128)S(1)} %collective-permute-done.refs_1_), channel_id=1, source_target_pairs={{0,4},{1,5},{2,6},{3,7},{4,0},{5,1},{6,2},{7,3},{8,12},{9,13},{10,... | collective-permute-start | bytes 491528 | tf_op jit(solution)/shard_map/ppermute | solution.py:286
  25.1 7.8 %collective-permute-start.12 = (f32[832,128]{1,0:T(8,128)S(1)}, f32[832,128]{1,0:T(8,128)S(1)}, u32[]{:S(2)}, u32[]{:S(2)}) collective-permute-start(f32[832,128]{1,0:T(8,128)S(1)} %collective-permute-done.6.refs_7_), channel_id=1, source_target_pairs={{0,1},{1,0},{2,3},{3,2},{4,5},{5,4},{6,7},{7,6},{8,9},{9,8},{10,11... | collective-permute-start | bytes 1277960 | tf_op jit(solution)/shard_map/ppermute | solution.py:286
  26.2 6.7 %collective-permute-start.9 = (f32[640,128]{1,0:T(8,128)}, f32[640,128]{1,0:T(8,128)S(1)}, u32[]{:S(2)}, u32[]{:S(2)}) collective-permute-start(f32[640,128]{1,0:T(8,128)} %pad_maximum_fusion.2), channel_id=1, source_target_pairs={{0,1},{1,0},{2,3},{3,2},{4,5},{5,4},{6,7},{7,6},{8,9},{9,8},{10,11... | collective-permute-start | bytes 983048 | tf_op jit(solution)/shard_map/ppermute | solution.py:286
  30.9 1.9 %collective-permute-start.10 = (f32[320,128]{1,0:T(8,128)S(1)}, f32[320,128]{1,0:T(8,128)}, u32[]{:S(2)}, u32[]{:S(2)}) collective-permute-start(f32[320,128]{1,0:T(8,128)S(1)} %collective-permute-done.4.refs_5_), channel_id=1, source_target_pairs={{0,1},{1,0},{2,3},{3,2},{4,5},{5,4},{6,7},{7,6},{8,9},{9,8},{10,11... | collective-permute-start | bytes 491528 | tf_op jit(solution)/shard_map/ppermute | solution.py:286
  31.7 1.2 %copy-start.1 = (s32[2,6]{1,0:T(2,128)S(1)}, s32[2,6]{1,0:T(2,128)}, u32[]{:S(2)}) copy-start(s32[2,6]{1,0:T(2,128)} %structure.3) | copy-start | bytes 148
  31.7 1.2 %copy-start.2 = (s32[2]{0:T(128)S(1)}, s32[2]{0:T(128)}, u32[]{:S(2)}) copy-start(s32[2]{0:T(128)} %live.3) | copy-start | bytes 28
  36.0 3.6 %collective-permute-start.13 = (f32[128,128]{1,0:T(8,128)S(1)}, f32[128,128]{1,0:T(8,128)S(1)}, u32[]{:S(2)}, u32[]{:S(2)}) collective-permute-start(f32[128,128]{1,0:T(8,128)S(1)} %get-tuple-element.35), channel_id=1, source_target_pairs={{0,4},{1,5},{2,6},{3,7},{4,0},{5,1},{6,2},{7,3},{8,12},{9,13},{10,... | collective-permute-start | bytes 196616 | tf_op jit(solution)/shard_map/ppermute | solution.py:286
  36.1 6.1 %collective-permute-start.15 = (f32[128,128]{1,0:T(8,128)S(1)}, f32[128,128]{1,0:T(8,128)S(1)}, u32[]{:S(2)}, u32[]{:S(2)}) collective-permute-start(f32[128,128]{1,0:T(8,128)S(1)} %get-tuple-element.39), channel_id=1, source_target_pairs={{0,8},{1,9},{2,10},{3,11},{4,12},{5,13},{6,14},{7,15},{8,0},{9,1},... | collective-permute-start | bytes 196616 | tf_op jit(solution)/shard_map/ppermute | solution.py:286
  38.5 4.9 %collective-permute-start.16 = (f32[128,128]{1,0:T(8,128)S(1)}, f32[128,128]{1,0:T(8,128)S(1)}, u32[]{:S(2)}, u32[]{:S(2)}) collective-permute-start(f32[128,128]{1,0:T(8,128)S(1)} %get-tuple-element.40), channel_id=1, source_target_pairs={{0,12},{1,13},{2,14},{3,15},{4,8},{5,9},{6,10},{7,11},{8,4},{9,5},... | collective-permute-start | bytes 196616 | tf_op jit(solution)/shard_map/ppermute | solution.py:286
  39.7 10.7 %collective-permute-start.14 = (f32[128,256]{1,0:T(8,128)S(1)}, f32[128,256]{1,0:T(8,128)S(1)}, u32[]{:S(2)}, u32[]{:S(2)}) collective-permute-start(f32[128,256]{1,0:T(8,128)S(1)} %get-tuple-element.36), channel_id=1, source_target_pairs={{0,2},{1,3},{2,0},{3,1},{4,6},{5,7},{6,4},{7,5},{8,10},{9,11},{10,... | collective-permute-start | bytes 393224 | tf_op jit(solution)/shard_map/ppermute | solution.py:286
  44.7 7.0 %collective-permute-start.17 = (f32[64,256]{1,0:T(8,128)S(1)}, f32[64,256]{1,0:T(8,128)S(1)}, u32[]{:S(2)}, u32[]{:S(2)}) collective-permute-start(f32[64,256]{1,0:T(8,128)S(1)} %get-tuple-element.53), channel_id=1, source_target_pairs={{0,1},{1,3},{2,0},{3,2},{4,5},{5,7},{6,4},{7,6},{8,9},{9,11},{10,8... | collective-permute-start | bytes 196616 | tf_op jit(solution)/shard_map/ppermute | solution.py:286
  44.9 7.4 %collective-permute-start.18 = (f32[64,256]{1,0:T(8,128)S(1)}, f32[64,256]{1,0:T(8,128)S(1)}, u32[]{:S(2)}, u32[]{:S(2)}) collective-permute-start(f32[64,256]{1,0:T(8,128)S(1)} %get-tuple-element.52.keep), channel_id=1, source_target_pairs={{1,2},{2,1},{5,6},{6,5},{9,10},{10,9},{13,14},{14,13},{17,18},{18,... | collective-permute-start | bytes 196616 | tf_op jit(solution)/shard_map/ppermute | solution.py:286
